TPU v7x, 32 devices: a whole 2x2x4 slice. The times are simulated.
32 devices in a mesh: prow: 8 (over y, x, core), pcol: 4 (over z).
Axes of the slice: x: 2, y: 2, z: 4, core: 2. Of those that a mesh axis runs over, the one named last changes fastest.
Arguments:
- matrix: bfloat16 [16384, 6144], P('prow', 'pcol')
- pivots: int32 [512], replicated, may hold values from 512 to 16383, as said below
- unit_inverse: bfloat16 [512, 512], replicated, as said below
Outputs:
- factored: bfloat16 [16384, 6144], P('prow', 'pcol')
Inputs may be any that keep to these rules, and one draw needn't show every extreme that they name: pivots are distinct rows, none among the first 512. unit_inverse is unit lower triangular.
All inputs are finite; a program needn't handle non-finite values.
Results may differ from a plain program's by a relative error of at most 0.0041.
Values may be sent and summed in bfloat16 or wider, within the bound.
No kernel may reach another device: no remote copies, remote signals or barrier semaphores. Data moves between devices by JAX's collectives and lax.ppermute only.
A program may use at most 64 MiB of HBM per device.

v0:
```python
import jax
import jax.numpy as jnp
from jax import lax
from jax.sharding import PartitionSpec as P


def from_root(value, axis, root):
    mine = lax.axis_index(axis) == root
    return lax.psum(jnp.where(mine, value, jnp.zeros_like(value)), axis)


def per_device(matrix, pivots, unit_inverse):
    local_rows, local_cols = matrix.shape
    width = unit_inverse.shape[0]
    row_place = lax.axis_index("prow")
    col_place = lax.axis_index("pcol")
    panel_rows = from_root(matrix[:, :width], "pcol", 0)
    owner_dev = pivots // local_rows
    within = pivots % local_rows
    picked = jnp.take(matrix, within, axis=0)
    mine = (owner_dev == row_place)[:, None]
    masked = jnp.where(mine, picked.astype(jnp.float32), 0.0)
    full_rows = lax.psum(masked, "prow").astype(jnp.bfloat16)
    upper = jnp.dot(unit_inverse, full_rows, preferred_element_type=jnp.float32).astype(
        jnp.bfloat16
    )
    displaced = from_root(matrix[:width], "prow", 0)
    global_row = row_place * local_rows + jnp.arange(local_rows, dtype=jnp.int32)
    matches = pivots[None, :] == global_row[:, None]
    has_pivot = jnp.any(matches, axis=1)
    slot_index = jnp.sum(jnp.where(matches, jnp.arange(width, dtype=jnp.int32)[None, :], 0), axis=1)
    swapped = jnp.where(has_pivot[:, None], jnp.take(displaced, slot_index, axis=0), matrix)
    updated = (
        swapped.astype(jnp.float32) - jnp.dot(panel_rows, upper, preferred_element_type=jnp.float32)
    ).astype(jnp.bfloat16)
    upper_rows = jnp.take(upper, jnp.minimum(global_row, width - 1), axis=0)
    result = jnp.where((global_row < width)[:, None], upper_rows, updated)
    global_col = col_place * local_cols + jnp.arange(local_cols, dtype=jnp.int32)
    return jnp.where((global_col < width)[None, :], matrix, result)


def solution(mesh):
    return jax.shard_map(
        per_device,
        mesh=mesh,
        in_specs=(P("prow", "pcol"), P(), P()),
        out_specs=P("prow", "pcol"),
        check_vma=False,
    )
```

profile of v0, /device:TPU:13, one launch (start us, length us, event | category | flops | bytes accessed | tf_op | source)
XLA Modules:
  0.0 182.7 jit_solution(15735781821528312352)
XLA Ops:
  6.5 0.0 copy-start
  6.5 0.0 all-reduce.4.cloned.1.call-start
  6.5 2.7 %slice_select_fusion.1 = bf16[512,1536]{1,0:T(8,128)(2,1)} fusion(bf16[2048,1536]{1,0:T(8,128)(2,1)} %param.5, pred[]{:T(512)S(6)} %eq.32), kind=kLoop, calls=%fused_computation.13 | loop fusion | flops 786432 | bytes 3145729 | tf_op jit(solution)/shard_map/jit(_where)/select_n | solution.py:9
  9.3 0.0 all-reduce.4.cloned.1.call-update
  9.3 0.0 all-reduce.6.cloned.1.call-start
  9.3 0.0 copy-start.2
  9.4 3.1 %slice_select_fusion = bf16[2048,512]{1,0:T(8,128)(2,1)} fusion(bf16[2048,1536]{1,0:T(8,128)(2,1)} %param.5, pred[]{:T(512)S(6)} %eq.33), kind=kLoop, calls=%fused_computation.12 | loop fusion | flops 1048576 | bytes 4194305 | tf_op jit(solution)/shard_map/jit(_where)/select_n | solution.py:9
  12.5 0.0 all-reduce.6.cloned.1.call-update
  12.5 0.0 copy-done.2
  12.6 7.2 %gather_fusion = bf16[512,1536]{1,0:T(8,128)(2,1)S(1)} fusion(bf16[2048,1536]{1,0:T(8,128)(2,1)} %param.5, s32[1024]{0:T(1024)S(1)} %pad_clamp_fusion), kind=kCustom, calls=%fused_computation.2 | custom fusion | bytes 3147776 | tf_op jit(solution)/shard_map/jit(_take)/gather | solution.py:20
  19.8 2.1 %convert_select_fusion = f32[512,1536]{1,0:T(8,128)} fusion(bf16[512,1536]{1,0:T(8,128)(2,1)S(1)} %gather_fusion, pred[512]{0:T(512)(128)(4,1)S(1)} %get-tuple-element.6, pred[512]{0:T(512)(128)(4,1)S(1)} %get-tuple-element.8), kind=kLoop, calls=%fused_computation.10 | loop fusion | flops 2359296 | bytes 4719616 | tf_op jit(solution)/shard_map/jit(_where)/select_n | solution.py:22
  21.8 78.9 %all-reduce.7 = bf16[512,1536]{1,0:T(8,128)(2,1)S(1)} all-reduce(f32[512,1536]{1,0:T(8,128)} %convert_select_fusion), channel_id=1, replica_groups=mesh['prow'=8,'pcol'=4] {'prow'}, use_global_device_ids=true, to_apply=%region_0.1 | all-reduce | flops 786432 | bytes 4718592 | tf_op jit(solution)/shard_map/psum | solution.py:23
  100.7 0.0 copy-done
  100.8 2.3 %convolution_convert_fusion = bf16[1536,512]{1,0:T(8,128)(2,1)} fusion(bf16[512,512]{1,0:T(8,128)(2,1)S(1)} %copy-done, bf16[512,1536]{1,0:T(8,128)(2,1)S(1)} %all-reduce.7), kind=kOutput, calls=%fused_computation.11 | convolution fusion | flops 806092800 | bytes 3670016 | tf_op jit(solution)/shard_map/dot_general | solution.py:24
  103.0 1.7 copy.5
  104.8 10.1 %gather_fusion.1 = bf16[2048,1536]{1,0:T(8,128)(2,1)} fusion(bf16[512,1536]{1,0:T(8,128)(2,1)S(1)} %copy.5, s32[2048]{0:T(1024)S(1)} %get-tuple-element.10), kind=kCustom, calls=%fused_computation.clone | custom fusion | bytes 12591104 | tf_op jit(solution)/shard_map/jit(_take)/gather | solution.py:36
  114.9 0.9 compare_reduce_fusion
  115.7 0.9 fusion.1
  116.7 0.0 copy-start.1
  116.7 0.0 all-reduce.4.cloned.1.call-done
  116.7 15.0 %gather_fusion.2 = bf16[2048,1536]{1,0:T(8,128)(2,1)} fusion(bf16[512,1536]{1,0:T(8,128)(2,1)} %all-reduce.4.cloned.1.call-done, s32[2048]{0:T(1024)S(1)} %fusion.5), kind=kCustom, calls=%fused_computation.1.clone | custom fusion | bytes 12591104 | tf_op jit(solution)/shard_map/jit(_take)/gather | solution.py:32
  131.7 33.1 %all-reduce.6.cloned.1.call-done = bf16[2048,512]{1,0:T(8,128)(2,1)} async-done(((bf16[2048,512]{1,0:T(8,128)(2,1)}), bf16[2048,512]{1,0:T(8,128)(2,1)}) %all-reduce.6.cloned.1.call-update) | async-done | bytes 2097168 | tf_op jit(solution)/shard_map/psum | solution.py:9
  164.8 0.0 copy-done.1
  164.8 11.0 %fusion = bf16[2048,1536]{1,0:T(8,128)(2,1)} fusion(bf16[2048,1536]{1,0:T(8,128)(2,1)} %param.5, bf16[2048,1536]{1,0:T(8,128)(2,1)} %gather_fusion.1, pred[2048]{0:T(1024)(128)(4,1)S(1)} %get-tuple-element.11, pred[2048]{0:T(1024)(128)(4,1)S(1)} %get-tuple-element.12, pred[1536]{0:T(1024)(128)(4,1)S(1)} %add_compare_fusion, ...), kind=kOutput, calls=%fused_computation.6 | convolution fusion | flops 3246391296 | bytes 28845568 | tf_op jit(solution)/shard_map/dot_general | solution.py:34
  (7 shorter events, 0.1 us)
Async XLA Ops:
  6.5 94.2 %copy-start = (bf16[512,512]{1,0:T(8,128)(2,1)S(1)}, bf16[512,512]{1,0:T(8,128)(2,1)}, u32[]{:S(2)}) copy-start(bf16[512,512]{1,0:T(8,128)(2,1)} %param.7) | copy-start | bytes 1572868
  6.5 110.2 %all-reduce.4.cloned.1.call-start = ((), (), s32[]{:S(2)}) async-start(), calls=%async_computation | async-start | bytes 3145728 | tf_op jit(solution)/shard_map/psum | solution.py:9
  9.3 155.5 %all-reduce.6.cloned.1.call-start = ((), (), s32[]{:S(2)}) async-start(), calls=%async_computation.1 | async-start | bytes 4194304 | tf_op jit(solution)/shard_map/psum | solution.py:9
  9.3 3.2 %copy-start.2 = (s32[512]{0:T(512)S(1)}, s32[512]{0:T(512)}, u32[]{:S(2)}) copy-start(s32[512]{0:T(512)} %param.6) | copy-start | bytes 6148
  116.7 48.2 %copy-start.1 = (bf16[1536,512]{1,0:T(8,128)(2,1)S(1)}, bf16[1536,512]{1,0:T(8,128)(2,1)}, u32[]{:S(2)}) copy-start(bf16[1536,512]{1,0:T(8,128)(2,1)} %convolution_convert_fusion) | copy-start | bytes 4718596
Sparse Core Ops, SparseCore 0:
  10.6 66.7 all-reduce.3
  79.9 84.9 all-reduce.5
where the time goes:
time: 186 us; the launch traced here: 183 us
  blocking collectives  78.9 us (42%)
  local copies, waits for them, and re-layouts  34 us (18%)
  waiting for transfers between devices  33.2 us (18%)
  between operations  13.5 us (7%)
  matrix products  13.3 us (7%)
  other arithmetic  9.77 us (5%)
    psum x1, blocking collectives, per_device(): full_rows = lax.psum(masked, 'prow').astype(jnp.bfloat16)  78.9 us
    psum x2, waiting for transfers between devices, from_root(): return lax.psum(jnp.where(mine, value, jnp.zeros_like(value)), axis)  33.1 us
    gather x1, local copies, waits for them, and re-layouts, per_device(): jnp.take(displaced, slot_index, axis=0)  15 us
    dot_general x1, matrix products, per_device(): jnp.dot(panel_rows, upper, preferred_element_type=jnp.float32)  11 us
    gather x1, local copies, waits for them, and re-layouts, per_device(): upper_rows = jnp.take(upper, jnp.minimum(global_row, width - 1), axis=0)  10.1 us
    gather x1, local copies, waits for them, and re-layouts, per_device(): picked = jnp.take(matrix, within, axis=0)  7.2 us
    select_n x2, other arithmetic, from_root(): return lax.psum(jnp.where(mine, value, jnp.zeros_like(value)), axis)  5.85 us
  transfers between devices with their start and end apart: 2, of which 1 were waited for; matrix products, arithmetic and copies ran while one was open for 24% of the time, Pallas kernels for 0%

commit v1 on v0

v1 whole, which is shorter than its diff:
```python
import functools

import jax
import jax.numpy as jnp
from jax import lax
from jax.experimental import pallas as pl
from jax.experimental.pallas import tpu as pltpu
from jax.sharding import PartitionSpec as P

GROUPS = 4
VMEM_BYTES = 48 * 2**20


def pick_kernel(place_ref, pivots_ref, matrix_ref, out_ref, onehot_ref):
    rows = matrix_ref.shape[0]
    width = pivots_ref.shape[0]

    @pl.when(pl.program_id(0) == 0)
    def _():
        row = lax.broadcasted_iota(jnp.int32, (width, rows), 1) + place_ref[0] * rows
        onehot_ref[...] = jnp.where(pivots_ref[...] == row, 1.0, 0.0).astype(jnp.bfloat16)

    out_ref[:width] = jnp.dot(
        onehot_ref[...], matrix_ref[...], preferred_element_type=jnp.float32
    ).astype(jnp.bfloat16)
    first = matrix_ref[:width]
    out_ref[width:] = jnp.where(place_ref[0] == 0, first, jnp.zeros_like(first))


def pick(place, pivots, matrix):
    rows, cols = matrix.shape
    width = pivots.shape[0]
    block = 256
    return pl.pallas_call(
        pick_kernel,
        grid_spec=pltpu.PrefetchScalarGridSpec(
            num_scalar_prefetch=1,
            grid=(cols // block,),
            in_specs=[
                pl.BlockSpec((width, 1), lambda i, s: (0, 0)),
                pl.BlockSpec((rows, block), lambda i, s: (0, i)),
            ],
            out_specs=pl.BlockSpec((2 * width, block), lambda i, s: (0, i)),
            scratch_shapes=[pltpu.VMEM((width, rows), jnp.bfloat16)],
        ),
        out_shape=jax.ShapeDtypeStruct((2 * width, cols), jnp.bfloat16),
        compiler_params=pltpu.CompilerParams(vmem_limit_bytes=VMEM_BYTES),
        cost_estimate=pl.CostEstimate(
            flops=2 * width * rows * cols, bytes_accessed=2 * rows * cols, transcendentals=0
        ),
        name="pick_rows",
    )(place, pivots[:, None], matrix)


def update_kernel(first_row, pick_source, n_sources, place_ref, pivots_ref, matrix_ref,
                  displaced_ref, upper_ref, *rest):
    sources = rest[:n_sources]
    out_ref, factors_ref, sem = rest[-3:]
    step = pl.program_id(0)
    block = matrix_ref.shape[0]
    width = upper_ref.shape[0]
    group_rows = factors_ref.shape[0]
    row_place, col_place, rows = place_ref[0], place_ref[1], place_ref[2]

    @pl.when(step == 0)
    def _():
        for number, source in enumerate(sources):
            @pl.when(pick_source(col_place) == number)
            def _():
                view = source
                if number == 0:
                    view = source.at[pl.ds(first_row, group_rows), pl.ds(0, width)]
                copy = pltpu.make_async_copy(view, factors_ref, sem)
                copy.start()
                copy.wait()

    local = first_row + step * block
    row = lax.broadcasted_iota(jnp.int32, (block, width), 0) + row_place * rows + local
    match = pivots_ref[...] == row
    onehot = jnp.where(match, 1.0, 0.0)
    has_pivot = jnp.max(onehot, axis=1, keepdims=True) > 0.0
    moved = jnp.dot(onehot.astype(jnp.bfloat16), displaced_ref[...],
                    preferred_element_type=jnp.float32)
    factors = factors_ref[pl.ds(pl.multiple_of(step * block, block), block), :]
    product = jnp.dot(factors, upper_ref[...], preferred_element_type=jnp.float32)
    swapped = jnp.where(has_pivot, moved, matrix_ref[...].astype(jnp.float32))
    out_ref[...] = (swapped - product).astype(jnp.bfloat16)

    if first_row < width:
        @pl.when((row_place == 0) & (local < width))
        def _():
            start = pl.multiple_of(jnp.minimum(local, width - block), block)
            out_ref[...] = upper_ref[pl.ds(start, block), :]

    @pl.when(col_place == 0)
    def _():
        out_ref[:, :width] = matrix_ref[:, :width]


def update(first_row, group_rows, pick_source, place, pivots, matrix, displaced, upper,
           received, out):
    rows, cols = matrix.shape
    width = upper.shape[0]
    block = 256
    offset = first_row // block
    sources = [matrix] + list(received)
    whole = lambda i, s: (0, 0)
    in_specs = [
        pl.BlockSpec((1, width), whole),
        pl.BlockSpec((block, cols), lambda i, s: (i + offset, 0)),
        pl.BlockSpec((width, cols), whole),
        pl.BlockSpec((width, cols), whole),
    ] + [pl.BlockSpec(memory_space=pl.ANY)] * len(sources)
    operands = [place, pivots[None, :], matrix, displaced, upper] + sources
    aliases = {}
    if out is not None:
        in_specs.append(pl.BlockSpec(memory_space=pl.ANY))
        aliases = {len(operands): 0}
        operands.append(out)
    return pl.pallas_call(
        functools.partial(update_kernel, first_row, pick_source, len(sources)),
        grid_spec=pltpu.PrefetchScalarGridSpec(
            num_scalar_prefetch=1,
            grid=(group_rows // block,),
            in_specs=in_specs,
            out_specs=pl.BlockSpec((block, cols), lambda i, s: (i + offset, 0)),
            scratch_shapes=[
                pltpu.VMEM((group_rows, width), jnp.bfloat16),
                pltpu.SemaphoreType.DMA,
            ],
        ),
        out_shape=jax.ShapeDtypeStruct((rows, cols), jnp.bfloat16),
        input_output_aliases=aliases,
        compiler_params=pltpu.CompilerParams(vmem_limit_bytes=VMEM_BYTES),
        cost_estimate=pl.CostEstimate(
            flops=4 * group_rows * width * cols,
            bytes_accessed=4 * group_rows * cols + 4 * width * cols,
            transcendentals=0,
        ),
        name="update_rows",
    )(*operands)


def reduce_scatter(value, axis, size, bits):
    place = lax.axis_index(axis)
    for bit in bits:
        pairs = [(i, i ^ (1 << bit)) for i in range(size)]
        half = value.shape[0] // 2
        mine = (place >> bit) & 1
        sent = lax.dynamic_slice_in_dim(value, (1 - mine) * half, half, 0)
        kept = lax.dynamic_slice_in_dim(value, mine * half, half, 0)
        value = kept + lax.ppermute(sent, axis, pairs)
    return value


def all_gather(value, axis, size, bits):
    place = lax.axis_index(axis)
    for bit in reversed(bits):
        pairs = [(i, i ^ (1 << bit)) for i in range(size)]
        other = lax.ppermute(value, axis, pairs)
        mine = (place >> bit) & 1
        both = jnp.concatenate([value, other, value], axis=0)
        value = lax.dynamic_slice_in_dim(both, mine * value.shape[0], 2 * value.shape[0], 0)
    return value


def sum_rows(value, axis, size):
    count = size.bit_length() - 1
    inner = list(range(1, count))
    part = reduce_scatter(value, axis, size, [0])
    half = part.shape[0] // 2
    parts = []
    for piece, bits in ((part[:half], inner), (part[half:], inner[::-1])):
        piece = reduce_scatter(piece, axis, size, bits)
        parts.append(all_gather(piece, axis, size, bits))
    return all_gather(jnp.concatenate(parts, axis=0), axis, size, [0])


def spread(panel, axis, size):
    middle = size // 2
    received = [lax.ppermute(panel, axis, [(0, middle)])]
    if middle > 1:
        received.append(lax.ppermute(received[0], axis, [(middle, middle - 1)]))
    if middle + 1 < size:
        received.append(lax.ppermute(received[0], axis, [(middle, middle + 1)]))
    distance = 1
    held = None
    while middle - distance > 1 or middle + distance + 1 < size:
        held = received[1] + received[2] if held is None else held
        pairs = []
        if middle - distance > 1:
            pairs.append((middle - distance, middle - distance - 1))
        if middle + distance + 1 < size:
            pairs.append((middle + distance, middle + distance + 1))
        held = lax.ppermute(held, axis, pairs)
        received.append(held)
        distance += 1
    return received


def source_of(size):
    middle = size // 2

    def pick_source(place):
        away = jnp.abs(place - middle)
        number = jnp.where(away >= 2, away + 1, jnp.where(place < middle, 1, 2) + 1)
        number = jnp.where(away == 0, 1, jnp.where(away == 1, number, away + 2))
        return jnp.where(place == 0, 0, number)

    return pick_source


def per_device(n_prow, n_pcol, matrix, pivots, unit_inverse):
    rows, cols = matrix.shape
    width = unit_inverse.shape[0]
    row_place = lax.axis_index("prow")
    col_place = lax.axis_index("pcol")
    place = jnp.stack([row_place, col_place, jnp.full_like(row_place, rows)]).astype(jnp.int32)
    group_rows = rows // GROUPS
    received = []
    for group in range(GROUPS):
        start = group * group_rows
        received.append(spread(matrix[start : start + group_rows, :width], "pcol", n_pcol))
    picked = pick(place, pivots, matrix)
    summed = sum_rows(picked, "prow", n_prow)
    full_rows, displaced = summed[:width], summed[width:]
    upper = jnp.dot(unit_inverse, full_rows, preferred_element_type=jnp.float32).astype(
        jnp.bfloat16
    )
    out = None
    for group in range(GROUPS):
        out = update(group * group_rows, group_rows, source_of(n_pcol), place, pivots, matrix,
                     displaced, upper, received[group], out)
    return out


def solution(mesh):
    return jax.shard_map(
        functools.partial(per_device, mesh.shape["prow"], mesh.shape["pcol"]),
        mesh=mesh,
        in_specs=(P("prow", "pcol"), P(), P()),
        out_specs=P("prow", "pcol"),
        check_vma=False,
    )
```

time: 186 us -> 141 us (0.76)
  blocking collectives: 78.9 us -> 0 us
  waiting for transfers between devices: 33.2 us -> 68.1 us
  Pallas kernels: 0 us -> 26.6 us
  starting transfers between devices: 0.04 us -> 20.3 us
  local copies, waits for them, and re-layouts: 34 us -> 14.9 us
  between operations: 13.5 us -> 0.33 us
  matrix products: 13.3 us -> 2.39 us
  other arithmetic: 9.77 us -> 5.93 us
    psum x1 -> x0, blocking collectives: 78.9 us -> none  [per_device(): full_rows = lax.psum(masked, 'prow').astype(jnp.bfloat16)]
    ppermute x0 -> x22, waiting for transfers between devices: none -> 68.1 us  [the longest x4 41.6 us: spread(): received.append(lax.ppermute(received[0], axis, [(middle, middle - 1)]))]
    psum x2 -> x0, waiting for transfers between devices: 33.1 us -> none  [from_root(): return lax.psum(jnp.where(mine, value, jnp.zeros_like(value)), axis)]
    gather x3 -> x0, local copies, waits for them, and re-layouts: 32.2 us -> none  [the longest x1 15 us: per_device(): jnp.take(displaced, slot_index, axis=0)]
    pallas_call x0 -> x5, Pallas kernels: none -> 26.6 us  [the longest x4 18.8 us: update(): pl.pallas_call(functools.partial(update_kernel, first_row, pick_source, l...]
    ppermute x0 -> x22, starting transfers between devices: none -> 20.3 us  [the longest x5 6.33 us: all_gather(): other = lax.ppermute(value, axis, pairs)]
    dot_general x1 -> x0, matrix products: 11 us -> none  [per_device(): jnp.dot(panel_rows, upper, preferred_element_type=jnp.float32)]
    select_n x3 -> x0, other arithmetic: 7.93 us -> none  [the longest x2 5.85 us: from_root(): return lax.psum(jnp.where(mine, value, jnp.zeros_like(value)), axis)]
  transfers between devices with their start and end apart: 2 -> 22, of which waited for: 1 -> 11; matrix products, arithmetic and copies ran while one was open for 24% -> 9% of each run, Pallas kernels for 0% -> 10%
where the time goes in v1:
time: 141 us; the launch traced here: 139 us
  waiting for transfers between devices  68.1 us (48%)
  Pallas kernels  26.6 us (19%)
  starting transfers between devices  20.3 us (14%)
  local copies, waits for them, and re-layouts  14.9 us (11%)
  other arithmetic  5.93 us (4%)
  matrix products  2.39 us (2%)
    ppermute x4, waiting for transfers between devices, spread(): received.append(lax.ppermute(received[0], axis, [(middle, middle - 1)]))  41.6 us
    pallas_call x4, Pallas kernels, update(): pl.pallas_call(functools.partial(update_kernel, first_row, pick_source, l...  18.8 us
    ppermute x5, waiting for transfers between devices, reduce_scatter(): value = kept + lax.ppermute(sent, axis, pairs)  16.5 us
    ppermute x5, waiting for transfers between devices, all_gather(): other = lax.ppermute(value, axis, pairs)  9.96 us
    pallas_call x1, Pallas kernels, pick(): pl.pallas_call(pick_kernel, grid_spec=pltpu.PrefetchScalarGridSpec(num_sc...  7.78 us
    unnamed x14, local copies, waits for them, and re-layouts  7.08 us
    ppermute x5, starting transfers between devices, all_gather(): other = lax.ppermute(value, axis, pairs)  6.33 us
    ppermute x4, starting transfers between devices, spread(): received.append(lax.ppermute(received[0], axis, [(middle, middle - 1)]))  5.17 us
  transfers between devices with their start and end apart: 22, of which 11 were waited for; matrix products, arithmetic and copies ran while one was open for 9% of the time, Pallas kernels for 10%

profile of v1, /device:TPU:13, one launch (start us, length us, event | category | flops | bytes accessed | tf_op | source)
XLA Modules:
  0.0 138.5 jit_solution(17932737624164691220)
XLA Ops:
  1.0 7.8 %pick_rows.1 = bf16[1024,1536]{1,0:T(8,128)(2,1)S(1)} custom-call(s32[3]{0:T(128)S(1)} %pad_add_fusion.place_ref, s32[512,1]{1,0:T(8,128)S(1)} %copy.8.pivots_ref, bf16[2048,1536]{1,0:T(8,128)(2,1)} %rest_0_.7), custom_call_target="tpu_custom_call" | custom-call | flops 3221225472 | bytes 6291456 | tf_op jit(solution)/shard_map/pick_rows/pallas_call | solution.py:34
  8.8 1.4 %constant_dynamic-slice_fusion.5 = bf16[512,1536]{1,0:T(8,128)(2,1)} fusion(bf16[1024,1536]{1,0:T(8,128)(2,1)S(1)} %pick_rows.1, s32[]{:T(128)S(6)} %select_n.46), kind=kLoop, calls=%fused_computation.40 | loop fusion | bytes 3145732 | tf_op jit(solution)/shard_map/dynamic_slice | solution.py:150
  11.6 3.2 %collective-permute-done = bf16[512,1536]{1,0:T(8,128)(2,1)S(1)} collective-permute-done((bf16[512,1536]{1,0:T(8,128)(2,1)}, bf16[512,1536]{1,0:T(8,128)(2,1)S(1)}, u32[]{:S(2)}, u32[]{:S(2)}) %collective-permute-start) | collective-permute-done | bytes 1572896 | tf_op jit(solution)/shard_map/ppermute | solution.py:152
  14.9 1.9 %dynamic-slice_add_fusion = bf16[512,1536]{1,0:T(8,128)(2,1)S(1)} fusion(bf16[512,1536]{1,0:T(8,128)(2,1)S(1)} %collective-permute-done, bf16[1024,1536]{1,0:T(8,128)(2,1)} %copy-done.1, s32[]{:T(128)S(6)} %select_n.45), kind=kLoop, calls=%fused_computation.4 | loop fusion | flops 3145728 | bytes 4718596 | tf_op jit(solution)/shard_map/add | solution.py:152
  16.9 1.3 collective-permute-start.1
  18.5 8.8 %collective-permute-done.1 = bf16[128,1536]{1,0:T(8,128)(2,1)S(1)} collective-permute-done((bf16[128,1536]{1,0:T(8,128)(2,1)S(1)}, bf16[128,1536]{1,0:T(8,128)(2,1)S(1)}, u32[]{:S(2)}, u32[]{:S(2)}) %collective-permute-start.1) | collective-permute-done | bytes 393248 | tf_op jit(solution)/shard_map/ppermute | solution.py:152
  29.1 3.6 %collective-permute-done.2 = bf16[64,1536]{1,0:T(8,128)(2,1)S(1)} collective-permute-done((bf16[64,1536]{1,0:T(8,128)(2,1)S(1)}, bf16[64,1536]{1,0:T(8,128)(2,1)S(1)}, u32[]{:S(2)}, u32[]{:S(2)}) %collective-permute-start.2) | collective-permute-done | bytes 196640 | tf_op jit(solution)/shard_map/ppermute | solution.py:152
  33.4 1.0 collective-permute-start.7
  34.4 3.0 %collective-permute-done.3 = bf16[64,1536]{1,0:T(8,128)(2,1)S(1)} collective-permute-done((bf16[64,1536]{1,0:T(8,128)(2,1)S(1)}, bf16[64,1536]{1,0:T(8,128)(2,1)S(1)}, u32[]{:S(2)}, u32[]{:S(2)}) %collective-permute-start.3) | collective-permute-done | bytes 196640 | tf_op jit(solution)/shard_map/ppermute | solution.py:160
  37.7 1.3 collective-permute-start.4
  39.6 7.0 %collective-permute-done.4 = bf16[128,1536]{1,0:T(8,128)(2,1)S(1)} collective-permute-done((bf16[128,1536]{1,0:T(8,128)(2,1)S(1)}, bf16[128,1536]{1,0:T(8,128)(2,1)S(1)}, u32[]{:S(2)}, u32[]{:S(2)}) %collective-permute-start.4) | collective-permute-done | bytes 393248 | tf_op jit(solution)/shard_map/ppermute | solution.py:160
  48.3 2.2 %copy-done.5 = bf16[1536,1536]{1,0:T(8,128)(2,1)} copy-done((bf16[1536,1536]{1,0:T(8,128)(2,1)}, bf16[1536,1536]{1,0:T(8,128)(2,1)S(1)}, u32[]{:S(2)}) %copy-start.5) | copy-done | bytes 4718616
  50.5 1.4 pad_maximum_fusion
  51.9 3.4 %collective-permute-start.9 = (bf16[512,1536]{1,0:T(8,128)(2,1)}, bf16[512,1536]{1,0:T(8,128)(2,1)}, u32[]{:S(2)}, u32[]{:S(2)}) collective-permute-start(bf16[512,1536]{1,0:T(8,128)(2,1)} %pad_maximum_fusion), channel_id=1, source_target_pairs={{0,4},{4,0},{8,12},{12,8},{16,20},{20,16},{24,28},{28,24},{1,5},{5... | collective-permute-start | bytes 4718600 | tf_op jit(solution)/shard_map/ppermute | solution.py:160
  55.4 2.9 %fusion.13 = (bf16[512,512]{1,0:T(8,128)(2,1)}, bf16[512,512]{1,0:T(8,128)(2,1)}, bf16[512,512]{1,0:T(8,128)(2,1)}, bf16[512,512]{1,0:T(8,128)(2,1)}) fusion(bf16[2048,1536]{1,0:T(8,128)(2,1)} %rest_0_.7), kind=kLoop, calls=%fused_computation.42 | loop fusion | bytes 4194304 | tf_op jit(solution)/shard_map/slice | solution.py:223
  61.1 1.3 collective-permute-start.20
  63.1 1.3 collective-permute-start.17
  64.4 2.7 %constant_dynamic-update-slice_fusion.2 = bf16[1536,1536]{1,0:T(8,128)(2,1)} fusion(bf16[1536,1536]{1,0:T(8,128)(2,1)} %copy-done.5, bf16[512,1536]{1,0:T(8,128)(2,1)} %collective-permute-done.9), kind=kLoop, calls=%fused_computation.31 | loop fusion | bytes 3145728
  67.0 0.9 constant_dynamic-update-slice_fusion.1
  68.5 0.9 constant_dynamic-update-slice_fusion
  70.1 2.4 %fusion.upper_ref = bf16[512,1536]{1,0:T(8,128)(2,1)S(1)} fusion(bf16[512,512]{1,0:T(8,128)(2,1)S(1)} %copy-done, bf16[1536,1536]{1,0:T(8,128)(2,1)} %constant_dynamic-update-slice_fusion, s32[]{:T(128)S(6)} %select_n.59), kind=kOutput, calls=%fused_computation.1 | convolution fusion | flops 806092800 | bytes 3670020 | tf_op jit(solution)/shard_map/dot_general | solution.py:227
  72.5 1.3 collective-permute-start.14
  73.8 14.6 %collective-permute-done.20.rest_2_ = bf16[512,512]{1,0:T(8,128)(2,1)S(1)} collective-permute-done((bf16[512,512]{1,0:T(8,128)(2,1)S(1)}, bf16[512,512]{1,0:T(8,128)(2,1)S(1)}, u32[]{:S(2)}, u32[]{:S(2)}) %collective-permute-start.20) | collective-permute-done | bytes 524320 | tf_op jit(solution)/shard_map/ppermute | solution.py:183
  89.1 1.3 collective-permute-start.11
  90.4 10.6 %collective-permute-done.17.rest_2_ = bf16[512,512]{1,0:T(8,128)(2,1)S(1)} collective-permute-done((bf16[512,512]{1,0:T(8,128)(2,1)S(1)}, bf16[512,512]{1,0:T(8,128)(2,1)S(1)}, u32[]{:S(2)}, u32[]{:S(2)}) %collective-permute-start.17) | collective-permute-done | bytes 524320 | tf_op jit(solution)/shard_map/ppermute | solution.py:183
  101.7 1.5 %constant_dynamic-slice_fusion.displaced_ref = bf16[512,1536]{1,0:T(8,128)(2,1)S(1)} fusion(bf16[1536,1536]{1,0:T(8,128)(2,1)} %constant_dynamic-update-slice_fusion, s32[]{:T(128)S(6)} %add.82), kind=kLoop, calls=%fused_computation.35 | loop fusion | bytes 3145732 | tf_op jit(solution)/shard_map/slice | solution.py:226
  103.2 4.7 %update_rows.4.rest_4_ = bf16[2048,1536]{1,0:T(8,128)(2,1)} custom-call(s32[3]{0:T(128)S(1)} %pad_add_fusion.place_ref, s32[1,512]{1,0:T(1,128)S(1)} %bitcast.8, bf16[2048,1536]{1,0:T(8,128)(2,1)} %rest_0_.7, bf16[512,1536]{1,0:T(8,128)(2,1)S(1)} %constant_dynamic-slice_fusion.displaced_ref, bf16[512,1536]{1,0:T(8,128)(2,1)S(1)} %fusion.upper_ref, ...), custom_call_target="tpu_custom_call" | custom-call | flops 1610612736 | bytes 6291456 | tf_op jit(solution)/shard_map/update_rows/pallas_call | solution.py:120
  108.0 4.7 %update_rows.5.rest_4_ = bf16[2048,1536]{1,0:T(8,128)(2,1)} custom-call(s32[3]{0:T(128)S(1)} %pad_add_fusion.place_ref, s32[1,512]{1,0:T(1,128)S(1)} %bitcast.9, bf16[2048,1536]{1,0:T(8,128)(2,1)} %rest_0_.7, bf16[512,1536]{1,0:T(8,128)(2,1)S(1)} %constant_dynamic-slice_fusion.displaced_ref, ...), custom_call_target="tpu_custom_call", output_to_operand_aliasing={{}: (9, {})} | custom-call | flops 1610612736 | bytes 6291456 | tf_op jit(solution)/shard_map/update_rows/pallas_call | solution.py:120
  112.7 9.9 %collective-permute-done.14.rest_2_ = bf16[512,512]{1,0:T(8,128)(2,1)S(1)} collective-permute-done((bf16[512,512]{1,0:T(8,128)(2,1)S(1)}, bf16[512,512]{1,0:T(8,128)(2,1)S(1)}, u32[]{:S(2)}, u32[]{:S(2)}) %collective-permute-start.14) | collective-permute-done | bytes 524320 | tf_op jit(solution)/shard_map/ppermute | solution.py:183
  122.6 4.7 %update_rows.6.rest_4_ = bf16[2048,1536]{1,0:T(8,128)(2,1)} custom-call(s32[3]{0:T(128)S(1)} %pad_add_fusion.place_ref, s32[1,512]{1,0:T(1,128)S(1)} %bitcast.10, bf16[2048,1536]{1,0:T(8,128)(2,1)} %rest_0_.7, bf16[512,1536]{1,0:T(8,128)(2,1)S(1)} %constant_dynamic-slice_fusion.displaced_ref, ...), custom_call_target="tpu_custom_call", output_to_operand_aliasing={{}: (9, {})} | custom-call | flops 1610612736 | bytes 6291456 | tf_op jit(solution)/shard_map/update_rows/pallas_call | solution.py:120
  127.3 6.5 %collective-permute-done.11.rest_2_ = bf16[512,512]{1,0:T(8,128)(2,1)S(1)} collective-permute-done((bf16[512,512]{1,0:T(8,128)(2,1)S(1)}, bf16[512,512]{1,0:T(8,128)(2,1)S(1)}, u32[]{:S(2)}, u32[]{:S(2)}) %collective-permute-start.11) | collective-permute-done | bytes 524320 | tf_op jit(solution)/shard_map/ppermute | solution.py:183
  133.8 4.7 %update_rows.7 = bf16[2048,1536]{1,0:T(8,128)(2,1)} custom-call(s32[3]{0:T(128)S(1)} %pad_add_fusion.place_ref, s32[1,512]{1,0:T(1,128)S(1)} %bitcast.11, bf16[2048,1536]{1,0:T(8,128)(2,1)} %rest_0_.7, bf16[512,1536]{1,0:T(8,128)(2,1)S(1)} %constant_dynamic-slice_fusion.displaced_ref, ...), custom_call_target="tpu_custom_call", output_to_operand_aliasing={{}: (9, {})} | custom-call | flops 1610612736 | bytes 6291456 | tf_op jit(solution)/shard_map/update_rows/pallas_call | solution.py:120
  (53 shorter events, 14.1 us)
Async XLA Ops:
  0.0 70.1 %copy-start = (bf16[512,512]{1,0:T(8,128)(2,1)S(1)}, bf16[512,512]{1,0:T(8,128)(2,1)}, u32[]{:S(2)}) copy-start(bf16[512,512]{1,0:T(8,128)(2,1)} %param.5) | copy-start | bytes 1572868
  8.8 2.2 %copy-start.1 = (bf16[1024,1536]{1,0:T(8,128)(2,1)}, bf16[1024,1536]{1,0:T(8,128)(2,1)S(1)}, u32[]{:S(2)}) copy-start(bf16[1024,1536]{1,0:T(8,128)(2,1)S(1)} %pick_rows.1) | copy-start | bytes 9437188
  10.9 3.9 %collective-permute-start = (bf16[512,1536]{1,0:T(8,128)(2,1)}, bf16[512,1536]{1,0:T(8,128)(2,1)S(1)}, u32[]{:S(2)}, u32[]{:S(2)}) collective-permute-start(bf16[512,1536]{1,0:T(8,128)(2,1)} %constant_dynamic-slice_fusion.5), channel_id=1, source_target_pairs={{0,4},{4,0},{8,12},{12,8},{16,20},{20,16},{24,28},{28,24},{1,5},{5... | collective-permute-start | bytes 4718600 | tf_op jit(solution)/shard_map/ppermute | solution.py:152
  16.9 10.4 %collective-permute-start.1 = (bf16[128,1536]{1,0:T(8,128)(2,1)S(1)}, bf16[128,1536]{1,0:T(8,128)(2,1)S(1)}, u32[]{:S(2)}, u32[]{:S(2)}) collective-permute-start(bf16[128,1536]{1,0:T(8,128)(2,1)S(1)} %constant_dynamic-slice_fusion.4), channel_id=1, source_target_pairs={{0,8},{4,12},{8,0},{12,4},{16,24},{20,28},{24,16},{28,20},{1,9},{5... | collective-permute-start | bytes 1179656 | tf_op jit(solution)/shard_map/ppermute | solution.py:152
  18.2 10.1 %collective-permute-start.5 = (bf16[128,1536]{1,0:T(8,128)(2,1)S(1)}, bf16[128,1536]{1,0:T(8,128)(2,1)S(1)}, u32[]{:S(2)}, u32[]{:S(2)}) collective-permute-start(bf16[128,1536]{1,0:T(8,128)(2,1)S(1)} %constant_dynamic-slice_fusion.2), channel_id=1, source_target_pairs={{0,16},{4,20},{8,24},{12,28},{16,0},{20,4},{24,8},{28,12},{1,17},{... | collective-permute-start | bytes 1179656 | tf_op jit(solution)/shard_map/ppermute | solution.py:152
  27.4 5.3 %collective-permute-start.2 = (bf16[64,1536]{1,0:T(8,128)(2,1)S(1)}, bf16[64,1536]{1,0:T(8,128)(2,1)S(1)}, u32[]{:S(2)}, u32[]{:S(2)}) collective-permute-start(bf16[64,1536]{1,0:T(8,128)(2,1)S(1)} %constant_dynamic-slice_fusion.3), channel_id=1, source_target_pairs={{0,16},{4,20},{8,24},{12,28},{16,0},{20,4},{24,8},{28,12},{1,17},{... | collective-permute-start | bytes 589832 | tf_op jit(solution)/shard_map/ppermute | solution.py:152
  28.4 4.9 %collective-permute-start.6 = (bf16[64,1536]{1,0:T(8,128)(2,1)S(1)}, bf16[64,1536]{1,0:T(8,128)(2,1)S(1)}, u32[]{:S(2)}, u32[]{:S(2)}) collective-permute-start(bf16[64,1536]{1,0:T(8,128)(2,1)S(1)} %constant_dynamic-slice_fusion.1), channel_id=1, source_target_pairs={{0,8},{4,12},{8,0},{12,4},{16,24},{20,28},{24,16},{28,20},{1,9},{5... | collective-permute-start | bytes 589832 | tf_op jit(solution)/shard_map/ppermute | solution.py:152
  32.8 4.6 %collective-permute-start.3 = (bf16[64,1536]{1,0:T(8,128)(2,1)S(1)}, bf16[64,1536]{1,0:T(8,128)(2,1)S(1)}, u32[]{:S(2)}, u32[]{:S(2)}) collective-permute-start(bf16[64,1536]{1,0:T(8,128)(2,1)S(1)} %dynamic-slice_add_fusion.4), channel_id=1, source_target_pairs={{0,16},{4,20},{8,24},{12,28},{16,0},{20,4},{24,8},{28,12},{1,17},{... | collective-permute-start | bytes 589832 | tf_op jit(solution)/shard_map/ppermute | solution.py:160
  33.4 5.5 %collective-permute-start.7 = (bf16[64,1536]{1,0:T(8,128)(2,1)S(1)}, bf16[64,1536]{1,0:T(8,128)(2,1)S(1)}, u32[]{:S(2)}, u32[]{:S(2)}) collective-permute-start(bf16[64,1536]{1,0:T(8,128)(2,1)S(1)} %dynamic-slice_add_fusion.3), channel_id=1, source_target_pairs={{0,8},{4,12},{8,0},{12,4},{16,24},{20,28},{24,16},{28,20},{1,9},{5... | collective-permute-start | bytes 589832 | tf_op jit(solution)/shard_map/ppermute | solution.py:160
  37.7 8.9 %collective-permute-start.4 = (bf16[128,1536]{1,0:T(8,128)(2,1)S(1)}, bf16[128,1536]{1,0:T(8,128)(2,1)S(1)}, u32[]{:S(2)}, u32[]{:S(2)}) collective-permute-start(bf16[128,1536]{1,0:T(8,128)(2,1)S(1)} %fusion.9), channel_id=1, source_target_pairs={{0,8},{4,12},{8,0},{12,4},{16,24},{20,28},{24,16},{28,20},{1,9},{5... | collective-permute-start | bytes 1179656 | tf_op jit(solution)/shard_map/ppermute | solution.py:160
  39.2 8.1 %collective-permute-start.8 = (bf16[128,1536]{1,0:T(8,128)(2,1)S(1)}, bf16[128,1536]{1,0:T(8,128)(2,1)S(1)}, u32[]{:S(2)}, u32[]{:S(2)}) collective-permute-start(bf16[128,1536]{1,0:T(8,128)(2,1)S(1)} %fusion.7), channel_id=1, source_target_pairs={{0,16},{4,20},{8,24},{12,28},{16,0},{20,4},{24,8},{28,12},{1,17},{... | collective-permute-start | bytes 1179656 | tf_op jit(solution)/shard_map/ppermute | solution.py:160
  48.3 2.2 %copy-start.5 = (bf16[1536,1536]{1,0:T(8,128)(2,1)}, bf16[1536,1536]{1,0:T(8,128)(2,1)S(1)}, u32[]{:S(2)}) copy-start(bf16[1536,1536]{1,0:T(8,128)(2,1)S(1)} %get-tuple-element.5) | copy-start | bytes 14155780
  50.5 1.4 %copy-start.3 = (bf16[256,1536]{1,0:T(8,128)(2,1)}, bf16[256,1536]{1,0:T(8,128)(2,1)S(1)}, u32[]{:S(2)}) copy-start(bf16[256,1536]{1,0:T(8,128)(2,1)S(1)} %get-tuple-element.6) | copy-start | bytes 2359300
  51.9 11.1 %collective-permute-start.9 = (bf16[512,1536]{1,0:T(8,128)(2,1)}, bf16[512,1536]{1,0:T(8,128)(2,1)}, u32[]{:S(2)}, u32[]{:S(2)}) collective-permute-start(bf16[512,1536]{1,0:T(8,128)(2,1)} %pad_maximum_fusion), channel_id=1, source_target_pairs={{0,4},{4,0},{8,12},{12,8},{16,20},{20,16},{24,28},{28,24},{1,5},{5... | collective-permute-start | bytes 4718600 | tf_op jit(solution)/shard_map/ppermute | solution.py:160
  58.2 2.8 %collective-permute-start.19 = (bf16[512,512]{1,0:T(8,128)(2,1)}, bf16[512,512]{1,0:T(8,128)(2,1)S(1)}, u32[]{:S(2)}, u32[]{:S(2)}) collective-permute-start(bf16[512,512]{1,0:T(8,128)(2,1)} %get-tuple-element.9), channel_id=1, source_target_pairs={{0,2},{4,6},{8,10},{12,14},{16,18},{20,22},{24,26},{28,30}} | collective-permute-start | bytes 1572872 | tf_op jit(solution)/shard_map/ppermute | solution.py:181
  58.9 3.4 %collective-permute-start.16 = (bf16[512,512]{1,0:T(8,128)(2,1)}, bf16[512,512]{1,0:T(8,128)(2,1)S(1)}, u32[]{:S(2)}, u32[]{:S(2)}) collective-permute-start(bf16[512,512]{1,0:T(8,128)(2,1)} %get-tuple-element.10), channel_id=1, source_target_pairs={{0,2},{4,6},{8,10},{12,14},{16,18},{20,22},{24,26},{28,30}} | collective-permute-start | bytes 1572872 | tf_op jit(solution)/shard_map/ppermute | solution.py:181
  59.6 9.7 %collective-permute-start.13 = (bf16[512,512]{1,0:T(8,128)(2,1)}, bf16[512,512]{1,0:T(8,128)(2,1)S(1)}, u32[]{:S(2)}, u32[]{:S(2)}) collective-permute-start(bf16[512,512]{1,0:T(8,128)(2,1)} %get-tuple-element.11), channel_id=1, source_target_pairs={{0,2},{4,6},{8,10},{12,14},{16,18},{20,22},{24,26},{28,30}} | collective-permute-start | bytes 1572872 | tf_op jit(solution)/shard_map/ppermute | solution.py:181
  60.3 12.2 %collective-permute-start.10 = (bf16[512,512]{1,0:T(8,128)(2,1)}, bf16[512,512]{1,0:T(8,128)(2,1)S(1)}, u32[]{:S(2)}, u32[]{:S(2)}) collective-permute-start(bf16[512,512]{1,0:T(8,128)(2,1)} %get-tuple-element.12), channel_id=1, source_target_pairs={{0,2},{4,6},{8,10},{12,14},{16,18},{20,22},{24,26},{28,30}} | collective-permute-start | bytes 1572872 | tf_op jit(solution)/shard_map/ppermute | solution.py:181
  61.1 27.4 %collective-permute-start.20 = (bf16[512,512]{1,0:T(8,128)(2,1)S(1)}, bf16[512,512]{1,0:T(8,128)(2,1)S(1)}, u32[]{:S(2)}, u32[]{:S(2)}) collective-permute-start(bf16[512,512]{1,0:T(8,128)(2,1)S(1)} %collective-permute-done.19.rest_1_), channel_id=1, source_target_pairs={{2,1},{6,5},{10,9},{14,13},{18,17},{22,21},{26,25},{30,29}} | collective-permute-start | bytes 1572872 | tf_op jit(solution)/shard_map/ppermute | solution.py:183
  62.4 26.8 %collective-permute-start.21 = (bf16[512,512]{1,0:T(8,128)(2,1)S(1)}, bf16[512,512]{1,0:T(8,128)(2,1)S(1)}, u32[]{:S(2)}, u32[]{:S(2)}) collective-permute-start(bf16[512,512]{1,0:T(8,128)(2,1)S(1)} %collective-permute-done.19.rest_1_), channel_id=1, source_target_pairs={{2,3},{6,7},{10,11},{14,15},{18,19},{22,23},{26,27},{30,31}} | collective-permute-start | bytes 1572872 | tf_op jit(solution)/shard_map/ppermute | solution.py:185
  63.1 37.9 %collective-permute-start.17 = (bf16[512,512]{1,0:T(8,128)(2,1)S(1)}, bf16[512,512]{1,0:T(8,128)(2,1)S(1)}, u32[]{:S(2)}, u32[]{:S(2)}) collective-permute-start(bf16[512,512]{1,0:T(8,128)(2,1)S(1)} %collective-permute-done.16.rest_1_), channel_id=1, source_target_pairs={{2,1},{6,5},{10,9},{14,13},{18,17},{22,21},{26,25},{30,29}} | collective-permute-start | bytes 1572872 | tf_op jit(solution)/shard_map/ppermute | solution.py:183
  67.0 1.4 %copy-start.4 = (bf16[256,1536]{1,0:T(8,128)(2,1)S(1)}, bf16[256,1536]{1,0:T(8,128)(2,1)}, u32[]{:S(2)}) copy-start(bf16[256,1536]{1,0:T(8,128)(2,1)} %copy-done.3) | copy-start | bytes 2359300
  69.4 38.6 %collective-permute-start.18 = (bf16[512,512]{1,0:T(8,128)(2,1)S(1)}, bf16[512,512]{1,0:T(8,128)(2,1)S(1)}, u32[]{:S(2)}, u32[]{:S(2)}) collective-permute-start(bf16[512,512]{1,0:T(8,128)(2,1)S(1)} %collective-permute-done.16.rest_1_), channel_id=1, source_target_pairs={{2,3},{6,7},{10,11},{14,15},{18,19},{22,23},{26,27},{30,31}} | collective-permute-start | bytes 1572872 | tf_op jit(solution)/shard_map/ppermute | solution.py:185
  72.5 30.7 %copy-start.2 = (s32[512]{0:T(512)S(1)}, s32[512]{0:T(512)}, u32[]{:S(2)}) copy-start(s32[512]{0:T(512)} %param.4) | copy-start | bytes 6148
  72.5 50.1 %collective-permute-start.14 = (bf16[512,512]{1,0:T(8,128)(2,1)S(1)}, bf16[512,512]{1,0:T(8,128)(2,1)S(1)}, u32[]{:S(2)}, u32[]{:S(2)}) collective-permute-start(bf16[512,512]{1,0:T(8,128)(2,1)S(1)} %collective-permute-done.13.rest_1_), channel_id=1, source_target_pairs={{2,1},{6,5},{10,9},{14,13},{18,17},{22,21},{26,25},{30,29}} | collective-permute-start | bytes 1572872 | tf_op jit(solution)/shard_map/ppermute | solution.py:183
  88.4 34.1 %collective-permute-start.15 = (bf16[512,512]{1,0:T(8,128)(2,1)S(1)}, bf16[512,512]{1,0:T(8,128)(2,1)S(1)}, u32[]{:S(2)}, u32[]{:S(2)}) collective-permute-start(bf16[512,512]{1,0:T(8,128)(2,1)S(1)} %collective-permute-done.13.rest_1_), channel_id=1, source_target_pairs={{2,3},{6,7},{10,11},{14,15},{18,19},{22,23},{26,27},{30,31}} | collective-permute-start | bytes 1572872 | tf_op jit(solution)/shard_map/ppermute | solution.py:185
  89.1 44.7 %collective-permute-start.11 = (bf16[512,512]{1,0:T(8,128)(2,1)S(1)}, bf16[512,512]{1,0:T(8,128)(2,1)S(1)}, u32[]{:S(2)}, u32[]{:S(2)}) collective-permute-start(bf16[512,512]{1,0:T(8,128)(2,1)S(1)} %collective-permute-done.10.rest_1_), channel_id=1, source_target_pairs={{2,1},{6,5},{10,9},{14,13},{18,17},{22,21},{26,25},{30,29}} | collective-permute-start | bytes 1572872 | tf_op jit(solution)/shard_map/ppermute | solution.py:183
  101.0 32.8 %collective-permute-start.12 = (bf16[512,512]{1,0:T(8,128)(2,1)S(1)}, bf16[512,512]{1,0:T(8,128)(2,1)S(1)}, u32[]{:S(2)}, u32[]{:S(2)}) collective-permute-start(bf16[512,512]{1,0:T(8,128)(2,1)S(1)} %collective-permute-done.10.rest_1_), channel_id=1, source_target_pairs={{2,3},{6,7},{10,11},{14,15},{18,19},{22,23},{26,27},{30,31}} | collective-permute-start | bytes 1572872 | tf_op jit(solution)/shard_map/ppermute | solution.py:185

commit v2 on v0

v2 whole, which is shorter than its diff:
```python
import functools

import jax
import jax.numpy as jnp
from jax import lax
from jax.experimental import pallas as pl
from jax.experimental.pallas import tpu as pltpu
from jax.sharding import PartitionSpec as P

GROUPS = 4
BLOCK = 512
F32, BF16 = jnp.float32, jnp.bfloat16
VMEM = pl.BlockSpec(memory_space=pltpu.VMEM)
ANY = pl.BlockSpec(memory_space=pl.ANY)
SMALL = pltpu.CompilerParams(vmem_limit_bytes=8 * 2**20)
LARGE = pltpu.CompilerParams(vmem_limit_bytes=28 * 2**20)


def cost(flops, moved):
    return pl.CostEstimate(flops=flops, bytes_accessed=moved, transcendentals=0)


def chunk_kernel(first_row, matrix_ref, out_ref, sem):
    rows, width = out_ref.shape
    copy = pltpu.make_async_copy(
        matrix_ref.at[pl.ds(first_row, rows), pl.ds(0, width)], out_ref, sem
    )
    copy.start()
    copy.wait()


def chunk(matrix, first_row, rows, width):
    return pl.pallas_call(
        functools.partial(chunk_kernel, first_row),
        in_specs=[pl.BlockSpec(memory_space=pltpu.HBM)],
        out_specs=ANY,
        out_shape=jax.ShapeDtypeStruct((rows, width), BF16),
        scratch_shapes=[pltpu.SemaphoreType.DMA],
        compiler_params=SMALL,
        cost_estimate=cost(0, 4 * rows * width),
        name="chunk",
    )(matrix)


def pick_kernel(place_ref, pivots_ref, matrix_ref, keep_ref, send_ref, onehot_ref):
    rows = matrix_ref.shape[0]
    width = pivots_ref.shape[0]
    half = width // 2

    @pl.when(pl.program_id(0) == 0)
    def _():
        row = lax.broadcasted_iota(jnp.int32, (width, rows), 1) + place_ref[0] * rows
        onehot_ref[...] = jnp.where(pivots_ref[...] == row, 1.0, 0.0).astype(BF16)

    block = matrix_ref[...]
    send_ref[...] = jnp.dot(onehot_ref[half:], block, preferred_element_type=F32).astype(BF16)
    keep_ref[...] = jnp.dot(onehot_ref[:half], block, preferred_element_type=F32).astype(BF16)


def pick(place, pivots, matrix):
    rows, cols = matrix.shape
    width = pivots.shape[0]
    block = min(BLOCK, cols)
    half = jax.ShapeDtypeStruct((width // 2, cols), BF16)
    return pl.pallas_call(
        pick_kernel,
        grid_spec=pltpu.PrefetchScalarGridSpec(
            num_scalar_prefetch=1,
            grid=(cols // block,),
            in_specs=[
                pl.BlockSpec((width, 1), lambda i, s: (0, 0)),
                pl.BlockSpec((rows, block), lambda i, s: (0, i)),
            ],
            out_specs=[pl.BlockSpec((width // 2, block), lambda i, s: (0, i))] * 2,
            scratch_shapes=[pltpu.VMEM((width, rows), BF16)],
        ),
        out_shape=[half, half],
        compiler_params=LARGE,
        cost_estimate=cost(2 * width * rows * cols, 2 * rows * cols),
        name="pick_rows",
    )(place, pivots[:, None], matrix)


def split_sum_kernel(own_ref, got_ref, *rest):
    first_ref, second_ref = rest[-2:]
    half = first_ref.shape[0]
    first_ref[...] = own_ref[:half] + got_ref[:half]
    second_ref[...] = own_ref[half:] + got_ref[half:]


def split_sum(own, got, after):
    half = jax.ShapeDtypeStruct((own.shape[0] // 2, own.shape[1]), BF16)
    return pl.pallas_call(
        split_sum_kernel,
        in_specs=[VMEM, VMEM] + [ANY] * len(after),
        out_specs=[VMEM, VMEM],
        out_shape=[half, half],
        compiler_params=SMALL,
        cost_estimate=cost(own.size, 6 * own.size),
        name="split_sum",
    )(own, got, *after)


def stack_sum_kernel(count, *refs):
    out_ref = refs[-1]
    start = 0
    for own_ref, got_ref in zip(refs[:count], refs[count : 2 * count]):
        rows = own_ref.shape[0]
        out_ref[start : start + rows] = own_ref[...] + got_ref[...]
        start += rows


def stack_sum(own, got, after):
    rows = sum(x.shape[0] for x in own)
    cols = own[0].shape[1]
    return pl.pallas_call(
        functools.partial(stack_sum_kernel, len(own)),
        in_specs=[VMEM] * (2 * len(own)) + [ANY] * len(after),
        out_specs=VMEM,
        out_shape=jax.ShapeDtypeStruct((rows, cols), BF16),
        compiler_params=SMALL,
        cost_estimate=cost(rows * cols, 6 * rows * cols),
        name="stack_sum",
    )(*own, *got, *after)


def merge_kernel(first_ref, first_got_ref, second_ref, second_got_ref, *rest):
    out_ref = rest[-1]
    rows = first_ref.shape[0] // 2
    for number, (own_ref, got_ref) in enumerate(
        ((first_ref, first_got_ref), (second_ref, second_got_ref))
    ):
        for part in range(2):
            start = (2 * part + number) * rows
            piece = slice(part * rows, (part + 1) * rows)
            out_ref[start : start + rows] = own_ref[piece] + got_ref[piece]


def merge(first, first_got, second, second_got, after):
    rows, cols = 2 * first.shape[0], first.shape[1]
    return pl.pallas_call(
        merge_kernel,
        in_specs=[VMEM] * 4 + [ANY] * len(after),
        out_specs=VMEM,
        out_shape=jax.ShapeDtypeStruct((rows, cols), BF16),
        compiler_params=SMALL,
        cost_estimate=cost(rows * cols, 6 * rows * cols),
        name="merge",
    )(first, first_got, second, second_got, *after)


def update_kernel(groups, group_rows, per_group, pick_source, make_upper, *refs):
    place_ref, pivots_ref, matrix_ref, mine_ref, other_ref, factor_ref = refs[:6]
    sources = refs[6 : 6 + 1 + per_group * len(groups)]
    if make_upper:
        out_ref, upper_ref = refs[-6:-4]
    else:
        out_ref, upper_ref = refs[-5], factor_ref
    onehot_ref, keep_ref, panel_ref, sem = refs[-4:]
    step = pl.program_id(0)
    width = panel_ref.shape[1]
    half = width // 2
    block = out_ref.shape[1]
    row_place, col_place, rows, core = (place_ref[i] for i in range(4))
    first_row = groups[0] * group_rows

    def fetch(action):
        for number, group in enumerate(groups):
            here = panel_ref.at[pl.ds(number * group_rows, group_rows)]
            views = [sources[0].at[pl.ds(group * group_rows, group_rows), pl.ds(0, width)]]
            views += sources[1 + number * per_group : 1 + (number + 1) * per_group]
            for choice, view in enumerate(views):
                @pl.when(pick_source(col_place) == choice)
                def _():
                    action(pltpu.make_async_copy(view, here, sem.at[number]))

    @pl.when(step == 0)
    def _():
        fetch(lambda copy: copy.start())
        for number in range(len(groups)):
            here = slice(number * group_rows, (number + 1) * group_rows)
            row = lax.broadcasted_iota(jnp.int32, (group_rows, width), 0)
            row = row + (row_place * rows + first_row + number * group_rows)
            onehot = jnp.where(pivots_ref[...] == row, 1.0, 0.0)
            onehot_ref[here] = onehot.astype(BF16)
            has_pivot = jnp.max(onehot, axis=1, keepdims=True)
            keep_ref[here] = jnp.broadcast_to(1.0 - has_pivot, (group_rows, 128))

    def in_order(start):
        mine, other = mine_ref[start : start + half], other_ref[start : start + half]
        return jnp.where(core == 0, mine, other), jnp.where(core == 0, other, mine)

    if make_upper:
        top, bottom = in_order(0)
        upper_ref[...] = (
            jnp.dot(factor_ref[:, :half], top, preferred_element_type=F32)
            + jnp.dot(factor_ref[:, half:], bottom, preferred_element_type=F32)
        ).astype(BF16)

    @pl.when(step == 0)
    def _():
        fetch(lambda copy: copy.wait())

    in_panel = (col_place == 0) & (step * block < width)

    @pl.when(in_panel)
    def _():
        out_ref[...] = matrix_ref[...]

    @pl.when(jnp.logical_not(in_panel))
    def _():
        upper = upper_ref[...]
        top, bottom = in_order(half)
        for number, group in enumerate(groups):
            here = slice(number * group_rows, (number + 1) * group_rows)
            keep = jnp.concatenate([keep_ref[here]] * (block // 128), axis=1)
            moved = jnp.dot(onehot_ref[here, :half], top, preferred_element_type=F32)
            moved += jnp.dot(onehot_ref[here, half:], bottom, preferred_element_type=F32)
            product = jnp.dot(panel_ref[here], upper, preferred_element_type=F32)
            swapped = matrix_ref[here].astype(F32) * keep + moved
            out_ref[here] = (swapped - product).astype(BF16)
        if first_row < width:
            @pl.when(row_place == 0)
            def _():
                out_ref[: width - first_row] = upper[first_row:]


def update(groups, group_rows, pick_source, place, pivots, matrix, mine, other, received,
           unit_inverse=None, upper=None, out=None):
    rows, cols = matrix.shape
    width = mine.shape[0]
    block = min(BLOCK, cols)
    count = group_rows * len(groups)
    position = groups[0] // len(groups)
    make_upper = upper is None
    by_column = pl.BlockSpec((width, block), lambda i, s: (0, i))
    in_specs = [
        pl.BlockSpec((1, width), lambda i, s: (0, 0)),
        pl.BlockSpec((count, block), lambda i, s: (position, i)),
        by_column,
        by_column,
        pl.BlockSpec((width, width), lambda i, s: (0, 0)) if make_upper else by_column,
    ]
    sources = [matrix] + [x for group in groups for x in received[group]]
    in_specs += [ANY] * len(sources)
    operands = [place, pivots[None, :], matrix, mine, other]
    operands += [unit_inverse if make_upper else upper] + sources
    aliases = {}
    if out is not None:
        in_specs.append(ANY)
        aliases = {len(operands): 0}
        operands.append(out)
    out_specs = [pl.BlockSpec((count, block), lambda i, s: (position, i))]
    out_shape = [jax.ShapeDtypeStruct((rows, cols), BF16)]
    if make_upper:
        out_specs.append(by_column)
        out_shape.append(jax.ShapeDtypeStruct((width, cols), BF16))
    return pl.pallas_call(
        functools.partial(
            update_kernel, groups, group_rows, len(received[0]), pick_source, make_upper
        ),
        grid_spec=pltpu.PrefetchScalarGridSpec(
            num_scalar_prefetch=1,
            grid=(cols // block,),
            in_specs=in_specs,
            out_specs=out_specs,
            scratch_shapes=[
                pltpu.VMEM((count, width), BF16),
                pltpu.VMEM((count, 128), F32),
                pltpu.VMEM((count, width), BF16),
                pltpu.SemaphoreType.DMA((len(groups),)),
            ],
        ),
        out_shape=out_shape,
        input_output_aliases=aliases,
        compiler_params=LARGE,
        cost_estimate=cost(4 * count * width * cols, 4 * count * cols + 4 * width * cols),
        name="update_rows",
    )(*operands)


def swap_pairs(size, bit):
    return [(i, i ^ (1 << bit)) for i in range(size)]


def grow_pairs(bits_so_far, bit):
    places = [0]
    for b in bits_so_far:
        places += [i | (1 << b) for i in places]
    return [(i, i | (1 << bit)) for i in places]


def spread(panel, axis, size):
    middle = size // 2
    received = [lax.ppermute(panel, axis, [(0, middle)])]
    received.append(lax.ppermute(received[0], axis, [(middle, middle - 1)]))
    received.append(lax.ppermute(received[0], axis, [(middle, middle + 1)]))
    held = received[1] + received[2] if size > 4 else None
    distance = 1
    while middle - distance > 1 or middle + distance + 1 < size:
        pairs = []
        if middle - distance > 1:
            pairs.append((middle - distance, middle - distance - 1))
        if middle + distance + 1 < size:
            pairs.append((middle + distance, middle + distance + 1))
        held = lax.ppermute(held, axis, pairs)
        received.append(held)
        distance += 1
    return received


def source_of(size):
    middle = size // 2

    def pick_source(place):
        away = jnp.abs(place - middle)
        number = jnp.where(away == 0, 1, jnp.where(place < middle, 2, 3))
        number = jnp.where(away >= 2, away + 2, number)
        return jnp.where(place == 0, 0, number)

    return pick_source


def per_device(n_prow, n_pcol, matrix, pivots, unit_inverse):
    rows, cols = matrix.shape
    width = unit_inverse.shape[0]
    half, quarter = width // 2, width // 4
    row_place = lax.axis_index("prow")
    col_place = lax.axis_index("pcol")
    core = row_place & 1
    place = jnp.stack([row_place, col_place, jnp.full_like(row_place, rows), core])
    place = place.astype(jnp.int32)
    group_rows = rows // GROUPS
    bits = list(range(1, n_prow.bit_length() - 1))

    received = []
    for group in range(GROUPS):
        panel = chunk(matrix, group * group_rows, group_rows, width)
        received.append(spread(panel, "pcol", n_pcol))

    got = lax.ppermute(matrix[half:width], "prow", [(0, 1)])
    down = [
        jnp.where(row_place == 0, matrix[:quarter], got[:quarter]),
        jnp.where(row_place == 0, matrix[quarter:half], got[quarter:]),
    ]
    order = jnp.where(core == 0, pivots, jnp.roll(pivots, half))
    keep, send = pick(place, order, matrix)
    up = split_sum(keep, lax.ppermute(send, "prow", swap_pairs(n_prow, 0)), received[0][:1])

    orders = [bits, bits[::-1]]
    for number in range(len(bits) - 1):
        up_got = [
            lax.ppermute(x, "prow", swap_pairs(n_prow, b[number])) for x, b in zip(up, orders)
        ]
        down_got = [
            lax.ppermute(x, "prow", grow_pairs([0] + b[:number], b[number]))
            for x, b in zip(down, orders)
        ]
        if number < len(bits) - 2:
            up = [x + y for x, y in zip(up, up_got)]
            down = [x + y for x, y in zip(down, down_got)]
    after = received[0][1:3] + received[1][:1]
    both = [
        stack_sum([u, d], [ug, dg], after)
        for u, ug, d, dg in zip(up, up_got, down, down_got)
    ]
    both_got = [
        lax.ppermute(x, "prow", swap_pairs(n_prow, b[-1])) for x, b in zip(both, orders)
    ]
    after = received[1][1:3] + received[2][:1]
    mine = merge(both[0], both_got[0], both[1], both_got[1], after)
    other = lax.ppermute(mine, "prow", swap_pairs(n_prow, 0))

    common = (group_rows, source_of(n_pcol), place, pivots, matrix, mine, other, received)
    out, upper = update(list(range(GROUPS - 1)), *common, unit_inverse=unit_inverse)
    (out,) = update([GROUPS - 1], *common, upper=upper, out=out)
    return out


def solution(mesh):
    return jax.shard_map(
        functools.partial(per_device, mesh.shape["prow"], mesh.shape["pcol"]),
        mesh=mesh,
        in_specs=(P("prow", "pcol"), P(), P()),
        out_specs=P("prow", "pcol"),
        check_vma=False,
    )
```

time: 186 us -> 114 us (0.61)
  the two profiles are of different devices: /device:TPU:13 before, /device:TPU:10 now
where the time goes in v2:
time: 114 us
  waiting for transfers between devices  54.4 us (48%)
  starting transfers between devices  25.8 us (23%)
  Pallas kernels  22.7 us (20%)
  local copies, waits for them, and re-layouts  8.95 us (8%)
  other arithmetic  1.53 us (1%)
    ppermute x4, waiting for transfers between devices, spread(): received.append(lax.ppermute(received[0], axis, [(middle, middle - 1)]))  49 us
    pallas_call x2, Pallas kernels, update(): pl.pallas_call(functools.partial(update_kernel, groups, group_rows, len(r...  14.3 us
    unnamed x16, local copies, waits for them, and re-layouts  6.73 us
    ppermute x2, starting transfers between devices, per_device(): lax.ppermute(x, 'prow', swap_pairs(n_prow, b[-1]))  6.1 us
    pallas_call x1, Pallas kernels, pick(): pl.pallas_call(pick_kernel, grid_spec=pltpu.PrefetchScalarGridSpec(num_sc...  5.88 us
    ppermute x2, waiting for transfers between devices, per_device(): lax.ppermute(x, 'prow', swap_pairs(n_prow, b[number]))  5.36 us
    ppermute x4, starting transfers between devices, spread(): received.append(lax.ppermute(received[0], axis, [(middle, middle - 1)]))  5.17 us
    ppermute x2, starting transfers between devices, per_device(): lax.ppermute(x, 'prow', swap_pairs(n_prow, b[number]))  4.31 us
  transfers between devices with their start and end apart: 21, of which 5 were waited for; matrix products, arithmetic and copies ran while one was open for 3% of the time, Pallas kernels for 16%

profile of v2, /device:TPU:10, one launch (start us, length us, event | category | flops | bytes accessed | tf_op | source)
XLA Modules:
  0.0 113.7 jit_solution(2432045659341322141)
XLA Ops:
  0.0 2.8 %copy-done = bf16[2048,1536]{1,0:T(8,128)(2,1)S(1)} copy-done((bf16[2048,1536]{1,0:T(8,128)(2,1)S(1)}, bf16[2048,1536]{1,0:T(8,128)(2,1)}, u32[]{:S(2)}) %copy-start) | copy-done | bytes 6291480
  2.8 1.5 %collective-permute-start.1 = (bf16[512,512]{1,0:T(8,128)(2,1)S(1)}, bf16[512,512]{1,0:T(8,128)(2,1)}, u32[]{:S(2)}, u32[]{:S(2)}) collective-permute-start(bf16[512,512]{1,0:T(8,128)(2,1)S(1)} %chunk.4), channel_id=1, source_target_pairs={{0,2},{4,6},{8,10},{12,14},{16,18},{20,22},{24,26},{28,30}} | collective-permute-start | bytes 1572872 | tf_op jit(solution)/shard_map/ppermute | solution.py:295
  4.3 2.1 %slice.26 = bf16[256,1536]{1,0:T(8,128)(2,1)} slice(bf16[2048,1536]{1,0:T(8,128)(2,1)} %refs_6_.3), slice={[256:512], [0:1536]} | slice | bytes 1572864 | tf_op jit(solution)/shard_map/slice | solution.py:341
  6.4 1.6 %collective-permute-start.2 = (bf16[256,1536]{1,0:T(8,128)(2,1)}, bf16[256,1536]{1,0:T(8,128)(2,1)}, u32[]{:S(2)}, u32[]{:S(2)}) collective-permute-start(bf16[256,1536]{1,0:T(8,128)(2,1)} %slice.26), channel_id=1, source_target_pairs={{0,4},{1,5},{2,6},{3,7}} | collective-permute-start | bytes 2359304 | tf_op jit(solution)/shard_map/ppermute | solution.py:341
  8.2 2.8 %copy-done.1 = bf16[2048,1536]{1,0:T(8,128)(2,1)S(1)} copy-done((bf16[2048,1536]{1,0:T(8,128)(2,1)S(1)}, bf16[2048,1536]{1,0:T(8,128)(2,1)}, u32[]{:S(2)}) %copy-start.1) | copy-done | bytes 6291480
  11.0 5.9 %pick_rows.1 = (bf16[256,1536]{1,0:T(8,128)(2,1)S(1)}, bf16[256,1536]{1,0:T(8,128)(2,1)}) custom-call(s32[4]{0:T(128)S(1)} %pad_add_fusion.place_ref.refs_0_, s32[512,1]{1,0:T(8,128)S(1)} %copy.5.pivots_ref, bf16[2048,1536]{1,0:T(8,128)(2,1)S(1)} %copy-done.1), custom_call_target="tpu_custom_call" | custom-call | flops 3221225472 | bytes 6291456 | tf_op jit(solution)/shard_map/pick_rows/pallas_call | solution.py:65
  16.9 0.8 chunk.5
  17.7 0.8 collective-permute-start.7
  18.6 0.7 collective-permute-start.6
  19.3 1.3 %collective-permute-start.5 = (bf16[512,512]{1,0:T(8,128)(2,1)}, bf16[512,512]{1,0:T(8,128)(2,1)S(1)}, u32[]{:S(2)}, u32[]{:S(2)}) collective-permute-start(bf16[512,512]{1,0:T(8,128)(2,1)} %collective-permute-done.1.rest_0_.refs_7_), channel_id=1, source_target_pairs={{2,1},{6,5},{10,9},{14,13},{18,17},{22,21},{26,25},{30,29}} | collective-permute-start | bytes 1572872 | tf_op jit(solution)/shard_map/ppermute | solution.py:296
  20.6 1.4 %slice_select_fusion = (bf16[128,1536]{1,0:T(8,128)(2,1)S(1)}, bf16[128,1536]{1,0:T(8,128)(2,1)S(1)}) fusion(bf16[256,1536]{1,0:T(8,128)(2,1)} %collective-permute-done.2, bf16[2048,1536]{1,0:T(8,128)(2,1)} %refs_6_.3, pred[]{:T(512)S(6)} %eq.8), kind=kLoop, calls=%fused_computation | loop fusion | flops 393216 | bytes 2359297 | tf_op jit(solution)/shard_map/jit(_where)/select_n | solution.py:344
  22.8 1.1 copy-done.3
  23.9 1.2 %split_sum.1 = (bf16[128,1536]{1,0:T(8,128)(2,1)S(1)}, bf16[128,1536]{1,0:T(8,128)(2,1)S(1)}) custom-call(bf16[256,1536]{1,0:T(8,128)(2,1)S(1)} %copy-done.3, bf16[256,1536]{1,0:T(8,128)(2,1)} %collective-permute-done.got_ref, bf16[512,512]{1,0:T(8,128)(2,1)} %collective-permute-done.1.rest_0_.refs_7_), custom_call_target="tpu_custom_call" | custom-call | flops 393216 | bytes 2359296 | tf_op jit(solution)/shard_map/split_sum/pallas_call | solution.py:93
  25.1 1.6 %collective-permute-start.9 = (bf16[128,1536]{1,0:T(8,128)(2,1)S(1)}, bf16[128,1536]{1,0:T(8,128)(2,1)S(1)}, u32[]{:S(2)}, u32[]{:S(2)}) collective-permute-start(bf16[128,1536]{1,0:T(8,128)(2,1)S(1)} %get-tuple-element.14.refs_0_), channel_id=1, source_target_pairs={{0,16},{4,20},{8,24},{12,28},{16,0},{20,4},{24,8},{28,12},{1,17},{... | collective-permute-start | bytes 1179656 | tf_op jit(solution)/shard_map/ppermute | solution.py:353
  26.7 1.3 %collective-permute-start.4 = (bf16[128,1536]{1,0:T(8,128)(2,1)S(1)}, bf16[128,1536]{1,0:T(8,128)(2,1)S(1)}, u32[]{:S(2)}, u32[]{:S(2)}) collective-permute-start(bf16[128,1536]{1,0:T(8,128)(2,1)S(1)} %get-tuple-element.18.refs_1_), channel_id=1, source_target_pairs={{0,8},{4,12},{1,9},{5,13},{2,10},{6,14},{3,11},{7,15}} | collective-permute-start | bytes 1179656 | tf_op jit(solution)/shard_map/ppermute | solution.py:356
  28.0 2.7 %collective-permute-start.3 = (bf16[128,1536]{1,0:T(8,128)(2,1)S(1)}, bf16[128,1536]{1,0:T(8,128)(2,1)S(1)}, u32[]{:S(2)}, u32[]{:S(2)}) collective-permute-start(bf16[128,1536]{1,0:T(8,128)(2,1)S(1)} %get-tuple-element.13.refs_0_), channel_id=1, source_target_pairs={{0,8},{4,12},{8,0},{12,4},{16,24},{20,28},{24,16},{28,20},{1,9},{5... | collective-permute-start | bytes 1179656 | tf_op jit(solution)/shard_map/ppermute | solution.py:353
  30.7 6.7 %collective-permute-done.5.refs_4_.refs_8_ = bf16[512,512]{1,0:T(8,128)(2,1)S(1)} collective-permute-done((bf16[512,512]{1,0:T(8,128)(2,1)}, bf16[512,512]{1,0:T(8,128)(2,1)S(1)}, u32[]{:S(2)}, u32[]{:S(2)}) %collective-permute-start.5) | collective-permute-done | bytes 524320 | tf_op jit(solution)/shard_map/ppermute | solution.py:296
  37.6 6.0 %collective-permute-start.11 = (bf16[256,1536]{1,0:T(8,128)(2,1)S(1)}, bf16[256,1536]{1,0:T(8,128)(2,1)S(1)}, u32[]{:S(2)}, u32[]{:S(2)}) collective-permute-start(bf16[256,1536]{1,0:T(8,128)(2,1)S(1)} %stack_sum.3.second_ref), channel_id=1, source_target_pairs={{0,8},{4,12},{8,0},{12,4},{16,24},{20,28},{24,16},{28,20},{1,9},{5... | collective-permute-start | bytes 2359304 | tf_op jit(solution)/shard_map/ppermute | solution.py:368
  43.6 5.4 %collective-permute-done.3.refs_2_ = bf16[128,1536]{1,0:T(8,128)(2,1)S(1)} collective-permute-done((bf16[128,1536]{1,0:T(8,128)(2,1)S(1)}, bf16[128,1536]{1,0:T(8,128)(2,1)S(1)}, u32[]{:S(2)}, u32[]{:S(2)}) %collective-permute-start.3) | collective-permute-done | bytes 393248 | tf_op jit(solution)/shard_map/ppermute | solution.py:353
  49.2 0.8 collective-permute-start.14
  50.0 0.7 collective-permute-start.13
  50.8 1.3 %collective-permute-start.12 = (bf16[512,512]{1,0:T(8,128)(2,1)S(1)}, bf16[512,512]{1,0:T(8,128)(2,1)S(1)}, u32[]{:S(2)}, u32[]{:S(2)}) collective-permute-start(bf16[512,512]{1,0:T(8,128)(2,1)S(1)} %collective-permute-done.7.refs_6_.refs_10_), channel_id=1, source_target_pairs={{2,1},{6,5},{10,9},{14,13},{18,17},{22,21},{26,25},{30,29}} | collective-permute-start | bytes 1572872 | tf_op jit(solution)/shard_map/ppermute | solution.py:296
  52.1 22.2 %collective-permute-done.12.rest_0_.refs_11_ = bf16[512,512]{1,0:T(8,128)(2,1)S(1)} collective-permute-done((bf16[512,512]{1,0:T(8,128)(2,1)S(1)}, bf16[512,512]{1,0:T(8,128)(2,1)S(1)}, u32[]{:S(2)}, u32[]{:S(2)}) %collective-permute-start.12) | collective-permute-done | bytes 524320 | tf_op jit(solution)/shard_map/ppermute | solution.py:296
  74.6 0.7 collective-permute-start.18
  75.3 0.7 collective-permute-start.17
  76.0 1.3 %collective-permute-start.16 = (bf16[512,512]{1,0:T(8,128)(2,1)S(1)}, bf16[512,512]{1,0:T(8,128)(2,1)S(1)}, u32[]{:S(2)}, u32[]{:S(2)}) collective-permute-start(bf16[512,512]{1,0:T(8,128)(2,1)S(1)} %collective-permute-done.14.rest_2_.refs_13_), channel_id=1, source_target_pairs={{2,1},{6,5},{10,9},{14,13},{18,17},{22,21},{26,25},{30,29}} | collective-permute-start | bytes 1572872 | tf_op jit(solution)/shard_map/ppermute | solution.py:296
  77.3 0.7 collective-permute-start.20
  78.0 1.3 %collective-permute-start.19 = (bf16[512,512]{1,0:T(8,128)(2,1)S(1)}, bf16[512,512]{1,0:T(8,128)(2,1)S(1)}, u32[]{:S(2)}, u32[]{:S(2)}) collective-permute-start(bf16[512,512]{1,0:T(8,128)(2,1)S(1)} %collective-permute-done.18.refs_7_), channel_id=1, source_target_pairs={{2,1},{6,5},{10,9},{14,13},{18,17},{22,21},{26,25},{30,29}} | collective-permute-start | bytes 1572872 | tf_op jit(solution)/shard_map/ppermute | solution.py:296
  79.4 15.0 %collective-permute-done.16.refs_14_ = bf16[512,512]{1,0:T(8,128)(2,1)S(1)} collective-permute-done((bf16[512,512]{1,0:T(8,128)(2,1)S(1)}, bf16[512,512]{1,0:T(8,128)(2,1)S(1)}, u32[]{:S(2)}, u32[]{:S(2)}) %collective-permute-start.16) | collective-permute-done | bytes 524320 | tf_op jit(solution)/shard_map/ppermute | solution.py:296
  94.3 9.9 %update_rows.2 = (bf16[2048,1536]{1,0:T(8,128)(2,1)}, bf16[512,1536]{1,0:T(8,128)(2,1)S(1)}) custom-call(s32[4]{0:T(128)S(1)} %pad_add_fusion.place_ref.refs_0_, s32[1,512]{1,0:T(1,128)S(1)} %bitcast.7, bf16[2048,1536]{1,0:T(8,128)(2,1)S(1)} %bitcast.6, bf16[512,1536]{1,0:T(8,128)(2,1)S(1)} %merge.1.refs_3_, ...), custom_call_target="tpu_custom_call" | custom-call | flops 4831838208 | bytes 12582912 | tf_op jit(solution)/shard_map/update_rows/pallas_call | solution.py:258
  104.3 5.1 %collective-permute-done.19.refs_8_ = bf16[512,512]{1,0:T(8,128)(2,1)S(1)} collective-permute-done((bf16[512,512]{1,0:T(8,128)(2,1)S(1)}, bf16[512,512]{1,0:T(8,128)(2,1)S(1)}, u32[]{:S(2)}, u32[]{:S(2)}) %collective-permute-start.19) | collective-permute-done | bytes 524320 | tf_op jit(solution)/shard_map/ppermute | solution.py:296
  109.3 4.4 %update_rows.3 = bf16[2048,1536]{1,0:T(8,128)(2,1)} custom-call(s32[4]{0:T(128)S(1)} %pad_add_fusion.place_ref.refs_0_, s32[1,512]{1,0:T(1,128)S(1)} %bitcast.8, bf16[2048,1536]{1,0:T(8,128)(2,1)S(1)} %bitcast.6, bf16[512,1536]{1,0:T(8,128)(2,1)S(1)} %merge.1.refs_3_, ...), custom_call_target="tpu_custom_call", output_to_operand_aliasing={{}: (10, {})} | custom-call | flops 1610612736 | bytes 6291456 | tf_op jit(solution)/shard_map/update_rows/pallas_call | solution.py:258
  (44 shorter events, 1.6 us)
Async XLA Ops:
  0.0 2.8 %copy-start = (bf16[2048,1536]{1,0:T(8,128)(2,1)S(1)}, bf16[2048,1536]{1,0:T(8,128)(2,1)}, u32[]{:S(2)}) copy-start(bf16[2048,1536]{1,0:T(8,128)(2,1)} %refs_6_.3) | copy-start | bytes 18874372
  2.8 5.2 %copy-start.5 = (s32[512]{0:T(512)S(1)}, s32[512]{0:T(512)}, u32[]{:S(2)}) copy-start(s32[512]{0:T(512)} %param.4) | copy-start | bytes 6148
  2.8 15.7 %collective-permute-start.1 = (bf16[512,512]{1,0:T(8,128)(2,1)S(1)}, bf16[512,512]{1,0:T(8,128)(2,1)}, u32[]{:S(2)}, u32[]{:S(2)}) collective-permute-start(bf16[512,512]{1,0:T(8,128)(2,1)S(1)} %chunk.4), channel_id=1, source_target_pairs={{0,2},{4,6},{8,10},{12,14},{16,18},{20,22},{24,26},{28,30}} | collective-permute-start | bytes 1572872 | tf_op jit(solution)/shard_map/ppermute | solution.py:295
  6.4 14.2 %collective-permute-start.2 = (bf16[256,1536]{1,0:T(8,128)(2,1)}, bf16[256,1536]{1,0:T(8,128)(2,1)}, u32[]{:S(2)}, u32[]{:S(2)}) collective-permute-start(bf16[256,1536]{1,0:T(8,128)(2,1)} %slice.26), channel_id=1, source_target_pairs={{0,4},{1,5},{2,6},{3,7}} | collective-permute-start | bytes 2359304 | tf_op jit(solution)/shard_map/ppermute | solution.py:341
  8.2 2.8 %copy-start.1 = (bf16[2048,1536]{1,0:T(8,128)(2,1)S(1)}, bf16[2048,1536]{1,0:T(8,128)(2,1)}, u32[]{:S(2)}) copy-start(bf16[2048,1536]{1,0:T(8,128)(2,1)} %refs_6_.3) | copy-start | bytes 18874372
  16.9 1.7 %copy-start.2 = (bf16[256,1536]{1,0:T(8,128)(2,1)}, bf16[256,1536]{1,0:T(8,128)(2,1)S(1)}, u32[]{:S(2)}) copy-start(bf16[256,1536]{1,0:T(8,128)(2,1)S(1)} %get-tuple-element.11.own_ref) | copy-start | bytes 2359300
  16.9 5.9 %collective-permute-start = (bf16[256,1536]{1,0:T(8,128)(2,1)}, bf16[256,1536]{1,0:T(8,128)(2,1)}, u32[]{:S(2)}, u32[]{:S(2)}) collective-permute-start(bf16[256,1536]{1,0:T(8,128)(2,1)} %get-tuple-element.12), channel_id=1, source_target_pairs={{0,4},{4,0},{8,12},{12,8},{16,20},{20,16},{24,28},{28,24},{1,5},{5... | collective-permute-start | bytes 2359304 | tf_op jit(solution)/shard_map/ppermute | solution.py:348
  17.7 31.4 %slice-start = ((s8[6291456]{0:T(1024)(128)(4,1)}), s8[2097152]{0:T(1024)(128)(4,1)S(1)}, s32[]{:S(2)}) async-start(s8[6291456]{0:T(1024)(128)(4,1)} %bitcast.5), calls=%async_computation | async-start | bytes 4194304
  17.7 9.0 %collective-permute-start.7 = (bf16[512,512]{1,0:T(8,128)(2,1)}, bf16[512,512]{1,0:T(8,128)(2,1)S(1)}, u32[]{:S(2)}, u32[]{:S(2)}) collective-permute-start(bf16[512,512]{1,0:T(8,128)(2,1)} %chunk.5), channel_id=1, source_target_pairs={{0,2},{4,6},{8,10},{12,14},{16,18},{20,22},{24,26},{28,30}} | collective-permute-start | bytes 1572872 | tf_op jit(solution)/shard_map/ppermute | solution.py:295
  18.6 9.4 %collective-permute-start.6 = (bf16[512,512]{1,0:T(8,128)(2,1)}, bf16[512,512]{1,0:T(8,128)(2,1)S(1)}, u32[]{:S(2)}, u32[]{:S(2)}) collective-permute-start(bf16[512,512]{1,0:T(8,128)(2,1)} %collective-permute-done.1.rest_0_.refs_7_), channel_id=1, source_target_pairs={{2,3},{6,7},{10,11},{14,15},{18,19},{22,23},{26,27},{30,31}} | collective-permute-start | bytes 1572872 | tf_op jit(solution)/shard_map/ppermute | solution.py:297
  19.3 18.2 %collective-permute-start.5 = (bf16[512,512]{1,0:T(8,128)(2,1)}, bf16[512,512]{1,0:T(8,128)(2,1)S(1)}, u32[]{:S(2)}, u32[]{:S(2)}) collective-permute-start(bf16[512,512]{1,0:T(8,128)(2,1)} %collective-permute-done.1.rest_0_.refs_7_), channel_id=1, source_target_pairs={{2,1},{6,5},{10,9},{14,13},{18,17},{22,21},{26,25},{30,29}} | collective-permute-start | bytes 1572872 | tf_op jit(solution)/shard_map/ppermute | solution.py:296
  22.0 15.4 %collective-permute-start.10 = (bf16[128,1536]{1,0:T(8,128)(2,1)S(1)}, bf16[128,1536]{1,0:T(8,128)(2,1)S(1)}, u32[]{:S(2)}, u32[]{:S(2)}) collective-permute-start(bf16[128,1536]{1,0:T(8,128)(2,1)S(1)} %get-tuple-element.17.refs_1_), channel_id=1, source_target_pairs={{0,16},{4,20},{1,17},{5,21},{2,18},{6,22},{3,19},{7,23}} | collective-permute-start | bytes 1179656 | tf_op jit(solution)/shard_map/ppermute | solution.py:356
  22.8 1.1 copy-start.3
  25.1 12.4 %collective-permute-start.9 = (bf16[128,1536]{1,0:T(8,128)(2,1)S(1)}, bf16[128,1536]{1,0:T(8,128)(2,1)S(1)}, u32[]{:S(2)}, u32[]{:S(2)}) collective-permute-start(bf16[128,1536]{1,0:T(8,128)(2,1)S(1)} %get-tuple-element.14.refs_0_), channel_id=1, source_target_pairs={{0,16},{4,20},{8,24},{12,28},{16,0},{20,4},{24,8},{28,12},{1,17},{... | collective-permute-start | bytes 1179656 | tf_op jit(solution)/shard_map/ppermute | solution.py:353
  26.7 16.9 %collective-permute-start.4 = (bf16[128,1536]{1,0:T(8,128)(2,1)S(1)}, bf16[128,1536]{1,0:T(8,128)(2,1)S(1)}, u32[]{:S(2)}, u32[]{:S(2)}) collective-permute-start(bf16[128,1536]{1,0:T(8,128)(2,1)S(1)} %get-tuple-element.18.refs_1_), channel_id=1, source_target_pairs={{0,8},{4,12},{1,9},{5,13},{2,10},{6,14},{3,11},{7,15}} | collective-permute-start | bytes 1179656 | tf_op jit(solution)/shard_map/ppermute | solution.py:356
  28.0 21.1 %slice-start.1 = ((s8[6291456]{0:T(1024)(128)(4,1)}), s8[4194304]{0:T(1024)(128)(4,1)S(1)}, s32[]{:S(2)}) async-start(s8[6291456]{0:T(1024)(128)(4,1)} %bitcast.5), calls=%async_computation.1 | async-start | bytes 8388608
  28.0 21.0 %collective-permute-start.3 = (bf16[128,1536]{1,0:T(8,128)(2,1)S(1)}, bf16[128,1536]{1,0:T(8,128)(2,1)S(1)}, u32[]{:S(2)}, u32[]{:S(2)}) collective-permute-start(bf16[128,1536]{1,0:T(8,128)(2,1)S(1)} %get-tuple-element.13.refs_0_), channel_id=1, source_target_pairs={{0,8},{4,12},{8,0},{12,4},{16,24},{20,28},{24,16},{28,20},{1,9},{5... | collective-permute-start | bytes 1179656 | tf_op jit(solution)/shard_map/ppermute | solution.py:353
  37.6 36.8 %collective-permute-start.11 = (bf16[256,1536]{1,0:T(8,128)(2,1)S(1)}, bf16[256,1536]{1,0:T(8,128)(2,1)S(1)}, u32[]{:S(2)}, u32[]{:S(2)}) collective-permute-start(bf16[256,1536]{1,0:T(8,128)(2,1)S(1)} %stack_sum.3.second_ref), channel_id=1, source_target_pairs={{0,8},{4,12},{8,0},{12,4},{16,24},{20,28},{24,16},{28,20},{1,9},{5... | collective-permute-start | bytes 2359304 | tf_op jit(solution)/shard_map/ppermute | solution.py:368
  49.0 25.3 %collective-permute-start.8 = (bf16[256,1536]{1,0:T(8,128)(2,1)S(1)}, bf16[256,1536]{1,0:T(8,128)(2,1)S(1)}, u32[]{:S(2)}, u32[]{:S(2)}) collective-permute-start(bf16[256,1536]{1,0:T(8,128)(2,1)S(1)} %stack_sum.2.first_ref), channel_id=1, source_target_pairs={{0,16},{4,20},{8,24},{12,28},{16,0},{20,4},{24,8},{28,12},{1,17},{... | collective-permute-start | bytes 2359304 | tf_op jit(solution)/shard_map/ppermute | solution.py:368
  49.2 45.1 %copy-start.4 = (bf16[512,512]{1,0:T(8,128)(2,1)S(1)}, bf16[512,512]{1,0:T(8,128)(2,1)}, u32[]{:S(2)}) copy-start(bf16[512,512]{1,0:T(8,128)(2,1)} %refs_5_.1) | copy-start | bytes 1572868
  49.2 2.8 %collective-permute-start.14 = (bf16[512,512]{1,0:T(8,128)(2,1)S(1)}, bf16[512,512]{1,0:T(8,128)(2,1)S(1)}, u32[]{:S(2)}, u32[]{:S(2)}) collective-permute-start(bf16[512,512]{1,0:T(8,128)(2,1)S(1)} %chunk.6), channel_id=1, source_target_pairs={{0,2},{4,6},{8,10},{12,14},{16,18},{20,22},{24,26},{28,30}} | collective-permute-start | bytes 1572872 | tf_op jit(solution)/shard_map/ppermute | solution.py:295
  50.0 2.0 %collective-permute-start.13 = (bf16[512,512]{1,0:T(8,128)(2,1)S(1)}, bf16[512,512]{1,0:T(8,128)(2,1)S(1)}, u32[]{:S(2)}, u32[]{:S(2)}) collective-permute-start(bf16[512,512]{1,0:T(8,128)(2,1)S(1)} %collective-permute-done.7.refs_6_.refs_10_), channel_id=1, source_target_pairs={{2,3},{6,7},{10,11},{14,15},{18,19},{22,23},{26,27},{30,31}} | collective-permute-start | bytes 1572872 | tf_op jit(solution)/shard_map/ppermute | solution.py:297
  50.8 23.6 %collective-permute-start.12 = (bf16[512,512]{1,0:T(8,128)(2,1)S(1)}, bf16[512,512]{1,0:T(8,128)(2,1)S(1)}, u32[]{:S(2)}, u32[]{:S(2)}) collective-permute-start(bf16[512,512]{1,0:T(8,128)(2,1)S(1)} %collective-permute-done.7.refs_6_.refs_10_), channel_id=1, source_target_pairs={{2,1},{6,5},{10,9},{14,13},{18,17},{22,21},{26,25},{30,29}} | collective-permute-start | bytes 1572872 | tf_op jit(solution)/shard_map/ppermute | solution.py:296
  74.5 19.8 %collective-permute-start.15 = (bf16[512,1536]{1,0:T(8,128)(2,1)S(1)}, bf16[512,1536]{1,0:T(8,128)(2,1)S(1)}, u32[]{:S(2)}, u32[]{:S(2)}) collective-permute-start(bf16[512,1536]{1,0:T(8,128)(2,1)S(1)} %merge.1.refs_3_), channel_id=1, source_target_pairs={{0,4},{4,0},{8,12},{12,8},{16,20},{20,16},{24,28},{28,24},{1,5},{5... | collective-permute-start | bytes 4718600 | tf_op jit(solution)/shard_map/ppermute | solution.py:372
  74.6 2.7 %collective-permute-start.18 = (bf16[512,512]{1,0:T(8,128)(2,1)S(1)}, bf16[512,512]{1,0:T(8,128)(2,1)S(1)}, u32[]{:S(2)}, u32[]{:S(2)}) collective-permute-start(bf16[512,512]{1,0:T(8,128)(2,1)S(1)} %chunk.7), channel_id=1, source_target_pairs={{0,2},{4,6},{8,10},{12,14},{16,18},{20,22},{24,26},{28,30}} | collective-permute-start | bytes 1572872 | tf_op jit(solution)/shard_map/ppermute | solution.py:295
  75.3 4.0 %collective-permute-start.17 = (bf16[512,512]{1,0:T(8,128)(2,1)S(1)}, bf16[512,512]{1,0:T(8,128)(2,1)S(1)}, u32[]{:S(2)}, u32[]{:S(2)}) collective-permute-start(bf16[512,512]{1,0:T(8,128)(2,1)S(1)} %collective-permute-done.14.rest_2_.refs_13_), channel_id=1, source_target_pairs={{2,3},{6,7},{10,11},{14,15},{18,19},{22,23},{26,27},{30,31}} | collective-permute-start | bytes 1572872 | tf_op jit(solution)/shard_map/ppermute | solution.py:297
  76.0 18.3 %collective-permute-start.16 = (bf16[512,512]{1,0:T(8,128)(2,1)S(1)}, bf16[512,512]{1,0:T(8,128)(2,1)S(1)}, u32[]{:S(2)}, u32[]{:S(2)}) collective-permute-start(bf16[512,512]{1,0:T(8,128)(2,1)S(1)} %collective-permute-done.14.rest_2_.refs_13_), channel_id=1, source_target_pairs={{2,1},{6,5},{10,9},{14,13},{18,17},{22,21},{26,25},{30,29}} | collective-permute-start | bytes 1572872 | tf_op jit(solution)/shard_map/ppermute | solution.py:296
  77.3 26.9 %collective-permute-start.20 = (bf16[512,512]{1,0:T(8,128)(2,1)S(1)}, bf16[512,512]{1,0:T(8,128)(2,1)S(1)}, u32[]{:S(2)}, u32[]{:S(2)}) collective-permute-start(bf16[512,512]{1,0:T(8,128)(2,1)S(1)} %collective-permute-done.18.refs_7_), channel_id=1, source_target_pairs={{2,3},{6,7},{10,11},{14,15},{18,19},{22,23},{26,27},{30,31}} | collective-permute-start | bytes 1572872 | tf_op jit(solution)/shard_map/ppermute | solution.py:297
  78.0 31.3 %collective-permute-start.19 = (bf16[512,512]{1,0:T(8,128)(2,1)S(1)}, bf16[512,512]{1,0:T(8,128)(2,1)S(1)}, u32[]{:S(2)}, u32[]{:S(2)}) collective-permute-start(bf16[512,512]{1,0:T(8,128)(2,1)S(1)} %collective-permute-done.18.refs_7_), channel_id=1, source_target_pairs={{2,1},{6,5},{10,9},{14,13},{18,17},{22,21},{26,25},{30,29}} | collective-permute-start | bytes 1572872 | tf_op jit(solution)/shard_map/ppermute | solution.py:296

commit v3 on v0

v3 whole, which is shorter than its diff:
```python
import functools

import jax
import jax.numpy as jnp
from jax import lax
from jax.experimental import pallas as pl
from jax.experimental.pallas import tpu as pltpu
from jax.sharding import PartitionSpec as P

GROUPS = 4
PARTS = 2
BLOCK = 512
F32, BF16 = jnp.float32, jnp.bfloat16
VMEM = pl.BlockSpec(memory_space=pltpu.VMEM)
ANY = pl.BlockSpec(memory_space=pl.ANY)
SMEM = pl.BlockSpec(memory_space=pltpu.SMEM)
SMALL = pltpu.CompilerParams(vmem_limit_bytes=8 * 2**20)
LARGE = pltpu.CompilerParams(vmem_limit_bytes=28 * 2**20)


def cost(flops, moved):
    return pl.CostEstimate(flops=flops, bytes_accessed=moved, transcendentals=0)


def chunk_kernel(first_row, axis, place_ref, matrix_ref, *refs):
    out_ref, sem = refs[-2:]
    rows, width = out_ref.shape

    @pl.when(place_ref[axis] == 0)
    def _():
        copy = pltpu.make_async_copy(
            matrix_ref.at[pl.ds(first_row, rows), pl.ds(0, width)], out_ref, sem
        )
        copy.start()
        copy.wait()


def chunk(place, axis, matrix, first_row, rows, width, held=None):
    in_specs, operands = [SMEM, ANY], [place, matrix]
    if held is not None:
        in_specs.append(ANY)
        operands.append(held)
    return pl.pallas_call(
        functools.partial(chunk_kernel, first_row, axis),
        in_specs=in_specs,
        out_specs=ANY,
        out_shape=jax.ShapeDtypeStruct((rows, width), BF16),
        scratch_shapes=[pltpu.SemaphoreType.DMA],
        input_output_aliases={} if held is None else {2: 0},
        compiler_params=SMALL,
        cost_estimate=cost(0, 4 * rows * width),
        name="chunk",
    )(*operands)


def pick_kernel(place_ref, pivots_ref, matrix_ref, *refs):
    onehot_ref = refs[PARTS * 2]
    rows = matrix_ref.shape[0]
    width = pivots_ref.shape[0]
    count = width // (2 * PARTS)

    @pl.when(pl.program_id(0) == 0)
    def _():
        row = lax.broadcasted_iota(jnp.int32, (width, rows), 1) + place_ref[0] * rows
        onehot_ref[...] = jnp.where(pivots_ref[...] == row, 1.0, 0.0).astype(BF16)

    picked = jnp.dot(onehot_ref[...], matrix_ref[...], preferred_element_type=F32).astype(BF16)
    for number, out_ref in enumerate(refs[: PARTS * 2]):
        out_ref[...] = picked[number * count : (number + 1) * count]


def pick(place, pivots, matrix):
    rows, cols = matrix.shape
    width = pivots.shape[0]
    block = min(BLOCK, cols)
    count = width // (2 * PARTS)
    return pl.pallas_call(
        pick_kernel,
        grid_spec=pltpu.PrefetchScalarGridSpec(
            num_scalar_prefetch=1,
            grid=(cols // block,),
            in_specs=[
                pl.BlockSpec((width, 1), lambda i, s: (0, 0)),
                pl.BlockSpec((rows, block), lambda i, s: (0, i)),
            ],
            out_specs=[pl.BlockSpec((count, block), lambda i, s: (0, i))] * (2 * PARTS),
            scratch_shapes=[pltpu.VMEM((width, rows), BF16)],
        ),
        out_shape=[jax.ShapeDtypeStruct((count, cols), BF16)] * (2 * PARTS),
        compiler_params=LARGE,
        cost_estimate=cost(2 * width * rows * cols, 2 * rows * cols),
        name="pick_rows",
    )(place, pivots[:, None], matrix)


def add_kernel(count, *refs):
    for own_ref, got_ref, out_ref in zip(refs[:count], refs[count:], refs[-count:]):
        out_ref[...] = own_ref[...] + got_ref[...]


def add(own, got, after=()):
    size = sum(x.size for x in own)
    return pl.pallas_call(
        functools.partial(add_kernel, len(own)),
        in_specs=[VMEM] * (2 * len(own)) + [ANY] * len(after),
        out_specs=[VMEM] * len(own),
        out_shape=[jax.ShapeDtypeStruct(x.shape, BF16) for x in own],
        compiler_params=SMALL,
        cost_estimate=cost(size, 6 * size),
        name="add",
    )(*own, *got, *after)


def exchange(parts, pairs):
    return [lax.ppermute(x, "prow", pairs) for x in parts]


def swap_kernel(place_ref, pivots_ref, matrix_ref, mine_ref, other_ref, *rest):
    out_ref, token_ref, onehot_ref, keep_ref = rest[-4:]
    token_ref[...] = jnp.zeros_like(token_ref)
    step = pl.program_id(0)
    rows, block = matrix_ref.shape
    width = pivots_ref.shape[1]
    half = width // 2
    row_place, col_place, core = (place_ref[i] for i in range(3))
    piece = min(rows, 512)

    @pl.when(step == 0)
    def _():
        for start in range(0, rows, piece):
            here = slice(start, start + piece)
            row = lax.broadcasted_iota(jnp.int32, (piece, width), 0) + row_place * rows + start
            onehot = jnp.where(pivots_ref[...] == row, 1.0, 0.0)
            onehot_ref[here] = onehot.astype(BF16)
            has_pivot = jnp.max(onehot, axis=1, keepdims=True)
            keep_ref[here] = jnp.broadcast_to(1.0 - has_pivot, (piece, 128))

    in_panel = (col_place == 0) & (step * block < width)

    @pl.when(in_panel)
    def _():
        out_ref[...] = matrix_ref[...]

    @pl.when(jnp.logical_not(in_panel))
    def _():
        mine, other = mine_ref[...], other_ref[...]
        top, bottom = jnp.where(core == 0, mine, other), jnp.where(core == 0, other, mine)
        for start in range(0, rows, piece):
            here = slice(start, start + piece)
            keep = jnp.concatenate([keep_ref[here]] * (block // 128), axis=1)
            moved = jnp.dot(onehot_ref[here, :half], top, preferred_element_type=F32)
            moved += jnp.dot(onehot_ref[here, half:], bottom, preferred_element_type=F32)
            out_ref[here] = (matrix_ref[here].astype(F32) * keep + moved).astype(BF16)


def swap(place, pivots, matrix, mine, other, after=()):
    rows, cols = matrix.shape
    width = pivots.shape[0]
    block = min(BLOCK, cols)
    by_column = pl.BlockSpec((rows, block), lambda i, s: (0, i))
    half_by_column = pl.BlockSpec((width // 2, block), lambda i, s: (0, i))
    return pl.pallas_call(
        swap_kernel,
        grid_spec=pltpu.PrefetchScalarGridSpec(
            num_scalar_prefetch=1,
            grid=(cols // block,),
            in_specs=[
                pl.BlockSpec((1, width), lambda i, s: (0, 0)),
                by_column,
                half_by_column,
                half_by_column,
            ]
            + [ANY] * len(after),
            out_specs=[by_column, pl.BlockSpec((8, 128), lambda i, s: (0, 0))],
            scratch_shapes=[pltpu.VMEM((rows, width), BF16), pltpu.VMEM((rows, 128), F32)],
        ),
        out_shape=[
            jax.ShapeDtypeStruct((rows, cols), BF16),
            jax.ShapeDtypeStruct((8, 128), F32),
        ],
        compiler_params=LARGE,
        cost_estimate=cost(2 * rows * width * cols, 4 * rows * cols),
        name="swap_rows",
    )(place, pivots[None, :], matrix, mine, other, *after)


def upper_kernel(place_ref, inverse_ref, *refs):
    mine_refs, other_refs, out_ref = refs[:PARTS], refs[PARTS : 2 * PARTS], refs[-1]
    width, cols = out_ref.shape
    count = width // (2 * PARTS)
    block = min(BLOCK, cols)
    for start in range(0, cols, block):
        here = slice(start, start + block)
        first = place_ref[2] == 0
        total = None
        for number in range(2 * PARTS):
            part = number % PARTS
            mine, other = mine_refs[part][:, here], other_refs[part][:, here]
            rows = jnp.where(first == (number < PARTS), mine, other)
            inverse = inverse_ref[:, number * count : (number + 1) * count]
            term = jnp.dot(inverse, rows, preferred_element_type=F32)
            total = term if total is None else total + term
        out_ref[:, here] = total.astype(BF16)


def upper_rows(place, unit_inverse, mine, other, after=()):
    width, cols = unit_inverse.shape[0], mine[0].shape[1]
    return pl.pallas_call(
        upper_kernel,
        in_specs=[SMEM] + [VMEM] * (1 + 2 * PARTS) + [ANY] * len(after),
        out_specs=VMEM,
        out_shape=jax.ShapeDtypeStruct((width, cols), BF16),
        compiler_params=pltpu.CompilerParams(vmem_limit_bytes=16 * 2**20),
        cost_estimate=cost(2 * width * width * cols, 4 * width * cols),
        name="upper",
    )(place, unit_inverse, *mine, *other, *after)


def update_kernel(groups, per_group, pick_source, place_ref, swapped_ref, upper_ref, *refs):
    sources = refs[: 1 + per_group * len(groups)]
    out_ref, panel_ref, sem = refs[-3:]
    step = pl.program_id(0)
    width = panel_ref.shape[1]
    block = out_ref.shape[1]
    row_place, col_place = place_ref[0], place_ref[1]
    first_row = groups[0][0]

    def fetch(number, action):
        start, count = groups[number]
        here = panel_ref.at[pl.ds(start - first_row, count)]
        views = [sources[0].at[pl.ds(start, count), pl.ds(0, width)]]
        views += sources[1 + number * per_group : 1 + (number + 1) * per_group]
        for choice, view in enumerate(views):
            @pl.when(pick_source(col_place) == choice)
            def _():
                action(pltpu.make_async_copy(view, here, sem.at[number]))

    @pl.when(step == 0)
    def _():
        for number in range(len(groups)):
            fetch(number, lambda copy: copy.start())
        for number in range(len(groups)):
            fetch(number, lambda copy: copy.wait())

    in_panel = (col_place == 0) & (step * block < width)

    @pl.when(in_panel)
    def _():
        out_ref[...] = swapped_ref[...]

    @pl.when(jnp.logical_not(in_panel))
    def _():
        upper = upper_ref[...]
        for start, count in groups:
            here = slice(start - first_row, start - first_row + count)
            product = jnp.dot(panel_ref[here], upper, preferred_element_type=F32)
            out_ref[here] = (swapped_ref[here].astype(F32) - product).astype(BF16)
        if first_row < width:
            @pl.when(row_place == 0)
            def _():
                out_ref[: width - first_row] = upper[first_row:]


def update(groups, pick_source, place, matrix, swapped, upper, received):
    rows, cols = matrix.shape
    width = upper.shape[0]
    block = min(BLOCK, cols)
    count = sum(size for _, size in groups)
    position = groups[0][0] // count
    by_column = pl.BlockSpec((count, block), lambda i, s: (position, i))
    sources = [matrix] + [x for group in received for x in group]
    return pl.pallas_call(
        functools.partial(update_kernel, groups, len(received[0]), pick_source),
        grid_spec=pltpu.PrefetchScalarGridSpec(
            num_scalar_prefetch=1,
            grid=(cols // block,),
            in_specs=[by_column, pl.BlockSpec((width, block), lambda i, s: (0, i))]
            + [ANY] * len(sources),
            out_specs=by_column,
            scratch_shapes=[
                pltpu.VMEM((count, width), BF16),
                pltpu.SemaphoreType.DMA((len(groups),)),
            ],
        ),
        out_shape=jax.ShapeDtypeStruct((rows, cols), BF16),
        input_output_aliases={1: 0},
        compiler_params=LARGE,
        cost_estimate=cost(2 * count * width * cols, 4 * count * cols),
        name="update_rows",
    )(place, swapped, upper, *sources)


def swap_pairs(size, orders, step):
    return [(i, i ^ (1 << orders[i & 1][step])) for i in range(size)]


def grow_pairs(orders, step):
    pairs = []
    for core, order in enumerate(orders):
        places = [core]
        for bit in order[:step]:
            places += [i | (1 << bit) for i in places]
        pairs += [(i, i | (1 << order[step])) for i in places]
    return pairs


def spread(place, matrix, width, groups, axis, size):
    middle = size // 2
    count = len(groups)
    held = []
    for number in range(count + 2):
        pairs = [(middle, middle - 1)]
        back = held[number - 2] if number >= 2 else None
        if number < count:
            pairs = [(0, middle)] + pairs * (number >= 2)
            sent = chunk(place, 1, matrix, *groups[number], width, back)
            if number >= 2:
                held[number - 2] = sent
        else:
            sent = back
        held.append(lax.ppermute(sent, axis, pairs))
    received = []
    for number in range(count):
        arrays = [held[number], held[number + 2]]
        arrays.append(lax.ppermute(held[number], axis, [(middle, middle + 1)]))
        distance = 1
        while middle - distance > 1 or middle + distance + 1 < size:
            if distance == 1:
                both = jnp.where(lax.axis_index(axis) < middle, arrays[1], arrays[2])
            pairs = []
            if middle - distance > 1:
                pairs.append((middle - distance, middle - distance - 1))
            if middle + distance + 1 < size:
                pairs.append((middle + distance, middle + distance + 1))
            both = lax.ppermute(both, axis, pairs)
            arrays.append(both)
            distance += 1
        received.append(arrays)
    return received


def source_of(size):
    middle = size // 2

    def pick_source(place):
        away = jnp.abs(place - middle)
        number = jnp.where(away == 0, 1, jnp.where(place < middle, 2, 3))
        number = jnp.where(away >= 2, away + 2, number)
        return jnp.where(place == 0, 0, number)

    return pick_source


def per_device(n_prow, n_pcol, matrix, pivots, unit_inverse):
    rows, cols = matrix.shape
    width = unit_inverse.shape[0]
    half = width // 2
    row_place = lax.axis_index("prow")
    col_place = lax.axis_index("pcol")
    core = row_place & 1
    place = jnp.stack([row_place, col_place, core]).astype(jnp.int32)
    matrix = pltpu.with_memory_space_constraint(matrix, pltpu.HBM)
    bits = list(range(1, n_prow.bit_length() - 1))
    orders = (bits, bits[::-1])
    cores = ([0], [0])
    last = len(bits) - 1

    size = rows // GROUPS
    groups = [(number * size, size) for number in range(GROUPS)]
    received = spread(place, matrix, width, groups, "pcol", n_pcol)
    arrived = [arrays[0] for arrays in received]
    arrived_left = [arrays[1] for arrays in received]
    arrived_right = [arrays[2] for arrays in received]

    order = jnp.where(core == 0, pivots, jnp.roll(pivots, half))
    down_got = lax.ppermute(chunk(place, 0, matrix, half, half, cols), "prow", [(0, 1)])
    picked = pick(place, order, matrix)
    up = picked[:PARTS]
    up_got = exchange(picked[PARTS:], swap_pairs(n_prow, cores, 0))
    down = chunk(place, 0, matrix, 0, half, cols, down_got)
    for step in range(last + 1):
        down_got = lax.ppermute(down, "prow", grow_pairs(orders, step))
        up = add(up, up_got, arrived[:1] if step == 0 else arrived[1:2] + arrived_right[:1])
        up_got = exchange(up, swap_pairs(n_prow, orders, step))
        (down,) = add([down], [down_got], up[-1:])
    down_got = lax.ppermute(down, "prow", swap_pairs(n_prow, cores, 0))
    swapped, token = swap(place, pivots, matrix, down, down_got, arrived[2:3])
    up = add(up, up_got, [token] + arrived_right[1:2])
    up_got = exchange(up, swap_pairs(n_prow, cores, 0))
    upper = upper_rows(place, unit_inverse, up, up_got, arrived[3:4])

    common = (source_of(n_pcol), place, matrix)
    out = update(groups[:-1], *common, swapped, upper, received[:-1])
    return update(groups[-1:], *common, out, upper, received[-1:])


def solution(mesh):
    return jax.shard_map(
        functools.partial(per_device, mesh.shape["prow"], mesh.shape["pcol"]),
        mesh=mesh,
        in_specs=(P("prow", "pcol"), P(), P()),
        out_specs=P("prow", "pcol"),
        check_vma=False,
    )
```

time: 186 us -> 102 us (0.55); the launches traced: 183 us -> 101 us
  blocking collectives: 78.9 us -> 0 us
  local copies, waits for them, and re-layouts: 34 us -> 0.16 us
  Pallas kernels: 0 us -> 33.8 us
  starting transfers between devices: 0.04 us -> 17.5 us
  waiting for transfers between devices: 33.2 us -> 48.9 us
  matrix products: 13.3 us -> 0 us
  between operations: 13.5 us -> 0.3 us
  other arithmetic: 9.77 us -> 0.08 us
    psum x1 -> x0, blocking collectives: 78.9 us -> none  [per_device(): full_rows = lax.psum(masked, 'prow').astype(jnp.bfloat16)]
    ppermute x0 -> x22, waiting for transfers between devices: none -> 48.9 us  [the longest x6 29.3 us: spread(): held.append(lax.ppermute(sent, axis, pairs))]
    pallas_call x0 -> x16, Pallas kernels: none -> 33.8 us  [the longest x2 11.8 us: update(): pl.pallas_call(functools.partial(update_kernel, groups, len(received[0]),...]
    psum x2 -> x0, waiting for transfers between devices: 33.1 us -> none  [from_root(): return lax.psum(jnp.where(mine, value, jnp.zeros_like(value)), axis)]
    gather x3 -> x0, local copies, waits for them, and re-layouts: 32.2 us -> none  [the longest x1 15 us: per_device(): jnp.take(displaced, slot_index, axis=0)]
    ppermute x0 -> x22, starting transfers between devices: none -> 17.5 us  [the longest x6 6.52 us: spread(): held.append(lax.ppermute(sent, axis, pairs))]
    dot_general x2 -> x0, matrix products: 13.3 us -> none  [the longest x1 11 us: per_device(): jnp.dot(panel_rows, upper, preferred_element_type=jnp.float32)]
    select_n x3 -> x1, other arithmetic: 7.93 us -> 0.01 us  [per_device(): order = jnp.where(core == 0, pivots, jnp.roll(pivots, half))]
  transfers between devices with their start and end apart: 2 -> 22, of which waited for: 1 -> 9; matrix products, arithmetic and copies ran while one was open for 24% -> 0% of each run, Pallas kernels for 0% -> 28%
where the time goes in v3:
time: 102 us; the launch traced here: 101 us
  waiting for transfers between devices  48.9 us (48%)
  Pallas kernels  33.8 us (33%)
  starting transfers between devices  17.5 us (17%)
    ppermute x6, waiting for transfers between devices, spread(): held.append(lax.ppermute(sent, axis, pairs))  29.3 us
    ppermute x8, waiting for transfers between devices, exchange(): return [lax.ppermute(x, 'prow', pairs) for x in parts]  16.5 us
    pallas_call x2, Pallas kernels, update(): pl.pallas_call(functools.partial(update_kernel, groups, len(received[0]),...  11.8 us
    pallas_call x1, Pallas kernels, swap(): pl.pallas_call(swap_kernel, grid_spec=pltpu.PrefetchScalarGridSpec(num_sc...  9.11 us
    pallas_call x1, Pallas kernels, pick(): pl.pallas_call(pick_kernel, grid_spec=pltpu.PrefetchScalarGridSpec(num_sc...  6.72 us
    ppermute x6, starting transfers between devices, spread(): held.append(lax.ppermute(sent, axis, pairs))  6.52 us
    ppermute x8, starting transfers between devices, exchange(): return [lax.ppermute(x, 'prow', pairs) for x in parts]  4.81 us
    pallas_call x6, Pallas kernels, chunk(): pl.pallas_call(functools.partial(chunk_kernel, first_row, axis), in_specs...  3.34 us
  transfers between devices with their start and end apart: 22, of which 9 were waited for; matrix products, arithmetic and copies ran while one was open for 0% of the time, Pallas kernels for 28%

profile of v3, /device:TPU:13, one launch (start us, length us, event | category | flops | bytes accessed | tf_op | source)
XLA Modules:
  0.0 100.7 jit_solution(20786607581771297)
XLA Ops:
  0.6 0.7 collective-permute-start
  1.4 0.6 chunk.8
  1.9 0.7 collective-permute-start.4
  3.2 1.3 %collective-permute-start.1 = (bf16[256,1536]{1,0:T(8,128)(2,1)S(1)}, bf16[256,1536]{1,0:T(8,128)(2,1)S(1)}, u32[]{:S(2)}, u32[]{:S(2)}) collective-permute-start(bf16[256,1536]{1,0:T(8,128)(2,1)S(1)} %chunk.7.refs_0_), channel_id=1, source_target_pairs={{0,8},{4,20},{1,9},{5,21},{2,10},{6,22},{3,11},{7,23}} | collective-permute-start | bytes 2359304 | tf_op jit(solution)/shard_map/ppermute | solution.py:382
  4.7 6.7 %pick_rows.1 = (bf16[128,1536]{1,0:T(8,128)(2,1)S(1)}, bf16[128,1536]{1,0:T(8,128)(2,1)S(1)}, bf16[128,1536]{1,0:T(8,128)(2,1)S(1)}, bf16[128,1536]{1,0:T(8,128)(2,1)S(1)}) custom-call(s32[3]{0:T(128)S(1)} %pad_add_fusion.place_ref, s32[512,1]{1,0:T(8,128)S(1)} %copy.9.pivots_ref, bf16[2048,1536]{1,0:T(8,128)(2,1)} %refs_0_.3), custom_call_target="tpu_custom_call" | custom-call | flops 3221225472 | bytes 6291456 | tf_op jit(solution)/shard_map/pick_rows/pallas_call | solution.py:77
  12.6 0.6 collective-permute-done.2.refs_2_
  13.2 0.6 collective-permute-done.3.refs_3_
  13.9 3.1 %collective-permute-done.1.refs_1_ = bf16[256,1536]{1,0:T(8,128)(2,1)S(1)} collective-permute-done((bf16[256,1536]{1,0:T(8,128)(2,1)S(1)}, bf16[256,1536]{1,0:T(8,128)(2,1)S(1)}, u32[]{:S(2)}, u32[]{:S(2)}) %collective-permute-start.1) | collective-permute-done | bytes 786464 | tf_op jit(solution)/shard_map/ppermute | solution.py:382
  17.0 1.3 %collective-permute-start.5 = (bf16[256,1536]{1,0:T(8,128)(2,1)S(1)}, bf16[256,1536]{1,0:T(8,128)(2,1)S(1)}, u32[]{:S(2)}, u32[]{:S(2)}) collective-permute-start(bf16[256,1536]{1,0:T(8,128)(2,1)S(1)} %add.12.refs_0_), channel_id=1, source_target_pairs={{0,16},{8,24},{4,12},{20,28},{1,17},{9,25},{5,13},{21,29},{2,18},{... | collective-permute-start | bytes 2359304 | tf_op jit(solution)/shard_map/ppermute | solution.py:382
  18.9 0.7 collective-permute-start.8
  19.6 0.7 collective-permute-start.9
  20.3 1.0 collective-permute-start.6
  22.4 9.2 %collective-permute-done.6.refs_2_ = bf16[128,1536]{1,0:T(8,128)(2,1)S(1)} collective-permute-done((bf16[128,1536]{1,0:T(8,128)(2,1)S(1)}, bf16[128,1536]{1,0:T(8,128)(2,1)S(1)}, u32[]{:S(2)}, u32[]{:S(2)}) %collective-permute-start.6) | collective-permute-done | bytes 393248 | tf_op jit(solution)/shard_map/ppermute | solution.py:115
  31.6 6.1 %collective-permute-done.7.refs_3_ = bf16[128,1536]{1,0:T(8,128)(2,1)S(1)} collective-permute-done((bf16[128,1536]{1,0:T(8,128)(2,1)S(1)}, bf16[128,1536]{1,0:T(8,128)(2,1)S(1)}, u32[]{:S(2)}, u32[]{:S(2)}) %collective-permute-start.7) | collective-permute-done | bytes 393248 | tf_op jit(solution)/shard_map/ppermute | solution.py:115
  38.0 1.3 %collective-permute-start.11 = (bf16[512,512]{1,0:T(8,128)(2,1)S(1)}, bf16[512,512]{1,0:T(8,128)(2,1)S(1)}, u32[]{:S(2)}, u32[]{:S(2)}) collective-permute-start(bf16[512,512]{1,0:T(8,128)(2,1)S(1)} %chunk.9.refs_4_.refs_1_), channel_id=1, source_target_pairs={{0,2},{2,1},{4,6},{6,5},{8,10},{10,9},{12,14},{14,13},{16,18},{18,... | collective-permute-start | bytes 1572872 | tf_op jit(solution)/shard_map/ppermute | solution.py:321
  39.3 0.7 collective-permute-start.14
  40.0 0.6 collective-permute-start.12
  40.6 0.9 collective-permute-start.13
  41.5 15.3 %collective-permute-done.11.rest_0_.refs_2_.refs_7_ = bf16[512,512]{1,0:T(8,128)(2,1)S(1)} collective-permute-done((bf16[512,512]{1,0:T(8,128)(2,1)S(1)}, bf16[512,512]{1,0:T(8,128)(2,1)S(1)}, u32[]{:S(2)}, u32[]{:S(2)}) %collective-permute-start.11) | collective-permute-done | bytes 524320 | tf_op jit(solution)/shard_map/ppermute | solution.py:321
  56.8 1.3 %collective-permute-start.17 = (bf16[512,512]{1,0:T(8,128)(2,1)S(1)}, bf16[512,512]{1,0:T(8,128)(2,1)S(1)}, u32[]{:S(2)}, u32[]{:S(2)}) collective-permute-start(bf16[512,512]{1,0:T(8,128)(2,1)S(1)} %chunk.11.refs_4_), channel_id=1, source_target_pairs={{0,2},{2,1},{4,6},{6,5},{8,10},{10,9},{12,14},{14,13},{16,18},{18,... | collective-permute-start | bytes 1572872 | tf_op jit(solution)/shard_map/ppermute | solution.py:321
  58.1 9.1 %swap_rows.1 = (bf16[2048,1536]{1,0:T(8,128)(2,1)}, f32[8,128]{1,0:T(8,128)S(1)}) custom-call(s32[3]{0:T(128)S(1)} %pad_add_fusion.place_ref, s32[1,512]{1,0:T(1,128)S(1)} %bitcast.5, bf16[2048,1536]{1,0:T(8,128)(2,1)} %refs_0_.3, bf16[256,1536]{1,0:T(8,128)(2,1)S(1)} %add.14.mine_ref, bf16[256,1536]{1,0:T(8,128)(2,1)S(1)} %collective-permute-done.10.other_ref, ...), custom_call_target="tpu_custom_call" | custom-call | flops 3221225472 | bytes 12582912 | tf_op jit(solution)/shard_map/swap_rows/pallas_call | solution.py:162
  67.3 1.1 %collective-permute-start.15 = (bf16[128,1536]{1,0:T(8,128)(2,1)S(1)}, bf16[128,1536]{1,0:T(8,128)(2,1)S(1)}, u32[]{:S(2)}, u32[]{:S(2)}) collective-permute-start(bf16[128,1536]{1,0:T(8,128)(2,1)S(1)} %get-tuple-element.27.refs_0_), channel_id=1, source_target_pairs={{0,4},{4,0},{8,12},{12,8},{16,20},{20,16},{24,28},{28,24},{1,5},{5... | collective-permute-start | bytes 1179656 | tf_op jit(solution)/shard_map/ppermute | solution.py:115
  68.4 1.3 %collective-permute-start.18 = (bf16[512,512]{1,0:T(8,128)(2,1)S(1)}, bf16[512,512]{1,0:T(8,128)(2,1)S(1)}, u32[]{:S(2)}, u32[]{:S(2)}) collective-permute-start(bf16[512,512]{1,0:T(8,128)(2,1)S(1)} %collective-permute-done.11.rest_0_.refs_2_.refs_7_), channel_id=1, source_target_pairs={{2,1},{6,5},{10,9},{14,13},{18,17},{22,21},{26,25},{30,29}} | collective-permute-start | bytes 1572872 | tf_op jit(solution)/shard_map/ppermute | solution.py:321
  69.7 0.7 collective-permute-start.19
  70.5 1.1 %collective-permute-done.17.refs_4_.refs_5_.refs_1_ = bf16[512,512]{1,0:T(8,128)(2,1)S(1)} collective-permute-done((bf16[512,512]{1,0:T(8,128)(2,1)S(1)}, bf16[512,512]{1,0:T(8,128)(2,1)S(1)}, u32[]{:S(2)}, u32[]{:S(2)}) %collective-permute-start.17) | collective-permute-done | bytes 524320 | tf_op jit(solution)/shard_map/ppermute | solution.py:321
  71.6 1.3 %collective-permute-start.20 = (bf16[512,512]{1,0:T(8,128)(2,1)S(1)}, bf16[512,512]{1,0:T(8,128)(2,1)S(1)}, u32[]{:S(2)}, u32[]{:S(2)}) collective-permute-start(bf16[512,512]{1,0:T(8,128)(2,1)S(1)} %collective-permute-done.17.refs_4_.refs_5_.refs_1_), channel_id=1, source_target_pairs={{2,1},{6,5},{10,9},{14,13},{18,17},{22,21},{26,25},{30,29}} | collective-permute-start | bytes 1572872 | tf_op jit(solution)/shard_map/ppermute | solution.py:321
  72.9 0.7 collective-permute-start.21
  73.7 2.4 %upper.1.upper_ref = bf16[512,1536]{1,0:T(8,128)(2,1)S(1)} custom-call(s32[3]{0:T(128)S(1)} %pad_add_fusion.place_ref, bf16[512,512]{1,0:T(8,128)(2,1)S(1)} %copy-done, bf16[128,1536]{1,0:T(8,128)(2,1)S(1)} %get-tuple-element.27.refs_0_, bf16[128,1536]{1,0:T(8,128)(2,1)S(1)} %get-tuple-element.28.refs_1_, ...), custom_call_target="tpu_custom_call" | custom-call | flops 805306368 | bytes 3145728 | tf_op jit(solution)/shard_map/upper/pallas_call | solution.py:208
  76.0 8.9 %collective-permute-done.18.refs_8_ = bf16[512,512]{1,0:T(8,128)(2,1)S(1)} collective-permute-done((bf16[512,512]{1,0:T(8,128)(2,1)S(1)}, bf16[512,512]{1,0:T(8,128)(2,1)S(1)}, u32[]{:S(2)}, u32[]{:S(2)}) %collective-permute-start.18) | collective-permute-done | bytes 524320 | tf_op jit(solution)/shard_map/ppermute | solution.py:321
  84.9 7.2 %update_rows.2.swapped_ref = bf16[2048,1536]{1,0:T(8,128)(2,1)} custom-call(s32[3]{0:T(128)S(1)} %pad_add_fusion.place_ref, bf16[2048,1536]{1,0:T(8,128)(2,1)} %get-tuple-element.24.swapped_ref, bf16[512,1536]{1,0:T(8,128)(2,1)S(1)} %upper.1.upper_ref, bf16[2048,1536]{1,0:T(8,128)(2,1)} %refs_0_.3, ...), custom_call_target="tpu_custom_call", output_to_operand_aliasing={{}: (1, {})} | custom-call | flops 2415919104 | bytes 9437184 | tf_op jit(solution)/shard_map/update_rows/pallas_call | solution.py:272
  92.2 4.0 %collective-permute-done.20.refs_2_ = bf16[512,512]{1,0:T(8,128)(2,1)S(1)} collective-permute-done((bf16[512,512]{1,0:T(8,128)(2,1)S(1)}, bf16[512,512]{1,0:T(8,128)(2,1)S(1)}, u32[]{:S(2)}, u32[]{:S(2)}) %collective-permute-start.20) | collective-permute-done | bytes 524320 | tf_op jit(solution)/shard_map/ppermute | solution.py:321
  96.2 4.6 %update_rows.3 = bf16[2048,1536]{1,0:T(8,128)(2,1)} custom-call(s32[3]{0:T(128)S(1)} %pad_add_fusion.place_ref, bf16[2048,1536]{1,0:T(8,128)(2,1)} %update_rows.2.swapped_ref, bf16[512,1536]{1,0:T(8,128)(2,1)S(1)} %upper.1.upper_ref, bf16[2048,1536]{1,0:T(8,128)(2,1)} %refs_0_.3, ...), custom_call_target="tpu_custom_call", output_to_operand_aliasing={{}: (1, {})} | custom-call | flops 805306368 | bytes 3145728 | tf_op jit(solution)/shard_map/update_rows/pallas_call | solution.py:272
  (36 shorter events, 4.8 us)
Async XLA Ops:
  0.1 2.6 %copy-start.1 = (s32[512]{0:T(512)S(1)}, s32[512]{0:T(512)}, u32[]{:S(2)}) copy-start(s32[512]{0:T(512)} %param.4) | copy-start | bytes 6148
  0.6 2.0 %collective-permute-start = (bf16[256,1536]{1,0:T(8,128)(2,1)S(1)}, bf16[256,1536]{1,0:T(8,128)(2,1)S(1)}, u32[]{:S(2)}, u32[]{:S(2)}) collective-permute-start(bf16[256,1536]{1,0:T(8,128)(2,1)S(1)} %chunk.6), channel_id=1, source_target_pairs={{0,4},{1,5},{2,6},{3,7}} | collective-permute-start | bytes 2359304 | tf_op jit(solution)/shard_map/ppermute | solution.py:376
  1.9 10.1 %collective-permute-start.4 = (bf16[512,512]{1,0:T(8,128)(2,1)S(1)}, bf16[512,512]{1,0:T(8,128)(2,1)S(1)}, u32[]{:S(2)}, u32[]{:S(2)}) collective-permute-start(bf16[512,512]{1,0:T(8,128)(2,1)S(1)} %chunk.8), channel_id=1, source_target_pairs={{0,2},{4,6},{8,10},{12,14},{16,18},{20,22},{24,26},{28,30}} | collective-permute-start | bytes 1572872 | tf_op jit(solution)/shard_map/ppermute | solution.py:321
  3.2 13.7 %collective-permute-start.1 = (bf16[256,1536]{1,0:T(8,128)(2,1)S(1)}, bf16[256,1536]{1,0:T(8,128)(2,1)S(1)}, u32[]{:S(2)}, u32[]{:S(2)}) collective-permute-start(bf16[256,1536]{1,0:T(8,128)(2,1)S(1)} %chunk.7.refs_0_), channel_id=1, source_target_pairs={{0,8},{4,20},{1,9},{5,21},{2,10},{6,22},{3,11},{7,23}} | collective-permute-start | bytes 2359304 | tf_op jit(solution)/shard_map/ppermute | solution.py:382
  11.4 1.8 %collective-permute-start.2 = (bf16[128,1536]{1,0:T(8,128)(2,1)S(1)}, bf16[128,1536]{1,0:T(8,128)(2,1)S(1)}, u32[]{:S(2)}, u32[]{:S(2)}) collective-permute-start(bf16[128,1536]{1,0:T(8,128)(2,1)S(1)} %get-tuple-element.19), channel_id=1, source_target_pairs={{0,4},{4,0},{8,12},{12,8},{16,20},{20,16},{24,28},{28,24},{1,5},{5... | collective-permute-start | bytes 1179656 | tf_op jit(solution)/shard_map/ppermute | solution.py:115
  11.6 2.2 %collective-permute-start.3 = (bf16[128,1536]{1,0:T(8,128)(2,1)S(1)}, bf16[128,1536]{1,0:T(8,128)(2,1)S(1)}, u32[]{:S(2)}, u32[]{:S(2)}) collective-permute-start(bf16[128,1536]{1,0:T(8,128)(2,1)S(1)} %get-tuple-element.20), channel_id=1, source_target_pairs={{0,4},{4,0},{8,12},{12,8},{16,20},{20,16},{24,28},{28,24},{1,5},{5... | collective-permute-start | bytes 1179656 | tf_op jit(solution)/shard_map/ppermute | solution.py:115
  17.0 20.8 %collective-permute-start.5 = (bf16[256,1536]{1,0:T(8,128)(2,1)S(1)}, bf16[256,1536]{1,0:T(8,128)(2,1)S(1)}, u32[]{:S(2)}, u32[]{:S(2)}) collective-permute-start(bf16[256,1536]{1,0:T(8,128)(2,1)S(1)} %add.12.refs_0_), channel_id=1, source_target_pairs={{0,16},{8,24},{4,12},{20,28},{1,17},{9,25},{5,13},{21,29},{2,18},{... | collective-permute-start | bytes 2359304 | tf_op jit(solution)/shard_map/ppermute | solution.py:382
  18.9 2.9 %collective-permute-start.8 = (bf16[512,512]{1,0:T(8,128)(2,1)S(1)}, bf16[512,512]{1,0:T(8,128)(2,1)S(1)}, u32[]{:S(2)}, u32[]{:S(2)}) collective-permute-start(bf16[512,512]{1,0:T(8,128)(2,1)S(1)} %chunk.10), channel_id=1, source_target_pairs={{0,2},{4,6},{8,10},{12,14},{16,18},{20,22},{24,26},{28,30}} | collective-permute-start | bytes 1572872 | tf_op jit(solution)/shard_map/ppermute | solution.py:321
  19.6 18.1 %collective-permute-start.9 = (bf16[512,512]{1,0:T(8,128)(2,1)S(1)}, bf16[512,512]{1,0:T(8,128)(2,1)S(1)}, u32[]{:S(2)}, u32[]{:S(2)}) collective-permute-start(bf16[512,512]{1,0:T(8,128)(2,1)S(1)} %chunk.9.refs_4_.refs_1_), channel_id=1, source_target_pairs={{2,3},{6,7},{10,11},{14,15},{18,19},{22,23},{26,27},{30,31}} | collective-permute-start | bytes 1572872 | tf_op jit(solution)/shard_map/ppermute | solution.py:325
  20.3 11.3 %collective-permute-start.6 = (bf16[128,1536]{1,0:T(8,128)(2,1)S(1)}, bf16[128,1536]{1,0:T(8,128)(2,1)S(1)}, u32[]{:S(2)}, u32[]{:S(2)}) collective-permute-start(bf16[128,1536]{1,0:T(8,128)(2,1)S(1)} %get-tuple-element.22.refs_0_), channel_id=1, source_target_pairs={{0,8},{4,20},{8,0},{12,28},{16,24},{20,4},{24,16},{28,12},{1,9},{5... | collective-permute-start | bytes 1179656 | tf_op jit(solution)/shard_map/ppermute | solution.py:115
  21.3 16.3 %collective-permute-start.7 = (bf16[128,1536]{1,0:T(8,128)(2,1)S(1)}, bf16[128,1536]{1,0:T(8,128)(2,1)S(1)}, u32[]{:S(2)}, u32[]{:S(2)}) collective-permute-start(bf16[128,1536]{1,0:T(8,128)(2,1)S(1)} %get-tuple-element.21.refs_2_.refs_1_), channel_id=1, source_target_pairs={{0,8},{4,20},{8,0},{12,28},{16,24},{20,4},{24,16},{28,12},{1,9},{5... | collective-permute-start | bytes 1179656 | tf_op jit(solution)/shard_map/ppermute | solution.py:115
  37.9 20.2 %collective-permute-start.10 = (bf16[256,1536]{1,0:T(8,128)(2,1)S(1)}, bf16[256,1536]{1,0:T(8,128)(2,1)S(1)}, u32[]{:S(2)}, u32[]{:S(2)}) collective-permute-start(bf16[256,1536]{1,0:T(8,128)(2,1)S(1)} %add.14.mine_ref), channel_id=1, source_target_pairs={{0,4},{4,0},{8,12},{12,8},{16,20},{20,16},{24,28},{28,24},{1,5},{5... | collective-permute-start | bytes 2359304 | tf_op jit(solution)/shard_map/ppermute | solution.py:386
  38.0 18.8 %collective-permute-start.11 = (bf16[512,512]{1,0:T(8,128)(2,1)S(1)}, bf16[512,512]{1,0:T(8,128)(2,1)S(1)}, u32[]{:S(2)}, u32[]{:S(2)}) collective-permute-start(bf16[512,512]{1,0:T(8,128)(2,1)S(1)} %chunk.9.refs_4_.refs_1_), channel_id=1, source_target_pairs={{0,2},{2,1},{4,6},{6,5},{8,10},{10,9},{12,14},{14,13},{16,18},{18,... | collective-permute-start | bytes 1572872 | tf_op jit(solution)/shard_map/ppermute | solution.py:321
  39.3 27.9 %collective-permute-start.14 = (bf16[512,512]{1,0:T(8,128)(2,1)S(1)}, bf16[512,512]{1,0:T(8,128)(2,1)S(1)}, u32[]{:S(2)}, u32[]{:S(2)}) collective-permute-start(bf16[512,512]{1,0:T(8,128)(2,1)S(1)} %chunk.11.refs_4_), channel_id=1, source_target_pairs={{2,3},{6,7},{10,11},{14,15},{18,19},{22,23},{26,27},{30,31}} | collective-permute-start | bytes 1572872 | tf_op jit(solution)/shard_map/ppermute | solution.py:325
  40.0 27.2 %collective-permute-start.12 = (bf16[128,1536]{1,0:T(8,128)(2,1)S(1)}, bf16[128,1536]{1,0:T(8,128)(2,1)S(1)}, u32[]{:S(2)}, u32[]{:S(2)}) collective-permute-start(bf16[128,1536]{1,0:T(8,128)(2,1)S(1)} %get-tuple-element.25.refs_0_), channel_id=1, source_target_pairs={{0,16},{4,12},{8,24},{12,4},{16,0},{20,28},{24,8},{28,20},{1,17},{... | collective-permute-start | bytes 1179656 | tf_op jit(solution)/shard_map/ppermute | solution.py:115
  40.6 26.6 %collective-permute-start.13 = (bf16[128,1536]{1,0:T(8,128)(2,1)S(1)}, bf16[128,1536]{1,0:T(8,128)(2,1)S(1)}, u32[]{:S(2)}, u32[]{:S(2)}) collective-permute-start(bf16[128,1536]{1,0:T(8,128)(2,1)S(1)} %get-tuple-element.23.refs_2_.refs_1_), channel_id=1, source_target_pairs={{0,16},{4,12},{8,24},{12,4},{16,0},{20,28},{24,8},{28,20},{1,17},{... | collective-permute-start | bytes 1179656 | tf_op jit(solution)/shard_map/ppermute | solution.py:115
  56.8 14.8 %collective-permute-start.17 = (bf16[512,512]{1,0:T(8,128)(2,1)S(1)}, bf16[512,512]{1,0:T(8,128)(2,1)S(1)}, u32[]{:S(2)}, u32[]{:S(2)}) collective-permute-start(bf16[512,512]{1,0:T(8,128)(2,1)S(1)} %chunk.11.refs_4_), channel_id=1, source_target_pairs={{0,2},{2,1},{4,6},{6,5},{8,10},{10,9},{12,14},{14,13},{16,18},{18,... | collective-permute-start | bytes 1572872 | tf_op jit(solution)/shard_map/ppermute | solution.py:321
  58.1 15.5 %copy-start = (bf16[512,512]{1,0:T(8,128)(2,1)S(1)}, bf16[512,512]{1,0:T(8,128)(2,1)}, u32[]{:S(2)}) copy-start(bf16[512,512]{1,0:T(8,128)(2,1)} %inverse_ref.1) | copy-start | bytes 1572868
  67.3 5.6 %collective-permute-start.15 = (bf16[128,1536]{1,0:T(8,128)(2,1)S(1)}, bf16[128,1536]{1,0:T(8,128)(2,1)S(1)}, u32[]{:S(2)}, u32[]{:S(2)}) collective-permute-start(bf16[128,1536]{1,0:T(8,128)(2,1)S(1)} %get-tuple-element.27.refs_0_), channel_id=1, source_target_pairs={{0,4},{4,0},{8,12},{12,8},{16,20},{20,16},{24,28},{28,24},{1,5},{5... | collective-permute-start | bytes 1179656 | tf_op jit(solution)/shard_map/ppermute | solution.py:115
  68.4 16.5 %collective-permute-start.18 = (bf16[512,512]{1,0:T(8,128)(2,1)S(1)}, bf16[512,512]{1,0:T(8,128)(2,1)S(1)}, u32[]{:S(2)}, u32[]{:S(2)}) collective-permute-start(bf16[512,512]{1,0:T(8,128)(2,1)S(1)} %collective-permute-done.11.rest_0_.refs_2_.refs_7_), channel_id=1, source_target_pairs={{2,1},{6,5},{10,9},{14,13},{18,17},{22,21},{26,25},{30,29}} | collective-permute-start | bytes 1572872 | tf_op jit(solution)/shard_map/ppermute | solution.py:321
  69.7 15.2 %collective-permute-start.19 = (bf16[512,512]{1,0:T(8,128)(2,1)S(1)}, bf16[512,512]{1,0:T(8,128)(2,1)S(1)}, u32[]{:S(2)}, u32[]{:S(2)}) collective-permute-start(bf16[512,512]{1,0:T(8,128)(2,1)S(1)} %collective-permute-done.11.rest_0_.refs_2_.refs_7_), channel_id=1, source_target_pairs={{2,3},{6,7},{10,11},{14,15},{18,19},{22,23},{26,27},{30,31}} | collective-permute-start | bytes 1572872 | tf_op jit(solution)/shard_map/ppermute | solution.py:325
  70.4 3.2 %collective-permute-start.16 = (bf16[128,1536]{1,0:T(8,128)(2,1)S(1)}, bf16[128,1536]{1,0:T(8,128)(2,1)S(1)}, u32[]{:S(2)}, u32[]{:S(2)}) collective-permute-start(bf16[128,1536]{1,0:T(8,128)(2,1)S(1)} %get-tuple-element.28.refs_1_), channel_id=1, source_target_pairs={{0,4},{4,0},{8,12},{12,8},{16,20},{20,16},{24,28},{28,24},{1,5},{5... | collective-permute-start | bytes 1179656 | tf_op jit(solution)/shard_map/ppermute | solution.py:115
  71.6 24.5 %collective-permute-start.20 = (bf16[512,512]{1,0:T(8,128)(2,1)S(1)}, bf16[512,512]{1,0:T(8,128)(2,1)S(1)}, u32[]{:S(2)}, u32[]{:S(2)}) collective-permute-start(bf16[512,512]{1,0:T(8,128)(2,1)S(1)} %collective-permute-done.17.refs_4_.refs_5_.refs_1_), channel_id=1, source_target_pairs={{2,1},{6,5},{10,9},{14,13},{18,17},{22,21},{26,25},{30,29}} | collective-permute-start | bytes 1572872 | tf_op jit(solution)/shard_map/ppermute | solution.py:321
  72.9 23.2 %collective-permute-start.21 = (bf16[512,512]{1,0:T(8,128)(2,1)S(1)}, bf16[512,512]{1,0:T(8,128)(2,1)S(1)}, u32[]{:S(2)}, u32[]{:S(2)}) collective-permute-start(bf16[512,512]{1,0:T(8,128)(2,1)S(1)} %collective-permute-done.17.refs_4_.refs_5_.refs_1_), channel_id=1, source_target_pairs={{2,3},{6,7},{10,11},{14,15},{18,19},{22,23},{26,27},{30,31}} | collective-permute-start | bytes 1572872 | tf_op jit(solution)/shard_map/ppermute | solution.py:325

commit v4 on v3

--- a/solution.py
+++ b/solution.py
@@ -7,8 +7,11 @@
 from jax.experimental.pallas import tpu as pltpu
 from jax.sharding import PartitionSpec as P
 
-GROUPS = 4
-PARTS = 2
+GROUPS = 2
+CHUNK_WEIGHTS = (5, 5)
+JOIN_WEIGHTS, JOIN_AFTER = (2, 2), ((0, 0), (3, 1))
+DOWN_WEIGHTS, DOWN_AFTER = (0, 20), ((1, 0), (0, 0))
+PIECES = 2
 BLOCK = 512
 F32, BF16 = jnp.float32, jnp.bfloat16
 VMEM = pl.BlockSpec(memory_space=pltpu.VMEM)
@@ -18,15 +21,17 @@
 LARGE = pltpu.CompilerParams(vmem_limit_bytes=28 * 2**20)
 
 
-def cost(flops, moved):
-    return pl.CostEstimate(flops=flops, bytes_accessed=moved, transcendentals=0)
-
-
-def chunk_kernel(first_row, axis, place_ref, matrix_ref, *refs):
+FREE = pl.CostEstimate(flops=0, bytes_accessed=0, transcendentals=0)
+def weight_of(x):
+    x = float(x)
+    return pl.CostEstimate(flops=int(x*1.15e9), bytes_accessed=int(x*3.69e6), transcendentals=0)
+
+
+def chunk_kernel(first_row, axis, core, place_ref, matrix_ref, *refs):
     out_ref, sem = refs[-2:]
     rows, width = out_ref.shape
 
-    @pl.when(place_ref[axis] == 0)
+    @pl.when((place_ref[axis] == 0) & (place_ref[2] == core))
     def _():
         copy = pltpu.make_async_copy(
             matrix_ref.at[pl.ds(first_row, rows), pl.ds(0, width)], out_ref, sem
@@ -35,29 +40,31 @@
         copy.wait()
 
 
-def chunk(place, axis, matrix, first_row, rows, width, held=None):
+def chunk(place, axis, core, matrix, first_row, rows, width, held=None, weight=0, after=()):
     in_specs, operands = [SMEM, ANY], [place, matrix]
     if held is not None:
         in_specs.append(ANY)
         operands.append(held)
-    return pl.pallas_call(
-        functools.partial(chunk_kernel, first_row, axis),
+    in_specs += [ANY] * len(after)
+    operands += after
+    return pl.pallas_call(
+        functools.partial(chunk_kernel, first_row, axis, core),
         in_specs=in_specs,
         out_specs=ANY,
         out_shape=jax.ShapeDtypeStruct((rows, width), BF16),
         scratch_shapes=[pltpu.SemaphoreType.DMA],
         input_output_aliases={} if held is None else {2: 0},
         compiler_params=SMALL,
-        cost_estimate=cost(0, 4 * rows * width),
+        cost_estimate=weight_of(weight),
         name="chunk",
     )(*operands)
 
 
 def pick_kernel(place_ref, pivots_ref, matrix_ref, *refs):
-    onehot_ref = refs[PARTS * 2]
+    onehot_ref = refs[-1]
     rows = matrix_ref.shape[0]
     width = pivots_ref.shape[0]
-    count = width // (2 * PARTS)
+    count = width // PIECES
 
     @pl.when(pl.program_id(0) == 0)
     def _():
@@ -65,7 +72,7 @@
         onehot_ref[...] = jnp.where(pivots_ref[...] == row, 1.0, 0.0).astype(BF16)
 
     picked = jnp.dot(onehot_ref[...], matrix_ref[...], preferred_element_type=F32).astype(BF16)
-    for number, out_ref in enumerate(refs[: PARTS * 2]):
+    for number, out_ref in enumerate(refs[:PIECES]):
         out_ref[...] = picked[number * count : (number + 1) * count]
 
 
@@ -73,7 +80,7 @@
     rows, cols = matrix.shape
     width = pivots.shape[0]
     block = min(BLOCK, cols)
-    count = width // (2 * PARTS)
+    count = width // PIECES
     return pl.pallas_call(
         pick_kernel,
         grid_spec=pltpu.PrefetchScalarGridSpec(
@@ -83,36 +90,36 @@
                 pl.BlockSpec((width, 1), lambda i, s: (0, 0)),
                 pl.BlockSpec((rows, block), lambda i, s: (0, i)),
             ],
-            out_specs=[pl.BlockSpec((count, block), lambda i, s: (0, i))] * (2 * PARTS),
+            out_specs=[pl.BlockSpec((count, block), lambda i, s: (0, i))] * PIECES,
             scratch_shapes=[pltpu.VMEM((width, rows), BF16)],
         ),
-        out_shape=[jax.ShapeDtypeStruct((count, cols), BF16)] * (2 * PARTS),
+        out_shape=[jax.ShapeDtypeStruct((count, cols), BF16)] * PIECES,
         compiler_params=LARGE,
-        cost_estimate=cost(2 * width * rows * cols, 2 * rows * cols),
+        cost_estimate=weight_of(0),
         name="pick_rows",
     )(place, pivots[:, None], matrix)
 
 
 def add_kernel(count, *refs):
-    for own_ref, got_ref, out_ref in zip(refs[:count], refs[count:], refs[-count:]):
-        out_ref[...] = own_ref[...] + got_ref[...]
-
-
-def add(own, got, after=()):
-    size = sum(x.size for x in own)
+    start = 0
+    out_ref = refs[-1]
+    for own_ref, got_ref in zip(refs[:count], refs[count : 2 * count]):
+        rows = own_ref.shape[0]
+        out_ref[start : start + rows] = own_ref[...] + got_ref[...]
+        start += rows
+
+
+def add(own, got, after=(), weight=0):
+    rows, cols = sum(x.shape[0] for x in own), own[0].shape[1]
     return pl.pallas_call(
         functools.partial(add_kernel, len(own)),
         in_specs=[VMEM] * (2 * len(own)) + [ANY] * len(after),
-        out_specs=[VMEM] * len(own),
-        out_shape=[jax.ShapeDtypeStruct(x.shape, BF16) for x in own],
+        out_specs=VMEM,
+        out_shape=jax.ShapeDtypeStruct((rows, cols), BF16),
         compiler_params=SMALL,
-        cost_estimate=cost(size, 6 * size),
+        cost_estimate=weight_of(weight),
         name="add",
     )(*own, *got, *after)
-
-
-def exchange(parts, pairs):
-    return [lax.ppermute(x, "prow", pairs) for x in parts]
 
 
 def swap_kernel(place_ref, pivots_ref, matrix_ref, mine_ref, other_ref, *rest):
@@ -179,41 +186,38 @@
             jax.ShapeDtypeStruct((8, 128), F32),
         ],
         compiler_params=LARGE,
-        cost_estimate=cost(2 * rows * width * cols, 4 * rows * cols),
+        cost_estimate=weight_of(0),
         name="swap_rows",
     )(place, pivots[None, :], matrix, mine, other, *after)
 
 
-def upper_kernel(place_ref, inverse_ref, *refs):
-    mine_refs, other_refs, out_ref = refs[:PARTS], refs[PARTS : 2 * PARTS], refs[-1]
+def upper_kernel(place_ref, inverse_ref, mine_ref, other_ref, *rest):
+    out_ref = rest[-1]
     width, cols = out_ref.shape
-    count = width // (2 * PARTS)
+    half = width // 2
     block = min(BLOCK, cols)
     for start in range(0, cols, block):
         here = slice(start, start + block)
+        mine, other = mine_ref[:, here], other_ref[:, here]
         first = place_ref[2] == 0
-        total = None
-        for number in range(2 * PARTS):
-            part = number % PARTS
-            mine, other = mine_refs[part][:, here], other_refs[part][:, here]
-            rows = jnp.where(first == (number < PARTS), mine, other)
-            inverse = inverse_ref[:, number * count : (number + 1) * count]
-            term = jnp.dot(inverse, rows, preferred_element_type=F32)
-            total = term if total is None else total + term
-        out_ref[:, here] = total.astype(BF16)
+        top, bottom = jnp.where(first, mine, other), jnp.where(first, other, mine)
+        out_ref[:, here] = (
+            jnp.dot(inverse_ref[:, :half], top, preferred_element_type=F32)
+            + jnp.dot(inverse_ref[:, half:], bottom, preferred_element_type=F32)
+        ).astype(BF16)
 
 
 def upper_rows(place, unit_inverse, mine, other, after=()):
-    width, cols = unit_inverse.shape[0], mine[0].shape[1]
+    width, cols = unit_inverse.shape[0], mine.shape[1]
     return pl.pallas_call(
         upper_kernel,
-        in_specs=[SMEM] + [VMEM] * (1 + 2 * PARTS) + [ANY] * len(after),
+        in_specs=[SMEM, VMEM, VMEM, VMEM] + [ANY] * len(after),
         out_specs=VMEM,
         out_shape=jax.ShapeDtypeStruct((width, cols), BF16),
         compiler_params=pltpu.CompilerParams(vmem_limit_bytes=16 * 2**20),
-        cost_estimate=cost(2 * width * width * cols, 4 * width * cols),
+        cost_estimate=weight_of(2),
         name="upper",
-    )(place, unit_inverse, *mine, *other, *after)
+    )(place, unit_inverse, mine, other, *after)
 
 
 def update_kernel(groups, per_group, pick_source, place_ref, swapped_ref, upper_ref, *refs):
@@ -231,7 +235,7 @@
         views = [sources[0].at[pl.ds(start, count), pl.ds(0, width)]]
         views += sources[1 + number * per_group : 1 + (number + 1) * per_group]
         for choice, view in enumerate(views):
-            @pl.when(pick_source(col_place) == choice)
+            @pl.when(pick_source(col_place, place_ref[2]) == choice)
             def _():
                 action(pltpu.make_async_copy(view, here, sem.at[number]))
 
@@ -266,8 +270,10 @@
     width = upper.shape[0]
     block = min(BLOCK, cols)
     count = sum(size for _, size in groups)
-    position = groups[0][0] // count
-    by_column = pl.BlockSpec((count, block), lambda i, s: (position, i))
+    first_row = groups[0][0]
+    by_column = pl.BlockSpec(
+        (pl.Element(count), pl.Element(block)), lambda i, s: (first_row, i * block)
+    )
     sources = [matrix] + [x for group in received for x in group]
     return pl.pallas_call(
         functools.partial(update_kernel, groups, len(received[0]), pick_source),
@@ -285,7 +291,7 @@
         out_shape=jax.ShapeDtypeStruct((rows, cols), BF16),
         input_output_aliases={1: 0},
         compiler_params=LARGE,
-        cost_estimate=cost(2 * count * width * cols, 4 * count * cols),
+        cost_estimate=weight_of(0),
         name="update_rows",
     )(place, swapped, upper, *sources)
 
@@ -304,49 +310,54 @@
     return pairs
 
 
-def spread(place, matrix, width, groups, axis, size):
+def spread(place, matrix, width, groups, core, n_prow, size):
     middle = size // 2
     count = len(groups)
+
+    def move(value, pairs):
+        pairs = [
+            (row * size + a, row * size + b) for row in range(core, n_prow, 2) for a, b in pairs
+        ]
+        return lax.ppermute(value, ("prow", "pcol"), pairs)
+
     held = []
-    for number in range(count + 2):
-        pairs = [(middle, middle - 1)]
-        back = held[number - 2] if number >= 2 else None
+    for number in range(count + 1):
+        pairs = [(middle, middle - 1)] * (number >= 1)
+        sent = held[number - 1] if number >= 1 else None
         if number < count:
-            pairs = [(0, middle)] + pairs * (number >= 2)
-            sent = chunk(place, 1, matrix, *groups[number], width, back)
-            if number >= 2:
-                held[number - 2] = sent
-        else:
-            sent = back
-        held.append(lax.ppermute(sent, axis, pairs))
+            pairs.append((0, middle))
+            sent = chunk(place, 1, core, matrix, *groups[number], width, sent, CHUNK_WEIGHTS[number])
+            if number >= 1:
+                held[number - 1] = sent
+        held.append(move(sent, pairs))
     received = []
     for number in range(count):
-        arrays = [held[number], held[number + 2]]
-        arrays.append(lax.ppermute(held[number], axis, [(middle, middle + 1)]))
+        arrays = [held[number], held[number + 1]]
+        arrays.append(move(held[number], [(middle, middle + 1)]))
         distance = 1
         while middle - distance > 1 or middle + distance + 1 < size:
             if distance == 1:
-                both = jnp.where(lax.axis_index(axis) < middle, arrays[1], arrays[2])
+                both = jnp.where(place[1] < middle, arrays[1], arrays[2])
             pairs = []
             if middle - distance > 1:
                 pairs.append((middle - distance, middle - distance - 1))
             if middle + distance + 1 < size:
                 pairs.append((middle + distance, middle + distance + 1))
-            both = lax.ppermute(both, axis, pairs)
+            both = move(both, pairs)
             arrays.append(both)
             distance += 1
         received.append(arrays)
     return received
 
 
-def source_of(size):
+def source_of(size, per_core):
     middle = size // 2
 
-    def pick_source(place):
+    def pick_source(place, core):
         away = jnp.abs(place - middle)
         number = jnp.where(away == 0, 1, jnp.where(place < middle, 2, 3))
         number = jnp.where(away >= 2, away + 2, number)
-        return jnp.where(place == 0, 0, number)
+        return jnp.where(place == 0, 0, number + core * per_core)
 
     return pick_source
 
@@ -367,29 +378,32 @@
 
     size = rows // GROUPS
     groups = [(number * size, size) for number in range(GROUPS)]
-    received = spread(place, matrix, width, groups, "pcol", n_pcol)
-    arrived = [arrays[0] for arrays in received]
-    arrived_left = [arrays[1] for arrays in received]
-    arrived_right = [arrays[2] for arrays in received]
+    by_core = [spread(place, matrix, width, groups, c, n_prow, n_pcol) for c in range(2)]
+    received = [first + second for first, second in zip(*by_core)]
+    pick_source = source_of(n_pcol, len(by_core[0][0]))
+    arrived = [x for pair in zip(*by_core) for x in (pair[0][0], pair[1][0])]
+    arrived_right = [x for pair in zip(*by_core) for x in (pair[0][2], pair[1][2])]
 
     order = jnp.where(core == 0, pivots, jnp.roll(pivots, half))
-    down_got = lax.ppermute(chunk(place, 0, matrix, half, half, cols), "prow", [(0, 1)])
-    picked = pick(place, order, matrix)
-    up = picked[:PARTS]
-    up_got = exchange(picked[PARTS:], swap_pairs(n_prow, cores, 0))
-    down = chunk(place, 0, matrix, 0, half, cols, down_got)
+    down_got = lax.ppermute(chunk(place, 0, 0, matrix, half, half, cols), "prow", [(0, 1)])
+    pieces = pick(place, order, matrix)
+    up, sent = pieces[: PIECES // 2], pieces[PIECES // 2 :]
+    up_got = [lax.ppermute(x, "prow", swap_pairs(n_prow, cores, 0)) for x in sent]
+    down = chunk(place, 0, 0, matrix, 0, half, cols, down_got)
+    def pins(a, b):
+        return arrived[max(a - 2, 0):a] + arrived_right[max(b - 2, 0):b]
     for step in range(last + 1):
         down_got = lax.ppermute(down, "prow", grow_pairs(orders, step))
-        up = add(up, up_got, arrived[:1] if step == 0 else arrived[1:2] + arrived_right[:1])
-        up_got = exchange(up, swap_pairs(n_prow, orders, step))
-        (down,) = add([down], [down_got], up[-1:])
+        up = [add(up, up_got, pins(*JOIN_AFTER[min(step, 1)]), JOIN_WEIGHTS[min(step, 1)])]
+        up_got = [lax.ppermute(up[0], "prow", swap_pairs(n_prow, orders, step))]
+        down = add([down], [down_got], [] + pins(*DOWN_AFTER[min(step, 1)]), DOWN_WEIGHTS[min(step, 1)])
     down_got = lax.ppermute(down, "prow", swap_pairs(n_prow, cores, 0))
-    swapped, token = swap(place, pivots, matrix, down, down_got, arrived[2:3])
-    up = add(up, up_got, [token] + arrived_right[1:2])
-    up_got = exchange(up, swap_pairs(n_prow, cores, 0))
-    upper = upper_rows(place, unit_inverse, up, up_got, arrived[3:4])
-
-    common = (source_of(n_pcol), place, matrix)
+    swapped, token = swap(place, pivots, matrix, down, down_got, pins(0, 0))
+    up = add(up, up_got, pins(2, 1), 0)
+    up_got = lax.ppermute(up, "prow", swap_pairs(n_prow, cores, 0))
+    upper = upper_rows(place, unit_inverse, up, up_got, pins(3, 2))
+
+    common = (pick_source, place, matrix)
     out = update(groups[:-1], *common, swapped, upper, received[:-1])
     return update(groups[-1:], *common, out, upper, received[-1:])
 

time: 102 us -> 116 us (1.14)
  the two profiles are of different devices: /device:TPU:13 before, /device:TPU:21 now
where the time goes in v4:
time: 116 us; the launch traced here: 115 us
  waiting for transfers between devices  59.5 us (51%)
  Pallas kernels  33 us (28%)
  starting transfers between devices  22.2 us (19%)
    ppermute x10, waiting for transfers between devices, move(): return lax.ppermute(value, ('prow', 'pcol'), pairs)  52.4 us
    pallas_call x2, Pallas kernels, update(): pl.pallas_call(functools.partial(update_kernel, groups, len(received[0]),...  11.9 us
    ppermute x10, starting transfers between devices, move(): return lax.ppermute(value, ('prow', 'pcol'), pairs)  10.9 us
    pallas_call x1, Pallas kernels, swap(): pl.pallas_call(swap_kernel, grid_spec=pltpu.PrefetchScalarGridSpec(num_sc...  9.11 us
    ppermute x2, waiting for transfers between devices, per_device(): down_got = lax.ppermute(down, 'prow', grow_pairs(orders, step))  7.1 us
    pallas_call x1, Pallas kernels, pick(): pl.pallas_call(pick_kernel, grid_spec=pltpu.PrefetchScalarGridSpec(num_sc...  6.7 us
    ppermute x2, starting transfers between devices, per_device(): up_got = [lax.ppermute(up[0], 'prow', swap_pairs(n_prow, orders, step))]  3.47 us
    pallas_call x6, Pallas kernels, chunk(): pl.pallas_call(functools.partial(chunk_kernel, first_row, axis, core), in...  3.34 us
  transfers between devices with their start and end apart: 18, of which 4 were waited for; matrix products, arithmetic and copies ran while one was open for 0% of the time, Pallas kernels for 23%

profile of v4, /device:TPU:21, one launch (start us, length us, event | category | flops | bytes accessed | tf_op | source)
XLA Modules:
  0.0 115.3 jit_solution(10446978857948591035)
XLA Ops:
  0.1 0.6 chunk.8
  0.7 0.7 collective-permute-start.2
  1.4 0.6 chunk.6
  2.0 0.7 collective-permute-start
  2.9 6.7 %pick_rows.1 = (bf16[256,1536]{1,0:T(8,128)(2,1)S(1)}, bf16[256,1536]{1,0:T(8,128)(2,1)S(1)}) custom-call(s32[3]{0:T(128)S(1)} %pad_add_fusion.place_ref, s32[512,1]{1,0:T(8,128)S(1)} %copy.9.pivots_ref, bf16[2048,1536]{1,0:T(8,128)(2,1)} %refs_0_.3), custom_call_target="tpu_custom_call" | custom-call | tf_op jit(solution)/shard_map/pick_rows/pallas_call | solution.py:84
  9.6 1.3 %collective-permute-start.5 = (bf16[256,1536]{1,0:T(8,128)(2,1)S(1)}, bf16[256,1536]{1,0:T(8,128)(2,1)S(1)}, u32[]{:S(2)}, u32[]{:S(2)}) collective-permute-start(bf16[256,1536]{1,0:T(8,128)(2,1)S(1)} %get-tuple-element.10), channel_id=1, source_target_pairs={{0,4},{4,0},{8,12},{12,8},{16,20},{20,16},{24,28},{28,24},{1,5},{5... | collective-permute-start | bytes 2359304 | tf_op jit(solution)/shard_map/ppermute | solution.py:391
  10.9 0.6 chunk.10
  11.4 1.3 %collective-permute-start.7 = (bf16[1024,512]{1,0:T(8,128)(2,1)S(1)}, bf16[1024,512]{1,0:T(8,128)(2,1)S(1)}, u32[]{:S(2)}, u32[]{:S(2)}) collective-permute-start(bf16[1024,512]{1,0:T(8,128)(2,1)S(1)} %chunk.10), channel_id=1, source_target_pairs={{4,6},{12,14},{20,22},{28,30}} | collective-permute-start | bytes 3145736 | tf_op jit(solution)/shard_map/ppermute | solution.py:321
  12.8 0.6 chunk.7.refs_0_
  13.3 1.3 %collective-permute-start.1 = (bf16[256,1536]{1,0:T(8,128)(2,1)S(1)}, bf16[256,1536]{1,0:T(8,128)(2,1)S(1)}, u32[]{:S(2)}, u32[]{:S(2)}) collective-permute-start(bf16[256,1536]{1,0:T(8,128)(2,1)S(1)} %chunk.7.refs_0_), channel_id=1, source_target_pairs={{0,8},{4,20},{1,9},{5,21},{2,10},{6,22},{3,11},{7,23}} | collective-permute-start | bytes 2359304 | tf_op jit(solution)/shard_map/ppermute | solution.py:396
  14.6 0.6 chunk.9.refs_2_.refs_1_
  15.2 0.7 collective-permute-start.8
  15.9 0.7 collective-permute-start.9
  16.8 2.2 %collective-permute-start.6 = (bf16[256,1536]{1,0:T(8,128)(2,1)S(1)}, bf16[256,1536]{1,0:T(8,128)(2,1)S(1)}, u32[]{:S(2)}, u32[]{:S(2)}) collective-permute-start(bf16[256,1536]{1,0:T(8,128)(2,1)S(1)} %add.13.refs_0_), channel_id=1, source_target_pairs={{0,8},{4,20},{8,0},{12,28},{16,24},{20,4},{24,16},{28,12},{1,9},{5... | collective-permute-start | bytes 2359304 | tf_op jit(solution)/shard_map/ppermute | solution.py:398
  19.0 7.1 %collective-permute-done.1.refs_1_ = bf16[256,1536]{1,0:T(8,128)(2,1)S(1)} collective-permute-done((bf16[256,1536]{1,0:T(8,128)(2,1)S(1)}, bf16[256,1536]{1,0:T(8,128)(2,1)S(1)}, u32[]{:S(2)}, u32[]{:S(2)}) %collective-permute-start.1) | collective-permute-done | bytes 786464 | tf_op jit(solution)/shard_map/ppermute | solution.py:396
  26.2 1.3 %collective-permute-start.3 = (bf16[256,1536]{1,0:T(8,128)(2,1)S(1)}, bf16[256,1536]{1,0:T(8,128)(2,1)S(1)}, u32[]{:S(2)}, u32[]{:S(2)}) collective-permute-start(bf16[256,1536]{1,0:T(8,128)(2,1)S(1)} %add.11.refs_0_), channel_id=1, source_target_pairs={{0,16},{8,24},{4,12},{20,28},{1,17},{9,25},{5,13},{21,29},{2,18},{... | collective-permute-start | bytes 2359304 | tf_op jit(solution)/shard_map/ppermute | solution.py:396
  27.5 36.2 %collective-permute-done.7.refs_0_ = bf16[1024,512]{1,0:T(8,128)(2,1)S(1)} collective-permute-done((bf16[1024,512]{1,0:T(8,128)(2,1)S(1)}, bf16[1024,512]{1,0:T(8,128)(2,1)S(1)}, u32[]{:S(2)}, u32[]{:S(2)}) %collective-permute-start.7) | collective-permute-done | bytes 1048608 | tf_op jit(solution)/shard_map/ppermute | solution.py:321
  63.7 0.6 chunk.11.refs_2_.refs_3_.rest_0_.refs_4_
  64.3 1.4 %collective-permute-start.12 = (bf16[1024,512]{1,0:T(8,128)(2,1)S(1)}, bf16[1024,512]{1,0:T(8,128)(2,1)S(1)}, u32[]{:S(2)}, u32[]{:S(2)}) collective-permute-start(bf16[1024,512]{1,0:T(8,128)(2,1)S(1)} %chunk.11.refs_2_.refs_3_.rest_0_.refs_4_), channel_id=1, source_target_pairs={{6,7},{14,15},{22,23},{30,31}} | collective-permute-start | bytes 3145736 | tf_op jit(solution)/shard_map/ppermute | solution.py:321
  65.7 1.9 %collective-permute-start.13 = (bf16[1024,512]{1,0:T(8,128)(2,1)S(1)}, bf16[1024,512]{1,0:T(8,128)(2,1)S(1)}, u32[]{:S(2)}, u32[]{:S(2)}) collective-permute-start(bf16[1024,512]{1,0:T(8,128)(2,1)S(1)} %chunk.11.refs_2_.refs_3_.rest_0_.refs_4_), channel_id=1, source_target_pairs={{6,5},{4,6},{14,13},{12,14},{22,21},{20,22},{30,29},{28,30}} | collective-permute-start | bytes 3145736 | tf_op jit(solution)/shard_map/ppermute | solution.py:321
  67.7 1.3 %collective-permute-start.10 = (bf16[256,1536]{1,0:T(8,128)(2,1)S(1)}, bf16[256,1536]{1,0:T(8,128)(2,1)S(1)}, u32[]{:S(2)}, u32[]{:S(2)}) collective-permute-start(bf16[256,1536]{1,0:T(8,128)(2,1)S(1)} %add.14.refs_0_), channel_id=1, source_target_pairs={{0,16},{4,12},{8,24},{12,4},{16,0},{20,28},{24,8},{28,20},{1,17},{... | collective-permute-start | bytes 2359304 | tf_op jit(solution)/shard_map/ppermute | solution.py:398
  69.1 3.1 %collective-permute-start.4 = (bf16[256,1536]{1,0:T(8,128)(2,1)S(1)}, bf16[256,1536]{1,0:T(8,128)(2,1)S(1)}, u32[]{:S(2)}, u32[]{:S(2)}) collective-permute-start(bf16[256,1536]{1,0:T(8,128)(2,1)S(1)} %add.12.mine_ref), channel_id=1, source_target_pairs={{0,4},{4,0},{8,12},{12,8},{16,20},{20,16},{24,28},{28,24},{1,5},{5... | collective-permute-start | bytes 2359304 | tf_op jit(solution)/shard_map/ppermute | solution.py:400
  72.2 0.7 collective-permute-start.14
  72.9 6.0 %collective-permute-done.12.rest_3_.refs_6_ = bf16[1024,512]{1,0:T(8,128)(2,1)S(1)} collective-permute-done((bf16[1024,512]{1,0:T(8,128)(2,1)S(1)}, bf16[1024,512]{1,0:T(8,128)(2,1)S(1)}, u32[]{:S(2)}, u32[]{:S(2)}) %collective-permute-start.12) | collective-permute-done | bytes 1048608 | tf_op jit(solution)/shard_map/ppermute | solution.py:321
  78.9 0.7 collective-permute-start.15
  79.6 10.2 %collective-permute-done.13.refs_5_.refs_4_ = bf16[1024,512]{1,0:T(8,128)(2,1)S(1)} collective-permute-done((bf16[1024,512]{1,0:T(8,128)(2,1)S(1)}, bf16[1024,512]{1,0:T(8,128)(2,1)S(1)}, u32[]{:S(2)}, u32[]{:S(2)}) %collective-permute-start.13) | collective-permute-done | bytes 1048608 | tf_op jit(solution)/shard_map/ppermute | solution.py:321
  89.8 1.3 %collective-permute-start.16 = (bf16[1024,512]{1,0:T(8,128)(2,1)S(1)}, bf16[1024,512]{1,0:T(8,128)(2,1)S(1)}, u32[]{:S(2)}, u32[]{:S(2)}) collective-permute-start(bf16[1024,512]{1,0:T(8,128)(2,1)S(1)} %collective-permute-done.13.refs_5_.refs_4_), channel_id=1, source_target_pairs={{6,5},{14,13},{22,21},{30,29}} | collective-permute-start | bytes 3145736 | tf_op jit(solution)/shard_map/ppermute | solution.py:321
  91.1 1.4 %collective-permute-start.17 = (bf16[1024,512]{1,0:T(8,128)(2,1)S(1)}, bf16[1024,512]{1,0:T(8,128)(2,1)S(1)}, u32[]{:S(2)}, u32[]{:S(2)}) collective-permute-start(bf16[1024,512]{1,0:T(8,128)(2,1)S(1)} %collective-permute-done.13.refs_5_.refs_4_), channel_id=1, source_target_pairs={{6,7},{14,15},{22,23},{30,31}} | collective-permute-start | bytes 3145736 | tf_op jit(solution)/shard_map/ppermute | solution.py:321
  92.7 9.1 %swap_rows.1 = (bf16[2048,1536]{1,0:T(8,128)(2,1)}, f32[8,128]{1,0:T(8,128)}) custom-call(s32[3]{0:T(128)S(1)} %pad_add_fusion.place_ref, s32[1,512]{1,0:T(1,128)S(1)} %bitcast.5, bf16[2048,1536]{1,0:T(8,128)(2,1)} %refs_0_.3, bf16[256,1536]{1,0:T(8,128)(2,1)S(1)} %add.12.mine_ref, bf16[256,1536]{1,0:T(8,128)(2,1)S(1)} %collective-permute-done.4.other_ref), custom_call_target="tpu_custom_call" | custom-call | tf_op jit(solution)/shard_map/swap_rows/pallas_call | solution.py:169
  101.8 1.6 %upper.1.upper_ref = bf16[512,1536]{1,0:T(8,128)(2,1)S(1)} custom-call(s32[3]{0:T(128)S(1)} %pad_add_fusion.place_ref, bf16[512,512]{1,0:T(8,128)(2,1)S(1)} %copy-done.1, bf16[256,1536]{1,0:T(8,128)(2,1)S(1)} %add.15.mine_ref, bf16[256,1536]{1,0:T(8,128)(2,1)S(1)} %collective-permute-done.11.other_ref, ...), custom_call_target="tpu_custom_call" | custom-call | flops 2300000000 | bytes 7380000 | tf_op jit(solution)/shard_map/upper/pallas_call | solution.py:212
  103.4 6.0 %update_rows.2.swapped_ref = bf16[2048,1536]{1,0:T(8,128)(2,1)} custom-call(s32[3]{0:T(128)S(1)} %pad_add_fusion.place_ref, bf16[2048,1536]{1,0:T(8,128)(2,1)} %get-tuple-element.8.swapped_ref, bf16[512,1536]{1,0:T(8,128)(2,1)S(1)} %upper.1.upper_ref, bf16[2048,1536]{1,0:T(8,128)(2,1)} %refs_0_.3, ...), custom_call_target="tpu_custom_call", output_to_operand_aliasing={{}: (1, {})} | custom-call | tf_op jit(solution)/shard_map/update_rows/pallas_call | solution.py:278
  109.4 5.9 %update_rows.3 = bf16[2048,1536]{1,0:T(8,128)(2,1)} custom-call(s32[3]{0:T(128)S(1)} %pad_add_fusion.place_ref, bf16[2048,1536]{1,0:T(8,128)(2,1)} %update_rows.2.swapped_ref, bf16[512,1536]{1,0:T(8,128)(2,1)S(1)} %upper.1.upper_ref, bf16[2048,1536]{1,0:T(8,128)(2,1)} %refs_0_.3, ...), custom_call_target="tpu_custom_call", output_to_operand_aliasing={{}: (1, {})} | custom-call | tf_op jit(solution)/shard_map/update_rows/pallas_call | solution.py:278
  (28 shorter events, 0.8 us)
Async XLA Ops:
  0.6 2.0 %copy-start = (s32[512]{0:T(512)S(1)}, s32[512]{0:T(512)}, u32[]{:S(2)}) copy-start(s32[512]{0:T(512)} %param.4) | copy-start | bytes 6148
  0.7 14.0 %collective-permute-start.2 = (bf16[1024,512]{1,0:T(8,128)(2,1)}, bf16[1024,512]{1,0:T(8,128)(2,1)S(1)}, u32[]{:S(2)}, u32[]{:S(2)}) collective-permute-start(bf16[1024,512]{1,0:T(8,128)(2,1)} %chunk.8), channel_id=1, source_target_pairs={{0,2},{8,10},{16,18},{24,26}} | collective-permute-start | bytes 3145736 | tf_op jit(solution)/shard_map/ppermute | solution.py:321
  2.0 10.8 %collective-permute-start = (bf16[256,1536]{1,0:T(8,128)(2,1)S(1)}, bf16[256,1536]{1,0:T(8,128)(2,1)S(1)}, u32[]{:S(2)}, u32[]{:S(2)}) collective-permute-start(bf16[256,1536]{1,0:T(8,128)(2,1)S(1)} %chunk.6), channel_id=1, source_target_pairs={{0,4},{1,5},{2,6},{3,7}} | collective-permute-start | bytes 2359304 | tf_op jit(solution)/shard_map/ppermute | solution.py:388
  9.6 7.1 %collective-permute-start.5 = (bf16[256,1536]{1,0:T(8,128)(2,1)S(1)}, bf16[256,1536]{1,0:T(8,128)(2,1)S(1)}, u32[]{:S(2)}, u32[]{:S(2)}) collective-permute-start(bf16[256,1536]{1,0:T(8,128)(2,1)S(1)} %get-tuple-element.10), channel_id=1, source_target_pairs={{0,4},{4,0},{8,12},{12,8},{16,20},{20,16},{24,28},{28,24},{1,5},{5... | collective-permute-start | bytes 2359304 | tf_op jit(solution)/shard_map/ppermute | solution.py:391
  11.4 52.3 %collective-permute-start.7 = (bf16[1024,512]{1,0:T(8,128)(2,1)S(1)}, bf16[1024,512]{1,0:T(8,128)(2,1)S(1)}, u32[]{:S(2)}, u32[]{:S(2)}) collective-permute-start(bf16[1024,512]{1,0:T(8,128)(2,1)S(1)} %chunk.10), channel_id=1, source_target_pairs={{4,6},{12,14},{20,22},{28,30}} | collective-permute-start | bytes 3145736 | tf_op jit(solution)/shard_map/ppermute | solution.py:321
  13.3 12.7 %collective-permute-start.1 = (bf16[256,1536]{1,0:T(8,128)(2,1)S(1)}, bf16[256,1536]{1,0:T(8,128)(2,1)S(1)}, u32[]{:S(2)}, u32[]{:S(2)}) collective-permute-start(bf16[256,1536]{1,0:T(8,128)(2,1)S(1)} %chunk.7.refs_0_), channel_id=1, source_target_pairs={{0,8},{4,20},{1,9},{5,21},{2,10},{6,22},{3,11},{7,23}} | collective-permute-start | bytes 2359304 | tf_op jit(solution)/shard_map/ppermute | solution.py:396
  15.2 52.4 %collective-permute-start.8 = (bf16[1024,512]{1,0:T(8,128)(2,1)S(1)}, bf16[1024,512]{1,0:T(8,128)(2,1)S(1)}, u32[]{:S(2)}, u32[]{:S(2)}) collective-permute-start(bf16[1024,512]{1,0:T(8,128)(2,1)S(1)} %chunk.9.refs_2_.refs_1_), channel_id=1, source_target_pairs={{2,1},{0,2},{10,9},{8,10},{18,17},{16,18},{26,25},{24,26}} | collective-permute-start | bytes 3145736 | tf_op jit(solution)/shard_map/ppermute | solution.py:321
  15.9 51.7 %collective-permute-start.9 = (bf16[1024,512]{1,0:T(8,128)(2,1)S(1)}, bf16[1024,512]{1,0:T(8,128)(2,1)S(1)}, u32[]{:S(2)}, u32[]{:S(2)}) collective-permute-start(bf16[1024,512]{1,0:T(8,128)(2,1)S(1)} %chunk.9.refs_2_.refs_1_), channel_id=1, source_target_pairs={{2,3},{10,11},{18,19},{26,27}} | collective-permute-start | bytes 3145736 | tf_op jit(solution)/shard_map/ppermute | solution.py:321
  16.8 48.9 %collective-permute-start.6 = (bf16[256,1536]{1,0:T(8,128)(2,1)S(1)}, bf16[256,1536]{1,0:T(8,128)(2,1)S(1)}, u32[]{:S(2)}, u32[]{:S(2)}) collective-permute-start(bf16[256,1536]{1,0:T(8,128)(2,1)S(1)} %add.13.refs_0_), channel_id=1, source_target_pairs={{0,8},{4,20},{8,0},{12,28},{16,24},{20,4},{24,16},{28,12},{1,9},{5... | collective-permute-start | bytes 2359304 | tf_op jit(solution)/shard_map/ppermute | solution.py:398
  26.2 42.8 %collective-permute-start.3 = (bf16[256,1536]{1,0:T(8,128)(2,1)S(1)}, bf16[256,1536]{1,0:T(8,128)(2,1)S(1)}, u32[]{:S(2)}, u32[]{:S(2)}) collective-permute-start(bf16[256,1536]{1,0:T(8,128)(2,1)S(1)} %add.11.refs_0_), channel_id=1, source_target_pairs={{0,16},{8,24},{4,12},{20,28},{1,17},{9,25},{5,13},{21,29},{2,18},{... | collective-permute-start | bytes 2359304 | tf_op jit(solution)/shard_map/ppermute | solution.py:396
  64.3 14.6 %collective-permute-start.12 = (bf16[1024,512]{1,0:T(8,128)(2,1)S(1)}, bf16[1024,512]{1,0:T(8,128)(2,1)S(1)}, u32[]{:S(2)}, u32[]{:S(2)}) collective-permute-start(bf16[1024,512]{1,0:T(8,128)(2,1)S(1)} %chunk.11.refs_2_.refs_3_.rest_0_.refs_4_), channel_id=1, source_target_pairs={{6,7},{14,15},{22,23},{30,31}} | collective-permute-start | bytes 3145736 | tf_op jit(solution)/shard_map/ppermute | solution.py:321
  65.7 24.1 %collective-permute-start.13 = (bf16[1024,512]{1,0:T(8,128)(2,1)S(1)}, bf16[1024,512]{1,0:T(8,128)(2,1)S(1)}, u32[]{:S(2)}, u32[]{:S(2)}) collective-permute-start(bf16[1024,512]{1,0:T(8,128)(2,1)S(1)} %chunk.11.refs_2_.refs_3_.rest_0_.refs_4_), channel_id=1, source_target_pairs={{6,5},{4,6},{14,13},{12,14},{22,21},{20,22},{30,29},{28,30}} | collective-permute-start | bytes 3145736 | tf_op jit(solution)/shard_map/ppermute | solution.py:321
  67.7 23.4 %collective-permute-start.10 = (bf16[256,1536]{1,0:T(8,128)(2,1)S(1)}, bf16[256,1536]{1,0:T(8,128)(2,1)S(1)}, u32[]{:S(2)}, u32[]{:S(2)}) collective-permute-start(bf16[256,1536]{1,0:T(8,128)(2,1)S(1)} %add.14.refs_0_), channel_id=1, source_target_pairs={{0,16},{4,12},{8,24},{12,4},{16,0},{20,28},{24,8},{28,20},{1,17},{... | collective-permute-start | bytes 2359304 | tf_op jit(solution)/shard_map/ppermute | solution.py:398
  69.1 32.7 %copy-start.1 = (bf16[512,512]{1,0:T(8,128)(2,1)S(1)}, bf16[512,512]{1,0:T(8,128)(2,1)}, u32[]{:S(2)}) copy-start(bf16[512,512]{1,0:T(8,128)(2,1)} %inverse_ref.1) | copy-start | bytes 1572868
  69.1 23.5 %collective-permute-start.4 = (bf16[256,1536]{1,0:T(8,128)(2,1)S(1)}, bf16[256,1536]{1,0:T(8,128)(2,1)S(1)}, u32[]{:S(2)}, u32[]{:S(2)}) collective-permute-start(bf16[256,1536]{1,0:T(8,128)(2,1)S(1)} %add.12.mine_ref), channel_id=1, source_target_pairs={{0,4},{4,0},{8,12},{12,8},{16,20},{20,16},{24,28},{28,24},{1,5},{5... | collective-permute-start | bytes 2359304 | tf_op jit(solution)/shard_map/ppermute | solution.py:400
  72.2 37.1 %collective-permute-start.14 = (bf16[1024,512]{1,0:T(8,128)(2,1)S(1)}, bf16[1024,512]{1,0:T(8,128)(2,1)S(1)}, u32[]{:S(2)}, u32[]{:S(2)}) collective-permute-start(bf16[1024,512]{1,0:T(8,128)(2,1)S(1)} %collective-permute-done.8.refs_3_.rest_1_.refs_2_.refs_1_), channel_id=1, source_target_pairs={{2,1},{10,9},{18,17},{26,25}} | collective-permute-start | bytes 3145736 | tf_op jit(solution)/shard_map/ppermute | solution.py:321
  78.9 30.4 %collective-permute-start.15 = (bf16[1024,512]{1,0:T(8,128)(2,1)S(1)}, bf16[1024,512]{1,0:T(8,128)(2,1)S(1)}, u32[]{:S(2)}, u32[]{:S(2)}) collective-permute-start(bf16[1024,512]{1,0:T(8,128)(2,1)S(1)} %collective-permute-done.8.refs_3_.rest_1_.refs_2_.refs_1_), channel_id=1, source_target_pairs={{2,3},{10,11},{18,19},{26,27}} | collective-permute-start | bytes 3145736 | tf_op jit(solution)/shard_map/ppermute | solution.py:321
  89.8 19.6 %collective-permute-start.16 = (bf16[1024,512]{1,0:T(8,128)(2,1)S(1)}, bf16[1024,512]{1,0:T(8,128)(2,1)S(1)}, u32[]{:S(2)}, u32[]{:S(2)}) collective-permute-start(bf16[1024,512]{1,0:T(8,128)(2,1)S(1)} %collective-permute-done.13.refs_5_.refs_4_), channel_id=1, source_target_pairs={{6,5},{14,13},{22,21},{30,29}} | collective-permute-start | bytes 3145736 | tf_op jit(solution)/shard_map/ppermute | solution.py:321
  91.1 18.2 %collective-permute-start.17 = (bf16[1024,512]{1,0:T(8,128)(2,1)S(1)}, bf16[1024,512]{1,0:T(8,128)(2,1)S(1)}, u32[]{:S(2)}, u32[]{:S(2)}) collective-permute-start(bf16[1024,512]{1,0:T(8,128)(2,1)S(1)} %collective-permute-done.13.refs_5_.refs_4_), channel_id=1, source_target_pairs={{6,7},{14,15},{22,23},{30,31}} | collective-permute-start | bytes 3145736 | tf_op jit(solution)/shard_map/ppermute | solution.py:321
  92.6 9.2 %collective-permute-start.11 = (bf16[256,1536]{1,0:T(8,128)(2,1)S(1)}, bf16[256,1536]{1,0:T(8,128)(2,1)S(1)}, u32[]{:S(2)}, u32[]{:S(2)}) collective-permute-start(bf16[256,1536]{1,0:T(8,128)(2,1)S(1)} %add.15.mine_ref), channel_id=1, source_target_pairs={{0,4},{4,0},{8,12},{12,8},{16,20},{20,16},{24,28},{28,24},{1,5},{5... | collective-permute-start | bytes 2359304 | tf_op jit(solution)/shard_map/ppermute | solution.py:403

commit v5 on v4

--- a/solution.py
+++ b/solution.py
@@ -43,14 +43,14 @@
 def chunk(place, axis, core, matrix, first_row, rows, width, held=None, weight=0, after=()):
     in_specs, operands = [SMEM, ANY], [place, matrix]
     if held is not None:
-        in_specs.append(ANY)
+        in_specs.append(VMEM)
         operands.append(held)
     in_specs += [ANY] * len(after)
     operands += after
     return pl.pallas_call(
         functools.partial(chunk_kernel, first_row, axis, core),
         in_specs=in_specs,
-        out_specs=ANY,
+        out_specs=VMEM,
         out_shape=jax.ShapeDtypeStruct((rows, width), BF16),
         scratch_shapes=[pltpu.SemaphoreType.DMA],
         input_output_aliases={} if held is None else {2: 0},

time: 116 us -> 89.5 us (0.77)
  waiting for transfers between devices: 59.5 us -> 32 us
    ppermute x10, waiting for transfers between devices: 52.4 us -> 20.3 us  [move(): return lax.ppermute(value, ('prow', 'pcol'), pairs)]
    ppermute x2, waiting for transfers between devices: 0.01 us -> 3.52 us  [per_device(): up_got = [lax.ppermute(up[0], 'prow', swap_pairs(n_prow, orders, step))]]
    ppermute x10, starting transfers between devices: 10.9 us -> 13.7 us  [move(): return lax.ppermute(value, ('prow', 'pcol'), pairs)]
    ppermute x1, starting transfers between devices: 3.1 us -> 1.53 us  [per_device(): down_got = lax.ppermute(down, 'prow', swap_pairs(n_prow, cores, 0))]
    ppermute x2, starting transfers between devices: 3.47 us -> 2.26 us  [per_device(): up_got = [lax.ppermute(up[0], 'prow', swap_pairs(n_prow, orders, step))]]
  transfers between devices with their start and end apart: 18 -> 18, of which waited for: 4 -> 6; matrix products, arithmetic and copies ran while one was open for 0% -> 0% of each run, Pallas kernels for 23% -> 30%
where the time goes in v5:
time: 89.5 us; the launch traced here: 88.8 us
  Pallas kernels  34 us (38%)
  waiting for transfers between devices  32 us (36%)
  starting transfers between devices  22.2 us (25%)
    ppermute x10, waiting for transfers between devices, move(): return lax.ppermute(value, ('prow', 'pcol'), pairs)  20.3 us
    ppermute x10, starting transfers between devices, move(): return lax.ppermute(value, ('prow', 'pcol'), pairs)  13.7 us
    pallas_call x2, Pallas kernels, update(): pl.pallas_call(functools.partial(update_kernel, groups, len(received[0]),...  11.9 us
    pallas_call x1, Pallas kernels, swap(): pl.pallas_call(swap_kernel, grid_spec=pltpu.PrefetchScalarGridSpec(num_sc...  9.11 us
    ppermute x2, waiting for transfers between devices, per_device(): down_got = lax.ppermute(down, 'prow', grow_pairs(orders, step))  8.11 us
    pallas_call x1, Pallas kernels, pick(): pl.pallas_call(pick_kernel, grid_spec=pltpu.PrefetchScalarGridSpec(num_sc...  6.7 us
    pallas_call x6, Pallas kernels, chunk(): pl.pallas_call(functools.partial(chunk_kernel, first_row, axis, core), in...  4.31 us
    ppermute x2, waiting for transfers between devices, per_device(): up_got = [lax.ppermute(up[0], 'prow', swap_pairs(n_prow, orders, step))]  3.52 us
  transfers between devices with their start and end apart: 18, of which 6 were waited for; matrix products, arithmetic and copies ran while one was open for 0% of the time, Pallas kernels for 30%

profile of v5, /device:TPU:21, one launch (start us, length us, event | category | flops | bytes accessed | tf_op | source)
XLA Modules:
  0.0 88.8 jit_solution(14742406976853947649)
XLA Ops:
  0.1 1.5 %chunk.8 = bf16[1024,512]{1,0:T(8,128)(2,1)} custom-call(s32[3]{0:T(128)S(1)} %pad_add_fusion.place_ref, bf16[2048,1536]{1,0:T(8,128)(2,1)} %refs_0_.3), custom_call_target="tpu_custom_call" | custom-call | flops 5750000128 | bytes 18450000 | tf_op jit(solution)/shard_map/chunk/pallas_call | solution.py:50
  1.6 0.7 collective-permute-start.2
  2.4 0.6 chunk.6
  2.9 0.7 collective-permute-start
  3.8 6.7 %pick_rows.1 = (bf16[256,1536]{1,0:T(8,128)(2,1)S(1)}, bf16[256,1536]{1,0:T(8,128)(2,1)S(1)}) custom-call(s32[3]{0:T(128)S(1)} %pad_add_fusion.place_ref, s32[512,1]{1,0:T(8,128)S(1)} %copy.9.pivots_ref, bf16[2048,1536]{1,0:T(8,128)(2,1)} %refs_0_.3), custom_call_target="tpu_custom_call" | custom-call | tf_op jit(solution)/shard_map/pick_rows/pallas_call | solution.py:84
  10.5 1.3 %collective-permute-start.5 = (bf16[256,1536]{1,0:T(8,128)(2,1)S(1)}, bf16[256,1536]{1,0:T(8,128)(2,1)S(1)}, u32[]{:S(2)}, u32[]{:S(2)}) collective-permute-start(bf16[256,1536]{1,0:T(8,128)(2,1)S(1)} %get-tuple-element.10), channel_id=1, source_target_pairs={{0,4},{4,0},{8,12},{12,8},{16,20},{20,16},{24,28},{28,24},{1,5},{5... | collective-permute-start | bytes 2359304 | tf_op jit(solution)/shard_map/ppermute | solution.py:391
  12.4 1.3 %collective-permute-start.7 = (bf16[1024,512]{1,0:T(8,128)(2,1)S(1)}, bf16[1024,512]{1,0:T(8,128)(2,1)S(1)}, u32[]{:S(2)}, u32[]{:S(2)}) collective-permute-start(bf16[1024,512]{1,0:T(8,128)(2,1)S(1)} %chunk.10), channel_id=1, source_target_pairs={{4,6},{12,14},{20,22},{28,30}} | collective-permute-start | bytes 3145736 | tf_op jit(solution)/shard_map/ppermute | solution.py:321
  13.7 0.6 chunk.7.refs_0_
  14.3 1.3 %collective-permute-start.1 = (bf16[256,1536]{1,0:T(8,128)(2,1)S(1)}, bf16[256,1536]{1,0:T(8,128)(2,1)S(1)}, u32[]{:S(2)}, u32[]{:S(2)}) collective-permute-start(bf16[256,1536]{1,0:T(8,128)(2,1)S(1)} %chunk.7.refs_0_), channel_id=1, source_target_pairs={{0,8},{4,20},{1,9},{5,21},{2,10},{6,22},{3,11},{7,23}} | collective-permute-start | bytes 2359304 | tf_op jit(solution)/shard_map/ppermute | solution.py:396
  15.6 0.6 chunk.9.refs_2_.refs_1_
  16.2 0.7 collective-permute-start.8
  16.9 0.7 collective-permute-start.9
  17.7 2.2 %collective-permute-start.6 = (bf16[256,1536]{1,0:T(8,128)(2,1)S(1)}, bf16[256,1536]{1,0:T(8,128)(2,1)S(1)}, u32[]{:S(2)}, u32[]{:S(2)}) collective-permute-start(bf16[256,1536]{1,0:T(8,128)(2,1)S(1)} %add.13.refs_0_), channel_id=1, source_target_pairs={{0,8},{4,20},{8,0},{12,28},{16,24},{20,4},{24,16},{28,12},{1,9},{5... | collective-permute-start | bytes 2359304 | tf_op jit(solution)/shard_map/ppermute | solution.py:398
  19.9 7.4 %collective-permute-done.1.refs_1_ = bf16[256,1536]{1,0:T(8,128)(2,1)S(1)} collective-permute-done((bf16[256,1536]{1,0:T(8,128)(2,1)S(1)}, bf16[256,1536]{1,0:T(8,128)(2,1)S(1)}, u32[]{:S(2)}, u32[]{:S(2)}) %collective-permute-start.1) | collective-permute-done | bytes 786464 | tf_op jit(solution)/shard_map/ppermute | solution.py:396
  27.4 1.3 %collective-permute-start.3 = (bf16[256,1536]{1,0:T(8,128)(2,1)S(1)}, bf16[256,1536]{1,0:T(8,128)(2,1)S(1)}, u32[]{:S(2)}, u32[]{:S(2)}) collective-permute-start(bf16[256,1536]{1,0:T(8,128)(2,1)S(1)} %add.11.refs_0_), channel_id=1, source_target_pairs={{0,16},{8,24},{4,12},{20,28},{1,17},{9,25},{5,13},{21,29},{2,18},{... | collective-permute-start | bytes 2359304 | tf_op jit(solution)/shard_map/ppermute | solution.py:396
  28.8 6.2 %collective-permute-done.7.refs_0_ = bf16[1024,512]{1,0:T(8,128)(2,1)S(1)} collective-permute-done((bf16[1024,512]{1,0:T(8,128)(2,1)S(1)}, bf16[1024,512]{1,0:T(8,128)(2,1)S(1)}, u32[]{:S(2)}, u32[]{:S(2)}) %collective-permute-start.7) | collective-permute-done | bytes 1048608 | tf_op jit(solution)/shard_map/ppermute | solution.py:321
  35.0 0.6 chunk.11.refs_2_.refs_3_.rest_0_.refs_4_
  35.6 1.4 %collective-permute-start.12 = (bf16[1024,512]{1,0:T(8,128)(2,1)S(1)}, bf16[1024,512]{1,0:T(8,128)(2,1)S(1)}, u32[]{:S(2)}, u32[]{:S(2)}) collective-permute-start(bf16[1024,512]{1,0:T(8,128)(2,1)S(1)} %chunk.11.refs_2_.refs_3_.rest_0_.refs_4_), channel_id=1, source_target_pairs={{6,7},{14,15},{22,23},{30,31}} | collective-permute-start | bytes 3145736 | tf_op jit(solution)/shard_map/ppermute | solution.py:321
  37.0 3.5 %collective-permute-done.6.refs_1_ = bf16[256,1536]{1,0:T(8,128)(2,1)S(1)} collective-permute-done((bf16[256,1536]{1,0:T(8,128)(2,1)S(1)}, bf16[256,1536]{1,0:T(8,128)(2,1)S(1)}, u32[]{:S(2)}, u32[]{:S(2)}) %collective-permute-start.6) | collective-permute-done | bytes 786464 | tf_op jit(solution)/shard_map/ppermute | solution.py:398
  40.5 1.9 %collective-permute-start.13 = (bf16[1024,512]{1,0:T(8,128)(2,1)S(1)}, bf16[1024,512]{1,0:T(8,128)(2,1)S(1)}, u32[]{:S(2)}, u32[]{:S(2)}) collective-permute-start(bf16[1024,512]{1,0:T(8,128)(2,1)S(1)} %chunk.11.refs_2_.refs_3_.rest_0_.refs_4_), channel_id=1, source_target_pairs={{6,5},{4,6},{14,13},{12,14},{22,21},{20,22},{30,29},{28,30}} | collective-permute-start | bytes 3145736 | tf_op jit(solution)/shard_map/ppermute | solution.py:321
  42.6 0.7 collective-permute-done.3.refs_1_
  43.4 1.5 %collective-permute-start.4 = (bf16[256,1536]{1,0:T(8,128)(2,1)S(1)}, bf16[256,1536]{1,0:T(8,128)(2,1)S(1)}, u32[]{:S(2)}, u32[]{:S(2)}) collective-permute-start(bf16[256,1536]{1,0:T(8,128)(2,1)S(1)} %add.12.mine_ref), channel_id=1, source_target_pairs={{0,4},{4,0},{8,12},{12,8},{16,20},{20,16},{24,28},{28,24},{1,5},{5... | collective-permute-start | bytes 2359304 | tf_op jit(solution)/shard_map/ppermute | solution.py:400
  44.9 0.7 collective-permute-start.14
  45.7 3.0 %collective-permute-done.12.rest_3_.refs_6_ = bf16[1024,512]{1,0:T(8,128)(2,1)S(1)} collective-permute-done((bf16[1024,512]{1,0:T(8,128)(2,1)S(1)}, bf16[1024,512]{1,0:T(8,128)(2,1)S(1)}, u32[]{:S(2)}, u32[]{:S(2)}) %collective-permute-start.12) | collective-permute-done | bytes 1048608 | tf_op jit(solution)/shard_map/ppermute | solution.py:321
  48.6 0.7 collective-permute-start.15
  49.3 11.1 %collective-permute-done.13.refs_5_.refs_4_ = bf16[1024,512]{1,0:T(8,128)(2,1)S(1)} collective-permute-done((bf16[1024,512]{1,0:T(8,128)(2,1)S(1)}, bf16[1024,512]{1,0:T(8,128)(2,1)S(1)}, u32[]{:S(2)}, u32[]{:S(2)}) %collective-permute-start.13) | collective-permute-done | bytes 1048608 | tf_op jit(solution)/shard_map/ppermute | solution.py:321
  60.4 4.2 %collective-permute-start.16 = (bf16[1024,512]{1,0:T(8,128)(2,1)S(1)}, bf16[1024,512]{1,0:T(8,128)(2,1)S(1)}, u32[]{:S(2)}, u32[]{:S(2)}) collective-permute-start(bf16[1024,512]{1,0:T(8,128)(2,1)S(1)} %collective-permute-done.13.refs_5_.refs_4_), channel_id=1, source_target_pairs={{6,5},{14,13},{22,21},{30,29}} | collective-permute-start | bytes 3145736 | tf_op jit(solution)/shard_map/ppermute | solution.py:321
  64.6 1.4 %collective-permute-start.17 = (bf16[1024,512]{1,0:T(8,128)(2,1)S(1)}, bf16[1024,512]{1,0:T(8,128)(2,1)S(1)}, u32[]{:S(2)}, u32[]{:S(2)}) collective-permute-start(bf16[1024,512]{1,0:T(8,128)(2,1)S(1)} %collective-permute-done.13.refs_5_.refs_4_), channel_id=1, source_target_pairs={{6,7},{14,15},{22,23},{30,31}} | collective-permute-start | bytes 3145736 | tf_op jit(solution)/shard_map/ppermute | solution.py:321
  66.2 9.1 %swap_rows.1 = (bf16[2048,1536]{1,0:T(8,128)(2,1)}, f32[8,128]{1,0:T(8,128)}) custom-call(s32[3]{0:T(128)S(1)} %pad_add_fusion.place_ref, s32[1,512]{1,0:T(1,128)S(1)} %bitcast.5, bf16[2048,1536]{1,0:T(8,128)(2,1)} %refs_0_.3, bf16[256,1536]{1,0:T(8,128)(2,1)S(1)} %add.12.mine_ref, bf16[256,1536]{1,0:T(8,128)(2,1)S(1)} %collective-permute-done.4.other_ref), custom_call_target="tpu_custom_call" | custom-call | tf_op jit(solution)/shard_map/swap_rows/pallas_call | solution.py:169
  75.3 1.5 %upper.1.upper_ref = bf16[512,1536]{1,0:T(8,128)(2,1)S(1)} custom-call(s32[3]{0:T(128)S(1)} %pad_add_fusion.place_ref, bf16[512,512]{1,0:T(8,128)(2,1)S(1)} %copy-done.1, bf16[256,1536]{1,0:T(8,128)(2,1)S(1)} %add.15.mine_ref, bf16[256,1536]{1,0:T(8,128)(2,1)S(1)} %collective-permute-done.11.other_ref, ...), custom_call_target="tpu_custom_call" | custom-call | flops 2300000000 | bytes 7380000 | tf_op jit(solution)/shard_map/upper/pallas_call | solution.py:212
  76.8 6.0 %update_rows.2.swapped_ref = bf16[2048,1536]{1,0:T(8,128)(2,1)} custom-call(s32[3]{0:T(128)S(1)} %pad_add_fusion.place_ref, bf16[2048,1536]{1,0:T(8,128)(2,1)} %get-tuple-element.8.swapped_ref, bf16[512,1536]{1,0:T(8,128)(2,1)S(1)} %upper.1.upper_ref, bf16[2048,1536]{1,0:T(8,128)(2,1)} %refs_0_.3, ...), custom_call_target="tpu_custom_call", output_to_operand_aliasing={{}: (1, {})} | custom-call | tf_op jit(solution)/shard_map/update_rows/pallas_call | solution.py:278
  82.8 5.9 %update_rows.3 = bf16[2048,1536]{1,0:T(8,128)(2,1)} custom-call(s32[3]{0:T(128)S(1)} %pad_add_fusion.place_ref, bf16[2048,1536]{1,0:T(8,128)(2,1)} %update_rows.2.swapped_ref, bf16[512,1536]{1,0:T(8,128)(2,1)S(1)} %upper.1.upper_ref, bf16[2048,1536]{1,0:T(8,128)(2,1)} %refs_0_.3, ...), custom_call_target="tpu_custom_call", output_to_operand_aliasing={{}: (1, {})} | custom-call | tf_op jit(solution)/shard_map/update_rows/pallas_call | solution.py:278
  (28 shorter events, 1.4 us)
Async XLA Ops:
  1.6 2.0 %copy-start = (s32[512]{0:T(512)S(1)}, s32[512]{0:T(512)}, u32[]{:S(2)}) copy-start(s32[512]{0:T(512)} %param.4) | copy-start | bytes 6148
  1.6 14.0 %collective-permute-start.2 = (bf16[1024,512]{1,0:T(8,128)(2,1)}, bf16[1024,512]{1,0:T(8,128)(2,1)S(1)}, u32[]{:S(2)}, u32[]{:S(2)}) collective-permute-start(bf16[1024,512]{1,0:T(8,128)(2,1)} %chunk.8), channel_id=1, source_target_pairs={{0,2},{8,10},{16,18},{24,26}} | collective-permute-start | bytes 3145736 | tf_op jit(solution)/shard_map/ppermute | solution.py:321
  2.9 10.8 %collective-permute-start = (bf16[256,1536]{1,0:T(8,128)(2,1)S(1)}, bf16[256,1536]{1,0:T(8,128)(2,1)S(1)}, u32[]{:S(2)}, u32[]{:S(2)}) collective-permute-start(bf16[256,1536]{1,0:T(8,128)(2,1)S(1)} %chunk.6), channel_id=1, source_target_pairs={{0,4},{1,5},{2,6},{3,7}} | collective-permute-start | bytes 2359304 | tf_op jit(solution)/shard_map/ppermute | solution.py:388
  10.5 7.1 %collective-permute-start.5 = (bf16[256,1536]{1,0:T(8,128)(2,1)S(1)}, bf16[256,1536]{1,0:T(8,128)(2,1)S(1)}, u32[]{:S(2)}, u32[]{:S(2)}) collective-permute-start(bf16[256,1536]{1,0:T(8,128)(2,1)S(1)} %get-tuple-element.10), channel_id=1, source_target_pairs={{0,4},{4,0},{8,12},{12,8},{16,20},{20,16},{24,28},{28,24},{1,5},{5... | collective-permute-start | bytes 2359304 | tf_op jit(solution)/shard_map/ppermute | solution.py:391
  12.4 22.6 %collective-permute-start.7 = (bf16[1024,512]{1,0:T(8,128)(2,1)S(1)}, bf16[1024,512]{1,0:T(8,128)(2,1)S(1)}, u32[]{:S(2)}, u32[]{:S(2)}) collective-permute-start(bf16[1024,512]{1,0:T(8,128)(2,1)S(1)} %chunk.10), channel_id=1, source_target_pairs={{4,6},{12,14},{20,22},{28,30}} | collective-permute-start | bytes 3145736 | tf_op jit(solution)/shard_map/ppermute | solution.py:321
  14.3 13.0 %collective-permute-start.1 = (bf16[256,1536]{1,0:T(8,128)(2,1)S(1)}, bf16[256,1536]{1,0:T(8,128)(2,1)S(1)}, u32[]{:S(2)}, u32[]{:S(2)}) collective-permute-start(bf16[256,1536]{1,0:T(8,128)(2,1)S(1)} %chunk.7.refs_0_), channel_id=1, source_target_pairs={{0,8},{4,20},{1,9},{5,21},{2,10},{6,22},{3,11},{7,23}} | collective-permute-start | bytes 2359304 | tf_op jit(solution)/shard_map/ppermute | solution.py:396
  16.2 26.2 %collective-permute-start.8 = (bf16[1024,512]{1,0:T(8,128)(2,1)S(1)}, bf16[1024,512]{1,0:T(8,128)(2,1)S(1)}, u32[]{:S(2)}, u32[]{:S(2)}) collective-permute-start(bf16[1024,512]{1,0:T(8,128)(2,1)S(1)} %chunk.9.refs_2_.refs_1_), channel_id=1, source_target_pairs={{2,1},{0,2},{10,9},{8,10},{18,17},{16,18},{26,25},{24,26}} | collective-permute-start | bytes 3145736 | tf_op jit(solution)/shard_map/ppermute | solution.py:321
  16.9 25.5 %collective-permute-start.9 = (bf16[1024,512]{1,0:T(8,128)(2,1)S(1)}, bf16[1024,512]{1,0:T(8,128)(2,1)S(1)}, u32[]{:S(2)}, u32[]{:S(2)}) collective-permute-start(bf16[1024,512]{1,0:T(8,128)(2,1)S(1)} %chunk.9.refs_2_.refs_1_), channel_id=1, source_target_pairs={{2,3},{10,11},{18,19},{26,27}} | collective-permute-start | bytes 3145736 | tf_op jit(solution)/shard_map/ppermute | solution.py:321
  17.7 22.7 %collective-permute-start.6 = (bf16[256,1536]{1,0:T(8,128)(2,1)S(1)}, bf16[256,1536]{1,0:T(8,128)(2,1)S(1)}, u32[]{:S(2)}, u32[]{:S(2)}) collective-permute-start(bf16[256,1536]{1,0:T(8,128)(2,1)S(1)} %add.13.refs_0_), channel_id=1, source_target_pairs={{0,8},{4,20},{8,0},{12,28},{16,24},{20,4},{24,16},{28,12},{1,9},{5... | collective-permute-start | bytes 2359304 | tf_op jit(solution)/shard_map/ppermute | solution.py:398
  27.4 15.9 %collective-permute-start.3 = (bf16[256,1536]{1,0:T(8,128)(2,1)S(1)}, bf16[256,1536]{1,0:T(8,128)(2,1)S(1)}, u32[]{:S(2)}, u32[]{:S(2)}) collective-permute-start(bf16[256,1536]{1,0:T(8,128)(2,1)S(1)} %add.11.refs_0_), channel_id=1, source_target_pairs={{0,16},{8,24},{4,12},{20,28},{1,17},{9,25},{5,13},{21,29},{2,18},{... | collective-permute-start | bytes 2359304 | tf_op jit(solution)/shard_map/ppermute | solution.py:396
  35.6 13.0 %collective-permute-start.12 = (bf16[1024,512]{1,0:T(8,128)(2,1)S(1)}, bf16[1024,512]{1,0:T(8,128)(2,1)S(1)}, u32[]{:S(2)}, u32[]{:S(2)}) collective-permute-start(bf16[1024,512]{1,0:T(8,128)(2,1)S(1)} %chunk.11.refs_2_.refs_3_.rest_0_.refs_4_), channel_id=1, source_target_pairs={{6,7},{14,15},{22,23},{30,31}} | collective-permute-start | bytes 3145736 | tf_op jit(solution)/shard_map/ppermute | solution.py:321
  40.5 20.0 %collective-permute-start.13 = (bf16[1024,512]{1,0:T(8,128)(2,1)S(1)}, bf16[1024,512]{1,0:T(8,128)(2,1)S(1)}, u32[]{:S(2)}, u32[]{:S(2)}) collective-permute-start(bf16[1024,512]{1,0:T(8,128)(2,1)S(1)} %chunk.11.refs_2_.refs_3_.rest_0_.refs_4_), channel_id=1, source_target_pairs={{6,5},{4,6},{14,13},{12,14},{22,21},{20,22},{30,29},{28,30}} | collective-permute-start | bytes 3145736 | tf_op jit(solution)/shard_map/ppermute | solution.py:321
  42.5 22.1 %collective-permute-start.10 = (bf16[256,1536]{1,0:T(8,128)(2,1)S(1)}, bf16[256,1536]{1,0:T(8,128)(2,1)S(1)}, u32[]{:S(2)}, u32[]{:S(2)}) collective-permute-start(bf16[256,1536]{1,0:T(8,128)(2,1)S(1)} %add.14.refs_0_), channel_id=1, source_target_pairs={{0,16},{4,12},{8,24},{12,4},{16,0},{20,28},{24,8},{28,20},{1,17},{... | collective-permute-start | bytes 2359304 | tf_op jit(solution)/shard_map/ppermute | solution.py:398
  43.4 31.9 %copy-start.1 = (bf16[512,512]{1,0:T(8,128)(2,1)S(1)}, bf16[512,512]{1,0:T(8,128)(2,1)}, u32[]{:S(2)}) copy-start(bf16[512,512]{1,0:T(8,128)(2,1)} %inverse_ref.1) | copy-start | bytes 1572868
  43.4 22.7 %collective-permute-start.4 = (bf16[256,1536]{1,0:T(8,128)(2,1)S(1)}, bf16[256,1536]{1,0:T(8,128)(2,1)S(1)}, u32[]{:S(2)}, u32[]{:S(2)}) collective-permute-start(bf16[256,1536]{1,0:T(8,128)(2,1)S(1)} %add.12.mine_ref), channel_id=1, source_target_pairs={{0,4},{4,0},{8,12},{12,8},{16,20},{20,16},{24,28},{28,24},{1,5},{5... | collective-permute-start | bytes 2359304 | tf_op jit(solution)/shard_map/ppermute | solution.py:400
  44.9 37.9 %collective-permute-start.14 = (bf16[1024,512]{1,0:T(8,128)(2,1)S(1)}, bf16[1024,512]{1,0:T(8,128)(2,1)S(1)}, u32[]{:S(2)}, u32[]{:S(2)}) collective-permute-start(bf16[1024,512]{1,0:T(8,128)(2,1)S(1)} %collective-permute-done.8.refs_3_.rest_1_.refs_2_.refs_1_), channel_id=1, source_target_pairs={{2,1},{10,9},{18,17},{26,25}} | collective-permute-start | bytes 3145736 | tf_op jit(solution)/shard_map/ppermute | solution.py:321
  48.6 34.2 %collective-permute-start.15 = (bf16[1024,512]{1,0:T(8,128)(2,1)S(1)}, bf16[1024,512]{1,0:T(8,128)(2,1)S(1)}, u32[]{:S(2)}, u32[]{:S(2)}) collective-permute-start(bf16[1024,512]{1,0:T(8,128)(2,1)S(1)} %collective-permute-done.8.refs_3_.rest_1_.refs_2_.refs_1_), channel_id=1, source_target_pairs={{2,3},{10,11},{18,19},{26,27}} | collective-permute-start | bytes 3145736 | tf_op jit(solution)/shard_map/ppermute | solution.py:321
  60.4 22.4 %collective-permute-start.16 = (bf16[1024,512]{1,0:T(8,128)(2,1)S(1)}, bf16[1024,512]{1,0:T(8,128)(2,1)S(1)}, u32[]{:S(2)}, u32[]{:S(2)}) collective-permute-start(bf16[1024,512]{1,0:T(8,128)(2,1)S(1)} %collective-permute-done.13.refs_5_.refs_4_), channel_id=1, source_target_pairs={{6,5},{14,13},{22,21},{30,29}} | collective-permute-start | bytes 3145736 | tf_op jit(solution)/shard_map/ppermute | solution.py:321
  64.6 18.2 %collective-permute-start.17 = (bf16[1024,512]{1,0:T(8,128)(2,1)S(1)}, bf16[1024,512]{1,0:T(8,128)(2,1)S(1)}, u32[]{:S(2)}, u32[]{:S(2)}) collective-permute-start(bf16[1024,512]{1,0:T(8,128)(2,1)S(1)} %collective-permute-done.13.refs_5_.refs_4_), channel_id=1, source_target_pairs={{6,7},{14,15},{22,23},{30,31}} | collective-permute-start | bytes 3145736 | tf_op jit(solution)/shard_map/ppermute | solution.py:321
  66.1 9.2 %collective-permute-start.11 = (bf16[256,1536]{1,0:T(8,128)(2,1)S(1)}, bf16[256,1536]{1,0:T(8,128)(2,1)S(1)}, u32[]{:S(2)}, u32[]{:S(2)}) collective-permute-start(bf16[256,1536]{1,0:T(8,128)(2,1)S(1)} %add.15.mine_ref), channel_id=1, source_target_pairs={{0,4},{4,0},{8,12},{12,8},{16,20},{20,16},{24,28},{28,24},{1,5},{5... | collective-permute-start | bytes 2359304 | tf_op jit(solution)/shard_map/ppermute | solution.py:403

commit v6 on v5

--- a/solution.py
+++ b/solution.py
@@ -8,11 +8,11 @@
 from jax.sharding import PartitionSpec as P
 
 GROUPS = 2
-CHUNK_WEIGHTS = (5, 5)
-JOIN_WEIGHTS, JOIN_AFTER = (2, 2), ((0, 0), (3, 1))
+CHUNK_WEIGHTS = (0, 5)
+JOIN_WEIGHTS, JOIN_AFTER = (2, 2), ((1, 0), (3, 1))
 DOWN_WEIGHTS, DOWN_AFTER = (0, 20), ((1, 0), (0, 0))
 PIECES = 2
-BLOCK = 512
+BLOCK = 256
 F32, BF16 = jnp.float32, jnp.bfloat16
 VMEM = pl.BlockSpec(memory_space=pltpu.VMEM)
 ANY = pl.BlockSpec(memory_space=pl.ANY)
@@ -60,44 +60,57 @@
     )(*operands)
 
 
+def columns(number, block):
+    return pl.ds(pl.multiple_of(number * block, block), block)
+
+
 def pick_kernel(place_ref, pivots_ref, matrix_ref, *refs):
-    onehot_ref = refs[-1]
-    rows = matrix_ref.shape[0]
+    whole_ref, onehot_ref, sem = refs[-3:]
+    outs = refs[-3 - PIECES : -3]
+    rows, cols = whole_ref.shape
     width = pivots_ref.shape[0]
+    block = min(BLOCK, cols)
     count = width // PIECES
 
-    @pl.when(pl.program_id(0) == 0)
-    def _():
-        row = lax.broadcasted_iota(jnp.int32, (width, rows), 1) + place_ref[0] * rows
-        onehot_ref[...] = jnp.where(pivots_ref[...] == row, 1.0, 0.0).astype(BF16)
-
-    picked = jnp.dot(onehot_ref[...], matrix_ref[...], preferred_element_type=F32).astype(BF16)
-    for number, out_ref in enumerate(refs[:PIECES]):
-        out_ref[...] = picked[number * count : (number + 1) * count]
-
-
-def pick(place, pivots, matrix):
+    def fetch(number):
+        here = columns(number, block)
+        return pltpu.make_async_copy(
+            matrix_ref.at[:, here], whole_ref.at[:, here], sem.at[number]
+        )
+
+    for number in range(cols // block):
+        fetch(number).start()
+    row = lax.broadcasted_iota(jnp.int32, (width, rows), 1) + place_ref[0] * rows
+    onehot_ref[...] = jnp.where(pivots_ref[...] == row, 1.0, 0.0).astype(BF16)
+
+    @pl.loop(0, cols // block)
+    def _(number):
+        fetch(number).wait()
+        here = columns(number, block)
+        picked = jnp.dot(onehot_ref[...], whole_ref[:, here], preferred_element_type=F32)
+        picked = picked.astype(BF16)
+        for piece, out_ref in enumerate(outs):
+            out_ref[:, here] = picked[piece * count : (piece + 1) * count]
+
+
+def pick(place, pivots, matrix, after=()):
     rows, cols = matrix.shape
     width = pivots.shape[0]
     block = min(BLOCK, cols)
-    count = width // PIECES
     return pl.pallas_call(
         pick_kernel,
-        grid_spec=pltpu.PrefetchScalarGridSpec(
-            num_scalar_prefetch=1,
-            grid=(cols // block,),
-            in_specs=[
-                pl.BlockSpec((width, 1), lambda i, s: (0, 0)),
-                pl.BlockSpec((rows, block), lambda i, s: (0, i)),
-            ],
-            out_specs=[pl.BlockSpec((count, block), lambda i, s: (0, i))] * PIECES,
-            scratch_shapes=[pltpu.VMEM((width, rows), BF16)],
-        ),
-        out_shape=[jax.ShapeDtypeStruct((count, cols), BF16)] * PIECES,
+        in_specs=[SMEM, VMEM, ANY] + [ANY] * len(after),
+        out_specs=[VMEM] * PIECES,
+        out_shape=[jax.ShapeDtypeStruct((width // PIECES, cols), BF16)] * PIECES,
+        scratch_shapes=[
+            pltpu.VMEM((rows, cols), BF16),
+            pltpu.VMEM((width, rows), BF16),
+            pltpu.SemaphoreType.DMA((cols // block,)),
+        ],
         compiler_params=LARGE,
         cost_estimate=weight_of(0),
         name="pick_rows",
-    )(place, pivots[:, None], matrix)
+    )(place, pivots[:, None], matrix, *after)
 
 
 def add_kernel(count, *refs):
@@ -123,67 +136,79 @@
 
 
 def swap_kernel(place_ref, pivots_ref, matrix_ref, mine_ref, other_ref, *rest):
-    out_ref, token_ref, onehot_ref, keep_ref = rest[-4:]
-    token_ref[...] = jnp.zeros_like(token_ref)
-    step = pl.program_id(0)
-    rows, block = matrix_ref.shape
+    out_ref, token_ref, whole_ref, onehot_ref, keep_ref, down_ref, in_sem, out_sem = rest[-8:]
+    rows, cols = whole_ref.shape
     width = pivots_ref.shape[1]
     half = width // 2
     row_place, col_place, core = (place_ref[i] for i in range(3))
+    block = min(BLOCK, cols)
     piece = min(rows, 512)
 
-    @pl.when(step == 0)
-    def _():
-        for start in range(0, rows, piece):
-            here = slice(start, start + piece)
-            row = lax.broadcasted_iota(jnp.int32, (piece, width), 0) + row_place * rows + start
-            onehot = jnp.where(pivots_ref[...] == row, 1.0, 0.0)
-            onehot_ref[here] = onehot.astype(BF16)
-            has_pivot = jnp.max(onehot, axis=1, keepdims=True)
-            keep_ref[here] = jnp.broadcast_to(1.0 - has_pivot, (piece, 128))
-
-    in_panel = (col_place == 0) & (step * block < width)
-
-    @pl.when(in_panel)
-    def _():
-        out_ref[...] = matrix_ref[...]
-
-    @pl.when(jnp.logical_not(in_panel))
-    def _():
-        mine, other = mine_ref[...], other_ref[...]
-        top, bottom = jnp.where(core == 0, mine, other), jnp.where(core == 0, other, mine)
-        for start in range(0, rows, piece):
-            here = slice(start, start + piece)
-            keep = jnp.concatenate([keep_ref[here]] * (block // 128), axis=1)
-            moved = jnp.dot(onehot_ref[here, :half], top, preferred_element_type=F32)
-            moved += jnp.dot(onehot_ref[here, half:], bottom, preferred_element_type=F32)
-            out_ref[here] = (matrix_ref[here].astype(F32) * keep + moved).astype(BF16)
+    def fetch(number):
+        here = columns(number, block)
+        return pltpu.make_async_copy(
+            matrix_ref.at[:, here], whole_ref.at[:, here], in_sem.at[number]
+        )
+
+    def store(number):
+        here = columns(number, block)
+        return pltpu.make_async_copy(
+            whole_ref.at[:, here], out_ref.at[:, here], out_sem.at[number]
+        )
+
+    for number in range(cols // block):
+        fetch(number).start()
+    token_ref[...] = jnp.zeros_like(token_ref)
+    down_ref[pl.ds(pl.multiple_of(core * half, half), half)] = mine_ref[...]
+    down_ref[pl.ds(pl.multiple_of((1 - core) * half, half), half)] = other_ref[...]
+    for start in range(0, rows, piece):
+        here = slice(start, start + piece)
+        row = lax.broadcasted_iota(jnp.int32, (piece, width), 0) + row_place * rows + start
+        onehot = jnp.where(pivots_ref[...] == row, 1.0, 0.0)
+        onehot_ref[here] = onehot.astype(BF16)
+        has_pivot = jnp.max(onehot, axis=1, keepdims=True)
+        keep_ref[here] = jnp.broadcast_to(1.0 - has_pivot, (piece, 128))
+
+    @pl.loop(0, cols // block)
+    def _(number):
+        fetch(number).wait()
+        there = columns(number, block)
+
+        @pl.when((col_place > 0) | (number * block >= width))
+        def _():
+            down = down_ref[:, there]
+            for start in range(0, rows, piece):
+                here = slice(start, start + piece)
+                keep = jnp.concatenate([keep_ref[here]] * (block // 128), axis=1)
+                moved = jnp.dot(onehot_ref[here], down, preferred_element_type=F32)
+                kept = whole_ref[here, there].astype(F32) * keep
+                whole_ref[here, there] = (kept + moved).astype(BF16)
+
+        store(number).start()
+
+    for number in range(cols // block):
+        store(number).wait()
 
 
 def swap(place, pivots, matrix, mine, other, after=()):
     rows, cols = matrix.shape
     width = pivots.shape[0]
-    block = min(BLOCK, cols)
-    by_column = pl.BlockSpec((rows, block), lambda i, s: (0, i))
-    half_by_column = pl.BlockSpec((width // 2, block), lambda i, s: (0, i))
+    count = cols // min(BLOCK, cols)
     return pl.pallas_call(
         swap_kernel,
-        grid_spec=pltpu.PrefetchScalarGridSpec(
-            num_scalar_prefetch=1,
-            grid=(cols // block,),
-            in_specs=[
-                pl.BlockSpec((1, width), lambda i, s: (0, 0)),
-                by_column,
-                half_by_column,
-                half_by_column,
-            ]
-            + [ANY] * len(after),
-            out_specs=[by_column, pl.BlockSpec((8, 128), lambda i, s: (0, 0))],
-            scratch_shapes=[pltpu.VMEM((rows, width), BF16), pltpu.VMEM((rows, 128), F32)],
-        ),
+        in_specs=[SMEM, VMEM, ANY, VMEM, VMEM] + [ANY] * len(after),
+        out_specs=[pl.BlockSpec(memory_space=pltpu.HBM), VMEM],
         out_shape=[
             jax.ShapeDtypeStruct((rows, cols), BF16),
             jax.ShapeDtypeStruct((8, 128), F32),
+        ],
+        scratch_shapes=[
+            pltpu.VMEM((rows, cols), BF16),
+            pltpu.VMEM((rows, width), BF16),
+            pltpu.VMEM((rows, 128), F32),
+            pltpu.VMEM((width, cols), BF16),
+            pltpu.SemaphoreType.DMA((count,)),
+            pltpu.SemaphoreType.DMA((count,)),
         ],
         compiler_params=LARGE,
         cost_estimate=weight_of(0),
@@ -220,75 +245,83 @@
     )(place, unit_inverse, mine, other, *after)
 
 
-def update_kernel(groups, per_group, pick_source, place_ref, swapped_ref, upper_ref, *refs):
-    sources = refs[: 1 + per_group * len(groups)]
-    out_ref, panel_ref, sem = refs[-3:]
-    step = pl.program_id(0)
-    width = panel_ref.shape[1]
-    block = out_ref.shape[1]
-    row_place, col_place = place_ref[0], place_ref[1]
-    first_row = groups[0][0]
-
-    def fetch(number, action):
-        start, count = groups[number]
-        here = panel_ref.at[pl.ds(start - first_row, count)]
-        views = [sources[0].at[pl.ds(start, count), pl.ds(0, width)]]
-        views += sources[1 + number * per_group : 1 + (number + 1) * per_group]
+def update_kernel(first_row, per_group, pick_source, place_ref, swapped_ref, upper_ref, *refs):
+    sources = refs[: 1 + per_group]
+    out_ref, rows_ref, panel_ref, in_sem, out_sem, sem = refs[-6:]
+    count, width = panel_ref.shape
+    cols = rows_ref.shape[1]
+    row_place, col_place, core = (place_ref[i] for i in range(3))
+    block = min(BLOCK, cols)
+    piece = min(count, 512)
+    rows = pl.ds(first_row, count)
+
+    def fetch_panel(action):
+        views = [sources[0].at[rows, pl.ds(0, width)], *sources[1:]]
         for choice, view in enumerate(views):
-            @pl.when(pick_source(col_place, place_ref[2]) == choice)
+            @pl.when(pick_source(col_place, core) == choice)
             def _():
-                action(pltpu.make_async_copy(view, here, sem.at[number]))
-
-    @pl.when(step == 0)
-    def _():
-        for number in range(len(groups)):
-            fetch(number, lambda copy: copy.start())
-        for number in range(len(groups)):
-            fetch(number, lambda copy: copy.wait())
-
-    in_panel = (col_place == 0) & (step * block < width)
-
-    @pl.when(in_panel)
-    def _():
-        out_ref[...] = swapped_ref[...]
-
-    @pl.when(jnp.logical_not(in_panel))
-    def _():
-        upper = upper_ref[...]
-        for start, count in groups:
-            here = slice(start - first_row, start - first_row + count)
-            product = jnp.dot(panel_ref[here], upper, preferred_element_type=F32)
-            out_ref[here] = (swapped_ref[here].astype(F32) - product).astype(BF16)
-        if first_row < width:
-            @pl.when(row_place == 0)
-            def _():
-                out_ref[: width - first_row] = upper[first_row:]
-
-
-def update(groups, pick_source, place, matrix, swapped, upper, received):
+                action(pltpu.make_async_copy(view, panel_ref, sem))
+
+    def fetch(number):
+        here = columns(number, block)
+        return pltpu.make_async_copy(
+            swapped_ref.at[rows, here], rows_ref.at[:, here], in_sem.at[number]
+        )
+
+    def store(number):
+        here = columns(number, block)
+        return pltpu.make_async_copy(
+            rows_ref.at[:, here], out_ref.at[rows, here], out_sem.at[number]
+        )
+
+    fetch_panel(lambda copy: copy.start())
+    for number in range(cols // block):
+        fetch(number).start()
+    fetch_panel(lambda copy: copy.wait())
+
+    @pl.loop(0, cols // block)
+    def _(number):
+        fetch(number).wait()
+        there = columns(number, block)
+
+        @pl.when((col_place > 0) | (number * block >= width))
+        def _():
+            upper = upper_ref[:, there]
+            for start in range(0, count, piece):
+                here = slice(start, start + piece)
+                product = jnp.dot(panel_ref[here], upper, preferred_element_type=F32)
+                left = rows_ref[here, there].astype(F32) - product
+                rows_ref[here, there] = left.astype(BF16)
+            if first_row < width:
+                @pl.when(row_place == 0)
+                def _():
+                    rows_ref[: width - first_row, there] = upper[first_row:]
+
+        store(number).start()
+
+    for number in range(cols // block):
+        store(number).wait()
+
+
+def update(group, pick_source, place, matrix, swapped, upper, received):
+    first_row, count = group
     rows, cols = matrix.shape
     width = upper.shape[0]
-    block = min(BLOCK, cols)
-    count = sum(size for _, size in groups)
-    first_row = groups[0][0]
-    by_column = pl.BlockSpec(
-        (pl.Element(count), pl.Element(block)), lambda i, s: (first_row, i * block)
-    )
-    sources = [matrix] + [x for group in received for x in group]
-    return pl.pallas_call(
-        functools.partial(update_kernel, groups, len(received[0]), pick_source),
-        grid_spec=pltpu.PrefetchScalarGridSpec(
-            num_scalar_prefetch=1,
-            grid=(cols // block,),
-            in_specs=[by_column, pl.BlockSpec((width, block), lambda i, s: (0, i))]
-            + [ANY] * len(sources),
-            out_specs=by_column,
-            scratch_shapes=[
-                pltpu.VMEM((count, width), BF16),
-                pltpu.SemaphoreType.DMA((len(groups),)),
-            ],
-        ),
+    blocks = cols // min(BLOCK, cols)
+    sources = [matrix] + received
+    hbm = pl.BlockSpec(memory_space=pltpu.HBM)
+    return pl.pallas_call(
+        functools.partial(update_kernel, first_row, len(received), pick_source),
+        in_specs=[SMEM, hbm, VMEM] + [ANY] * len(sources),
+        out_specs=hbm,
         out_shape=jax.ShapeDtypeStruct((rows, cols), BF16),
+        scratch_shapes=[
+            pltpu.VMEM((count, cols), BF16),
+            pltpu.VMEM((count, width), BF16),
+            pltpu.SemaphoreType.DMA((blocks,)),
+            pltpu.SemaphoreType.DMA((blocks,)),
+            pltpu.SemaphoreType.DMA,
+        ],
         input_output_aliases={1: 0},
         compiler_params=LARGE,
         cost_estimate=weight_of(0),
@@ -386,26 +419,32 @@
 
     order = jnp.where(core == 0, pivots, jnp.roll(pivots, half))
     down_got = lax.ppermute(chunk(place, 0, 0, matrix, half, half, cols), "prow", [(0, 1)])
-    pieces = pick(place, order, matrix)
+    if 0 < 2:
+        down = chunk(place, 0, 0, matrix, 0, half, cols, down_got)
+    pieces = pick(place, order, matrix, [down] if 0 == 1 else [])
     up, sent = pieces[: PIECES // 2], pieces[PIECES // 2 :]
     up_got = [lax.ppermute(x, "prow", swap_pairs(n_prow, cores, 0)) for x in sent]
-    down = chunk(place, 0, 0, matrix, 0, half, cols, down_got)
+    if 0 == 3:
+        down = chunk(place, 0, 0, matrix, 0, half, cols, down_got, after=pieces[:1])
     def pins(a, b):
         return arrived[max(a - 2, 0):a] + arrived_right[max(b - 2, 0):b]
     for step in range(last + 1):
+        up = [add(up, up_got, pins(*JOIN_AFTER[min(step, 1)]), JOIN_WEIGHTS[min(step, 1)])]
+        if step == 0 and 0 == 2:
+            down = chunk(place, 0, 0, matrix, 0, half, cols, down_got, after=up)
         down_got = lax.ppermute(down, "prow", grow_pairs(orders, step))
-        up = [add(up, up_got, pins(*JOIN_AFTER[min(step, 1)]), JOIN_WEIGHTS[min(step, 1)])]
         up_got = [lax.ppermute(up[0], "prow", swap_pairs(n_prow, orders, step))]
         down = add([down], [down_got], [] + pins(*DOWN_AFTER[min(step, 1)]), DOWN_WEIGHTS[min(step, 1)])
     down_got = lax.ppermute(down, "prow", swap_pairs(n_prow, cores, 0))
-    swapped, token = swap(place, pivots, matrix, down, down_got, pins(0, 0))
-    up = add(up, up_got, pins(2, 1), 0)
+    swapped, token = swap(place, pivots, matrix, down, down_got, pins(3, 1))
+    up = add(up, up_got, pins(0, 0), 0)
     up_got = lax.ppermute(up, "prow", swap_pairs(n_prow, cores, 0))
     upper = upper_rows(place, unit_inverse, up, up_got, pins(3, 2))
 
-    common = (pick_source, place, matrix)
-    out = update(groups[:-1], *common, swapped, upper, received[:-1])
-    return update(groups[-1:], *common, out, upper, received[-1:])
+    out = swapped
+    for group, arrays in zip(groups, received):
+        out = update(group, pick_source, place, matrix, out, upper, arrays)
+    return out
 
 
 def solution(mesh):

time: 89.5 us -> 87 us (0.972)
  the two profiles are of different devices: /device:TPU:21 before, /device:TPU:17 now
where the time goes in v6:
time: 87 us; the launch traced here: 86.6 us
  waiting for transfers between devices  34.2 us (39%)
  Pallas kernels  30.8 us (35%)
  starting transfers between devices  20.9 us (24%)
    ppermute x10, waiting for transfers between devices, move(): return lax.ppermute(value, ('prow', 'pcol'), pairs)  26.5 us
    ppermute x10, starting transfers between devices, move(): return lax.ppermute(value, ('prow', 'pcol'), pairs)  13.7 us
    pallas_call x2, Pallas kernels, update(): pl.pallas_call(functools.partial(update_kernel, first_row, len(received),...  10.6 us
    pallas_call x1, Pallas kernels, swap(): pl.pallas_call(swap_kernel, in_specs=[SMEM, VMEM, ANY, VMEM, VMEM] + [ANY...  7.85 us
    ppermute x2, waiting for transfers between devices, per_device(): down_got = lax.ppermute(down, 'prow', grow_pairs(orders, step))  7.67 us
    pallas_call x1, Pallas kernels, pick(): pl.pallas_call(pick_kernel, in_specs=[SMEM, VMEM, ANY] + [ANY] * len(afte...  6.15 us
    pallas_call x6, Pallas kernels, chunk(): pl.pallas_call(functools.partial(chunk_kernel, first_row, axis, core), in...  4.21 us
    ppermute x2, starting transfers between devices, per_device(): down_got = lax.ppermute(down, 'prow', grow_pairs(orders, step))  2.77 us
  transfers between devices with their start and end apart: 18, of which 5 were waited for; matrix products, arithmetic and copies ran while one was open for 0% of the time, Pallas kernels for 29%

profile of v6, /device:TPU:17, one launch (start us, length us, event | category | flops | bytes accessed | tf_op | source)
XLA Modules:
  0.0 86.6 jit_solution(12810255365993462197)
XLA Ops:
  0.1 0.6 chunk.8
  0.6 0.7 collective-permute-start.2
  1.4 1.4 %chunk.6 = bf16[256,1536]{1,0:T(8,128)(2,1)} custom-call(s32[3]{0:T(128)S(1)} %pad_add_fusion.place_ref, bf16[2048,1536]{1,0:T(8,128)(2,1)} %refs_0_.3), custom_call_target="tpu_custom_call" | custom-call | tf_op jit(solution)/shard_map/chunk/pallas_call | solution.py:50
  2.8 1.3 %collective-permute-start = (bf16[256,1536]{1,0:T(8,128)(2,1)}, bf16[256,1536]{1,0:T(8,128)(2,1)S(1)}, u32[]{:S(2)}, u32[]{:S(2)}) collective-permute-start(bf16[256,1536]{1,0:T(8,128)(2,1)} %chunk.6), channel_id=1, source_target_pairs={{0,4},{1,5},{2,6},{3,7}} | collective-permute-start | bytes 2359304 | tf_op jit(solution)/shard_map/ppermute | solution.py:421
  4.2 0.1 copy.9.pivots_ref
  4.3 6.1 %pick_rows.1 = (bf16[256,1536]{1,0:T(8,128)(2,1)S(1)}, bf16[256,1536]{1,0:T(8,128)(2,1)S(1)}) custom-call(s32[3]{0:T(128)S(1)} %pad_add_fusion.place_ref, s32[512,1]{1,0:T(8,128)S(1)} %copy.9.pivots_ref, bf16[2048,1536]{1,0:T(8,128)(2,1)} %refs_0_.3), custom_call_target="tpu_custom_call" | custom-call | tf_op jit(solution)/shard_map/pick_rows/pallas_call | solution.py:100
  10.5 2.5 %collective-permute-start.8 = (bf16[256,1536]{1,0:T(8,128)(2,1)S(1)}, bf16[256,1536]{1,0:T(8,128)(2,1)S(1)}, u32[]{:S(2)}, u32[]{:S(2)}) collective-permute-start(bf16[256,1536]{1,0:T(8,128)(2,1)S(1)} %get-tuple-element.10), channel_id=1, source_target_pairs={{0,4},{4,0},{8,12},{12,8},{16,20},{20,16},{24,28},{28,24},{1,5},{5... | collective-permute-start | bytes 2359304 | tf_op jit(solution)/shard_map/ppermute | solution.py:426
  13.0 0.6 chunk.10
  13.5 1.3 %collective-permute-start.5 = (bf16[1024,512]{1,0:T(8,128)(2,1)S(1)}, bf16[1024,512]{1,0:T(8,128)(2,1)S(1)}, u32[]{:S(2)}, u32[]{:S(2)}) collective-permute-start(bf16[1024,512]{1,0:T(8,128)(2,1)S(1)} %chunk.10), channel_id=1, source_target_pairs={{4,6},{12,14},{20,22},{28,30}} | collective-permute-start | bytes 3145736 | tf_op jit(solution)/shard_map/ppermute | solution.py:354
  14.8 0.6 chunk.7.refs_0_
  15.4 1.4 %collective-permute-start.1 = (bf16[256,1536]{1,0:T(8,128)(2,1)S(1)}, bf16[256,1536]{1,0:T(8,128)(2,1)S(1)}, u32[]{:S(2)}, u32[]{:S(2)}) collective-permute-start(bf16[256,1536]{1,0:T(8,128)(2,1)S(1)} %chunk.7.refs_0_), channel_id=1, source_target_pairs={{0,8},{4,20},{1,9},{5,21},{2,10},{6,22},{3,11},{7,23}} | collective-permute-start | bytes 2359304 | tf_op jit(solution)/shard_map/ppermute | solution.py:435
  16.8 0.6 chunk.9.refs_2_.refs_1_
  17.4 0.7 collective-permute-start.6
  18.1 0.7 collective-permute-start.7
  19.1 6.6 %collective-permute-done.1.refs_1_ = bf16[256,1536]{1,0:T(8,128)(2,1)S(1)} collective-permute-done((bf16[256,1536]{1,0:T(8,128)(2,1)S(1)}, bf16[256,1536]{1,0:T(8,128)(2,1)S(1)}, u32[]{:S(2)}, u32[]{:S(2)}) %collective-permute-start.1) | collective-permute-done | bytes 786464 | tf_op jit(solution)/shard_map/ppermute | solution.py:435
  25.8 1.3 %collective-permute-start.3 = (bf16[256,1536]{1,0:T(8,128)(2,1)S(1)}, bf16[256,1536]{1,0:T(8,128)(2,1)S(1)}, u32[]{:S(2)}, u32[]{:S(2)}) collective-permute-start(bf16[256,1536]{1,0:T(8,128)(2,1)S(1)} %add.11.refs_0_), channel_id=1, source_target_pairs={{0,16},{8,24},{4,12},{20,28},{1,17},{9,25},{5,13},{21,29},{2,18},{... | collective-permute-start | bytes 2359304 | tf_op jit(solution)/shard_map/ppermute | solution.py:435
  27.2 11.0 %collective-permute-done.5.refs_0_ = bf16[1024,512]{1,0:T(8,128)(2,1)S(1)} collective-permute-done((bf16[1024,512]{1,0:T(8,128)(2,1)S(1)}, bf16[1024,512]{1,0:T(8,128)(2,1)S(1)}, u32[]{:S(2)}, u32[]{:S(2)}) %collective-permute-start.5) | collective-permute-done | bytes 1048608 | tf_op jit(solution)/shard_map/ppermute | solution.py:354
  38.1 0.6 chunk.11.rest_0_.refs_2_.refs_4_
  38.7 1.4 %collective-permute-start.12 = (bf16[1024,512]{1,0:T(8,128)(2,1)S(1)}, bf16[1024,512]{1,0:T(8,128)(2,1)S(1)}, u32[]{:S(2)}, u32[]{:S(2)}) collective-permute-start(bf16[1024,512]{1,0:T(8,128)(2,1)S(1)} %chunk.11.rest_0_.refs_2_.refs_4_), channel_id=1, source_target_pairs={{6,7},{14,15},{22,23},{30,31}} | collective-permute-start | bytes 3145736 | tf_op jit(solution)/shard_map/ppermute | solution.py:354
  40.1 1.9 %collective-permute-start.13 = (bf16[1024,512]{1,0:T(8,128)(2,1)S(1)}, bf16[1024,512]{1,0:T(8,128)(2,1)S(1)}, u32[]{:S(2)}, u32[]{:S(2)}) collective-permute-start(bf16[1024,512]{1,0:T(8,128)(2,1)S(1)} %chunk.11.rest_0_.refs_2_.refs_4_), channel_id=1, source_target_pairs={{6,5},{4,6},{14,13},{12,14},{22,21},{20,22},{30,29},{28,30}} | collective-permute-start | bytes 3145736 | tf_op jit(solution)/shard_map/ppermute | solution.py:354
  42.2 1.0 %collective-permute-done.3.refs_1_ = bf16[256,1536]{1,0:T(8,128)(2,1)S(1)} collective-permute-done((bf16[256,1536]{1,0:T(8,128)(2,1)S(1)}, bf16[256,1536]{1,0:T(8,128)(2,1)S(1)}, u32[]{:S(2)}, u32[]{:S(2)}) %collective-permute-start.3) | collective-permute-done | bytes 786464 | tf_op jit(solution)/shard_map/ppermute | solution.py:435
  43.3 0.5 collective-permute-start.4
  43.8 0.7 collective-permute-start.14
  44.5 10.4 %collective-permute-done.12.rest_3_.refs_6_ = bf16[1024,512]{1,0:T(8,128)(2,1)S(1)} collective-permute-done((bf16[1024,512]{1,0:T(8,128)(2,1)S(1)}, bf16[1024,512]{1,0:T(8,128)(2,1)S(1)}, u32[]{:S(2)}, u32[]{:S(2)}) %collective-permute-start.12) | collective-permute-done | bytes 1048608 | tf_op jit(solution)/shard_map/ppermute | solution.py:354
  54.9 0.7 collective-permute-start.15
  55.6 5.2 %collective-permute-done.13.refs_5_.refs_4_ = bf16[1024,512]{1,0:T(8,128)(2,1)S(1)} collective-permute-done((bf16[1024,512]{1,0:T(8,128)(2,1)S(1)}, bf16[1024,512]{1,0:T(8,128)(2,1)S(1)}, u32[]{:S(2)}, u32[]{:S(2)}) %collective-permute-start.13) | collective-permute-done | bytes 1048608 | tf_op jit(solution)/shard_map/ppermute | solution.py:354
  60.8 4.2 %collective-permute-start.16 = (bf16[1024,512]{1,0:T(8,128)(2,1)S(1)}, bf16[1024,512]{1,0:T(8,128)(2,1)S(1)}, u32[]{:S(2)}, u32[]{:S(2)}) collective-permute-start(bf16[1024,512]{1,0:T(8,128)(2,1)S(1)} %collective-permute-done.13.refs_5_.refs_4_), channel_id=1, source_target_pairs={{6,5},{14,13},{22,21},{30,29}} | collective-permute-start | bytes 3145736 | tf_op jit(solution)/shard_map/ppermute | solution.py:354
  65.0 1.4 %collective-permute-start.17 = (bf16[1024,512]{1,0:T(8,128)(2,1)S(1)}, bf16[1024,512]{1,0:T(8,128)(2,1)S(1)}, u32[]{:S(2)}, u32[]{:S(2)}) collective-permute-start(bf16[1024,512]{1,0:T(8,128)(2,1)S(1)} %collective-permute-done.13.refs_5_.refs_4_), channel_id=1, source_target_pairs={{6,7},{14,15},{22,23},{30,31}} | collective-permute-start | bytes 3145736 | tf_op jit(solution)/shard_map/ppermute | solution.py:354
  66.5 7.9 %swap_rows.1 = (bf16[2048,1536]{1,0:T(8,128)(2,1)}, f32[8,128]{1,0:T(8,128)}) custom-call(s32[3]{0:T(128)S(1)} %pad_add_fusion.place_ref, s32[1,512]{1,0:T(1,128)S(1)} %bitcast.5, bf16[2048,1536]{1,0:T(8,128)(2,1)} %refs_0_.3, bf16[256,1536]{1,0:T(8,128)(2,1)S(1)} %add.12.mine_ref, bf16[256,1536]{1,0:T(8,128)(2,1)S(1)} %collective-permute-done.4.other_ref, ...), custom_call_target="tpu_custom_call" | custom-call | tf_op jit(solution)/shard_map/swap_rows/pallas_call | solution.py:197
  74.4 1.6 %upper.1.upper_ref = bf16[512,1536]{1,0:T(8,128)(2,1)S(1)} custom-call(s32[3]{0:T(128)S(1)} %pad_add_fusion.place_ref, bf16[512,512]{1,0:T(8,128)(2,1)S(1)} %copy-done.1, bf16[256,1536]{1,0:T(8,128)(2,1)S(1)} %add.15.mine_ref, bf16[256,1536]{1,0:T(8,128)(2,1)S(1)} %collective-permute-done.11.other_ref, bf16[1024,512]{1,0:T(8,128)(2,1)S(1)} %chunk.11.rest_0_.refs_2_.refs_4_, ...), custom_call_target="tpu_custom_call" | custom-call | flops 2300000000 | bytes 7380000 | tf_op jit(solution)/shard_map/upper/pallas_call | solution.py:237
  76.0 5.3 %update_rows.2.swapped_ref = bf16[2048,1536]{1,0:T(8,128)(2,1)} custom-call(s32[3]{0:T(128)S(1)} %pad_add_fusion.place_ref, bf16[2048,1536]{1,0:T(8,128)(2,1)} %get-tuple-element.8.swapped_ref, bf16[512,1536]{1,0:T(8,128)(2,1)S(1)} %upper.1.upper_ref, bf16[2048,1536]{1,0:T(8,128)(2,1)} %refs_0_.3, ...), custom_call_target="tpu_custom_call", output_to_operand_aliasing={{}: (1, {})} | custom-call | tf_op jit(solution)/shard_map/update_rows/pallas_call | solution.py:313
  81.3 5.3 %update_rows.3 = bf16[2048,1536]{1,0:T(8,128)(2,1)} custom-call(s32[3]{0:T(128)S(1)} %pad_add_fusion.place_ref, bf16[2048,1536]{1,0:T(8,128)(2,1)} %update_rows.2.swapped_ref, bf16[512,1536]{1,0:T(8,128)(2,1)S(1)} %upper.1.upper_ref, bf16[2048,1536]{1,0:T(8,128)(2,1)} %refs_0_.3, ...), custom_call_target="tpu_custom_call", output_to_operand_aliasing={{}: (1, {})} | custom-call | tf_op jit(solution)/shard_map/update_rows/pallas_call | solution.py:313
  (28 shorter events, 0.8 us)
Async XLA Ops:
  0.1 4.1 %copy-start = (s32[512]{0:T(512)S(1)}, s32[512]{0:T(512)}, u32[]{:S(2)}) copy-start(s32[512]{0:T(512)} %param.4) | copy-start | bytes 6148
  0.6 16.2 %collective-permute-start.2 = (bf16[1024,512]{1,0:T(8,128)(2,1)S(1)}, bf16[1024,512]{1,0:T(8,128)(2,1)S(1)}, u32[]{:S(2)}, u32[]{:S(2)}) collective-permute-start(bf16[1024,512]{1,0:T(8,128)(2,1)S(1)} %chunk.8), channel_id=1, source_target_pairs={{0,2},{8,10},{16,18},{24,26}} | collective-permute-start | bytes 3145736 | tf_op jit(solution)/shard_map/ppermute | solution.py:354
  2.8 12.0 %collective-permute-start = (bf16[256,1536]{1,0:T(8,128)(2,1)}, bf16[256,1536]{1,0:T(8,128)(2,1)S(1)}, u32[]{:S(2)}, u32[]{:S(2)}) collective-permute-start(bf16[256,1536]{1,0:T(8,128)(2,1)} %chunk.6), channel_id=1, source_target_pairs={{0,4},{1,5},{2,6},{3,7}} | collective-permute-start | bytes 2359304 | tf_op jit(solution)/shard_map/ppermute | solution.py:421
  10.5 8.4 %collective-permute-start.8 = (bf16[256,1536]{1,0:T(8,128)(2,1)S(1)}, bf16[256,1536]{1,0:T(8,128)(2,1)S(1)}, u32[]{:S(2)}, u32[]{:S(2)}) collective-permute-start(bf16[256,1536]{1,0:T(8,128)(2,1)S(1)} %get-tuple-element.10), channel_id=1, source_target_pairs={{0,4},{4,0},{8,12},{12,8},{16,20},{20,16},{24,28},{28,24},{1,5},{5... | collective-permute-start | bytes 2359304 | tf_op jit(solution)/shard_map/ppermute | solution.py:426
  13.5 24.6 %collective-permute-start.5 = (bf16[1024,512]{1,0:T(8,128)(2,1)S(1)}, bf16[1024,512]{1,0:T(8,128)(2,1)S(1)}, u32[]{:S(2)}, u32[]{:S(2)}) collective-permute-start(bf16[1024,512]{1,0:T(8,128)(2,1)S(1)} %chunk.10), channel_id=1, source_target_pairs={{4,6},{12,14},{20,22},{28,30}} | collective-permute-start | bytes 3145736 | tf_op jit(solution)/shard_map/ppermute | solution.py:354
  15.4 10.3 %collective-permute-start.1 = (bf16[256,1536]{1,0:T(8,128)(2,1)S(1)}, bf16[256,1536]{1,0:T(8,128)(2,1)S(1)}, u32[]{:S(2)}, u32[]{:S(2)}) collective-permute-start(bf16[256,1536]{1,0:T(8,128)(2,1)S(1)} %chunk.7.refs_0_), channel_id=1, source_target_pairs={{0,8},{4,20},{1,9},{5,21},{2,10},{6,22},{3,11},{7,23}} | collective-permute-start | bytes 2359304 | tf_op jit(solution)/shard_map/ppermute | solution.py:435
  17.4 24.6 %collective-permute-start.6 = (bf16[1024,512]{1,0:T(8,128)(2,1)S(1)}, bf16[1024,512]{1,0:T(8,128)(2,1)S(1)}, u32[]{:S(2)}, u32[]{:S(2)}) collective-permute-start(bf16[1024,512]{1,0:T(8,128)(2,1)S(1)} %chunk.9.refs_2_.refs_1_), channel_id=1, source_target_pairs={{2,1},{0,2},{10,9},{8,10},{18,17},{16,18},{26,25},{24,26}} | collective-permute-start | bytes 3145736 | tf_op jit(solution)/shard_map/ppermute | solution.py:354
  18.1 23.9 %collective-permute-start.7 = (bf16[1024,512]{1,0:T(8,128)(2,1)S(1)}, bf16[1024,512]{1,0:T(8,128)(2,1)S(1)}, u32[]{:S(2)}, u32[]{:S(2)}) collective-permute-start(bf16[1024,512]{1,0:T(8,128)(2,1)S(1)} %chunk.9.refs_2_.refs_1_), channel_id=1, source_target_pairs={{2,3},{10,11},{18,19},{26,27}} | collective-permute-start | bytes 3145736 | tf_op jit(solution)/shard_map/ppermute | solution.py:354
  19.0 21.1 %collective-permute-start.9 = (bf16[256,1536]{1,0:T(8,128)(2,1)S(1)}, bf16[256,1536]{1,0:T(8,128)(2,1)S(1)}, u32[]{:S(2)}, u32[]{:S(2)}) collective-permute-start(bf16[256,1536]{1,0:T(8,128)(2,1)S(1)} %add.13.refs_0_), channel_id=1, source_target_pairs={{0,8},{4,20},{8,0},{12,28},{16,24},{20,4},{24,16},{28,12},{1,9},{5... | collective-permute-start | bytes 2359304 | tf_op jit(solution)/shard_map/ppermute | solution.py:436
  25.8 17.4 %collective-permute-start.3 = (bf16[256,1536]{1,0:T(8,128)(2,1)S(1)}, bf16[256,1536]{1,0:T(8,128)(2,1)S(1)}, u32[]{:S(2)}, u32[]{:S(2)}) collective-permute-start(bf16[256,1536]{1,0:T(8,128)(2,1)S(1)} %add.11.refs_0_), channel_id=1, source_target_pairs={{0,16},{8,24},{4,12},{20,28},{1,17},{9,25},{5,13},{21,29},{2,18},{... | collective-permute-start | bytes 2359304 | tf_op jit(solution)/shard_map/ppermute | solution.py:435
  38.7 16.2 %collective-permute-start.12 = (bf16[1024,512]{1,0:T(8,128)(2,1)S(1)}, bf16[1024,512]{1,0:T(8,128)(2,1)S(1)}, u32[]{:S(2)}, u32[]{:S(2)}) collective-permute-start(bf16[1024,512]{1,0:T(8,128)(2,1)S(1)} %chunk.11.rest_0_.refs_2_.refs_4_), channel_id=1, source_target_pairs={{6,7},{14,15},{22,23},{30,31}} | collective-permute-start | bytes 3145736 | tf_op jit(solution)/shard_map/ppermute | solution.py:354
  40.1 20.7 %collective-permute-start.13 = (bf16[1024,512]{1,0:T(8,128)(2,1)S(1)}, bf16[1024,512]{1,0:T(8,128)(2,1)S(1)}, u32[]{:S(2)}, u32[]{:S(2)}) collective-permute-start(bf16[1024,512]{1,0:T(8,128)(2,1)S(1)} %chunk.11.rest_0_.refs_2_.refs_4_), channel_id=1, source_target_pairs={{6,5},{4,6},{14,13},{12,14},{22,21},{20,22},{30,29},{28,30}} | collective-permute-start | bytes 3145736 | tf_op jit(solution)/shard_map/ppermute | solution.py:354
  42.1 22.9 %collective-permute-start.10 = (bf16[256,1536]{1,0:T(8,128)(2,1)S(1)}, bf16[256,1536]{1,0:T(8,128)(2,1)S(1)}, u32[]{:S(2)}, u32[]{:S(2)}) collective-permute-start(bf16[256,1536]{1,0:T(8,128)(2,1)S(1)} %add.14.refs_0_), channel_id=1, source_target_pairs={{0,16},{4,12},{8,24},{12,4},{16,0},{20,28},{24,8},{28,20},{1,17},{... | collective-permute-start | bytes 2359304 | tf_op jit(solution)/shard_map/ppermute | solution.py:436
  43.3 31.1 %copy-start.1 = (bf16[512,512]{1,0:T(8,128)(2,1)S(1)}, bf16[512,512]{1,0:T(8,128)(2,1)}, u32[]{:S(2)}) copy-start(bf16[512,512]{1,0:T(8,128)(2,1)} %inverse_ref.1) | copy-start | bytes 1572868
  43.3 23.1 %collective-permute-start.4 = (bf16[256,1536]{1,0:T(8,128)(2,1)S(1)}, bf16[256,1536]{1,0:T(8,128)(2,1)S(1)}, u32[]{:S(2)}, u32[]{:S(2)}) collective-permute-start(bf16[256,1536]{1,0:T(8,128)(2,1)S(1)} %add.12.mine_ref), channel_id=1, source_target_pairs={{0,4},{4,0},{8,12},{12,8},{16,20},{20,16},{24,28},{28,24},{1,5},{5... | collective-permute-start | bytes 2359304 | tf_op jit(solution)/shard_map/ppermute | solution.py:438
  43.8 37.5 %collective-permute-start.14 = (bf16[1024,512]{1,0:T(8,128)(2,1)S(1)}, bf16[1024,512]{1,0:T(8,128)(2,1)S(1)}, u32[]{:S(2)}, u32[]{:S(2)}) collective-permute-start(bf16[1024,512]{1,0:T(8,128)(2,1)S(1)} %collective-permute-done.6.rest_1_.refs_3_.refs_2_.refs_1_), channel_id=1, source_target_pairs={{2,1},{10,9},{18,17},{26,25}} | collective-permute-start | bytes 3145736 | tf_op jit(solution)/shard_map/ppermute | solution.py:354
  54.9 26.4 %collective-permute-start.15 = (bf16[1024,512]{1,0:T(8,128)(2,1)S(1)}, bf16[1024,512]{1,0:T(8,128)(2,1)S(1)}, u32[]{:S(2)}, u32[]{:S(2)}) collective-permute-start(bf16[1024,512]{1,0:T(8,128)(2,1)S(1)} %collective-permute-done.6.rest_1_.refs_3_.refs_2_.refs_1_), channel_id=1, source_target_pairs={{2,3},{10,11},{18,19},{26,27}} | collective-permute-start | bytes 3145736 | tf_op jit(solution)/shard_map/ppermute | solution.py:354
  60.8 20.5 %collective-permute-start.16 = (bf16[1024,512]{1,0:T(8,128)(2,1)S(1)}, bf16[1024,512]{1,0:T(8,128)(2,1)S(1)}, u32[]{:S(2)}, u32[]{:S(2)}) collective-permute-start(bf16[1024,512]{1,0:T(8,128)(2,1)S(1)} %collective-permute-done.13.refs_5_.refs_4_), channel_id=1, source_target_pairs={{6,5},{14,13},{22,21},{30,29}} | collective-permute-start | bytes 3145736 | tf_op jit(solution)/shard_map/ppermute | solution.py:354
  65.0 16.3 %collective-permute-start.17 = (bf16[1024,512]{1,0:T(8,128)(2,1)S(1)}, bf16[1024,512]{1,0:T(8,128)(2,1)S(1)}, u32[]{:S(2)}, u32[]{:S(2)}) collective-permute-start(bf16[1024,512]{1,0:T(8,128)(2,1)S(1)} %collective-permute-done.13.refs_5_.refs_4_), channel_id=1, source_target_pairs={{6,7},{14,15},{22,23},{30,31}} | collective-permute-start | bytes 3145736 | tf_op jit(solution)/shard_map/ppermute | solution.py:354
  66.5 7.9 %collective-permute-start.11 = (bf16[256,1536]{1,0:T(8,128)(2,1)S(1)}, bf16[256,1536]{1,0:T(8,128)(2,1)S(1)}, u32[]{:S(2)}, u32[]{:S(2)}) collective-permute-start(bf16[256,1536]{1,0:T(8,128)(2,1)S(1)} %add.15.mine_ref), channel_id=1, source_target_pairs={{0,4},{4,0},{8,12},{12,8},{16,20},{20,16},{24,28},{28,24},{1,5},{5... | collective-permute-start | bytes 2359304 | tf_op jit(solution)/shard_map/ppermute | solution.py:441

commit v7 on v6

v7 whole, which is shorter than its diff:
```python
import functools

import jax
import jax.numpy as jnp
from jax import lax
from jax.experimental import pallas as pl
from jax.experimental.pallas import tpu as pltpu
from jax.sharding import PartitionSpec as P

GROUPS = 2
CHUNK_WEIGHTS = (0, 5)
JOIN_WEIGHTS, JOIN_AFTER = (0, 5), ((1, 0), (2, 1))
DOWN_WEIGHTS, DOWN_AFTER = (0, 2), ((0, 0), (0, 0))
PIECES = 2
BLOCK = 256
F32, BF16 = jnp.float32, jnp.bfloat16
VMEM = pl.BlockSpec(memory_space=pltpu.VMEM)
ANY = pl.BlockSpec(memory_space=pl.ANY)
SMEM = pl.BlockSpec(memory_space=pltpu.SMEM)
SMALL = pltpu.CompilerParams(vmem_limit_bytes=8 * 2**20)
LARGE = pltpu.CompilerParams(vmem_limit_bytes=28 * 2**20)


FREE = pl.CostEstimate(flops=0, bytes_accessed=0, transcendentals=0)
def weight_of(x):
    x = float(x)
    return pl.CostEstimate(flops=int(x*1.15e9), bytes_accessed=int(x*3.69e6), transcendentals=0)


def chunk_kernel(first_row, axis, core, place_ref, matrix_ref, *refs):
    out_ref, sem = refs[-2:]
    rows, width = out_ref.shape

    @pl.when((place_ref[axis] == 0) & (place_ref[2] == core))
    def _():
        copy = pltpu.make_async_copy(
            matrix_ref.at[pl.ds(first_row, rows), pl.ds(0, width)], out_ref, sem
        )
        copy.start()
        copy.wait()


def chunk(place, axis, core, matrix, first_row, rows, width, held=None, weight=0, after=()):
    in_specs, operands = [SMEM, ANY], [place, matrix]
    if held is not None:
        in_specs.append(VMEM)
        operands.append(held)
    in_specs += [ANY] * len(after)
    operands += after
    return pl.pallas_call(
        functools.partial(chunk_kernel, first_row, axis, core),
        in_specs=in_specs,
        out_specs=VMEM,
        out_shape=jax.ShapeDtypeStruct((rows, width), BF16),
        scratch_shapes=[pltpu.SemaphoreType.DMA],
        input_output_aliases={} if held is None else {2: 0},
        compiler_params=SMALL,
        cost_estimate=weight_of(weight),
        name="chunk",
    )(*operands)


def columns(number, block):
    return pl.ds(pl.multiple_of(number * block, block), block)


def pick_kernel(place_ref, pivots_ref, matrix_ref, *refs):
    whole_ref, onehot_ref, sem = refs[-3:]
    outs = refs[-3 - PIECES : -3]
    rows, cols = whole_ref.shape
    width = pivots_ref.shape[0]
    block = min(BLOCK, cols)
    count = width // PIECES

    def fetch(number):
        here = columns(number, block)
        return pltpu.make_async_copy(
            matrix_ref.at[:, here], whole_ref.at[:, here], sem.at[number]
        )

    for number in range(cols // block):
        fetch(number).start()
    row = lax.broadcasted_iota(jnp.int32, (width, rows), 1) + place_ref[0] * rows
    onehot_ref[...] = jnp.where(pivots_ref[...] == row, 1.0, 0.0).astype(BF16)

    @pl.loop(0, cols // block)
    def _(number):
        fetch(number).wait()
        here = columns(number, block)
        picked = jnp.dot(onehot_ref[...], whole_ref[:, here], preferred_element_type=F32)
        picked = picked.astype(BF16)
        for piece, out_ref in enumerate(outs):
            out_ref[:, here] = picked[piece * count : (piece + 1) * count]


def pick(place, pivots, matrix, after=()):
    rows, cols = matrix.shape
    width = pivots.shape[0]
    block = min(BLOCK, cols)
    return pl.pallas_call(
        pick_kernel,
        in_specs=[SMEM, VMEM, ANY] + [ANY] * len(after),
        out_specs=[VMEM] * PIECES,
        out_shape=[jax.ShapeDtypeStruct((width // PIECES, cols), BF16)] * PIECES,
        scratch_shapes=[
            pltpu.VMEM((rows, cols), BF16),
            pltpu.VMEM((width, rows), BF16),
            pltpu.SemaphoreType.DMA((cols // block,)),
        ],
        compiler_params=LARGE,
        cost_estimate=weight_of(0),
        name="pick_rows",
    )(place, pivots[:, None], matrix, *after)


def add_kernel(count, *refs):
    start = 0
    out_ref = refs[-1]
    for own_ref, got_ref in zip(refs[:count], refs[count : 2 * count]):
        rows = own_ref.shape[0]
        out_ref[start : start + rows] = own_ref[...] + got_ref[...]
        start += rows


def add(own, got, after=(), weight=0):
    rows, cols = sum(x.shape[0] for x in own), own[0].shape[1]
    return pl.pallas_call(
        functools.partial(add_kernel, len(own)),
        in_specs=[VMEM] * (2 * len(own)) + [ANY] * len(after),
        out_specs=VMEM,
        out_shape=jax.ShapeDtypeStruct((rows, cols), BF16),
        compiler_params=SMALL,
        cost_estimate=weight_of(weight),
        name="add",
    )(*own, *got, *after)


def in_order(core, mine, other, out_ref):
    half = mine.shape[0]
    out_ref[pl.ds(pl.multiple_of(core * half, half), half)] = mine
    out_ref[pl.ds(pl.multiple_of((1 - core) * half, half), half)] = other


def update_kernel(first_row, per_group, pick_source, make_upper, place_ref, pivots_ref,
                  matrix_ref, down_ref, down_got_ref, *refs):
    if make_upper:
        inverse_ref, up_ref, up_got_ref = refs[:3]
        sources = refs[3 : 4 + per_group]
        out_ref, upper_ref = refs[-10:-8]
    else:
        upper_ref = refs[0]
        sources = refs[1 : 2 + per_group]
        out_ref = refs[-9]
    rows_ref, left_ref, right_ref, keep_ref, pivot_rows_ref, in_sem, out_sem, sem = refs[-8:]
    count, cols = rows_ref.shape
    width = left_ref.shape[1] // 2
    row_place, col_place, core, rows = (place_ref[i] for i in range(4))
    block = min(BLOCK, cols)
    piece = min(count, 512)
    here = pl.ds(first_row, count)

    def fetch_panel(action):
        views = [sources[0].at[here, pl.ds(0, width)], *sources[1:]]
        panel_ref = left_ref.at[pl.ds(0, count), pl.ds(width, width)]
        for choice, view in enumerate(views):
            @pl.when(pick_source(col_place, core) == choice)
            def _():
                action(pltpu.make_async_copy(view, panel_ref, sem))

    def fetch(number):
        there = columns(number, block)
        return pltpu.make_async_copy(
            matrix_ref.at[here, there], rows_ref.at[:, there], in_sem.at[number]
        )

    def store(number):
        there = columns(number, block)
        return pltpu.make_async_copy(
            rows_ref.at[:, there], out_ref.at[here, there], out_sem.at[number]
        )

    fetch_panel(lambda copy: copy.start())
    for number in range(cols // block):
        fetch(number).start()
    for start in range(0, count, piece):
        these = slice(start, start + piece)
        row = lax.broadcasted_iota(jnp.int32, (piece, width), 0)
        row = row + (row_place * rows + first_row + start)
        onehot = jnp.where(pivots_ref[...] == row, 1.0, 0.0)
        left_ref[these, :width] = onehot.astype(BF16)
        has_pivot = jnp.max(onehot, axis=1, keepdims=True)
        keep_ref[these] = jnp.broadcast_to(1.0 - has_pivot, (piece, 128))
    fetch_panel(lambda copy: copy.wait())

    @pl.loop(0, cols // block)
    def _(number):
        there = columns(number, block)
        if make_upper:
            in_order(core, up_ref[:, there], up_got_ref[:, there], pivot_rows_ref)
            upper_ref[:, there] = jnp.dot(
                inverse_ref[...], pivot_rows_ref[...], preferred_element_type=F32
            ).astype(BF16)
        fetch(number).wait()

        @pl.when((col_place > 0) | (number * block >= width))
        def _():
            in_order(core, down_ref[:, there], down_got_ref[:, there], right_ref)
            upper = upper_ref[:, there]
            right_ref[width:] = -upper
            right = right_ref[...]
            for start in range(0, count, piece):
                these = slice(start, start + piece)
                change = jnp.dot(left_ref[these], right, preferred_element_type=F32)
                keep = jnp.concatenate([keep_ref[these]] * (block // 128), axis=1)
                kept = rows_ref[these, there].astype(F32) * keep
                rows_ref[these, there] = (kept + change).astype(BF16)
            if first_row < width:
                @pl.when(row_place == 0)
                def _():
                    rows_ref[: width - first_row, there] = upper[first_row:]

        store(number).start()

    for number in range(cols // block):
        store(number).wait()


def update(group, pick_source, place, pivots, matrix, down, down_got, received,
           upper_terms=None, upper=None, out=None):
    first_row, count = group
    rows, cols = matrix.shape
    width = pivots.shape[0]
    make_upper = upper is None
    block = min(BLOCK, cols)
    operands = [place, pivots[None, :], matrix, down, down_got]
    in_specs = [SMEM, VMEM, ANY, VMEM, VMEM]
    terms = list(upper_terms) if make_upper else [upper]
    operands += terms + [matrix] + received
    in_specs += [VMEM] * len(terms) + [ANY] * (1 + len(received))
    hbm = pl.BlockSpec(memory_space=pltpu.HBM)
    aliases = {}
    if out is not None:
        aliases = {len(operands): 0}
        operands.append(out)
        in_specs.append(hbm)
    out_shape = [jax.ShapeDtypeStruct((rows, cols), BF16)]
    if make_upper:
        out_shape.append(jax.ShapeDtypeStruct((width, cols), BF16))
    return pl.pallas_call(
        functools.partial(update_kernel, first_row, len(received), pick_source, make_upper),
        in_specs=in_specs,
        out_specs=[hbm, VMEM][: len(out_shape)],
        out_shape=out_shape,
        scratch_shapes=[
            pltpu.VMEM((count, cols), BF16),
            pltpu.VMEM((count, 2 * width), BF16),
            pltpu.VMEM((2 * width, block), BF16),
            pltpu.VMEM((count, 128), F32),
            pltpu.VMEM((width, block), BF16),
            pltpu.SemaphoreType.DMA((cols // block,)),
            pltpu.SemaphoreType.DMA((cols // block,)),
            pltpu.SemaphoreType.DMA,
        ],
        input_output_aliases=aliases,
        compiler_params=LARGE,
        cost_estimate=weight_of(0),
        name="update_rows",
    )(*operands)


def swap_pairs(size, orders, step):
    return [(i, i ^ (1 << orders[i & 1][step])) for i in range(size)]


def grow_pairs(orders, step):
    pairs = []
    for core, order in enumerate(orders):
        places = [core]
        for bit in order[:step]:
            places += [i | (1 << bit) for i in places]
        pairs += [(i, i | (1 << order[step])) for i in places]
    return pairs


def move(value, pairs, core, n_prow, size):
    pairs = [(row * size + a, row * size + b) for row in range(core, n_prow, 2) for a, b in pairs]
    return lax.ppermute(value, ("prow", "pcol"), pairs)


def send(place, matrix, width, groups, core, n_prow, size):
    middle = size // 2
    held = []
    for number, group in enumerate(groups):
        last = held[-1] if held else None
        sent = chunk(place, 1, core, matrix, *group, width, last, CHUNK_WEIGHTS[number])
        if held:
            held[-1] = sent
        pairs = [(0, middle)] + [(middle, middle - 1)] * bool(held[:1])
        held.append(move(sent, pairs, core, n_prow, size))
    return held


def pass_on(place, held, rights, core, n_prow, size):
    middle = size // 2
    last = move(held[-1], [(middle, middle - 1)], core, n_prow, size)
    received = []
    for number, value in enumerate(held):
        left = held[number + 1] if number + 1 < len(held) else last
        right = rights[number] if number < len(rights) else None
        if right is None:
            right = move(value, [(middle, middle + 1)], core, n_prow, size)
        arrays = [value, left, right]
        both = jnp.where(place[1] < middle, left, right) if size > 4 else None
        distance = 1
        while middle - distance > 1 or middle + distance + 1 < size:
            pairs = []
            if middle - distance > 1:
                pairs.append((middle - distance, middle - distance - 1))
            if middle + distance + 1 < size:
                pairs.append((middle + distance, middle + distance + 1))
            both = move(both, pairs, core, n_prow, size)
            arrays.append(both)
            distance += 1
        received.append(arrays)
    return received


def source_of(size, per_core):
    middle = size // 2

    def pick_source(place, core):
        away = jnp.abs(place - middle)
        number = jnp.where(away == 0, 1, jnp.where(place < middle, 2, 3))
        number = jnp.where(away >= 2, away + 2, number)
        return jnp.where(place == 0, 0, number + core * per_core)

    return pick_source


def per_device(n_prow, n_pcol, matrix, pivots, unit_inverse):
    rows, cols = matrix.shape
    width = unit_inverse.shape[0]
    half = width // 2
    row_place = lax.axis_index("prow")
    col_place = lax.axis_index("pcol")
    core = row_place & 1
    place = jnp.stack([row_place, col_place, core, jnp.full_like(core, rows)]).astype(jnp.int32)
    matrix = pltpu.with_memory_space_constraint(matrix, pltpu.HBM)
    bits = list(range(1, n_prow.bit_length() - 1))
    orders = (bits, bits[::-1])
    cores = ([0], [0])
    last = len(bits) - 1

    size = rows // GROUPS
    groups = [(number * size, size) for number in range(GROUPS)]
    held = [send(place, matrix, width, groups, c, n_prow, n_pcol) for c in range(2)]
    arrived = [x for pair in zip(*held) for x in pair]
    middle = n_pcol // 2
    rights = [
        [move(x, [(middle, middle + 1)], c, n_prow, n_pcol) for x in held[c][: GROUPS - c]]
        for c in range(2)
    ]
    arrived_right = [rights[0][0], rights[1][0]] + rights[0][1:]

    order = jnp.where(core == 0, pivots, jnp.roll(pivots, half))
    down_got = lax.ppermute(chunk(place, 0, 0, matrix, half, half, cols), "prow", [(0, 1)])
    down = chunk(place, 0, 0, matrix, 0, half, cols, down_got)
    pieces = pick(place, order, matrix, [down])
    up, sent = pieces[: PIECES // 2], pieces[PIECES // 2 :]
    up_got = [lax.ppermute(x, "prow", swap_pairs(n_prow, cores, 0)) for x in sent]
    def pins(a, b):
        return arrived[max(a - 2, 0):a] + arrived_right[max(b - 2, 0):b]
    for step in range(last + 1):
        up = [add(up, up_got, pins(*JOIN_AFTER[min(step, 1)]), JOIN_WEIGHTS[min(step, 1)])]
        down_got = lax.ppermute(down, "prow", grow_pairs(orders, step))
        up_got = [lax.ppermute(up[0], "prow", swap_pairs(n_prow, orders, step))]
        down = add([down], [down_got], up + pins(*DOWN_AFTER[min(step, 1)]), DOWN_WEIGHTS[min(step, 1)])
    down_got = lax.ppermute(down, "prow", swap_pairs(n_prow, cores, 0))
    up = add(up, up_got, pins(0, 0), 0)
    up_got = lax.ppermute(up, "prow", swap_pairs(n_prow, cores, 0))

    by_core = [pass_on(place, held[c], rights[c], c, n_prow, n_pcol) for c in range(2)]
    received = [first + second for first, second in zip(*by_core)]
    common = (source_of(n_pcol, len(by_core[0][0])), place, pivots, matrix, down, down_got)
    out, upper = update(groups[0], *common, received[0], upper_terms=(unit_inverse, up, up_got))
    for group, arrays in zip(groups[1:], received[1:]):
        (out,) = update(group, *common, arrays, upper=upper, out=out)
    return out


def solution(mesh):
    return jax.shard_map(
        functools.partial(per_device, mesh.shape["prow"], mesh.shape["pcol"]),
        mesh=mesh,
        in_specs=(P("prow", "pcol"), P(), P()),
        out_specs=P("prow", "pcol"),
        check_vma=False,
    )
```

time: 87 us -> 94.9 us (1.091)
  the two profiles are of different devices: /device:TPU:17 before, /device:TPU:13 now
where the time goes in v7:
time: 94.9 us; the launch traced here: 94.4 us
  waiting for transfers between devices  44.9 us (47%)
  Pallas kernels  29.2 us (31%)
  starting transfers between devices  19.7 us (21%)
    ppermute x10, waiting for transfers between devices, move(): return lax.ppermute(value, ('prow', 'pcol'), pairs)  31.5 us
    pallas_call x2, Pallas kernels, update(): pl.pallas_call(functools.partial(update_kernel, first_row, len(received),...  16.3 us
    ppermute x2, waiting for transfers between devices, per_device(): up_got = [lax.ppermute(up[0], 'prow', swap_pairs(n_prow, orders, step))]  9.87 us
    ppermute x10, starting transfers between devices, move(): return lax.ppermute(value, ('prow', 'pcol'), pairs)  8.37 us
    pallas_call x6, Pallas kernels, chunk(): pl.pallas_call(functools.partial(chunk_kernel, first_row, axis, core), in...  6.22 us
    pallas_call x1, Pallas kernels, pick(): pl.pallas_call(pick_kernel, in_specs=[SMEM, VMEM, ANY] + [ANY] * len(afte...  6.15 us
    ppermute x2, starting transfers between devices, per_device(): up_got = [lax.ppermute(up[0], 'prow', swap_pairs(n_prow, orders, step))]  3.59 us
    ppermute x1, starting transfers between devices, per_device(): down_got = lax.ppermute(down, 'prow', swap_pairs(n_prow, cores, 0))  2.9 us
  transfers between devices with their start and end apart: 18, of which 6 were waited for; matrix products, arithmetic and copies ran while one was open for 0% of the time, Pallas kernels for 21%

profile of v7, /device:TPU:13, one launch (start us, length us, event | category | flops | bytes accessed | tf_op | source)
XLA Modules:
  0.0 94.4 jit_solution(2020052770185965421)
XLA Ops:
  0.1 1.5 %chunk.8 = bf16[1024,512]{1,0:T(8,128)(2,1)} custom-call(s32[4]{0:T(128)S(1)} %pad_add_fusion.place_ref, bf16[2048,1536]{1,0:T(8,128)(2,1)} %refs_1_.1), custom_call_target="tpu_custom_call" | custom-call | tf_op jit(solution)/shard_map/chunk/pallas_call | solution.py:50
  1.6 0.7 collective-permute-start.3
  2.4 1.5 %chunk.6 = bf16[256,1536]{1,0:T(8,128)(2,1)} custom-call(s32[4]{0:T(128)S(1)} %pad_add_fusion.place_ref, bf16[2048,1536]{1,0:T(8,128)(2,1)} %refs_1_.1), custom_call_target="tpu_custom_call" | custom-call | tf_op jit(solution)/shard_map/chunk/pallas_call | solution.py:50
  3.8 0.7 collective-permute-start
  4.6 1.6 %chunk.10 = bf16[1024,512]{1,0:T(8,128)(2,1)} custom-call(s32[4]{0:T(128)S(1)} %pad_add_fusion.place_ref, bf16[2048,1536]{1,0:T(8,128)(2,1)} %refs_1_.1), custom_call_target="tpu_custom_call" | custom-call | tf_op jit(solution)/shard_map/chunk/pallas_call | solution.py:50
  6.1 0.7 collective-permute-start.6
  7.1 0.6 chunk.7.refs_0_
  7.6 1.3 %collective-permute-start.1 = (bf16[256,1536]{1,0:T(8,128)(2,1)S(1)}, bf16[256,1536]{1,0:T(8,128)(2,1)S(1)}, u32[]{:S(2)}, u32[]{:S(2)}) collective-permute-start(bf16[256,1536]{1,0:T(8,128)(2,1)S(1)} %chunk.7.refs_0_), channel_id=1, source_target_pairs={{0,8},{4,20},{1,9},{5,21},{2,10},{6,22},{3,11},{7,23}} | collective-permute-start | bytes 2359304 | tf_op jit(solution)/shard_map/ppermute | solution.py:375
  8.9 6.1 %pick_rows.1 = (bf16[256,1536]{1,0:T(8,128)(2,1)S(1)}, bf16[256,1536]{1,0:T(8,128)(2,1)S(1)}) custom-call(s32[4]{0:T(128)S(1)} %pad_add_fusion.place_ref, s32[512,1]{1,0:T(8,128)S(1)} %copy.8.pivots_ref, bf16[2048,1536]{1,0:T(8,128)(2,1)} %refs_1_.1, bf16[256,1536]{1,0:T(8,128)(2,1)S(1)} %chunk.7.refs_0_), custom_call_target="tpu_custom_call" | custom-call | tf_op jit(solution)/shard_map/pick_rows/pallas_call | solution.py:100
  15.1 0.2 collective-permute-start.2
  15.2 0.6 chunk.9.refs_2_.refs_4_
  15.8 0.7 collective-permute-start.7
  16.5 0.9 collective-permute-done.2.refs_1_
  17.5 3.5 %collective-permute-start.5 = (bf16[256,1536]{1,0:T(8,128)(2,1)S(1)}, bf16[256,1536]{1,0:T(8,128)(2,1)S(1)}, u32[]{:S(2)}, u32[]{:S(2)}) collective-permute-start(bf16[256,1536]{1,0:T(8,128)(2,1)S(1)} %add.13.refs_2_.refs_0_), channel_id=1, source_target_pairs={{0,8},{4,20},{8,0},{12,28},{16,24},{20,4},{24,16},{28,12},{1,9},{5... | collective-permute-start | bytes 2359304 | tf_op jit(solution)/shard_map/ppermute | solution.py:376
  21.0 0.7 collective-permute-start.11
  21.9 1.3 %collective-permute-start.4 = (bf16[256,1536]{1,0:T(8,128)(2,1)S(1)}, bf16[256,1536]{1,0:T(8,128)(2,1)S(1)}, u32[]{:S(2)}, u32[]{:S(2)}) collective-permute-start(bf16[256,1536]{1,0:T(8,128)(2,1)S(1)} %add.14.refs_0_), channel_id=1, source_target_pairs={{0,16},{8,24},{4,12},{20,28},{1,17},{9,25},{5,13},{21,29},{2,18},{... | collective-permute-start | bytes 2359304 | tf_op jit(solution)/shard_map/ppermute | solution.py:375
  23.2 0.6 chunk.11.refs_3_.refs_7_
  23.8 0.7 collective-permute-start.13
  24.6 1.3 %collective-permute-start.12 = (bf16[1024,512]{1,0:T(8,128)(2,1)S(1)}, bf16[1024,512]{1,0:T(8,128)(2,1)S(1)}, u32[]{:S(2)}, u32[]{:S(2)}) collective-permute-start(bf16[1024,512]{1,0:T(8,128)(2,1)S(1)} %chunk.11.refs_3_.refs_7_), channel_id=1, source_target_pairs={{4,6},{6,5},{12,14},{14,13},{20,22},{22,21},{28,30},{30,29}} | collective-permute-start | bytes 3145736 | tf_op jit(solution)/shard_map/ppermute | solution.py:287
  25.9 9.9 %collective-permute-done.5.refs_1_ = bf16[256,1536]{1,0:T(8,128)(2,1)S(1)} collective-permute-done((bf16[256,1536]{1,0:T(8,128)(2,1)S(1)}, bf16[256,1536]{1,0:T(8,128)(2,1)S(1)}, u32[]{:S(2)}, u32[]{:S(2)}) %collective-permute-start.5) | collective-permute-done | bytes 786464 | tf_op jit(solution)/shard_map/ppermute | solution.py:376
  35.9 0.8 collective-permute-done.4.refs_1_
  36.8 2.9 %collective-permute-start.8 = (bf16[256,1536]{1,0:T(8,128)(2,1)S(1)}, bf16[256,1536]{1,0:T(8,128)(2,1)S(1)}, u32[]{:S(2)}, u32[]{:S(2)}) collective-permute-start(bf16[256,1536]{1,0:T(8,128)(2,1)S(1)} %add.16.down_ref), channel_id=1, source_target_pairs={{0,4},{4,0},{8,12},{12,8},{16,20},{20,16},{24,28},{28,24},{1,5},{5... | collective-permute-start | bytes 2359304 | tf_op jit(solution)/shard_map/ppermute | solution.py:378
  39.7 0.7 collective-permute-start.15
  40.5 0.7 collective-permute-start.14
  41.2 17.1 %collective-permute-done.12.refs_8_.refs_5_ = bf16[1024,512]{1,0:T(8,128)(2,1)S(1)} collective-permute-done((bf16[1024,512]{1,0:T(8,128)(2,1)S(1)}, bf16[1024,512]{1,0:T(8,128)(2,1)S(1)}, u32[]{:S(2)}, u32[]{:S(2)}) %collective-permute-start.12) | collective-permute-done | bytes 1048608 | tf_op jit(solution)/shard_map/ppermute | solution.py:287
  58.3 0.7 collective-permute-start.17
  59.0 1.3 %collective-permute-start.16 = (bf16[1024,512]{1,0:T(8,128)(2,1)S(1)}, bf16[1024,512]{1,0:T(8,128)(2,1)S(1)}, u32[]{:S(2)}, u32[]{:S(2)}) collective-permute-start(bf16[1024,512]{1,0:T(8,128)(2,1)S(1)} %collective-permute-done.12.refs_8_.refs_5_), channel_id=1, source_target_pairs={{6,5},{14,13},{22,21},{30,29}} | collective-permute-start | bytes 3145736 | tf_op jit(solution)/shard_map/ppermute | solution.py:287
  60.4 1.3 %collective-permute-start.10 = (bf16[256,1536]{1,0:T(8,128)(2,1)S(1)}, bf16[256,1536]{1,0:T(8,128)(2,1)S(1)}, u32[]{:S(2)}, u32[]{:S(2)}) collective-permute-start(bf16[256,1536]{1,0:T(8,128)(2,1)S(1)} %add.17.refs_1_), channel_id=1, source_target_pairs={{0,4},{4,0},{8,12},{12,8},{16,20},{20,16},{24,28},{28,24},{1,5},{5... | collective-permute-start | bytes 2359304 | tf_op jit(solution)/shard_map/ppermute | solution.py:380
  61.7 1.9 %collective-permute-done.10.refs_2_ = bf16[256,1536]{1,0:T(8,128)(2,1)S(1)} collective-permute-done((bf16[256,1536]{1,0:T(8,128)(2,1)S(1)}, bf16[256,1536]{1,0:T(8,128)(2,1)S(1)}, u32[]{:S(2)}, u32[]{:S(2)}) %collective-permute-start.10) | collective-permute-done | bytes 786464 | tf_op jit(solution)/shard_map/ppermute | solution.py:380
  63.7 8.9 %update_rows.2 = (bf16[2048,1536]{1,0:T(8,128)(2,1)}, bf16[512,1536]{1,0:T(8,128)(2,1)S(1)}) custom-call(s32[4]{0:T(128)S(1)} %pad_add_fusion.place_ref, s32[1,512]{1,0:T(1,128)S(1)} %bitcast.5, bf16[2048,1536]{1,0:T(8,128)(2,1)} %refs_1_.1, bf16[256,1536]{1,0:T(8,128)(2,1)S(1)} %add.16.down_ref, bf16[256,1536]{1,0:T(8,128)(2,1)S(1)} %collective-permute-done.8.down_got_ref, ...), custom_call_target="tpu_custom_call" | custom-call | tf_op jit(solution)/shard_map/update_rows/pallas_call | solution.py:249
  72.6 14.4 %collective-permute-done.16.refs_6_ = bf16[1024,512]{1,0:T(8,128)(2,1)S(1)} collective-permute-done((bf16[1024,512]{1,0:T(8,128)(2,1)S(1)}, bf16[1024,512]{1,0:T(8,128)(2,1)S(1)}, u32[]{:S(2)}, u32[]{:S(2)}) %collective-permute-start.16) | collective-permute-done | bytes 1048608 | tf_op jit(solution)/shard_map/ppermute | solution.py:287
  87.0 7.4 %update_rows.3 = bf16[2048,1536]{1,0:T(8,128)(2,1)} custom-call(s32[4]{0:T(128)S(1)} %pad_add_fusion.place_ref, s32[1,512]{1,0:T(1,128)S(1)} %bitcast.6, bf16[2048,1536]{1,0:T(8,128)(2,1)} %refs_1_.1, bf16[256,1536]{1,0:T(8,128)(2,1)S(1)} %add.16.down_ref, ...), custom_call_target="tpu_custom_call", output_to_operand_aliasing={{}: (13, {})} | custom-call | tf_op jit(solution)/shard_map/update_rows/pallas_call | solution.py:249
  (26 shorter events, 0.8 us)
Async XLA Ops:
  1.6 5.2 %copy-start.1 = (s32[512]{0:T(512)S(1)}, s32[512]{0:T(512)}, u32[]{:S(2)}) copy-start(s32[512]{0:T(512)} %param.4) | copy-start | bytes 6148
  1.6 13.6 %collective-permute-start.3 = (bf16[1024,512]{1,0:T(8,128)(2,1)}, bf16[1024,512]{1,0:T(8,128)(2,1)S(1)}, u32[]{:S(2)}, u32[]{:S(2)}) collective-permute-start(bf16[1024,512]{1,0:T(8,128)(2,1)} %chunk.8), channel_id=1, source_target_pairs={{0,2},{8,10},{16,18},{24,26}} | collective-permute-start | bytes 3145736 | tf_op jit(solution)/shard_map/ppermute | solution.py:287
  3.8 3.2 %collective-permute-start = (bf16[256,1536]{1,0:T(8,128)(2,1)}, bf16[256,1536]{1,0:T(8,128)(2,1)S(1)}, u32[]{:S(2)}, u32[]{:S(2)}) collective-permute-start(bf16[256,1536]{1,0:T(8,128)(2,1)} %chunk.6), channel_id=1, source_target_pairs={{0,4},{1,5},{2,6},{3,7}} | collective-permute-start | bytes 2359304 | tf_op jit(solution)/shard_map/ppermute | solution.py:366
  6.1 17.1 %collective-permute-start.6 = (bf16[1024,512]{1,0:T(8,128)(2,1)}, bf16[1024,512]{1,0:T(8,128)(2,1)S(1)}, u32[]{:S(2)}, u32[]{:S(2)}) collective-permute-start(bf16[1024,512]{1,0:T(8,128)(2,1)} %chunk.10), channel_id=1, source_target_pairs={{4,6},{12,14},{20,22},{28,30}} | collective-permute-start | bytes 3145736 | tf_op jit(solution)/shard_map/ppermute | solution.py:287
  7.6 14.1 %collective-permute-start.1 = (bf16[256,1536]{1,0:T(8,128)(2,1)S(1)}, bf16[256,1536]{1,0:T(8,128)(2,1)S(1)}, u32[]{:S(2)}, u32[]{:S(2)}) collective-permute-start(bf16[256,1536]{1,0:T(8,128)(2,1)S(1)} %chunk.7.refs_0_), channel_id=1, source_target_pairs={{0,8},{4,20},{1,9},{5,21},{2,10},{6,22},{3,11},{7,23}} | collective-permute-start | bytes 2359304 | tf_op jit(solution)/shard_map/ppermute | solution.py:375
  15.1 2.4 %collective-permute-start.2 = (bf16[256,1536]{1,0:T(8,128)(2,1)S(1)}, bf16[256,1536]{1,0:T(8,128)(2,1)S(1)}, u32[]{:S(2)}, u32[]{:S(2)}) collective-permute-start(bf16[256,1536]{1,0:T(8,128)(2,1)S(1)} %get-tuple-element.10), channel_id=1, source_target_pairs={{0,4},{4,0},{8,12},{12,8},{16,20},{20,16},{24,28},{28,24},{1,5},{5... | collective-permute-start | bytes 2359304 | tf_op jit(solution)/shard_map/ppermute | solution.py:370
  15.8 8.7 %collective-permute-start.7 = (bf16[1024,512]{1,0:T(8,128)(2,1)S(1)}, bf16[1024,512]{1,0:T(8,128)(2,1)S(1)}, u32[]{:S(2)}, u32[]{:S(2)}) collective-permute-start(bf16[1024,512]{1,0:T(8,128)(2,1)S(1)} %chunk.9.refs_2_.refs_4_), channel_id=1, source_target_pairs={{2,3},{10,11},{18,19},{26,27}} | collective-permute-start | bytes 3145736 | tf_op jit(solution)/shard_map/ppermute | solution.py:287
  17.5 18.2 %collective-permute-start.5 = (bf16[256,1536]{1,0:T(8,128)(2,1)S(1)}, bf16[256,1536]{1,0:T(8,128)(2,1)S(1)}, u32[]{:S(2)}, u32[]{:S(2)}) collective-permute-start(bf16[256,1536]{1,0:T(8,128)(2,1)S(1)} %add.13.refs_2_.refs_0_), channel_id=1, source_target_pairs={{0,8},{4,20},{8,0},{12,28},{16,24},{20,4},{24,16},{28,12},{1,9},{5... | collective-permute-start | bytes 2359304 | tf_op jit(solution)/shard_map/ppermute | solution.py:376
  21.0 18.7 %collective-permute-start.11 = (bf16[1024,512]{1,0:T(8,128)(2,1)S(1)}, bf16[1024,512]{1,0:T(8,128)(2,1)S(1)}, u32[]{:S(2)}, u32[]{:S(2)}) collective-permute-start(bf16[1024,512]{1,0:T(8,128)(2,1)S(1)} %chunk.9.refs_2_.refs_4_), channel_id=1, source_target_pairs={{0,2},{2,1},{8,10},{10,9},{16,18},{18,17},{24,26},{26,25}} | collective-permute-start | bytes 3145736 | tf_op jit(solution)/shard_map/ppermute | solution.py:287
  21.9 14.8 %collective-permute-start.4 = (bf16[256,1536]{1,0:T(8,128)(2,1)S(1)}, bf16[256,1536]{1,0:T(8,128)(2,1)S(1)}, u32[]{:S(2)}, u32[]{:S(2)}) collective-permute-start(bf16[256,1536]{1,0:T(8,128)(2,1)S(1)} %add.14.refs_0_), channel_id=1, source_target_pairs={{0,16},{8,24},{4,12},{20,28},{1,17},{9,25},{5,13},{21,29},{2,18},{... | collective-permute-start | bytes 2359304 | tf_op jit(solution)/shard_map/ppermute | solution.py:375
  23.8 16.6 %collective-permute-start.13 = (bf16[1024,512]{1,0:T(8,128)(2,1)S(1)}, bf16[1024,512]{1,0:T(8,128)(2,1)S(1)}, u32[]{:S(2)}, u32[]{:S(2)}) collective-permute-start(bf16[1024,512]{1,0:T(8,128)(2,1)S(1)} %chunk.11.refs_3_.refs_7_), channel_id=1, source_target_pairs={{6,7},{14,15},{22,23},{30,31}} | collective-permute-start | bytes 3145736 | tf_op jit(solution)/shard_map/ppermute | solution.py:287
  24.6 33.7 %collective-permute-start.12 = (bf16[1024,512]{1,0:T(8,128)(2,1)S(1)}, bf16[1024,512]{1,0:T(8,128)(2,1)S(1)}, u32[]{:S(2)}, u32[]{:S(2)}) collective-permute-start(bf16[1024,512]{1,0:T(8,128)(2,1)S(1)} %chunk.11.refs_3_.refs_7_), channel_id=1, source_target_pairs={{4,6},{6,5},{12,14},{14,13},{20,22},{22,21},{28,30},{30,29}} | collective-permute-start | bytes 3145736 | tf_op jit(solution)/shard_map/ppermute | solution.py:287
  35.8 27.8 %copy-start = (bf16[512,512]{1,0:T(8,128)(2,1)S(1)}, bf16[512,512]{1,0:T(8,128)(2,1)}, u32[]{:S(2)}) copy-start(bf16[512,512]{1,0:T(8,128)(2,1)} %refs_0_.1) | copy-start | bytes 1572868
  35.8 23.2 %collective-permute-start.9 = (bf16[256,1536]{1,0:T(8,128)(2,1)S(1)}, bf16[256,1536]{1,0:T(8,128)(2,1)S(1)}, u32[]{:S(2)}, u32[]{:S(2)}) collective-permute-start(bf16[256,1536]{1,0:T(8,128)(2,1)S(1)} %add.15.refs_2_.refs_0_), channel_id=1, source_target_pairs={{0,16},{4,12},{8,24},{12,4},{16,0},{20,28},{24,8},{28,20},{1,17},{... | collective-permute-start | bytes 2359304 | tf_op jit(solution)/shard_map/ppermute | solution.py:376
  36.8 23.6 %collective-permute-start.8 = (bf16[256,1536]{1,0:T(8,128)(2,1)S(1)}, bf16[256,1536]{1,0:T(8,128)(2,1)S(1)}, u32[]{:S(2)}, u32[]{:S(2)}) collective-permute-start(bf16[256,1536]{1,0:T(8,128)(2,1)S(1)} %add.16.down_ref), channel_id=1, source_target_pairs={{0,4},{4,0},{8,12},{12,8},{16,20},{20,16},{24,28},{28,24},{1,5},{5... | collective-permute-start | bytes 2359304 | tf_op jit(solution)/shard_map/ppermute | solution.py:378
  39.7 32.9 %collective-permute-start.15 = (bf16[1024,512]{1,0:T(8,128)(2,1)S(1)}, bf16[1024,512]{1,0:T(8,128)(2,1)S(1)}, u32[]{:S(2)}, u32[]{:S(2)}) collective-permute-start(bf16[1024,512]{1,0:T(8,128)(2,1)S(1)} %collective-permute-done.11.refs_5_.refs_2_), channel_id=1, source_target_pairs={{2,3},{10,11},{18,19},{26,27}} | collective-permute-start | bytes 3145736 | tf_op jit(solution)/shard_map/ppermute | solution.py:287
  40.5 32.2 %collective-permute-start.14 = (bf16[1024,512]{1,0:T(8,128)(2,1)S(1)}, bf16[1024,512]{1,0:T(8,128)(2,1)S(1)}, u32[]{:S(2)}, u32[]{:S(2)}) collective-permute-start(bf16[1024,512]{1,0:T(8,128)(2,1)S(1)} %collective-permute-done.11.refs_5_.refs_2_), channel_id=1, source_target_pairs={{2,1},{10,9},{18,17},{26,25}} | collective-permute-start | bytes 3145736 | tf_op jit(solution)/shard_map/ppermute | solution.py:287
  58.3 14.4 %collective-permute-start.17 = (bf16[1024,512]{1,0:T(8,128)(2,1)S(1)}, bf16[1024,512]{1,0:T(8,128)(2,1)S(1)}, u32[]{:S(2)}, u32[]{:S(2)}) collective-permute-start(bf16[1024,512]{1,0:T(8,128)(2,1)S(1)} %collective-permute-done.12.refs_8_.refs_5_), channel_id=1, source_target_pairs={{6,7},{14,15},{22,23},{30,31}} | collective-permute-start | bytes 3145736 | tf_op jit(solution)/shard_map/ppermute | solution.py:287
  59.0 28.0 %collective-permute-start.16 = (bf16[1024,512]{1,0:T(8,128)(2,1)S(1)}, bf16[1024,512]{1,0:T(8,128)(2,1)S(1)}, u32[]{:S(2)}, u32[]{:S(2)}) collective-permute-start(bf16[1024,512]{1,0:T(8,128)(2,1)S(1)} %collective-permute-done.12.refs_8_.refs_5_), channel_id=1, source_target_pairs={{6,5},{14,13},{22,21},{30,29}} | collective-permute-start | bytes 3145736 | tf_op jit(solution)/shard_map/ppermute | solution.py:287
  60.4 3.2 %collective-permute-start.10 = (bf16[256,1536]{1,0:T(8,128)(2,1)S(1)}, bf16[256,1536]{1,0:T(8,128)(2,1)S(1)}, u32[]{:S(2)}, u32[]{:S(2)}) collective-permute-start(bf16[256,1536]{1,0:T(8,128)(2,1)S(1)} %add.17.refs_1_), channel_id=1, source_target_pairs={{0,4},{4,0},{8,12},{12,8},{16,20},{20,16},{24,28},{28,24},{1,5},{5... | collective-permute-start | bytes 2359304 | tf_op jit(solution)/shard_map/ppermute | solution.py:380

commit v8 on v7

--- a/solution.py
+++ b/solution.py
@@ -9,8 +9,8 @@
 
 GROUPS = 2
 CHUNK_WEIGHTS = (0, 5)
-JOIN_WEIGHTS, JOIN_AFTER = (0, 5), ((1, 0), (2, 1))
-DOWN_WEIGHTS, DOWN_AFTER = (0, 2), ((0, 0), (0, 0))
+JOIN_WEIGHTS, JOIN_AFTER = (2, 2), ((1, 0), (3, 1))
+DOWN_WEIGHTS, DOWN_AFTER = (0, 20), ((1, 0), (0, 0))
 PIECES = 2
 BLOCK = 256
 F32, BF16 = jnp.float32, jnp.bfloat16
@@ -365,7 +365,7 @@
     order = jnp.where(core == 0, pivots, jnp.roll(pivots, half))
     down_got = lax.ppermute(chunk(place, 0, 0, matrix, half, half, cols), "prow", [(0, 1)])
     down = chunk(place, 0, 0, matrix, 0, half, cols, down_got)
-    pieces = pick(place, order, matrix, [down])
+    pieces = pick(place, order, matrix, [])
     up, sent = pieces[: PIECES // 2], pieces[PIECES // 2 :]
     up_got = [lax.ppermute(x, "prow", swap_pairs(n_prow, cores, 0)) for x in sent]
     def pins(a, b):
@@ -374,7 +374,7 @@
         up = [add(up, up_got, pins(*JOIN_AFTER[min(step, 1)]), JOIN_WEIGHTS[min(step, 1)])]
         down_got = lax.ppermute(down, "prow", grow_pairs(orders, step))
         up_got = [lax.ppermute(up[0], "prow", swap_pairs(n_prow, orders, step))]
-        down = add([down], [down_got], up + pins(*DOWN_AFTER[min(step, 1)]), DOWN_WEIGHTS[min(step, 1)])
+        down = add([down], [down_got], [] + pins(*DOWN_AFTER[min(step, 1)]), DOWN_WEIGHTS[min(step, 1)])
     down_got = lax.ppermute(down, "prow", swap_pairs(n_prow, cores, 0))
     up = add(up, up_got, pins(0, 0), 0)
     up_got = lax.ppermute(up, "prow", swap_pairs(n_prow, cores, 0))

time: 94.9 us -> 86 us (0.906)
  waiting for transfers between devices: 44.9 us -> 39.3 us
  Pallas kernels: 29.2 us -> 27.3 us
  starting transfers between devices: 19.7 us -> 18.5 us
    ppermute x10, waiting for transfers between devices: 31.5 us -> 19.3 us  [move(): return lax.ppermute(value, ('prow', 'pcol'), pairs)]
    ppermute x2, waiting for transfers between devices: 0.79 us -> 7.37 us  [per_device(): down_got = lax.ppermute(down, 'prow', grow_pairs(orders, step))]
    pallas_call x6, Pallas kernels: 6.22 us -> 4.22 us  [chunk(): pl.pallas_call(functools.partial(chunk_kernel, first_row, axis, core), in...]
    ppermute x2, starting transfers between devices: 3.59 us -> 2.26 us  [per_device(): up_got = [lax.ppermute(up[0], 'prow', swap_pairs(n_prow, orders, step))]]
    ppermute x1, starting transfers between devices: 1.33 us -> 0.07 us  [per_device(): up_got = lax.ppermute(up, 'prow', swap_pairs(n_prow, cores, 0))]
  transfers between devices with their start and end apart: 18 -> 18, of which waited for: 6 -> 5; matrix products, arithmetic and copies ran while one was open for 0% -> 0% of each run, Pallas kernels for 21% -> 23%
where the time goes in v8:
time: 86 us; the launch traced here: 85.6 us
  waiting for transfers between devices  39.3 us (46%)
  Pallas kernels  27.3 us (32%)
  starting transfers between devices  18.5 us (22%)
    ppermute x10, waiting for transfers between devices, move(): return lax.ppermute(value, ('prow', 'pcol'), pairs)  19.3 us
    pallas_call x2, Pallas kernels, update(): pl.pallas_call(functools.partial(update_kernel, first_row, len(received),...  16.3 us
    ppermute x2, waiting for transfers between devices, per_device(): up_got = [lax.ppermute(up[0], 'prow', swap_pairs(n_prow, orders, step))]  10.3 us
    ppermute x10, starting transfers between devices, move(): return lax.ppermute(value, ('prow', 'pcol'), pairs)  8.37 us
    ppermute x2, waiting for transfers between devices, per_device(): down_got = lax.ppermute(down, 'prow', grow_pairs(orders, step))  7.37 us
    pallas_call x1, Pallas kernels, pick(): pl.pallas_call(pick_kernel, in_specs=[SMEM, VMEM, ANY] + [ANY] * len(afte...  6.16 us
    pallas_call x6, Pallas kernels, chunk(): pl.pallas_call(functools.partial(chunk_kernel, first_row, axis, core), in...  4.22 us
    ppermute x1, starting transfers between devices, per_device(): down_got = lax.ppermute(down, 'prow', swap_pairs(n_prow, cores, 0))  3.67 us
  transfers between devices with their start and end apart: 18, of which 5 were waited for; matrix products, arithmetic and copies ran while one was open for 0% of the time, Pallas kernels for 23%

profile of v8, /device:TPU:13, one launch (start us, length us, event | category | flops | bytes accessed | tf_op | source)
XLA Modules:
  0.0 85.6 jit_solution(1191528544474726695)
XLA Ops:
  0.1 0.6 chunk.8
  0.6 0.7 collective-permute-start.2
  1.4 1.4 %chunk.6 = bf16[256,1536]{1,0:T(8,128)(2,1)} custom-call(s32[4]{0:T(128)S(1)} %pad_add_fusion.place_ref, bf16[2048,1536]{1,0:T(8,128)(2,1)} %refs_1_.1), custom_call_target="tpu_custom_call" | custom-call | tf_op jit(solution)/shard_map/chunk/pallas_call | solution.py:50
  2.8 0.7 collective-permute-start
  3.6 0.1 copy.8.pivots_ref
  3.7 6.2 %pick_rows.1 = (bf16[256,1536]{1,0:T(8,128)(2,1)S(1)}, bf16[256,1536]{1,0:T(8,128)(2,1)S(1)}) custom-call(s32[4]{0:T(128)S(1)} %pad_add_fusion.place_ref, s32[512,1]{1,0:T(8,128)S(1)} %copy.8.pivots_ref, bf16[2048,1536]{1,0:T(8,128)(2,1)} %refs_1_.1), custom_call_target="tpu_custom_call" | custom-call | tf_op jit(solution)/shard_map/pick_rows/pallas_call | solution.py:100
  9.9 0.7 collective-permute-start.5
  10.6 0.6 chunk.10
  11.2 0.7 collective-permute-start.7
  11.9 0.6 chunk.7.refs_0_
  12.5 1.3 %collective-permute-start.1 = (bf16[256,1536]{1,0:T(8,128)(2,1)S(1)}, bf16[256,1536]{1,0:T(8,128)(2,1)S(1)}, u32[]{:S(2)}, u32[]{:S(2)}) collective-permute-start(bf16[256,1536]{1,0:T(8,128)(2,1)S(1)} %chunk.7.refs_0_), channel_id=1, source_target_pairs={{0,8},{4,20},{1,9},{5,21},{2,10},{6,22},{3,11},{7,23}} | collective-permute-start | bytes 2359304 | tf_op jit(solution)/shard_map/ppermute | solution.py:375
  13.8 0.6 chunk.9.refs_2_.refs_4_
  14.4 0.7 collective-permute-start.9
  15.1 0.7 collective-permute-start.8
  16.0 2.2 %collective-permute-start.6 = (bf16[256,1536]{1,0:T(8,128)(2,1)S(1)}, bf16[256,1536]{1,0:T(8,128)(2,1)S(1)}, u32[]{:S(2)}, u32[]{:S(2)}) collective-permute-start(bf16[256,1536]{1,0:T(8,128)(2,1)S(1)} %add.15.refs_0_), channel_id=1, source_target_pairs={{0,8},{4,20},{8,0},{12,28},{16,24},{20,4},{24,16},{28,12},{1,9},{5... | collective-permute-start | bytes 2359304 | tf_op jit(solution)/shard_map/ppermute | solution.py:376
  18.2 7.4 %collective-permute-done.1.refs_1_ = bf16[256,1536]{1,0:T(8,128)(2,1)S(1)} collective-permute-done((bf16[256,1536]{1,0:T(8,128)(2,1)S(1)}, bf16[256,1536]{1,0:T(8,128)(2,1)S(1)}, u32[]{:S(2)}, u32[]{:S(2)}) %collective-permute-start.1) | collective-permute-done | bytes 786464 | tf_op jit(solution)/shard_map/ppermute | solution.py:375
  25.7 1.3 %collective-permute-start.3 = (bf16[256,1536]{1,0:T(8,128)(2,1)S(1)}, bf16[256,1536]{1,0:T(8,128)(2,1)S(1)}, u32[]{:S(2)}, u32[]{:S(2)}) collective-permute-start(bf16[256,1536]{1,0:T(8,128)(2,1)S(1)} %add.13.refs_0_), channel_id=1, source_target_pairs={{0,16},{8,24},{4,12},{20,28},{1,17},{9,25},{5,13},{21,29},{2,18},{... | collective-permute-start | bytes 2359304 | tf_op jit(solution)/shard_map/ppermute | solution.py:375
  27.0 0.6 chunk.11.refs_2_.refs_7_
  27.6 0.7 collective-permute-start.13
  28.3 10.3 %collective-permute-done.6.refs_1_ = bf16[256,1536]{1,0:T(8,128)(2,1)S(1)} collective-permute-done((bf16[256,1536]{1,0:T(8,128)(2,1)S(1)}, bf16[256,1536]{1,0:T(8,128)(2,1)S(1)}, u32[]{:S(2)}, u32[]{:S(2)}) %collective-permute-start.6) | collective-permute-done | bytes 786464 | tf_op jit(solution)/shard_map/ppermute | solution.py:376
  38.6 1.3 %collective-permute-start.12 = (bf16[1024,512]{1,0:T(8,128)(2,1)S(1)}, bf16[1024,512]{1,0:T(8,128)(2,1)S(1)}, u32[]{:S(2)}, u32[]{:S(2)}) collective-permute-start(bf16[1024,512]{1,0:T(8,128)(2,1)S(1)} %chunk.11.refs_2_.refs_7_), channel_id=1, source_target_pairs={{4,6},{6,5},{12,14},{14,13},{20,22},{22,21},{28,30},{30,29}} | collective-permute-start | bytes 3145736 | tf_op jit(solution)/shard_map/ppermute | solution.py:287
  39.9 0.1 add.16.refs_0_
  40.3 3.7 %collective-permute-start.4 = (bf16[256,1536]{1,0:T(8,128)(2,1)S(1)}, bf16[256,1536]{1,0:T(8,128)(2,1)S(1)}, u32[]{:S(2)}, u32[]{:S(2)}) collective-permute-start(bf16[256,1536]{1,0:T(8,128)(2,1)S(1)} %add.14.down_ref), channel_id=1, source_target_pairs={{0,4},{4,0},{8,12},{12,8},{16,20},{20,16},{24,28},{28,24},{1,5},{5... | collective-permute-start | bytes 2359304 | tf_op jit(solution)/shard_map/ppermute | solution.py:378
  43.9 0.7 collective-permute-start.15
  44.7 0.7 collective-permute-start.14
  45.4 15.0 %collective-permute-done.12.refs_8_.refs_5_ = bf16[1024,512]{1,0:T(8,128)(2,1)S(1)} collective-permute-done((bf16[1024,512]{1,0:T(8,128)(2,1)S(1)}, bf16[1024,512]{1,0:T(8,128)(2,1)S(1)}, u32[]{:S(2)}, u32[]{:S(2)}) %collective-permute-start.12) | collective-permute-done | bytes 1048608 | tf_op jit(solution)/shard_map/ppermute | solution.py:287
  60.4 0.7 collective-permute-start.17
  61.1 1.3 %collective-permute-start.16 = (bf16[1024,512]{1,0:T(8,128)(2,1)S(1)}, bf16[1024,512]{1,0:T(8,128)(2,1)S(1)}, u32[]{:S(2)}, u32[]{:S(2)}) collective-permute-start(bf16[1024,512]{1,0:T(8,128)(2,1)S(1)} %collective-permute-done.12.refs_8_.refs_5_), channel_id=1, source_target_pairs={{6,5},{14,13},{22,21},{30,29}} | collective-permute-start | bytes 3145736 | tf_op jit(solution)/shard_map/ppermute | solution.py:287
  62.6 2.3 %collective-permute-done.11.refs_2_ = bf16[256,1536]{1,0:T(8,128)(2,1)S(1)} collective-permute-done((bf16[256,1536]{1,0:T(8,128)(2,1)S(1)}, bf16[256,1536]{1,0:T(8,128)(2,1)S(1)}, u32[]{:S(2)}, u32[]{:S(2)}) %collective-permute-start.11) | collective-permute-done | bytes 786464 | tf_op jit(solution)/shard_map/ppermute | solution.py:380
  64.9 8.9 %update_rows.2 = (bf16[2048,1536]{1,0:T(8,128)(2,1)}, bf16[512,1536]{1,0:T(8,128)(2,1)S(1)}) custom-call(s32[4]{0:T(128)S(1)} %pad_add_fusion.place_ref, s32[1,512]{1,0:T(1,128)S(1)} %bitcast.5, bf16[2048,1536]{1,0:T(8,128)(2,1)} %refs_1_.1, bf16[256,1536]{1,0:T(8,128)(2,1)S(1)} %add.14.down_ref, bf16[256,1536]{1,0:T(8,128)(2,1)S(1)} %collective-permute-done.4.down_got_ref, ...), custom_call_target="tpu_custom_call" | custom-call | tf_op jit(solution)/shard_map/update_rows/pallas_call | solution.py:249
  73.9 4.3 %collective-permute-done.16.refs_6_ = bf16[1024,512]{1,0:T(8,128)(2,1)S(1)} collective-permute-done((bf16[1024,512]{1,0:T(8,128)(2,1)S(1)}, bf16[1024,512]{1,0:T(8,128)(2,1)S(1)}, u32[]{:S(2)}, u32[]{:S(2)}) %collective-permute-start.16) | collective-permute-done | bytes 1048608 | tf_op jit(solution)/shard_map/ppermute | solution.py:287
  78.2 7.4 %update_rows.3 = bf16[2048,1536]{1,0:T(8,128)(2,1)} custom-call(s32[4]{0:T(128)S(1)} %pad_add_fusion.place_ref, s32[1,512]{1,0:T(1,128)S(1)} %bitcast.6, bf16[2048,1536]{1,0:T(8,128)(2,1)} %refs_1_.1, bf16[256,1536]{1,0:T(8,128)(2,1)S(1)} %add.14.down_ref, ...), custom_call_target="tpu_custom_call", output_to_operand_aliasing={{}: (13, {})} | custom-call | tf_op jit(solution)/shard_map/update_rows/pallas_call | solution.py:249
  (26 shorter events, 0.7 us)
Async XLA Ops:
  0.1 3.5 %copy-start.1 = (s32[512]{0:T(512)S(1)}, s32[512]{0:T(512)}, u32[]{:S(2)}) copy-start(s32[512]{0:T(512)} %param.4) | copy-start | bytes 6148
  0.6 13.2 %collective-permute-start.2 = (bf16[1024,512]{1,0:T(8,128)(2,1)S(1)}, bf16[1024,512]{1,0:T(8,128)(2,1)S(1)}, u32[]{:S(2)}, u32[]{:S(2)}) collective-permute-start(bf16[1024,512]{1,0:T(8,128)(2,1)S(1)} %chunk.8), channel_id=1, source_target_pairs={{0,2},{8,10},{16,18},{24,26}} | collective-permute-start | bytes 3145736 | tf_op jit(solution)/shard_map/ppermute | solution.py:287
  2.8 9.1 %collective-permute-start = (bf16[256,1536]{1,0:T(8,128)(2,1)}, bf16[256,1536]{1,0:T(8,128)(2,1)S(1)}, u32[]{:S(2)}, u32[]{:S(2)}) collective-permute-start(bf16[256,1536]{1,0:T(8,128)(2,1)} %chunk.6), channel_id=1, source_target_pairs={{0,4},{1,5},{2,6},{3,7}} | collective-permute-start | bytes 2359304 | tf_op jit(solution)/shard_map/ppermute | solution.py:366
  9.9 6.0 %collective-permute-start.5 = (bf16[256,1536]{1,0:T(8,128)(2,1)S(1)}, bf16[256,1536]{1,0:T(8,128)(2,1)S(1)}, u32[]{:S(2)}, u32[]{:S(2)}) collective-permute-start(bf16[256,1536]{1,0:T(8,128)(2,1)S(1)} %get-tuple-element.10), channel_id=1, source_target_pairs={{0,4},{4,0},{8,12},{12,8},{16,20},{20,16},{24,28},{28,24},{1,5},{5... | collective-permute-start | bytes 2359304 | tf_op jit(solution)/shard_map/ppermute | solution.py:370
  11.2 15.8 %collective-permute-start.7 = (bf16[1024,512]{1,0:T(8,128)(2,1)S(1)}, bf16[1024,512]{1,0:T(8,128)(2,1)S(1)}, u32[]{:S(2)}, u32[]{:S(2)}) collective-permute-start(bf16[1024,512]{1,0:T(8,128)(2,1)S(1)} %chunk.10), channel_id=1, source_target_pairs={{4,6},{12,14},{20,22},{28,30}} | collective-permute-start | bytes 3145736 | tf_op jit(solution)/shard_map/ppermute | solution.py:287
  12.5 13.0 %collective-permute-start.1 = (bf16[256,1536]{1,0:T(8,128)(2,1)S(1)}, bf16[256,1536]{1,0:T(8,128)(2,1)S(1)}, u32[]{:S(2)}, u32[]{:S(2)}) collective-permute-start(bf16[256,1536]{1,0:T(8,128)(2,1)S(1)} %chunk.7.refs_0_), channel_id=1, source_target_pairs={{0,8},{4,20},{1,9},{5,21},{2,10},{6,22},{3,11},{7,23}} | collective-permute-start | bytes 2359304 | tf_op jit(solution)/shard_map/ppermute | solution.py:375
  14.4 25.5 %collective-permute-start.9 = (bf16[1024,512]{1,0:T(8,128)(2,1)S(1)}, bf16[1024,512]{1,0:T(8,128)(2,1)S(1)}, u32[]{:S(2)}, u32[]{:S(2)}) collective-permute-start(bf16[1024,512]{1,0:T(8,128)(2,1)S(1)} %chunk.9.refs_2_.refs_4_), channel_id=1, source_target_pairs={{2,3},{10,11},{18,19},{26,27}} | collective-permute-start | bytes 3145736 | tf_op jit(solution)/shard_map/ppermute | solution.py:287
  15.1 24.8 %collective-permute-start.8 = (bf16[1024,512]{1,0:T(8,128)(2,1)S(1)}, bf16[1024,512]{1,0:T(8,128)(2,1)S(1)}, u32[]{:S(2)}, u32[]{:S(2)}) collective-permute-start(bf16[1024,512]{1,0:T(8,128)(2,1)S(1)} %chunk.9.refs_2_.refs_4_), channel_id=1, source_target_pairs={{0,2},{2,1},{8,10},{10,9},{16,18},{18,17},{24,26},{26,25}} | collective-permute-start | bytes 3145736 | tf_op jit(solution)/shard_map/ppermute | solution.py:287
  16.0 22.6 %collective-permute-start.6 = (bf16[256,1536]{1,0:T(8,128)(2,1)S(1)}, bf16[256,1536]{1,0:T(8,128)(2,1)S(1)}, u32[]{:S(2)}, u32[]{:S(2)}) collective-permute-start(bf16[256,1536]{1,0:T(8,128)(2,1)S(1)} %add.15.refs_0_), channel_id=1, source_target_pairs={{0,8},{4,20},{8,0},{12,28},{16,24},{20,4},{24,16},{28,12},{1,9},{5... | collective-permute-start | bytes 2359304 | tf_op jit(solution)/shard_map/ppermute | solution.py:376
  25.7 14.5 %collective-permute-start.3 = (bf16[256,1536]{1,0:T(8,128)(2,1)S(1)}, bf16[256,1536]{1,0:T(8,128)(2,1)S(1)}, u32[]{:S(2)}, u32[]{:S(2)}) collective-permute-start(bf16[256,1536]{1,0:T(8,128)(2,1)S(1)} %add.13.refs_0_), channel_id=1, source_target_pairs={{0,16},{8,24},{4,12},{20,28},{1,17},{9,25},{5,13},{21,29},{2,18},{... | collective-permute-start | bytes 2359304 | tf_op jit(solution)/shard_map/ppermute | solution.py:375
  27.6 17.1 %collective-permute-start.13 = (bf16[1024,512]{1,0:T(8,128)(2,1)S(1)}, bf16[1024,512]{1,0:T(8,128)(2,1)S(1)}, u32[]{:S(2)}, u32[]{:S(2)}) collective-permute-start(bf16[1024,512]{1,0:T(8,128)(2,1)S(1)} %chunk.11.refs_2_.refs_7_), channel_id=1, source_target_pairs={{6,7},{14,15},{22,23},{30,31}} | collective-permute-start | bytes 3145736 | tf_op jit(solution)/shard_map/ppermute | solution.py:287
  38.6 21.8 %collective-permute-start.12 = (bf16[1024,512]{1,0:T(8,128)(2,1)S(1)}, bf16[1024,512]{1,0:T(8,128)(2,1)S(1)}, u32[]{:S(2)}, u32[]{:S(2)}) collective-permute-start(bf16[1024,512]{1,0:T(8,128)(2,1)S(1)} %chunk.11.refs_2_.refs_7_), channel_id=1, source_target_pairs={{4,6},{6,5},{12,14},{14,13},{20,22},{22,21},{28,30},{30,29}} | collective-permute-start | bytes 3145736 | tf_op jit(solution)/shard_map/ppermute | solution.py:287
  40.1 24.9 %copy-start = (bf16[512,512]{1,0:T(8,128)(2,1)S(1)}, bf16[512,512]{1,0:T(8,128)(2,1)}, u32[]{:S(2)}) copy-start(bf16[512,512]{1,0:T(8,128)(2,1)} %refs_0_.1) | copy-start | bytes 1572868
  40.1 21.1 %collective-permute-start.10 = (bf16[256,1536]{1,0:T(8,128)(2,1)S(1)}, bf16[256,1536]{1,0:T(8,128)(2,1)S(1)}, u32[]{:S(2)}, u32[]{:S(2)}) collective-permute-start(bf16[256,1536]{1,0:T(8,128)(2,1)S(1)} %add.16.refs_0_), channel_id=1, source_target_pairs={{0,16},{4,12},{8,24},{12,4},{16,0},{20,28},{24,8},{28,20},{1,17},{... | collective-permute-start | bytes 2359304 | tf_op jit(solution)/shard_map/ppermute | solution.py:376
  40.3 22.3 %collective-permute-start.4 = (bf16[256,1536]{1,0:T(8,128)(2,1)S(1)}, bf16[256,1536]{1,0:T(8,128)(2,1)S(1)}, u32[]{:S(2)}, u32[]{:S(2)}) collective-permute-start(bf16[256,1536]{1,0:T(8,128)(2,1)S(1)} %add.14.down_ref), channel_id=1, source_target_pairs={{0,4},{4,0},{8,12},{12,8},{16,20},{20,16},{24,28},{28,24},{1,5},{5... | collective-permute-start | bytes 2359304 | tf_op jit(solution)/shard_map/ppermute | solution.py:378
  43.9 29.9 %collective-permute-start.15 = (bf16[1024,512]{1,0:T(8,128)(2,1)S(1)}, bf16[1024,512]{1,0:T(8,128)(2,1)S(1)}, u32[]{:S(2)}, u32[]{:S(2)}) collective-permute-start(bf16[1024,512]{1,0:T(8,128)(2,1)S(1)} %collective-permute-done.8.refs_3_.refs_5_.refs_2_), channel_id=1, source_target_pairs={{2,3},{10,11},{18,19},{26,27}} | collective-permute-start | bytes 3145736 | tf_op jit(solution)/shard_map/ppermute | solution.py:287
  44.7 29.2 %collective-permute-start.14 = (bf16[1024,512]{1,0:T(8,128)(2,1)S(1)}, bf16[1024,512]{1,0:T(8,128)(2,1)S(1)}, u32[]{:S(2)}, u32[]{:S(2)}) collective-permute-start(bf16[1024,512]{1,0:T(8,128)(2,1)S(1)} %collective-permute-done.8.refs_3_.refs_5_.refs_2_), channel_id=1, source_target_pairs={{2,1},{10,9},{18,17},{26,25}} | collective-permute-start | bytes 3145736 | tf_op jit(solution)/shard_map/ppermute | solution.py:287
  60.4 13.5 %collective-permute-start.17 = (bf16[1024,512]{1,0:T(8,128)(2,1)S(1)}, bf16[1024,512]{1,0:T(8,128)(2,1)S(1)}, u32[]{:S(2)}, u32[]{:S(2)}) collective-permute-start(bf16[1024,512]{1,0:T(8,128)(2,1)S(1)} %collective-permute-done.12.refs_8_.refs_5_), channel_id=1, source_target_pairs={{6,7},{14,15},{22,23},{30,31}} | collective-permute-start | bytes 3145736 | tf_op jit(solution)/shard_map/ppermute | solution.py:287
  61.1 17.0 %collective-permute-start.16 = (bf16[1024,512]{1,0:T(8,128)(2,1)S(1)}, bf16[1024,512]{1,0:T(8,128)(2,1)S(1)}, u32[]{:S(2)}, u32[]{:S(2)}) collective-permute-start(bf16[1024,512]{1,0:T(8,128)(2,1)S(1)} %collective-permute-done.12.refs_8_.refs_5_), channel_id=1, source_target_pairs={{6,5},{14,13},{22,21},{30,29}} | collective-permute-start | bytes 3145736 | tf_op jit(solution)/shard_map/ppermute | solution.py:287
  62.5 2.4 %collective-permute-start.11 = (bf16[256,1536]{1,0:T(8,128)(2,1)S(1)}, bf16[256,1536]{1,0:T(8,128)(2,1)S(1)}, u32[]{:S(2)}, u32[]{:S(2)}) collective-permute-start(bf16[256,1536]{1,0:T(8,128)(2,1)S(1)} %add.17.refs_1_), channel_id=1, source_target_pairs={{0,4},{4,0},{8,12},{12,8},{16,20},{20,16},{24,28},{28,24},{1,5},{5... | collective-permute-start | bytes 2359304 | tf_op jit(solution)/shard_map/ppermute | solution.py:380

commit v9 on v8

--- a/solution.py
+++ b/solution.py
@@ -12,7 +12,7 @@
 JOIN_WEIGHTS, JOIN_AFTER = (2, 2), ((1, 0), (3, 1))
 DOWN_WEIGHTS, DOWN_AFTER = (0, 20), ((1, 0), (0, 0))
 PIECES = 2
-BLOCK = 256
+PICK_BLOCK, UPDATE_BLOCK = 256, 512
 F32, BF16 = jnp.float32, jnp.bfloat16
 VMEM = pl.BlockSpec(memory_space=pltpu.VMEM)
 ANY = pl.BlockSpec(memory_space=pl.ANY)
@@ -61,7 +61,7 @@
 
 
 def columns(number, block):
-    return pl.ds(pl.multiple_of(number * block, block), block)
+    return pl.ds(number * block, block)
 
 
 def pick_kernel(place_ref, pivots_ref, matrix_ref, *refs):
@@ -69,7 +69,7 @@
     outs = refs[-3 - PIECES : -3]
     rows, cols = whole_ref.shape
     width = pivots_ref.shape[0]
-    block = min(BLOCK, cols)
+    block = min(PICK_BLOCK, cols)
     count = width // PIECES
 
     def fetch(number):
@@ -83,8 +83,7 @@
     row = lax.broadcasted_iota(jnp.int32, (width, rows), 1) + place_ref[0] * rows
     onehot_ref[...] = jnp.where(pivots_ref[...] == row, 1.0, 0.0).astype(BF16)
 
-    @pl.loop(0, cols // block)
-    def _(number):
+    for number in range(cols // block):
         fetch(number).wait()
         here = columns(number, block)
         picked = jnp.dot(onehot_ref[...], whole_ref[:, here], preferred_element_type=F32)
@@ -96,7 +95,7 @@
 def pick(place, pivots, matrix, after=()):
     rows, cols = matrix.shape
     width = pivots.shape[0]
-    block = min(BLOCK, cols)
+    block = min(PICK_BLOCK, cols)
     return pl.pallas_call(
         pick_kernel,
         in_specs=[SMEM, VMEM, ANY] + [ANY] * len(after),
@@ -155,7 +154,7 @@
     count, cols = rows_ref.shape
     width = left_ref.shape[1] // 2
     row_place, col_place, core, rows = (place_ref[i] for i in range(4))
-    block = min(BLOCK, cols)
+    block = min(UPDATE_BLOCK, cols)
     piece = min(count, 512)
     here = pl.ds(first_row, count)
 
@@ -192,8 +191,7 @@
         keep_ref[these] = jnp.broadcast_to(1.0 - has_pivot, (piece, 128))
     fetch_panel(lambda copy: copy.wait())
 
-    @pl.loop(0, cols // block)
-    def _(number):
+    for number in range(cols // block):
         there = columns(number, block)
         if make_upper:
             in_order(core, up_ref[:, there], up_got_ref[:, there], pivot_rows_ref)
@@ -231,7 +229,7 @@
     rows, cols = matrix.shape
     width = pivots.shape[0]
     make_upper = upper is None
-    block = min(BLOCK, cols)
+    block = min(UPDATE_BLOCK, cols)
     operands = [place, pivots[None, :], matrix, down, down_got]
     in_specs = [SMEM, VMEM, ANY, VMEM, VMEM]
     terms = list(upper_terms) if make_upper else [upper]

time: 86 us -> 88.9 us (1.034)
  Pallas kernels: 27.3 us -> 29.1 us
    pallas_call x1, Pallas kernels: 6.16 us -> 9.22 us  [pick(): pl.pallas_call(pick_kernel, in_specs=[SMEM, VMEM, ANY] + [ANY] * len(afte...]
    pallas_call x2, Pallas kernels: 16.3 us -> 15.1 us  [update(): pl.pallas_call(functools.partial(update_kernel, first_row, len(received),...]
  transfers between devices with their start and end apart: 18 -> 18, of which waited for: 5 -> 5; matrix products, arithmetic and copies ran while one was open for 0% -> 0% of each run, Pallas kernels for 23% -> 24%
where the time goes in v9:
time: 88.9 us; the launch traced here: 88.5 us
  waiting for transfers between devices  40.1 us (45%)
  Pallas kernels  29.1 us (33%)
  starting transfers between devices  18.5 us (21%)
    ppermute x10, waiting for transfers between devices, move(): return lax.ppermute(value, ('prow', 'pcol'), pairs)  20.2 us
    pallas_call x2, Pallas kernels, update(): pl.pallas_call(functools.partial(update_kernel, first_row, len(received),...  15.1 us
    ppermute x2, waiting for transfers between devices, per_device(): up_got = [lax.ppermute(up[0], 'prow', swap_pairs(n_prow, orders, step))]  10.3 us
    pallas_call x1, Pallas kernels, pick(): pl.pallas_call(pick_kernel, in_specs=[SMEM, VMEM, ANY] + [ANY] * len(afte...  9.22 us
    ppermute x10, starting transfers between devices, move(): return lax.ppermute(value, ('prow', 'pcol'), pairs)  8.37 us
    ppermute x2, waiting for transfers between devices, per_device(): down_got = lax.ppermute(down, 'prow', grow_pairs(orders, step))  7.37 us
    pallas_call x6, Pallas kernels, chunk(): pl.pallas_call(functools.partial(chunk_kernel, first_row, axis, core), in...  4.22 us
    ppermute x1, starting transfers between devices, per_device(): down_got = lax.ppermute(down, 'prow', swap_pairs(n_prow, cores, 0))  3.68 us
  transfers between devices with their start and end apart: 18, of which 5 were waited for; matrix products, arithmetic and copies ran while one was open for 0% of the time, Pallas kernels for 24%

profile of v9, /device:TPU:13, one launch (start us, length us, event | category | flops | bytes accessed | tf_op | source)
XLA Modules:
  0.0 88.5 jit_solution(8893434461145287537)
XLA Ops:
  0.1 0.6 chunk.8
  0.6 0.7 collective-permute-start.2
  1.4 1.4 %chunk.6 = bf16[256,1536]{1,0:T(8,128)(2,1)} custom-call(s32[4]{0:T(128)S(1)} %pad_add_fusion.place_ref, bf16[2048,1536]{1,0:T(8,128)(2,1)} %refs_1_.1), custom_call_target="tpu_custom_call" | custom-call | tf_op jit(solution)/shard_map/chunk/pallas_call | solution.py:50
  2.8 0.7 collective-permute-start
  3.6 0.1 copy.8.pivots_ref
  3.7 9.2 %pick_rows.1 = (bf16[256,1536]{1,0:T(8,128)(2,1)S(1)}, bf16[256,1536]{1,0:T(8,128)(2,1)S(1)}) custom-call(s32[4]{0:T(128)S(1)} %pad_add_fusion.place_ref, s32[512,1]{1,0:T(8,128)S(1)} %copy.8.pivots_ref, bf16[2048,1536]{1,0:T(8,128)(2,1)} %refs_1_.1), custom_call_target="tpu_custom_call" | custom-call | tf_op jit(solution)/shard_map/pick_rows/pallas_call | solution.py:99
  13.0 0.7 collective-permute-start.5
  13.7 0.6 chunk.10
  14.3 0.7 collective-permute-start.7
  15.0 0.6 chunk.7.refs_0_
  15.6 1.3 %collective-permute-start.1 = (bf16[256,1536]{1,0:T(8,128)(2,1)S(1)}, bf16[256,1536]{1,0:T(8,128)(2,1)S(1)}, u32[]{:S(2)}, u32[]{:S(2)}) collective-permute-start(bf16[256,1536]{1,0:T(8,128)(2,1)S(1)} %chunk.7.refs_0_), channel_id=1, source_target_pairs={{0,8},{4,20},{1,9},{5,21},{2,10},{6,22},{3,11},{7,23}} | collective-permute-start | bytes 2359304 | tf_op jit(solution)/shard_map/ppermute | solution.py:373
  16.9 0.6 chunk.9.refs_2_.refs_4_
  17.4 0.7 collective-permute-start.9
  18.2 0.7 collective-permute-start.8
  19.0 2.2 %collective-permute-start.6 = (bf16[256,1536]{1,0:T(8,128)(2,1)S(1)}, bf16[256,1536]{1,0:T(8,128)(2,1)S(1)}, u32[]{:S(2)}, u32[]{:S(2)}) collective-permute-start(bf16[256,1536]{1,0:T(8,128)(2,1)S(1)} %add.15.refs_0_), channel_id=1, source_target_pairs={{0,8},{4,20},{8,0},{12,28},{16,24},{20,4},{24,16},{28,12},{1,9},{5... | collective-permute-start | bytes 2359304 | tf_op jit(solution)/shard_map/ppermute | solution.py:374
  21.2 7.4 %collective-permute-done.1.refs_1_ = bf16[256,1536]{1,0:T(8,128)(2,1)S(1)} collective-permute-done((bf16[256,1536]{1,0:T(8,128)(2,1)S(1)}, bf16[256,1536]{1,0:T(8,128)(2,1)S(1)}, u32[]{:S(2)}, u32[]{:S(2)}) %collective-permute-start.1) | collective-permute-done | bytes 786464 | tf_op jit(solution)/shard_map/ppermute | solution.py:373
  28.7 1.3 %collective-permute-start.3 = (bf16[256,1536]{1,0:T(8,128)(2,1)S(1)}, bf16[256,1536]{1,0:T(8,128)(2,1)S(1)}, u32[]{:S(2)}, u32[]{:S(2)}) collective-permute-start(bf16[256,1536]{1,0:T(8,128)(2,1)S(1)} %add.13.refs_0_), channel_id=1, source_target_pairs={{0,16},{8,24},{4,12},{20,28},{1,17},{9,25},{5,13},{21,29},{2,18},{... | collective-permute-start | bytes 2359304 | tf_op jit(solution)/shard_map/ppermute | solution.py:373
  30.1 0.6 chunk.11.refs_2_.refs_7_
  30.6 0.7 collective-permute-start.13
  31.4 10.3 %collective-permute-done.6.refs_1_ = bf16[256,1536]{1,0:T(8,128)(2,1)S(1)} collective-permute-done((bf16[256,1536]{1,0:T(8,128)(2,1)S(1)}, bf16[256,1536]{1,0:T(8,128)(2,1)S(1)}, u32[]{:S(2)}, u32[]{:S(2)}) %collective-permute-start.6) | collective-permute-done | bytes 786464 | tf_op jit(solution)/shard_map/ppermute | solution.py:374
  41.7 1.3 %collective-permute-start.12 = (bf16[1024,512]{1,0:T(8,128)(2,1)S(1)}, bf16[1024,512]{1,0:T(8,128)(2,1)S(1)}, u32[]{:S(2)}, u32[]{:S(2)}) collective-permute-start(bf16[1024,512]{1,0:T(8,128)(2,1)S(1)} %chunk.11.refs_2_.refs_7_), channel_id=1, source_target_pairs={{4,6},{6,5},{12,14},{14,13},{20,22},{22,21},{28,30},{30,29}} | collective-permute-start | bytes 3145736 | tf_op jit(solution)/shard_map/ppermute | solution.py:285
  43.0 0.1 add.16.refs_0_
  43.3 3.7 %collective-permute-start.4 = (bf16[256,1536]{1,0:T(8,128)(2,1)S(1)}, bf16[256,1536]{1,0:T(8,128)(2,1)S(1)}, u32[]{:S(2)}, u32[]{:S(2)}) collective-permute-start(bf16[256,1536]{1,0:T(8,128)(2,1)S(1)} %add.14.down_ref), channel_id=1, source_target_pairs={{0,4},{4,0},{8,12},{12,8},{16,20},{20,16},{24,28},{28,24},{1,5},{5... | collective-permute-start | bytes 2359304 | tf_op jit(solution)/shard_map/ppermute | solution.py:376
  47.0 0.7 collective-permute-start.15
  47.7 0.7 collective-permute-start.14
  48.5 15.0 %collective-permute-done.12.refs_8_.refs_5_ = bf16[1024,512]{1,0:T(8,128)(2,1)S(1)} collective-permute-done((bf16[1024,512]{1,0:T(8,128)(2,1)S(1)}, bf16[1024,512]{1,0:T(8,128)(2,1)S(1)}, u32[]{:S(2)}, u32[]{:S(2)}) %collective-permute-start.12) | collective-permute-done | bytes 1048608 | tf_op jit(solution)/shard_map/ppermute | solution.py:285
  63.4 0.7 collective-permute-start.17
  64.2 1.3 %collective-permute-start.16 = (bf16[1024,512]{1,0:T(8,128)(2,1)S(1)}, bf16[1024,512]{1,0:T(8,128)(2,1)S(1)}, u32[]{:S(2)}, u32[]{:S(2)}) collective-permute-start(bf16[1024,512]{1,0:T(8,128)(2,1)S(1)} %collective-permute-done.12.refs_8_.refs_5_), channel_id=1, source_target_pairs={{6,5},{14,13},{22,21},{30,29}} | collective-permute-start | bytes 3145736 | tf_op jit(solution)/shard_map/ppermute | solution.py:285
  65.7 2.3 %collective-permute-done.11.refs_2_ = bf16[256,1536]{1,0:T(8,128)(2,1)S(1)} collective-permute-done((bf16[256,1536]{1,0:T(8,128)(2,1)S(1)}, bf16[256,1536]{1,0:T(8,128)(2,1)S(1)}, u32[]{:S(2)}, u32[]{:S(2)}) %collective-permute-start.11) | collective-permute-done | bytes 786464 | tf_op jit(solution)/shard_map/ppermute | solution.py:378
  68.0 8.1 %update_rows.2 = (bf16[2048,1536]{1,0:T(8,128)(2,1)}, bf16[512,1536]{1,0:T(8,128)(2,1)S(1)}) custom-call(s32[4]{0:T(128)S(1)} %pad_add_fusion.place_ref, s32[1,512]{1,0:T(1,128)S(1)} %bitcast.5, bf16[2048,1536]{1,0:T(8,128)(2,1)} %refs_1_.1, bf16[256,1536]{1,0:T(8,128)(2,1)S(1)} %add.14.down_ref, bf16[256,1536]{1,0:T(8,128)(2,1)S(1)} %collective-permute-done.4.down_got_ref, ...), custom_call_target="tpu_custom_call" | custom-call | tf_op jit(solution)/shard_map/update_rows/pallas_call | solution.py:247
  76.1 5.2 %collective-permute-done.16.refs_6_ = bf16[1024,512]{1,0:T(8,128)(2,1)S(1)} collective-permute-done((bf16[1024,512]{1,0:T(8,128)(2,1)S(1)}, bf16[1024,512]{1,0:T(8,128)(2,1)S(1)}, u32[]{:S(2)}, u32[]{:S(2)}) %collective-permute-start.16) | collective-permute-done | bytes 1048608 | tf_op jit(solution)/shard_map/ppermute | solution.py:285
  81.2 7.1 %update_rows.3 = bf16[2048,1536]{1,0:T(8,128)(2,1)} custom-call(s32[4]{0:T(128)S(1)} %pad_add_fusion.place_ref, s32[1,512]{1,0:T(1,128)S(1)} %bitcast.6, bf16[2048,1536]{1,0:T(8,128)(2,1)} %refs_1_.1, bf16[256,1536]{1,0:T(8,128)(2,1)S(1)} %add.14.down_ref, ...), custom_call_target="tpu_custom_call", output_to_operand_aliasing={{}: (13, {})} | custom-call | tf_op jit(solution)/shard_map/update_rows/pallas_call | solution.py:247
  (26 shorter events, 0.7 us)
Async XLA Ops:
  0.1 3.5 %copy-start.1 = (s32[512]{0:T(512)S(1)}, s32[512]{0:T(512)}, u32[]{:S(2)}) copy-start(s32[512]{0:T(512)} %param.4) | copy-start | bytes 6148
  0.6 16.2 %collective-permute-start.2 = (bf16[1024,512]{1,0:T(8,128)(2,1)S(1)}, bf16[1024,512]{1,0:T(8,128)(2,1)S(1)}, u32[]{:S(2)}, u32[]{:S(2)}) collective-permute-start(bf16[1024,512]{1,0:T(8,128)(2,1)S(1)} %chunk.8), channel_id=1, source_target_pairs={{0,2},{8,10},{16,18},{24,26}} | collective-permute-start | bytes 3145736 | tf_op jit(solution)/shard_map/ppermute | solution.py:285
  2.8 12.2 %collective-permute-start = (bf16[256,1536]{1,0:T(8,128)(2,1)}, bf16[256,1536]{1,0:T(8,128)(2,1)S(1)}, u32[]{:S(2)}, u32[]{:S(2)}) collective-permute-start(bf16[256,1536]{1,0:T(8,128)(2,1)} %chunk.6), channel_id=1, source_target_pairs={{0,4},{1,5},{2,6},{3,7}} | collective-permute-start | bytes 2359304 | tf_op jit(solution)/shard_map/ppermute | solution.py:364
  13.0 6.0 %collective-permute-start.5 = (bf16[256,1536]{1,0:T(8,128)(2,1)S(1)}, bf16[256,1536]{1,0:T(8,128)(2,1)S(1)}, u32[]{:S(2)}, u32[]{:S(2)}) collective-permute-start(bf16[256,1536]{1,0:T(8,128)(2,1)S(1)} %get-tuple-element.10), channel_id=1, source_target_pairs={{0,4},{4,0},{8,12},{12,8},{16,20},{20,16},{24,28},{28,24},{1,5},{5... | collective-permute-start | bytes 2359304 | tf_op jit(solution)/shard_map/ppermute | solution.py:368
  14.3 15.8 %collective-permute-start.7 = (bf16[1024,512]{1,0:T(8,128)(2,1)S(1)}, bf16[1024,512]{1,0:T(8,128)(2,1)S(1)}, u32[]{:S(2)}, u32[]{:S(2)}) collective-permute-start(bf16[1024,512]{1,0:T(8,128)(2,1)S(1)} %chunk.10), channel_id=1, source_target_pairs={{4,6},{12,14},{20,22},{28,30}} | collective-permute-start | bytes 3145736 | tf_op jit(solution)/shard_map/ppermute | solution.py:285
  15.6 13.0 %collective-permute-start.1 = (bf16[256,1536]{1,0:T(8,128)(2,1)S(1)}, bf16[256,1536]{1,0:T(8,128)(2,1)S(1)}, u32[]{:S(2)}, u32[]{:S(2)}) collective-permute-start(bf16[256,1536]{1,0:T(8,128)(2,1)S(1)} %chunk.7.refs_0_), channel_id=1, source_target_pairs={{0,8},{4,20},{1,9},{5,21},{2,10},{6,22},{3,11},{7,23}} | collective-permute-start | bytes 2359304 | tf_op jit(solution)/shard_map/ppermute | solution.py:373
  17.4 25.5 %collective-permute-start.9 = (bf16[1024,512]{1,0:T(8,128)(2,1)S(1)}, bf16[1024,512]{1,0:T(8,128)(2,1)S(1)}, u32[]{:S(2)}, u32[]{:S(2)}) collective-permute-start(bf16[1024,512]{1,0:T(8,128)(2,1)S(1)} %chunk.9.refs_2_.refs_4_), channel_id=1, source_target_pairs={{2,3},{10,11},{18,19},{26,27}} | collective-permute-start | bytes 3145736 | tf_op jit(solution)/shard_map/ppermute | solution.py:285
  18.2 24.8 %collective-permute-start.8 = (bf16[1024,512]{1,0:T(8,128)(2,1)S(1)}, bf16[1024,512]{1,0:T(8,128)(2,1)S(1)}, u32[]{:S(2)}, u32[]{:S(2)}) collective-permute-start(bf16[1024,512]{1,0:T(8,128)(2,1)S(1)} %chunk.9.refs_2_.refs_4_), channel_id=1, source_target_pairs={{0,2},{2,1},{8,10},{10,9},{16,18},{18,17},{24,26},{26,25}} | collective-permute-start | bytes 3145736 | tf_op jit(solution)/shard_map/ppermute | solution.py:285
  19.0 22.6 %collective-permute-start.6 = (bf16[256,1536]{1,0:T(8,128)(2,1)S(1)}, bf16[256,1536]{1,0:T(8,128)(2,1)S(1)}, u32[]{:S(2)}, u32[]{:S(2)}) collective-permute-start(bf16[256,1536]{1,0:T(8,128)(2,1)S(1)} %add.15.refs_0_), channel_id=1, source_target_pairs={{0,8},{4,20},{8,0},{12,28},{16,24},{20,4},{24,16},{28,12},{1,9},{5... | collective-permute-start | bytes 2359304 | tf_op jit(solution)/shard_map/ppermute | solution.py:374
  28.7 14.5 %collective-permute-start.3 = (bf16[256,1536]{1,0:T(8,128)(2,1)S(1)}, bf16[256,1536]{1,0:T(8,128)(2,1)S(1)}, u32[]{:S(2)}, u32[]{:S(2)}) collective-permute-start(bf16[256,1536]{1,0:T(8,128)(2,1)S(1)} %add.13.refs_0_), channel_id=1, source_target_pairs={{0,16},{8,24},{4,12},{20,28},{1,17},{9,25},{5,13},{21,29},{2,18},{... | collective-permute-start | bytes 2359304 | tf_op jit(solution)/shard_map/ppermute | solution.py:373
  30.6 17.1 %collective-permute-start.13 = (bf16[1024,512]{1,0:T(8,128)(2,1)S(1)}, bf16[1024,512]{1,0:T(8,128)(2,1)S(1)}, u32[]{:S(2)}, u32[]{:S(2)}) collective-permute-start(bf16[1024,512]{1,0:T(8,128)(2,1)S(1)} %chunk.11.refs_2_.refs_7_), channel_id=1, source_target_pairs={{6,7},{14,15},{22,23},{30,31}} | collective-permute-start | bytes 3145736 | tf_op jit(solution)/shard_map/ppermute | solution.py:285
  41.7 21.8 %collective-permute-start.12 = (bf16[1024,512]{1,0:T(8,128)(2,1)S(1)}, bf16[1024,512]{1,0:T(8,128)(2,1)S(1)}, u32[]{:S(2)}, u32[]{:S(2)}) collective-permute-start(bf16[1024,512]{1,0:T(8,128)(2,1)S(1)} %chunk.11.refs_2_.refs_7_), channel_id=1, source_target_pairs={{4,6},{6,5},{12,14},{14,13},{20,22},{22,21},{28,30},{30,29}} | collective-permute-start | bytes 3145736 | tf_op jit(solution)/shard_map/ppermute | solution.py:285
  43.1 24.9 %copy-start = (bf16[512,512]{1,0:T(8,128)(2,1)S(1)}, bf16[512,512]{1,0:T(8,128)(2,1)}, u32[]{:S(2)}) copy-start(bf16[512,512]{1,0:T(8,128)(2,1)} %refs_0_.1) | copy-start | bytes 1572868
  43.1 21.1 %collective-permute-start.10 = (bf16[256,1536]{1,0:T(8,128)(2,1)S(1)}, bf16[256,1536]{1,0:T(8,128)(2,1)S(1)}, u32[]{:S(2)}, u32[]{:S(2)}) collective-permute-start(bf16[256,1536]{1,0:T(8,128)(2,1)S(1)} %add.16.refs_0_), channel_id=1, source_target_pairs={{0,16},{4,12},{8,24},{12,4},{16,0},{20,28},{24,8},{28,20},{1,17},{... | collective-permute-start | bytes 2359304 | tf_op jit(solution)/shard_map/ppermute | solution.py:374
  43.3 22.3 %collective-permute-start.4 = (bf16[256,1536]{1,0:T(8,128)(2,1)S(1)}, bf16[256,1536]{1,0:T(8,128)(2,1)S(1)}, u32[]{:S(2)}, u32[]{:S(2)}) collective-permute-start(bf16[256,1536]{1,0:T(8,128)(2,1)S(1)} %add.14.down_ref), channel_id=1, source_target_pairs={{0,4},{4,0},{8,12},{12,8},{16,20},{20,16},{24,28},{28,24},{1,5},{5... | collective-permute-start | bytes 2359304 | tf_op jit(solution)/shard_map/ppermute | solution.py:376
  47.0 29.0 %collective-permute-start.15 = (bf16[1024,512]{1,0:T(8,128)(2,1)S(1)}, bf16[1024,512]{1,0:T(8,128)(2,1)S(1)}, u32[]{:S(2)}, u32[]{:S(2)}) collective-permute-start(bf16[1024,512]{1,0:T(8,128)(2,1)S(1)} %collective-permute-done.8.refs_3_.refs_5_.refs_2_), channel_id=1, source_target_pairs={{2,3},{10,11},{18,19},{26,27}} | collective-permute-start | bytes 3145736 | tf_op jit(solution)/shard_map/ppermute | solution.py:285
  47.7 28.3 %collective-permute-start.14 = (bf16[1024,512]{1,0:T(8,128)(2,1)S(1)}, bf16[1024,512]{1,0:T(8,128)(2,1)S(1)}, u32[]{:S(2)}, u32[]{:S(2)}) collective-permute-start(bf16[1024,512]{1,0:T(8,128)(2,1)S(1)} %collective-permute-done.8.refs_3_.refs_5_.refs_2_), channel_id=1, source_target_pairs={{2,1},{10,9},{18,17},{26,25}} | collective-permute-start | bytes 3145736 | tf_op jit(solution)/shard_map/ppermute | solution.py:285
  63.4 12.6 %collective-permute-start.17 = (bf16[1024,512]{1,0:T(8,128)(2,1)S(1)}, bf16[1024,512]{1,0:T(8,128)(2,1)S(1)}, u32[]{:S(2)}, u32[]{:S(2)}) collective-permute-start(bf16[1024,512]{1,0:T(8,128)(2,1)S(1)} %collective-permute-done.12.refs_8_.refs_5_), channel_id=1, source_target_pairs={{6,7},{14,15},{22,23},{30,31}} | collective-permute-start | bytes 3145736 | tf_op jit(solution)/shard_map/ppermute | solution.py:285
  64.2 17.0 %collective-permute-start.16 = (bf16[1024,512]{1,0:T(8,128)(2,1)S(1)}, bf16[1024,512]{1,0:T(8,128)(2,1)S(1)}, u32[]{:S(2)}, u32[]{:S(2)}) collective-permute-start(bf16[1024,512]{1,0:T(8,128)(2,1)S(1)} %collective-permute-done.12.refs_8_.refs_5_), channel_id=1, source_target_pairs={{6,5},{14,13},{22,21},{30,29}} | collective-permute-start | bytes 3145736 | tf_op jit(solution)/shard_map/ppermute | solution.py:285
  65.6 2.4 %collective-permute-start.11 = (bf16[256,1536]{1,0:T(8,128)(2,1)S(1)}, bf16[256,1536]{1,0:T(8,128)(2,1)S(1)}, u32[]{:S(2)}, u32[]{:S(2)}) collective-permute-start(bf16[256,1536]{1,0:T(8,128)(2,1)S(1)} %add.17.refs_1_), channel_id=1, source_target_pairs={{0,4},{4,0},{8,12},{12,8},{16,20},{20,16},{24,28},{28,24},{1,5},{5... | collective-permute-start | bytes 2359304 | tf_op jit(solution)/shard_map/ppermute | solution.py:378

commit v10 on v9

--- a/solution.py
+++ b/solution.py
@@ -61,7 +61,7 @@
 
 
 def columns(number, block):
-    return pl.ds(number * block, block)
+    return pl.ds(pl.multiple_of(number * block, block), block)
 
 
 def pick_kernel(place_ref, pivots_ref, matrix_ref, *refs):
@@ -83,7 +83,8 @@
     row = lax.broadcasted_iota(jnp.int32, (width, rows), 1) + place_ref[0] * rows
     onehot_ref[...] = jnp.where(pivots_ref[...] == row, 1.0, 0.0).astype(BF16)
 
-    for number in range(cols // block):
+    @pl.loop(0, cols // block)
+    def _(number):
         fetch(number).wait()
         here = columns(number, block)
         picked = jnp.dot(onehot_ref[...], whole_ref[:, here], preferred_element_type=F32)
@@ -191,7 +192,8 @@
         keep_ref[these] = jnp.broadcast_to(1.0 - has_pivot, (piece, 128))
     fetch_panel(lambda copy: copy.wait())
 
-    for number in range(cols // block):
+    @pl.loop(0, cols // block)
+    def _(number):
         there = columns(number, block)
         if make_upper:
             in_order(core, up_ref[:, there], up_got_ref[:, there], pivot_rows_ref)

time: 88.9 us -> 85.7 us (0.964)
  Pallas kernels: 29.1 us -> 26.1 us
    pallas_call x1, Pallas kernels: 9.22 us -> 6.16 us  [pick(): pl.pallas_call(pick_kernel, in_specs=[SMEM, VMEM, ANY] + [ANY] * len(afte...]
  transfers between devices with their start and end apart: 18 -> 18, of which waited for: 5 -> 5; matrix products, arithmetic and copies ran while one was open for 0% -> 0% of each run, Pallas kernels for 24% -> 22%
where the time goes in v10:
time: 85.7 us; the launch traced here: 85.3 us
  waiting for transfers between devices  40.1 us (47%)
  Pallas kernels  26.1 us (30%)
  starting transfers between devices  18.5 us (22%)
    ppermute x10, waiting for transfers between devices, move(): return lax.ppermute(value, ('prow', 'pcol'), pairs)  20.2 us
    pallas_call x2, Pallas kernels, update(): pl.pallas_call(functools.partial(update_kernel, first_row, len(received),...  15.2 us
    ppermute x2, waiting for transfers between devices, per_device(): up_got = [lax.ppermute(up[0], 'prow', swap_pairs(n_prow, orders, step))]  10.3 us
    ppermute x10, starting transfers between devices, move(): return lax.ppermute(value, ('prow', 'pcol'), pairs)  8.37 us
    ppermute x2, waiting for transfers between devices, per_device(): down_got = lax.ppermute(down, 'prow', grow_pairs(orders, step))  7.37 us
    pallas_call x1, Pallas kernels, pick(): pl.pallas_call(pick_kernel, in_specs=[SMEM, VMEM, ANY] + [ANY] * len(afte...  6.16 us
    pallas_call x6, Pallas kernels, chunk(): pl.pallas_call(functools.partial(chunk_kernel, first_row, axis, core), in...  4.22 us
    ppermute x1, starting transfers between devices, per_device(): down_got = lax.ppermute(down, 'prow', swap_pairs(n_prow, cores, 0))  3.67 us
  transfers between devices with their start and end apart: 18, of which 5 were waited for; matrix products, arithmetic and copies ran while one was open for 0% of the time, Pallas kernels for 22%

profile of v10, /device:TPU:13, one launch (start us, length us, event | category | flops | bytes accessed | tf_op | source)
XLA Modules:
  0.0 85.3 jit_solution(12265194711993513215)
XLA Ops:
  0.1 0.6 chunk.8
  0.6 0.7 collective-permute-start.2
  1.4 1.4 %chunk.6 = bf16[256,1536]{1,0:T(8,128)(2,1)} custom-call(s32[4]{0:T(128)S(1)} %pad_add_fusion.place_ref, bf16[2048,1536]{1,0:T(8,128)(2,1)} %refs_1_.1), custom_call_target="tpu_custom_call" | custom-call | tf_op jit(solution)/shard_map/chunk/pallas_call | solution.py:50
  2.8 0.7 collective-permute-start
  3.6 0.1 copy.8.pivots_ref
  3.7 6.2 %pick_rows.1 = (bf16[256,1536]{1,0:T(8,128)(2,1)S(1)}, bf16[256,1536]{1,0:T(8,128)(2,1)S(1)}) custom-call(s32[4]{0:T(128)S(1)} %pad_add_fusion.place_ref, s32[512,1]{1,0:T(8,128)S(1)} %copy.8.pivots_ref, bf16[2048,1536]{1,0:T(8,128)(2,1)} %refs_1_.1), custom_call_target="tpu_custom_call" | custom-call | tf_op jit(solution)/shard_map/pick_rows/pallas_call | solution.py:100
  9.9 0.7 collective-permute-start.5
  10.6 0.6 chunk.10
  11.2 0.7 collective-permute-start.7
  11.9 0.6 chunk.7.refs_0_
  12.5 1.3 %collective-permute-start.1 = (bf16[256,1536]{1,0:T(8,128)(2,1)S(1)}, bf16[256,1536]{1,0:T(8,128)(2,1)S(1)}, u32[]{:S(2)}, u32[]{:S(2)}) collective-permute-start(bf16[256,1536]{1,0:T(8,128)(2,1)S(1)} %chunk.7.refs_0_), channel_id=1, source_target_pairs={{0,8},{4,20},{1,9},{5,21},{2,10},{6,22},{3,11},{7,23}} | collective-permute-start | bytes 2359304 | tf_op jit(solution)/shard_map/ppermute | solution.py:375
  13.8 0.6 chunk.9.refs_2_.refs_4_
  14.4 0.7 collective-permute-start.9
  15.1 0.7 collective-permute-start.8
  16.0 2.2 %collective-permute-start.6 = (bf16[256,1536]{1,0:T(8,128)(2,1)S(1)}, bf16[256,1536]{1,0:T(8,128)(2,1)S(1)}, u32[]{:S(2)}, u32[]{:S(2)}) collective-permute-start(bf16[256,1536]{1,0:T(8,128)(2,1)S(1)} %add.15.refs_0_), channel_id=1, source_target_pairs={{0,8},{4,20},{8,0},{12,28},{16,24},{20,4},{24,16},{28,12},{1,9},{5... | collective-permute-start | bytes 2359304 | tf_op jit(solution)/shard_map/ppermute | solution.py:376
  18.2 7.4 %collective-permute-done.1.refs_1_ = bf16[256,1536]{1,0:T(8,128)(2,1)S(1)} collective-permute-done((bf16[256,1536]{1,0:T(8,128)(2,1)S(1)}, bf16[256,1536]{1,0:T(8,128)(2,1)S(1)}, u32[]{:S(2)}, u32[]{:S(2)}) %collective-permute-start.1) | collective-permute-done | bytes 786464 | tf_op jit(solution)/shard_map/ppermute | solution.py:375
  25.7 1.3 %collective-permute-start.3 = (bf16[256,1536]{1,0:T(8,128)(2,1)S(1)}, bf16[256,1536]{1,0:T(8,128)(2,1)S(1)}, u32[]{:S(2)}, u32[]{:S(2)}) collective-permute-start(bf16[256,1536]{1,0:T(8,128)(2,1)S(1)} %add.13.refs_0_), channel_id=1, source_target_pairs={{0,16},{8,24},{4,12},{20,28},{1,17},{9,25},{5,13},{21,29},{2,18},{... | collective-permute-start | bytes 2359304 | tf_op jit(solution)/shard_map/ppermute | solution.py:375
  27.0 0.6 chunk.11.refs_2_.refs_7_
  27.6 0.7 collective-permute-start.13
  28.3 10.3 %collective-permute-done.6.refs_1_ = bf16[256,1536]{1,0:T(8,128)(2,1)S(1)} collective-permute-done((bf16[256,1536]{1,0:T(8,128)(2,1)S(1)}, bf16[256,1536]{1,0:T(8,128)(2,1)S(1)}, u32[]{:S(2)}, u32[]{:S(2)}) %collective-permute-start.6) | collective-permute-done | bytes 786464 | tf_op jit(solution)/shard_map/ppermute | solution.py:376
  38.6 1.3 %collective-permute-start.12 = (bf16[1024,512]{1,0:T(8,128)(2,1)S(1)}, bf16[1024,512]{1,0:T(8,128)(2,1)S(1)}, u32[]{:S(2)}, u32[]{:S(2)}) collective-permute-start(bf16[1024,512]{1,0:T(8,128)(2,1)S(1)} %chunk.11.refs_2_.refs_7_), channel_id=1, source_target_pairs={{4,6},{6,5},{12,14},{14,13},{20,22},{22,21},{28,30},{30,29}} | collective-permute-start | bytes 3145736 | tf_op jit(solution)/shard_map/ppermute | solution.py:287
  39.9 0.1 add.16.refs_0_
  40.3 3.7 %collective-permute-start.4 = (bf16[256,1536]{1,0:T(8,128)(2,1)S(1)}, bf16[256,1536]{1,0:T(8,128)(2,1)S(1)}, u32[]{:S(2)}, u32[]{:S(2)}) collective-permute-start(bf16[256,1536]{1,0:T(8,128)(2,1)S(1)} %add.14.down_ref), channel_id=1, source_target_pairs={{0,4},{4,0},{8,12},{12,8},{16,20},{20,16},{24,28},{28,24},{1,5},{5... | collective-permute-start | bytes 2359304 | tf_op jit(solution)/shard_map/ppermute | solution.py:378
  43.9 0.7 collective-permute-start.15
  44.7 0.7 collective-permute-start.14
  45.4 15.0 %collective-permute-done.12.refs_8_.refs_5_ = bf16[1024,512]{1,0:T(8,128)(2,1)S(1)} collective-permute-done((bf16[1024,512]{1,0:T(8,128)(2,1)S(1)}, bf16[1024,512]{1,0:T(8,128)(2,1)S(1)}, u32[]{:S(2)}, u32[]{:S(2)}) %collective-permute-start.12) | collective-permute-done | bytes 1048608 | tf_op jit(solution)/shard_map/ppermute | solution.py:287
  60.4 0.7 collective-permute-start.17
  61.1 1.3 %collective-permute-start.16 = (bf16[1024,512]{1,0:T(8,128)(2,1)S(1)}, bf16[1024,512]{1,0:T(8,128)(2,1)S(1)}, u32[]{:S(2)}, u32[]{:S(2)}) collective-permute-start(bf16[1024,512]{1,0:T(8,128)(2,1)S(1)} %collective-permute-done.12.refs_8_.refs_5_), channel_id=1, source_target_pairs={{6,5},{14,13},{22,21},{30,29}} | collective-permute-start | bytes 3145736 | tf_op jit(solution)/shard_map/ppermute | solution.py:287
  62.6 2.3 %collective-permute-done.11.refs_2_ = bf16[256,1536]{1,0:T(8,128)(2,1)S(1)} collective-permute-done((bf16[256,1536]{1,0:T(8,128)(2,1)S(1)}, bf16[256,1536]{1,0:T(8,128)(2,1)S(1)}, u32[]{:S(2)}, u32[]{:S(2)}) %collective-permute-start.11) | collective-permute-done | bytes 786464 | tf_op jit(solution)/shard_map/ppermute | solution.py:380
  64.9 8.1 %update_rows.2 = (bf16[2048,1536]{1,0:T(8,128)(2,1)}, bf16[512,1536]{1,0:T(8,128)(2,1)S(1)}) custom-call(s32[4]{0:T(128)S(1)} %pad_add_fusion.place_ref, s32[1,512]{1,0:T(1,128)S(1)} %bitcast.5, bf16[2048,1536]{1,0:T(8,128)(2,1)} %refs_1_.1, bf16[256,1536]{1,0:T(8,128)(2,1)S(1)} %add.14.down_ref, bf16[256,1536]{1,0:T(8,128)(2,1)S(1)} %collective-permute-done.4.down_got_ref, ...), custom_call_target="tpu_custom_call" | custom-call | tf_op jit(solution)/shard_map/update_rows/pallas_call | solution.py:249
  73.0 5.1 %collective-permute-done.16.refs_6_ = bf16[1024,512]{1,0:T(8,128)(2,1)S(1)} collective-permute-done((bf16[1024,512]{1,0:T(8,128)(2,1)S(1)}, bf16[1024,512]{1,0:T(8,128)(2,1)S(1)}, u32[]{:S(2)}, u32[]{:S(2)}) %collective-permute-start.16) | collective-permute-done | bytes 1048608 | tf_op jit(solution)/shard_map/ppermute | solution.py:287
  78.2 7.1 %update_rows.3 = bf16[2048,1536]{1,0:T(8,128)(2,1)} custom-call(s32[4]{0:T(128)S(1)} %pad_add_fusion.place_ref, s32[1,512]{1,0:T(1,128)S(1)} %bitcast.6, bf16[2048,1536]{1,0:T(8,128)(2,1)} %refs_1_.1, bf16[256,1536]{1,0:T(8,128)(2,1)S(1)} %add.14.down_ref, ...), custom_call_target="tpu_custom_call", output_to_operand_aliasing={{}: (13, {})} | custom-call | tf_op jit(solution)/shard_map/update_rows/pallas_call | solution.py:249
  (26 shorter events, 0.7 us)
Async XLA Ops:
  0.1 3.5 %copy-start.1 = (s32[512]{0:T(512)S(1)}, s32[512]{0:T(512)}, u32[]{:S(2)}) copy-start(s32[512]{0:T(512)} %param.4) | copy-start | bytes 6148
  0.6 13.2 %collective-permute-start.2 = (bf16[1024,512]{1,0:T(8,128)(2,1)S(1)}, bf16[1024,512]{1,0:T(8,128)(2,1)S(1)}, u32[]{:S(2)}, u32[]{:S(2)}) collective-permute-start(bf16[1024,512]{1,0:T(8,128)(2,1)S(1)} %chunk.8), channel_id=1, source_target_pairs={{0,2},{8,10},{16,18},{24,26}} | collective-permute-start | bytes 3145736 | tf_op jit(solution)/shard_map/ppermute | solution.py:287
  2.8 9.1 %collective-permute-start = (bf16[256,1536]{1,0:T(8,128)(2,1)}, bf16[256,1536]{1,0:T(8,128)(2,1)S(1)}, u32[]{:S(2)}, u32[]{:S(2)}) collective-permute-start(bf16[256,1536]{1,0:T(8,128)(2,1)} %chunk.6), channel_id=1, source_target_pairs={{0,4},{1,5},{2,6},{3,7}} | collective-permute-start | bytes 2359304 | tf_op jit(solution)/shard_map/ppermute | solution.py:366
  9.9 6.0 %collective-permute-start.5 = (bf16[256,1536]{1,0:T(8,128)(2,1)S(1)}, bf16[256,1536]{1,0:T(8,128)(2,1)S(1)}, u32[]{:S(2)}, u32[]{:S(2)}) collective-permute-start(bf16[256,1536]{1,0:T(8,128)(2,1)S(1)} %get-tuple-element.10), channel_id=1, source_target_pairs={{0,4},{4,0},{8,12},{12,8},{16,20},{20,16},{24,28},{28,24},{1,5},{5... | collective-permute-start | bytes 2359304 | tf_op jit(solution)/shard_map/ppermute | solution.py:370
  11.2 15.8 %collective-permute-start.7 = (bf16[1024,512]{1,0:T(8,128)(2,1)S(1)}, bf16[1024,512]{1,0:T(8,128)(2,1)S(1)}, u32[]{:S(2)}, u32[]{:S(2)}) collective-permute-start(bf16[1024,512]{1,0:T(8,128)(2,1)S(1)} %chunk.10), channel_id=1, source_target_pairs={{4,6},{12,14},{20,22},{28,30}} | collective-permute-start | bytes 3145736 | tf_op jit(solution)/shard_map/ppermute | solution.py:287
  12.5 13.0 %collective-permute-start.1 = (bf16[256,1536]{1,0:T(8,128)(2,1)S(1)}, bf16[256,1536]{1,0:T(8,128)(2,1)S(1)}, u32[]{:S(2)}, u32[]{:S(2)}) collective-permute-start(bf16[256,1536]{1,0:T(8,128)(2,1)S(1)} %chunk.7.refs_0_), channel_id=1, source_target_pairs={{0,8},{4,20},{1,9},{5,21},{2,10},{6,22},{3,11},{7,23}} | collective-permute-start | bytes 2359304 | tf_op jit(solution)/shard_map/ppermute | solution.py:375
  14.4 25.5 %collective-permute-start.9 = (bf16[1024,512]{1,0:T(8,128)(2,1)S(1)}, bf16[1024,512]{1,0:T(8,128)(2,1)S(1)}, u32[]{:S(2)}, u32[]{:S(2)}) collective-permute-start(bf16[1024,512]{1,0:T(8,128)(2,1)S(1)} %chunk.9.refs_2_.refs_4_), channel_id=1, source_target_pairs={{2,3},{10,11},{18,19},{26,27}} | collective-permute-start | bytes 3145736 | tf_op jit(solution)/shard_map/ppermute | solution.py:287
  15.1 24.8 %collective-permute-start.8 = (bf16[1024,512]{1,0:T(8,128)(2,1)S(1)}, bf16[1024,512]{1,0:T(8,128)(2,1)S(1)}, u32[]{:S(2)}, u32[]{:S(2)}) collective-permute-start(bf16[1024,512]{1,0:T(8,128)(2,1)S(1)} %chunk.9.refs_2_.refs_4_), channel_id=1, source_target_pairs={{0,2},{2,1},{8,10},{10,9},{16,18},{18,17},{24,26},{26,25}} | collective-permute-start | bytes 3145736 | tf_op jit(solution)/shard_map/ppermute | solution.py:287
  16.0 22.6 %collective-permute-start.6 = (bf16[256,1536]{1,0:T(8,128)(2,1)S(1)}, bf16[256,1536]{1,0:T(8,128)(2,1)S(1)}, u32[]{:S(2)}, u32[]{:S(2)}) collective-permute-start(bf16[256,1536]{1,0:T(8,128)(2,1)S(1)} %add.15.refs_0_), channel_id=1, source_target_pairs={{0,8},{4,20},{8,0},{12,28},{16,24},{20,4},{24,16},{28,12},{1,9},{5... | collective-permute-start | bytes 2359304 | tf_op jit(solution)/shard_map/ppermute | solution.py:376
  25.7 14.5 %collective-permute-start.3 = (bf16[256,1536]{1,0:T(8,128)(2,1)S(1)}, bf16[256,1536]{1,0:T(8,128)(2,1)S(1)}, u32[]{:S(2)}, u32[]{:S(2)}) collective-permute-start(bf16[256,1536]{1,0:T(8,128)(2,1)S(1)} %add.13.refs_0_), channel_id=1, source_target_pairs={{0,16},{8,24},{4,12},{20,28},{1,17},{9,25},{5,13},{21,29},{2,18},{... | collective-permute-start | bytes 2359304 | tf_op jit(solution)/shard_map/ppermute | solution.py:375
  27.6 17.1 %collective-permute-start.13 = (bf16[1024,512]{1,0:T(8,128)(2,1)S(1)}, bf16[1024,512]{1,0:T(8,128)(2,1)S(1)}, u32[]{:S(2)}, u32[]{:S(2)}) collective-permute-start(bf16[1024,512]{1,0:T(8,128)(2,1)S(1)} %chunk.11.refs_2_.refs_7_), channel_id=1, source_target_pairs={{6,7},{14,15},{22,23},{30,31}} | collective-permute-start | bytes 3145736 | tf_op jit(solution)/shard_map/ppermute | solution.py:287
  38.6 21.8 %collective-permute-start.12 = (bf16[1024,512]{1,0:T(8,128)(2,1)S(1)}, bf16[1024,512]{1,0:T(8,128)(2,1)S(1)}, u32[]{:S(2)}, u32[]{:S(2)}) collective-permute-start(bf16[1024,512]{1,0:T(8,128)(2,1)S(1)} %chunk.11.refs_2_.refs_7_), channel_id=1, source_target_pairs={{4,6},{6,5},{12,14},{14,13},{20,22},{22,21},{28,30},{30,29}} | collective-permute-start | bytes 3145736 | tf_op jit(solution)/shard_map/ppermute | solution.py:287
  40.1 24.9 %copy-start = (bf16[512,512]{1,0:T(8,128)(2,1)S(1)}, bf16[512,512]{1,0:T(8,128)(2,1)}, u32[]{:S(2)}) copy-start(bf16[512,512]{1,0:T(8,128)(2,1)} %refs_0_.1) | copy-start | bytes 1572868
  40.1 21.1 %collective-permute-start.10 = (bf16[256,1536]{1,0:T(8,128)(2,1)S(1)}, bf16[256,1536]{1,0:T(8,128)(2,1)S(1)}, u32[]{:S(2)}, u32[]{:S(2)}) collective-permute-start(bf16[256,1536]{1,0:T(8,128)(2,1)S(1)} %add.16.refs_0_), channel_id=1, source_target_pairs={{0,16},{4,12},{8,24},{12,4},{16,0},{20,28},{24,8},{28,20},{1,17},{... | collective-permute-start | bytes 2359304 | tf_op jit(solution)/shard_map/ppermute | solution.py:376
  40.3 22.3 %collective-permute-start.4 = (bf16[256,1536]{1,0:T(8,128)(2,1)S(1)}, bf16[256,1536]{1,0:T(8,128)(2,1)S(1)}, u32[]{:S(2)}, u32[]{:S(2)}) collective-permute-start(bf16[256,1536]{1,0:T(8,128)(2,1)S(1)} %add.14.down_ref), channel_id=1, source_target_pairs={{0,4},{4,0},{8,12},{12,8},{16,20},{20,16},{24,28},{28,24},{1,5},{5... | collective-permute-start | bytes 2359304 | tf_op jit(solution)/shard_map/ppermute | solution.py:378
  43.9 29.1 %collective-permute-start.15 = (bf16[1024,512]{1,0:T(8,128)(2,1)S(1)}, bf16[1024,512]{1,0:T(8,128)(2,1)S(1)}, u32[]{:S(2)}, u32[]{:S(2)}) collective-permute-start(bf16[1024,512]{1,0:T(8,128)(2,1)S(1)} %collective-permute-done.8.refs_3_.refs_5_.refs_2_), channel_id=1, source_target_pairs={{2,3},{10,11},{18,19},{26,27}} | collective-permute-start | bytes 3145736 | tf_op jit(solution)/shard_map/ppermute | solution.py:287
  44.7 28.3 %collective-permute-start.14 = (bf16[1024,512]{1,0:T(8,128)(2,1)S(1)}, bf16[1024,512]{1,0:T(8,128)(2,1)S(1)}, u32[]{:S(2)}, u32[]{:S(2)}) collective-permute-start(bf16[1024,512]{1,0:T(8,128)(2,1)S(1)} %collective-permute-done.8.refs_3_.refs_5_.refs_2_), channel_id=1, source_target_pairs={{2,1},{10,9},{18,17},{26,25}} | collective-permute-start | bytes 3145736 | tf_op jit(solution)/shard_map/ppermute | solution.py:287
  60.4 12.6 %collective-permute-start.17 = (bf16[1024,512]{1,0:T(8,128)(2,1)S(1)}, bf16[1024,512]{1,0:T(8,128)(2,1)S(1)}, u32[]{:S(2)}, u32[]{:S(2)}) collective-permute-start(bf16[1024,512]{1,0:T(8,128)(2,1)S(1)} %collective-permute-done.12.refs_8_.refs_5_), channel_id=1, source_target_pairs={{6,7},{14,15},{22,23},{30,31}} | collective-permute-start | bytes 3145736 | tf_op jit(solution)/shard_map/ppermute | solution.py:287
  61.1 17.0 %collective-permute-start.16 = (bf16[1024,512]{1,0:T(8,128)(2,1)S(1)}, bf16[1024,512]{1,0:T(8,128)(2,1)S(1)}, u32[]{:S(2)}, u32[]{:S(2)}) collective-permute-start(bf16[1024,512]{1,0:T(8,128)(2,1)S(1)} %collective-permute-done.12.refs_8_.refs_5_), channel_id=1, source_target_pairs={{6,5},{14,13},{22,21},{30,29}} | collective-permute-start | bytes 3145736 | tf_op jit(solution)/shard_map/ppermute | solution.py:287
  62.5 2.4 %collective-permute-start.11 = (bf16[256,1536]{1,0:T(8,128)(2,1)S(1)}, bf16[256,1536]{1,0:T(8,128)(2,1)S(1)}, u32[]{:S(2)}, u32[]{:S(2)}) collective-permute-start(bf16[256,1536]{1,0:T(8,128)(2,1)S(1)} %add.17.refs_1_), channel_id=1, source_target_pairs={{0,4},{4,0},{8,12},{12,8},{16,20},{20,16},{24,28},{28,24},{1,5},{5... | collective-permute-start | bytes 2359304 | tf_op jit(solution)/shard_map/ppermute | solution.py:380

commit v11 on v10

--- a/solution.py
+++ b/solution.py
@@ -13,6 +13,7 @@
 DOWN_WEIGHTS, DOWN_AFTER = (0, 20), ((1, 0), (0, 0))
 PIECES = 2
 PICK_BLOCK, UPDATE_BLOCK = 256, 512
+COPIES = 4
 F32, BF16 = jnp.float32, jnp.bfloat16
 VMEM = pl.BlockSpec(memory_space=pltpu.VMEM)
 ANY = pl.BlockSpec(memory_space=pl.ANY)
@@ -27,17 +28,28 @@
     return pl.CostEstimate(flops=int(x*1.15e9), bytes_accessed=int(x*3.69e6), transcendentals=0)
 
 
+def row_copies(source, target, sem):
+    rows = target.shape[0] // COPIES
+    return [
+        pltpu.make_async_copy(
+            source.at[pl.ds(part * rows, rows)], target.at[pl.ds(part * rows, rows)], sem.at[part]
+        )
+        for part in range(COPIES)
+    ]
+
+
 def chunk_kernel(first_row, axis, core, place_ref, matrix_ref, *refs):
     out_ref, sem = refs[-2:]
     rows, width = out_ref.shape
 
     @pl.when((place_ref[axis] == 0) & (place_ref[2] == core))
     def _():
-        copy = pltpu.make_async_copy(
-            matrix_ref.at[pl.ds(first_row, rows), pl.ds(0, width)], out_ref, sem
-        )
-        copy.start()
-        copy.wait()
+        view = matrix_ref.at[pl.ds(first_row, rows), pl.ds(0, width)]
+        copies = row_copies(view, out_ref, sem)
+        for copy in copies:
+            copy.start()
+        for copy in copies:
+            copy.wait()
 
 
 def chunk(place, axis, core, matrix, first_row, rows, width, held=None, weight=0, after=()):
@@ -52,7 +64,7 @@
         in_specs=in_specs,
         out_specs=VMEM,
         out_shape=jax.ShapeDtypeStruct((rows, width), BF16),
-        scratch_shapes=[pltpu.SemaphoreType.DMA],
+        scratch_shapes=[pltpu.SemaphoreType.DMA((COPIES,))],
         input_output_aliases={} if held is None else {2: 0},
         compiler_params=SMALL,
         cost_estimate=weight_of(weight),
@@ -165,7 +177,8 @@
         for choice, view in enumerate(views):
             @pl.when(pick_source(col_place, core) == choice)
             def _():
-                action(pltpu.make_async_copy(view, panel_ref, sem))
+                for copy in row_copies(view, panel_ref, sem):
+                    action(copy)
 
     def fetch(number):
         there = columns(number, block)
@@ -259,7 +272,7 @@
             pltpu.VMEM((width, block), BF16),
             pltpu.SemaphoreType.DMA((cols // block,)),
             pltpu.SemaphoreType.DMA((cols // block,)),
-            pltpu.SemaphoreType.DMA,
+            pltpu.SemaphoreType.DMA((COPIES,)),
         ],
         input_output_aliases=aliases,
         compiler_params=LARGE,

time: 85.7 us -> 85.6 us (level)
  no operation moved by 1% of the time
where the time goes in v11:
time: 85.6 us; the launch traced here: 85.2 us
  waiting for transfers between devices  39.4 us (46%)
  Pallas kernels  26.2 us (31%)
  starting transfers between devices  18.9 us (22%)
    ppermute x10, waiting for transfers between devices, move(): return lax.ppermute(value, ('prow', 'pcol'), pairs)  19.7 us
    pallas_call x2, Pallas kernels, update(): pl.pallas_call(functools.partial(update_kernel, first_row, len(received),...  15.1 us
    ppermute x2, waiting for transfers between devices, per_device(): up_got = [lax.ppermute(up[0], 'prow', swap_pairs(n_prow, orders, step))]  10.1 us
    ppermute x10, starting transfers between devices, move(): return lax.ppermute(value, ('prow', 'pcol'), pairs)  8.37 us
    ppermute x2, waiting for transfers between devices, per_device(): down_got = lax.ppermute(down, 'prow', grow_pairs(orders, step))  7.33 us
    pallas_call x1, Pallas kernels, pick(): pl.pallas_call(pick_kernel, in_specs=[SMEM, VMEM, ANY] + [ANY] * len(afte...  6.15 us
    pallas_call x6, Pallas kernels, chunk(): pl.pallas_call(functools.partial(chunk_kernel, first_row, axis, core), in...  4.41 us
    ppermute x1, starting transfers between devices, per_device(): down_got = lax.ppermute(down, 'prow', swap_pairs(n_prow, cores, 0))  4.16 us
  transfers between devices with their start and end apart: 18, of which 5 were waited for; matrix products, arithmetic and copies ran while one was open for 0% of the time, Pallas kernels for 22%

profile of v11, /device:TPU:13, one launch (start us, length us, event | category | flops | bytes accessed | tf_op | source)
XLA Modules:
  0.0 85.2 jit_solution(8913152227547639176)
XLA Ops:
  0.1 0.6 chunk.8
  0.7 0.7 collective-permute-start.2
  1.4 1.5 %chunk.6 = bf16[256,1536]{1,0:T(8,128)(2,1)} custom-call(s32[4]{0:T(128)S(1)} %pad_add_fusion.place_ref, bf16[2048,1536]{1,0:T(8,128)(2,1)} %refs_1_.1), custom_call_target="tpu_custom_call" | custom-call | tf_op jit(solution)/shard_map/chunk/pallas_call | solution.py:62
  2.9 0.7 collective-permute-start
  3.6 0.1 copy.8.pivots_ref
  3.8 6.1 %pick_rows.1 = (bf16[256,1536]{1,0:T(8,128)(2,1)S(1)}, bf16[256,1536]{1,0:T(8,128)(2,1)S(1)}) custom-call(s32[4]{0:T(128)S(1)} %pad_add_fusion.place_ref, s32[512,1]{1,0:T(8,128)S(1)} %copy.8.pivots_ref, bf16[2048,1536]{1,0:T(8,128)(2,1)} %refs_1_.1), custom_call_target="tpu_custom_call" | custom-call | tf_op jit(solution)/shard_map/pick_rows/pallas_call | solution.py:112
  10.0 0.7 collective-permute-start.5
  10.7 0.6 chunk.10
  11.3 0.7 collective-permute-start.7
  12.0 0.6 chunk.7.refs_0_
  12.6 1.3 %collective-permute-start.1 = (bf16[256,1536]{1,0:T(8,128)(2,1)S(1)}, bf16[256,1536]{1,0:T(8,128)(2,1)S(1)}, u32[]{:S(2)}, u32[]{:S(2)}) collective-permute-start(bf16[256,1536]{1,0:T(8,128)(2,1)S(1)} %chunk.7.refs_0_), channel_id=1, source_target_pairs={{0,8},{4,20},{1,9},{5,21},{2,10},{6,22},{3,11},{7,23}} | collective-permute-start | bytes 2359304 | tf_op jit(solution)/shard_map/ppermute | solution.py:388
  13.9 0.6 chunk.9.refs_2_.refs_4_
  14.5 0.7 collective-permute-start.9
  15.3 0.7 collective-permute-start.8
  16.1 2.2 %collective-permute-start.6 = (bf16[256,1536]{1,0:T(8,128)(2,1)S(1)}, bf16[256,1536]{1,0:T(8,128)(2,1)S(1)}, u32[]{:S(2)}, u32[]{:S(2)}) collective-permute-start(bf16[256,1536]{1,0:T(8,128)(2,1)S(1)} %add.15.refs_0_), channel_id=1, source_target_pairs={{0,8},{4,20},{8,0},{12,28},{16,24},{20,4},{24,16},{28,12},{1,9},{5... | collective-permute-start | bytes 2359304 | tf_op jit(solution)/shard_map/ppermute | solution.py:389
  18.3 7.3 %collective-permute-done.1.refs_1_ = bf16[256,1536]{1,0:T(8,128)(2,1)S(1)} collective-permute-done((bf16[256,1536]{1,0:T(8,128)(2,1)S(1)}, bf16[256,1536]{1,0:T(8,128)(2,1)S(1)}, u32[]{:S(2)}, u32[]{:S(2)}) %collective-permute-start.1) | collective-permute-done | bytes 786464 | tf_op jit(solution)/shard_map/ppermute | solution.py:388
  25.8 1.3 %collective-permute-start.3 = (bf16[256,1536]{1,0:T(8,128)(2,1)S(1)}, bf16[256,1536]{1,0:T(8,128)(2,1)S(1)}, u32[]{:S(2)}, u32[]{:S(2)}) collective-permute-start(bf16[256,1536]{1,0:T(8,128)(2,1)S(1)} %add.13.refs_0_), channel_id=1, source_target_pairs={{0,16},{8,24},{4,12},{20,28},{1,17},{9,25},{5,13},{21,29},{2,18},{... | collective-permute-start | bytes 2359304 | tf_op jit(solution)/shard_map/ppermute | solution.py:388
  27.1 0.6 chunk.11.refs_2_.refs_7_
  27.7 0.7 collective-permute-start.13
  28.5 10.1 %collective-permute-done.6.refs_1_ = bf16[256,1536]{1,0:T(8,128)(2,1)S(1)} collective-permute-done((bf16[256,1536]{1,0:T(8,128)(2,1)S(1)}, bf16[256,1536]{1,0:T(8,128)(2,1)S(1)}, u32[]{:S(2)}, u32[]{:S(2)}) %collective-permute-start.6) | collective-permute-done | bytes 786464 | tf_op jit(solution)/shard_map/ppermute | solution.py:389
  38.6 1.3 %collective-permute-start.12 = (bf16[1024,512]{1,0:T(8,128)(2,1)S(1)}, bf16[1024,512]{1,0:T(8,128)(2,1)S(1)}, u32[]{:S(2)}, u32[]{:S(2)}) collective-permute-start(bf16[1024,512]{1,0:T(8,128)(2,1)S(1)} %chunk.11.refs_2_.refs_7_), channel_id=1, source_target_pairs={{4,6},{6,5},{12,14},{14,13},{20,22},{22,21},{28,30},{30,29}} | collective-permute-start | bytes 3145736 | tf_op jit(solution)/shard_map/ppermute | solution.py:300
  39.9 0.1 add.16.refs_0_
  40.2 4.2 %collective-permute-start.4 = (bf16[256,1536]{1,0:T(8,128)(2,1)S(1)}, bf16[256,1536]{1,0:T(8,128)(2,1)S(1)}, u32[]{:S(2)}, u32[]{:S(2)}) collective-permute-start(bf16[256,1536]{1,0:T(8,128)(2,1)S(1)} %add.14.down_ref), channel_id=1, source_target_pairs={{0,4},{4,0},{8,12},{12,8},{16,20},{20,16},{24,28},{28,24},{1,5},{5... | collective-permute-start | bytes 2359304 | tf_op jit(solution)/shard_map/ppermute | solution.py:391
  44.4 0.7 collective-permute-start.15
  45.1 0.7 collective-permute-start.14
  45.8 14.0 %collective-permute-done.12.refs_8_.refs_5_ = bf16[1024,512]{1,0:T(8,128)(2,1)S(1)} collective-permute-done((bf16[1024,512]{1,0:T(8,128)(2,1)S(1)}, bf16[1024,512]{1,0:T(8,128)(2,1)S(1)}, u32[]{:S(2)}, u32[]{:S(2)}) %collective-permute-start.12) | collective-permute-done | bytes 1048608 | tf_op jit(solution)/shard_map/ppermute | solution.py:300
  59.9 0.7 collective-permute-start.17
  60.6 1.3 %collective-permute-start.16 = (bf16[1024,512]{1,0:T(8,128)(2,1)S(1)}, bf16[1024,512]{1,0:T(8,128)(2,1)S(1)}, u32[]{:S(2)}, u32[]{:S(2)}) collective-permute-start(bf16[1024,512]{1,0:T(8,128)(2,1)S(1)} %collective-permute-done.12.refs_8_.refs_5_), channel_id=1, source_target_pairs={{6,5},{14,13},{22,21},{30,29}} | collective-permute-start | bytes 3145736 | tf_op jit(solution)/shard_map/ppermute | solution.py:300
  62.1 2.3 %collective-permute-done.11.refs_2_ = bf16[256,1536]{1,0:T(8,128)(2,1)S(1)} collective-permute-done((bf16[256,1536]{1,0:T(8,128)(2,1)S(1)}, bf16[256,1536]{1,0:T(8,128)(2,1)S(1)}, u32[]{:S(2)}, u32[]{:S(2)}) %collective-permute-start.11) | collective-permute-done | bytes 786464 | tf_op jit(solution)/shard_map/ppermute | solution.py:393
  64.4 8.0 %update_rows.2 = (bf16[2048,1536]{1,0:T(8,128)(2,1)}, bf16[512,1536]{1,0:T(8,128)(2,1)S(1)}) custom-call(s32[4]{0:T(128)S(1)} %pad_add_fusion.place_ref, s32[1,512]{1,0:T(1,128)S(1)} %bitcast.5, bf16[2048,1536]{1,0:T(8,128)(2,1)} %refs_1_.1, bf16[256,1536]{1,0:T(8,128)(2,1)S(1)} %add.14.down_ref, bf16[256,1536]{1,0:T(8,128)(2,1)S(1)} %collective-permute-done.4.down_got_ref, ...), custom_call_target="tpu_custom_call" | custom-call | tf_op jit(solution)/shard_map/update_rows/pallas_call | solution.py:262
  72.5 5.7 %collective-permute-done.16.refs_6_ = bf16[1024,512]{1,0:T(8,128)(2,1)S(1)} collective-permute-done((bf16[1024,512]{1,0:T(8,128)(2,1)S(1)}, bf16[1024,512]{1,0:T(8,128)(2,1)S(1)}, u32[]{:S(2)}, u32[]{:S(2)}) %collective-permute-start.16) | collective-permute-done | bytes 1048608 | tf_op jit(solution)/shard_map/ppermute | solution.py:300
  78.1 7.1 %update_rows.3 = bf16[2048,1536]{1,0:T(8,128)(2,1)} custom-call(s32[4]{0:T(128)S(1)} %pad_add_fusion.place_ref, s32[1,512]{1,0:T(1,128)S(1)} %bitcast.6, bf16[2048,1536]{1,0:T(8,128)(2,1)} %refs_1_.1, bf16[256,1536]{1,0:T(8,128)(2,1)S(1)} %add.14.down_ref, ...), custom_call_target="tpu_custom_call", output_to_operand_aliasing={{}: (13, {})} | custom-call | tf_op jit(solution)/shard_map/update_rows/pallas_call | solution.py:262
  (26 shorter events, 0.7 us)
Async XLA Ops:
  0.1 3.5 %copy-start.1 = (s32[512]{0:T(512)S(1)}, s32[512]{0:T(512)}, u32[]{:S(2)}) copy-start(s32[512]{0:T(512)} %param.4) | copy-start | bytes 6148
  0.7 13.3 %collective-permute-start.2 = (bf16[1024,512]{1,0:T(8,128)(2,1)S(1)}, bf16[1024,512]{1,0:T(8,128)(2,1)S(1)}, u32[]{:S(2)}, u32[]{:S(2)}) collective-permute-start(bf16[1024,512]{1,0:T(8,128)(2,1)S(1)} %chunk.8), channel_id=1, source_target_pairs={{0,2},{8,10},{16,18},{24,26}} | collective-permute-start | bytes 3145736 | tf_op jit(solution)/shard_map/ppermute | solution.py:300
  2.9 9.1 %collective-permute-start = (bf16[256,1536]{1,0:T(8,128)(2,1)}, bf16[256,1536]{1,0:T(8,128)(2,1)S(1)}, u32[]{:S(2)}, u32[]{:S(2)}) collective-permute-start(bf16[256,1536]{1,0:T(8,128)(2,1)} %chunk.6), channel_id=1, source_target_pairs={{0,4},{1,5},{2,6},{3,7}} | collective-permute-start | bytes 2359304 | tf_op jit(solution)/shard_map/ppermute | solution.py:379
  10.0 6.1 %collective-permute-start.5 = (bf16[256,1536]{1,0:T(8,128)(2,1)S(1)}, bf16[256,1536]{1,0:T(8,128)(2,1)S(1)}, u32[]{:S(2)}, u32[]{:S(2)}) collective-permute-start(bf16[256,1536]{1,0:T(8,128)(2,1)S(1)} %get-tuple-element.10), channel_id=1, source_target_pairs={{0,4},{4,0},{8,12},{12,8},{16,20},{20,16},{24,28},{28,24},{1,5},{5... | collective-permute-start | bytes 2359304 | tf_op jit(solution)/shard_map/ppermute | solution.py:383
  11.3 15.8 %collective-permute-start.7 = (bf16[1024,512]{1,0:T(8,128)(2,1)S(1)}, bf16[1024,512]{1,0:T(8,128)(2,1)S(1)}, u32[]{:S(2)}, u32[]{:S(2)}) collective-permute-start(bf16[1024,512]{1,0:T(8,128)(2,1)S(1)} %chunk.10), channel_id=1, source_target_pairs={{4,6},{12,14},{20,22},{28,30}} | collective-permute-start | bytes 3145736 | tf_op jit(solution)/shard_map/ppermute | solution.py:300
  12.6 13.0 %collective-permute-start.1 = (bf16[256,1536]{1,0:T(8,128)(2,1)S(1)}, bf16[256,1536]{1,0:T(8,128)(2,1)S(1)}, u32[]{:S(2)}, u32[]{:S(2)}) collective-permute-start(bf16[256,1536]{1,0:T(8,128)(2,1)S(1)} %chunk.7.refs_0_), channel_id=1, source_target_pairs={{0,8},{4,20},{1,9},{5,21},{2,10},{6,22},{3,11},{7,23}} | collective-permute-start | bytes 2359304 | tf_op jit(solution)/shard_map/ppermute | solution.py:388
  14.5 25.3 %collective-permute-start.9 = (bf16[1024,512]{1,0:T(8,128)(2,1)S(1)}, bf16[1024,512]{1,0:T(8,128)(2,1)S(1)}, u32[]{:S(2)}, u32[]{:S(2)}) collective-permute-start(bf16[1024,512]{1,0:T(8,128)(2,1)S(1)} %chunk.9.refs_2_.refs_4_), channel_id=1, source_target_pairs={{2,3},{10,11},{18,19},{26,27}} | collective-permute-start | bytes 3145736 | tf_op jit(solution)/shard_map/ppermute | solution.py:300
  15.3 24.6 %collective-permute-start.8 = (bf16[1024,512]{1,0:T(8,128)(2,1)S(1)}, bf16[1024,512]{1,0:T(8,128)(2,1)S(1)}, u32[]{:S(2)}, u32[]{:S(2)}) collective-permute-start(bf16[1024,512]{1,0:T(8,128)(2,1)S(1)} %chunk.9.refs_2_.refs_4_), channel_id=1, source_target_pairs={{0,2},{2,1},{8,10},{10,9},{16,18},{18,17},{24,26},{26,25}} | collective-permute-start | bytes 3145736 | tf_op jit(solution)/shard_map/ppermute | solution.py:300
  16.1 22.4 %collective-permute-start.6 = (bf16[256,1536]{1,0:T(8,128)(2,1)S(1)}, bf16[256,1536]{1,0:T(8,128)(2,1)S(1)}, u32[]{:S(2)}, u32[]{:S(2)}) collective-permute-start(bf16[256,1536]{1,0:T(8,128)(2,1)S(1)} %add.15.refs_0_), channel_id=1, source_target_pairs={{0,8},{4,20},{8,0},{12,28},{16,24},{20,4},{24,16},{28,12},{1,9},{5... | collective-permute-start | bytes 2359304 | tf_op jit(solution)/shard_map/ppermute | solution.py:389
  25.8 14.3 %collective-permute-start.3 = (bf16[256,1536]{1,0:T(8,128)(2,1)S(1)}, bf16[256,1536]{1,0:T(8,128)(2,1)S(1)}, u32[]{:S(2)}, u32[]{:S(2)}) collective-permute-start(bf16[256,1536]{1,0:T(8,128)(2,1)S(1)} %add.13.refs_0_), channel_id=1, source_target_pairs={{0,16},{8,24},{4,12},{20,28},{1,17},{9,25},{5,13},{21,29},{2,18},{... | collective-permute-start | bytes 2359304 | tf_op jit(solution)/shard_map/ppermute | solution.py:388
  27.7 17.4 %collective-permute-start.13 = (bf16[1024,512]{1,0:T(8,128)(2,1)S(1)}, bf16[1024,512]{1,0:T(8,128)(2,1)S(1)}, u32[]{:S(2)}, u32[]{:S(2)}) collective-permute-start(bf16[1024,512]{1,0:T(8,128)(2,1)S(1)} %chunk.11.refs_2_.refs_7_), channel_id=1, source_target_pairs={{6,7},{14,15},{22,23},{30,31}} | collective-permute-start | bytes 3145736 | tf_op jit(solution)/shard_map/ppermute | solution.py:300
  38.6 21.3 %collective-permute-start.12 = (bf16[1024,512]{1,0:T(8,128)(2,1)S(1)}, bf16[1024,512]{1,0:T(8,128)(2,1)S(1)}, u32[]{:S(2)}, u32[]{:S(2)}) collective-permute-start(bf16[1024,512]{1,0:T(8,128)(2,1)S(1)} %chunk.11.refs_2_.refs_7_), channel_id=1, source_target_pairs={{4,6},{6,5},{12,14},{14,13},{20,22},{22,21},{28,30},{30,29}} | collective-permute-start | bytes 3145736 | tf_op jit(solution)/shard_map/ppermute | solution.py:300
  40.0 24.4 %copy-start = (bf16[512,512]{1,0:T(8,128)(2,1)S(1)}, bf16[512,512]{1,0:T(8,128)(2,1)}, u32[]{:S(2)}) copy-start(bf16[512,512]{1,0:T(8,128)(2,1)} %refs_0_.1) | copy-start | bytes 1572868
  40.0 20.6 %collective-permute-start.10 = (bf16[256,1536]{1,0:T(8,128)(2,1)S(1)}, bf16[256,1536]{1,0:T(8,128)(2,1)S(1)}, u32[]{:S(2)}, u32[]{:S(2)}) collective-permute-start(bf16[256,1536]{1,0:T(8,128)(2,1)S(1)} %add.16.refs_0_), channel_id=1, source_target_pairs={{0,16},{4,12},{8,24},{12,4},{16,0},{20,28},{24,8},{28,20},{1,17},{... | collective-permute-start | bytes 2359304 | tf_op jit(solution)/shard_map/ppermute | solution.py:389
  40.2 21.8 %collective-permute-start.4 = (bf16[256,1536]{1,0:T(8,128)(2,1)S(1)}, bf16[256,1536]{1,0:T(8,128)(2,1)S(1)}, u32[]{:S(2)}, u32[]{:S(2)}) collective-permute-start(bf16[256,1536]{1,0:T(8,128)(2,1)S(1)} %add.14.down_ref), channel_id=1, source_target_pairs={{0,4},{4,0},{8,12},{12,8},{16,20},{20,16},{24,28},{28,24},{1,5},{5... | collective-permute-start | bytes 2359304 | tf_op jit(solution)/shard_map/ppermute | solution.py:391
  44.4 28.1 %collective-permute-start.15 = (bf16[1024,512]{1,0:T(8,128)(2,1)S(1)}, bf16[1024,512]{1,0:T(8,128)(2,1)S(1)}, u32[]{:S(2)}, u32[]{:S(2)}) collective-permute-start(bf16[1024,512]{1,0:T(8,128)(2,1)S(1)} %collective-permute-done.8.refs_3_.refs_5_.refs_2_), channel_id=1, source_target_pairs={{2,3},{10,11},{18,19},{26,27}} | collective-permute-start | bytes 3145736 | tf_op jit(solution)/shard_map/ppermute | solution.py:300
  45.1 27.3 %collective-permute-start.14 = (bf16[1024,512]{1,0:T(8,128)(2,1)S(1)}, bf16[1024,512]{1,0:T(8,128)(2,1)S(1)}, u32[]{:S(2)}, u32[]{:S(2)}) collective-permute-start(bf16[1024,512]{1,0:T(8,128)(2,1)S(1)} %collective-permute-done.8.refs_3_.refs_5_.refs_2_), channel_id=1, source_target_pairs={{2,1},{10,9},{18,17},{26,25}} | collective-permute-start | bytes 3145736 | tf_op jit(solution)/shard_map/ppermute | solution.py:300
  59.9 12.6 %collective-permute-start.17 = (bf16[1024,512]{1,0:T(8,128)(2,1)S(1)}, bf16[1024,512]{1,0:T(8,128)(2,1)S(1)}, u32[]{:S(2)}, u32[]{:S(2)}) collective-permute-start(bf16[1024,512]{1,0:T(8,128)(2,1)S(1)} %collective-permute-done.12.refs_8_.refs_5_), channel_id=1, source_target_pairs={{6,7},{14,15},{22,23},{30,31}} | collective-permute-start | bytes 3145736 | tf_op jit(solution)/shard_map/ppermute | solution.py:300
  60.6 17.5 %collective-permute-start.16 = (bf16[1024,512]{1,0:T(8,128)(2,1)S(1)}, bf16[1024,512]{1,0:T(8,128)(2,1)S(1)}, u32[]{:S(2)}, u32[]{:S(2)}) collective-permute-start(bf16[1024,512]{1,0:T(8,128)(2,1)S(1)} %collective-permute-done.12.refs_8_.refs_5_), channel_id=1, source_target_pairs={{6,5},{14,13},{22,21},{30,29}} | collective-permute-start | bytes 3145736 | tf_op jit(solution)/shard_map/ppermute | solution.py:300
  62.0 2.4 %collective-permute-start.11 = (bf16[256,1536]{1,0:T(8,128)(2,1)S(1)}, bf16[256,1536]{1,0:T(8,128)(2,1)S(1)}, u32[]{:S(2)}, u32[]{:S(2)}) collective-permute-start(bf16[256,1536]{1,0:T(8,128)(2,1)S(1)} %add.17.refs_1_), channel_id=1, source_target_pairs={{0,4},{4,0},{8,12},{12,8},{16,20},{20,16},{24,28},{28,24},{1,5},{5... | collective-permute-start | bytes 2359304 | tf_op jit(solution)/shard_map/ppermute | solution.py:393

commit v12 on v11

--- a/solution.py
+++ b/solution.py
@@ -281,6 +281,150 @@
     )(*operands)
 
 
+def swap_kernel(first_row, place_ref, pivots_ref, matrix_ref, down_ref, down_got_ref, out_ref,
+                onehot_ref, right_ref, keep_ref, sem):
+    count, cols = out_ref.shape
+    width = pivots_ref.shape[1]
+    row_place, col_place, core, rows = (place_ref[i] for i in range(4))
+    block = min(UPDATE_BLOCK, cols)
+    piece = min(count, 512)
+
+    def fetch(number):
+        there = columns(number, block)
+        return pltpu.make_async_copy(
+            matrix_ref.at[pl.ds(first_row, count), there], out_ref.at[:, there], sem.at[number]
+        )
+
+    for number in range(cols // block):
+        fetch(number).start()
+    for start in range(0, count, piece):
+        these = slice(start, start + piece)
+        row = lax.broadcasted_iota(jnp.int32, (piece, width), 0)
+        row = row + (row_place * rows + first_row + start)
+        onehot = jnp.where(pivots_ref[...] == row, 1.0, 0.0)
+        onehot_ref[these] = onehot.astype(BF16)
+        has_pivot = jnp.max(onehot, axis=1, keepdims=True)
+        keep_ref[these] = jnp.broadcast_to(1.0 - has_pivot, (piece, 128))
+
+    @pl.loop(0, cols // block)
+    def _(number):
+        there = columns(number, block)
+        fetch(number).wait()
+
+        @pl.when((col_place > 0) | (number * block >= width))
+        def _():
+            in_order(core, down_ref[:, there], down_got_ref[:, there], right_ref)
+            right = right_ref[...]
+            for start in range(0, count, piece):
+                these = slice(start, start + piece)
+                moved = jnp.dot(onehot_ref[these], right, preferred_element_type=F32)
+                keep = jnp.concatenate([keep_ref[these]] * (block // 128), axis=1)
+                kept = out_ref[these, there].astype(F32) * keep
+                out_ref[these, there] = (kept + moved).astype(BF16)
+
+
+def swap(group, place, pivots, matrix, down, down_got):
+    first_row, count = group
+    cols = matrix.shape[1]
+    width = pivots.shape[0]
+    block = min(UPDATE_BLOCK, cols)
+    return pl.pallas_call(
+        functools.partial(swap_kernel, first_row),
+        in_specs=[SMEM, VMEM, ANY, VMEM, VMEM],
+        out_specs=VMEM,
+        out_shape=jax.ShapeDtypeStruct((count, cols), BF16),
+        scratch_shapes=[
+            pltpu.VMEM((count, width), BF16),
+            pltpu.VMEM((width, block), BF16),
+            pltpu.VMEM((count, 128), F32),
+            pltpu.SemaphoreType.DMA((cols // block,)),
+        ],
+        compiler_params=LARGE,
+        cost_estimate=FREE,
+        name="swap_rows",
+    )(place, pivots[None, :], matrix, down, down_got)
+
+
+def finish_kernel(first_row, per_group, pick_source, place_ref, matrix_ref, swapped_ref,
+                  upper_ref, *refs):
+    sources = [matrix_ref, *refs[:per_group]]
+    out_ref, rows_ref, panel_ref, out_sem, sem = refs[-5:]
+    count, width = panel_ref.shape
+    cols = rows_ref.shape[1]
+    row_place, col_place, core = (place_ref[i] for i in range(3))
+    block = min(UPDATE_BLOCK, cols)
+    piece = min(count, 512)
+    here = pl.ds(first_row, count)
+
+    def fetch_panel(action):
+        views = [sources[0].at[here, pl.ds(0, width)], *sources[1:]]
+        for choice, view in enumerate(views):
+            @pl.when(pick_source(col_place, core) == choice)
+            def _():
+                for copy in row_copies(view, panel_ref, sem):
+                    action(copy)
+
+    def store(number):
+        there = columns(number, block)
+        return pltpu.make_async_copy(
+            rows_ref.at[:, there], out_ref.at[here, there], out_sem.at[number]
+        )
+
+    fetch_panel(lambda copy: copy.start())
+    fetch_panel(lambda copy: copy.wait())
+
+    @pl.loop(0, cols // block)
+    def _(number):
+        there = columns(number, block)
+        updated = (col_place > 0) | (number * block >= width)
+
+        @pl.when(jnp.logical_not(updated))
+        def _():
+            rows_ref[:, there] = swapped_ref[:, there]
+
+        @pl.when(updated)
+        def _():
+            upper = upper_ref[:, there]
+            for start in range(0, count, piece):
+                these = slice(start, start + piece)
+                product = jnp.dot(panel_ref[these], upper, preferred_element_type=F32)
+                left = swapped_ref[these, there].astype(F32) - product
+                rows_ref[these, there] = left.astype(BF16)
+            if first_row < width:
+                @pl.when(row_place == 0)
+                def _():
+                    rows_ref[: width - first_row, there] = upper[first_row:]
+
+        store(number).start()
+
+    for number in range(cols // block):
+        store(number).wait()
+
+
+def finish(group, pick_source, place, matrix, swapped, upper, received, out):
+    first_row, count = group
+    rows, cols = matrix.shape
+    width = upper.shape[0]
+    block = min(UPDATE_BLOCK, cols)
+    hbm = pl.BlockSpec(memory_space=pltpu.HBM)
+    return pl.pallas_call(
+        functools.partial(finish_kernel, first_row, len(received), pick_source),
+        in_specs=[SMEM, ANY, VMEM, VMEM] + [ANY] * len(received) + [hbm],
+        out_specs=hbm,
+        out_shape=jax.ShapeDtypeStruct((rows, cols), BF16),
+        scratch_shapes=[
+            pltpu.VMEM((count, cols), BF16),
+            pltpu.VMEM((count, width), BF16),
+            pltpu.SemaphoreType.DMA((cols // block,)),
+            pltpu.SemaphoreType.DMA((COPIES,)),
+        ],
+        input_output_aliases={4 + len(received): 0},
+        compiler_params=LARGE,
+        cost_estimate=FREE,
+        name="finish_rows",
+    )(place, matrix, swapped, upper, *received, out)
+
+
 def swap_pairs(size, orders, step):
     return [(i, i ^ (1 << orders[i & 1][step])) for i in range(size)]
 
@@ -396,9 +540,12 @@
     received = [first + second for first, second in zip(*by_core)]
     common = (source_of(n_pcol, len(by_core[0][0])), place, pivots, matrix, down, down_got)
     out, upper = update(groups[0], *common, received[0], upper_terms=(unit_inverse, up, up_got))
-    for group, arrays in zip(groups[1:], received[1:]):
+    for group, arrays in zip(groups[1:-1], received[1:-1]):
         (out,) = update(group, *common, arrays, upper=upper, out=out)
-    return out
+    swapped = swap(groups[-1], *common[1:])
+    return finish(
+        groups[-1], common[0], place, matrix, swapped, upper, received[-1], out
+    )
 
 
 def solution(mesh):

time: 85.6 us -> 82.4 us (0.963)
  waiting for transfers between devices: 39.4 us -> 35.3 us
  Pallas kernels: 26.2 us -> 27.2 us
    pallas_call x0 -> x2, Pallas kernels: none -> 8.06 us  [the longest x1 4.19 us: swap(): pl.pallas_call(functools.partial(swap_kernel, first_row), in_specs=[SMEM,...]
    pallas_call x2 -> x1, Pallas kernels: 15.1 us -> 8.04 us  [update(): pl.pallas_call(functools.partial(update_kernel, first_row, len(received),...]
    ppermute x1, waiting for transfers between devices: 2.27 us -> 0.01 us  [per_device(): up_got = lax.ppermute(up, 'prow', swap_pairs(n_prow, cores, 0))]
    ppermute x10, waiting for transfers between devices: 19.7 us -> 17.8 us  [move(): return lax.ppermute(value, ('prow', 'pcol'), pairs)]
  transfers between devices with their start and end apart: 18 -> 18, of which waited for: 5 -> 4; matrix products, arithmetic and copies ran while one was open for 0% -> 0% of each run, Pallas kernels for 22% -> 28%
where the time goes in v12:
time: 82.4 us; the launch traced here: 82 us
  waiting for transfers between devices  35.3 us (43%)
  Pallas kernels  27.2 us (33%)
  starting transfers between devices  18.9 us (23%)
    ppermute x10, waiting for transfers between devices, move(): return lax.ppermute(value, ('prow', 'pcol'), pairs)  17.8 us
    ppermute x2, waiting for transfers between devices, per_device(): up_got = [lax.ppermute(up[0], 'prow', swap_pairs(n_prow, orders, step))]  10.1 us
    ppermute x10, starting transfers between devices, move(): return lax.ppermute(value, ('prow', 'pcol'), pairs)  8.37 us
    pallas_call x1, Pallas kernels, update(): pl.pallas_call(functools.partial(update_kernel, first_row, len(received),...  8.04 us
    ppermute x2, waiting for transfers between devices, per_device(): down_got = lax.ppermute(down, 'prow', grow_pairs(orders, step))  7.34 us
    pallas_call x1, Pallas kernels, pick(): pl.pallas_call(pick_kernel, in_specs=[SMEM, VMEM, ANY] + [ANY] * len(afte...  6.15 us
    pallas_call x6, Pallas kernels, chunk(): pl.pallas_call(functools.partial(chunk_kernel, first_row, axis, core), in...  4.41 us
    pallas_call x1, Pallas kernels, swap(): pl.pallas_call(functools.partial(swap_kernel, first_row), in_specs=[SMEM,...  4.19 us
  transfers between devices with their start and end apart: 18, of which 4 were waited for; matrix products, arithmetic and copies ran while one was open for 0% of the time, Pallas kernels for 28%

profile of v12, /device:TPU:13, one launch (start us, length us, event | category | flops | bytes accessed | tf_op | source)
XLA Modules:
  0.0 82.0 jit_solution(12234146020521526601)
XLA Ops:
  0.1 0.6 chunk.8
  0.7 0.7 collective-permute-start.2
  1.4 1.5 %chunk.6 = bf16[256,1536]{1,0:T(8,128)(2,1)} custom-call(s32[4]{0:T(128)S(1)} %pad_add_fusion.place_ref, bf16[2048,1536]{1,0:T(8,128)(2,1)} %matrix_ref.19), custom_call_target="tpu_custom_call" | custom-call | tf_op jit(solution)/shard_map/chunk/pallas_call | solution.py:62
  2.9 0.7 collective-permute-start
  3.6 0.1 copy.8.pivots_ref
  3.8 6.1 %pick_rows.1 = (bf16[256,1536]{1,0:T(8,128)(2,1)S(1)}, bf16[256,1536]{1,0:T(8,128)(2,1)S(1)}) custom-call(s32[4]{0:T(128)S(1)} %pad_add_fusion.place_ref, s32[512,1]{1,0:T(8,128)S(1)} %copy.8.pivots_ref, bf16[2048,1536]{1,0:T(8,128)(2,1)} %matrix_ref.19), custom_call_target="tpu_custom_call" | custom-call | tf_op jit(solution)/shard_map/pick_rows/pallas_call | solution.py:112
  10.0 0.7 collective-permute-start.5
  10.7 0.6 chunk.10
  11.3 0.7 collective-permute-start.7
  12.0 0.6 chunk.7.refs_0_
  12.6 1.3 %collective-permute-start.1 = (bf16[256,1536]{1,0:T(8,128)(2,1)S(1)}, bf16[256,1536]{1,0:T(8,128)(2,1)S(1)}, u32[]{:S(2)}, u32[]{:S(2)}) collective-permute-start(bf16[256,1536]{1,0:T(8,128)(2,1)S(1)} %chunk.7.refs_0_), channel_id=1, source_target_pairs={{0,8},{4,20},{1,9},{5,21},{2,10},{6,22},{3,11},{7,23}} | collective-permute-start | bytes 2359304 | tf_op jit(solution)/shard_map/ppermute | solution.py:532
  13.9 0.6 chunk.9.refs_2_.refs_4_
  14.5 0.7 collective-permute-start.9
  15.3 0.7 collective-permute-start.8
  16.1 2.2 %collective-permute-start.6 = (bf16[256,1536]{1,0:T(8,128)(2,1)S(1)}, bf16[256,1536]{1,0:T(8,128)(2,1)S(1)}, u32[]{:S(2)}, u32[]{:S(2)}) collective-permute-start(bf16[256,1536]{1,0:T(8,128)(2,1)S(1)} %add.15.refs_0_), channel_id=1, source_target_pairs={{0,8},{4,20},{8,0},{12,28},{16,24},{20,4},{24,16},{28,12},{1,9},{5... | collective-permute-start | bytes 2359304 | tf_op jit(solution)/shard_map/ppermute | solution.py:533
  18.3 7.3 %collective-permute-done.1.refs_1_ = bf16[256,1536]{1,0:T(8,128)(2,1)S(1)} collective-permute-done((bf16[256,1536]{1,0:T(8,128)(2,1)S(1)}, bf16[256,1536]{1,0:T(8,128)(2,1)S(1)}, u32[]{:S(2)}, u32[]{:S(2)}) %collective-permute-start.1) | collective-permute-done | bytes 786464 | tf_op jit(solution)/shard_map/ppermute | solution.py:532
  25.8 1.3 %collective-permute-start.3 = (bf16[256,1536]{1,0:T(8,128)(2,1)S(1)}, bf16[256,1536]{1,0:T(8,128)(2,1)S(1)}, u32[]{:S(2)}, u32[]{:S(2)}) collective-permute-start(bf16[256,1536]{1,0:T(8,128)(2,1)S(1)} %add.13.refs_0_), channel_id=1, source_target_pairs={{0,16},{8,24},{4,12},{20,28},{1,17},{9,25},{5,13},{21,29},{2,18},{... | collective-permute-start | bytes 2359304 | tf_op jit(solution)/shard_map/ppermute | solution.py:532
  27.1 0.6 chunk.11.refs_2_.refs_7_
  27.7 0.7 collective-permute-start.13
  28.5 10.1 %collective-permute-done.6.refs_1_ = bf16[256,1536]{1,0:T(8,128)(2,1)S(1)} collective-permute-done((bf16[256,1536]{1,0:T(8,128)(2,1)S(1)}, bf16[256,1536]{1,0:T(8,128)(2,1)S(1)}, u32[]{:S(2)}, u32[]{:S(2)}) %collective-permute-start.6) | collective-permute-done | bytes 786464 | tf_op jit(solution)/shard_map/ppermute | solution.py:533
  38.6 1.3 %collective-permute-start.12 = (bf16[1024,512]{1,0:T(8,128)(2,1)S(1)}, bf16[1024,512]{1,0:T(8,128)(2,1)S(1)}, u32[]{:S(2)}, u32[]{:S(2)}) collective-permute-start(bf16[1024,512]{1,0:T(8,128)(2,1)S(1)} %chunk.11.refs_2_.refs_7_), channel_id=1, source_target_pairs={{4,6},{6,5},{12,14},{14,13},{20,22},{22,21},{28,30},{30,29}} | collective-permute-start | bytes 3145736 | tf_op jit(solution)/shard_map/ppermute | solution.py:444
  40.2 4.2 %collective-permute-start.4 = (bf16[256,1536]{1,0:T(8,128)(2,1)S(1)}, bf16[256,1536]{1,0:T(8,128)(2,1)S(1)}, u32[]{:S(2)}, u32[]{:S(2)}) collective-permute-start(bf16[256,1536]{1,0:T(8,128)(2,1)S(1)} %add.14.down_ref), channel_id=1, source_target_pairs={{0,4},{4,0},{8,12},{12,8},{16,20},{20,16},{24,28},{28,24},{1,5},{5... | collective-permute-start | bytes 2359304 | tf_op jit(solution)/shard_map/ppermute | solution.py:535
  44.4 0.7 collective-permute-start.15
  45.1 0.7 collective-permute-start.14
  45.8 14.0 %collective-permute-done.12.refs_8_.refs_3_ = bf16[1024,512]{1,0:T(8,128)(2,1)S(1)} collective-permute-done((bf16[1024,512]{1,0:T(8,128)(2,1)S(1)}, bf16[1024,512]{1,0:T(8,128)(2,1)S(1)}, u32[]{:S(2)}, u32[]{:S(2)}) %collective-permute-start.12) | collective-permute-done | bytes 1048608 | tf_op jit(solution)/shard_map/ppermute | solution.py:444
  59.8 0.7 collective-permute-start.17
  60.5 1.3 %collective-permute-start.16 = (bf16[1024,512]{1,0:T(8,128)(2,1)S(1)}, bf16[1024,512]{1,0:T(8,128)(2,1)S(1)}, u32[]{:S(2)}, u32[]{:S(2)}) collective-permute-start(bf16[1024,512]{1,0:T(8,128)(2,1)S(1)} %collective-permute-done.12.refs_8_.refs_3_), channel_id=1, source_target_pairs={{6,5},{14,13},{22,21},{30,29}} | collective-permute-start | bytes 3145736 | tf_op jit(solution)/shard_map/ppermute | solution.py:444
  61.8 0.1 add.17.refs_1_
  62.0 4.2 %swap_rows.1.swapped_ref = bf16[1024,1536]{1,0:T(8,128)(2,1)S(1)} custom-call(s32[4]{0:T(128)S(1)} %pad_add_fusion.place_ref, s32[1,512]{1,0:T(1,128)S(1)} %bitcast.5, bf16[2048,1536]{1,0:T(8,128)(2,1)} %matrix_ref.19, bf16[256,1536]{1,0:T(8,128)(2,1)S(1)} %add.14.down_ref, bf16[256,1536]{1,0:T(8,128)(2,1)S(1)} %collective-permute-done.4.down_got_ref), custom_call_target="tpu_custom_call" | custom-call | tf_op jit(solution)/shard_map/swap_rows/pallas_call | solution.py:331
  66.2 8.0 %update_rows.1 = (bf16[2048,1536]{1,0:T(8,128)(2,1)}, bf16[512,1536]{1,0:T(8,128)(2,1)S(1)}) custom-call(s32[4]{0:T(128)S(1)} %pad_add_fusion.place_ref, s32[1,512]{1,0:T(1,128)S(1)} %bitcast.6, bf16[2048,1536]{1,0:T(8,128)(2,1)} %matrix_ref.19, bf16[256,1536]{1,0:T(8,128)(2,1)S(1)} %add.14.down_ref, ...), custom_call_target="tpu_custom_call" | custom-call | tf_op jit(solution)/shard_map/update_rows/pallas_call | solution.py:262
  74.3 3.8 %collective-permute-done.16.refs_4_ = bf16[1024,512]{1,0:T(8,128)(2,1)S(1)} collective-permute-done((bf16[1024,512]{1,0:T(8,128)(2,1)S(1)}, bf16[1024,512]{1,0:T(8,128)(2,1)S(1)}, u32[]{:S(2)}, u32[]{:S(2)}) %collective-permute-start.16) | collective-permute-done | bytes 1048608 | tf_op jit(solution)/shard_map/ppermute | solution.py:444
  78.1 3.9 %finish_rows.1 = bf16[2048,1536]{1,0:T(8,128)(2,1)} custom-call(s32[4]{0:T(128)S(1)} %pad_add_fusion.place_ref, bf16[2048,1536]{1,0:T(8,128)(2,1)} %matrix_ref.19, bf16[1024,1536]{1,0:T(8,128)(2,1)S(1)} %swap_rows.1.swapped_ref, bf16[512,1536]{1,0:T(8,128)(2,1)S(1)} %get-tuple-element.11.upper_ref, ...), custom_call_target="tpu_custom_call", output_to_operand_aliasing={{}: (10, {})} | custom-call | tf_op jit(solution)/shard_map/finish_rows/pallas_call | solution.py:410
  (27 shorter events, 0.7 us)
Async XLA Ops:
  0.1 3.5 %copy-start.1 = (s32[512]{0:T(512)S(1)}, s32[512]{0:T(512)}, u32[]{:S(2)}) copy-start(s32[512]{0:T(512)} %param.4) | copy-start | bytes 6148
  0.7 13.3 %collective-permute-start.2 = (bf16[1024,512]{1,0:T(8,128)(2,1)S(1)}, bf16[1024,512]{1,0:T(8,128)(2,1)S(1)}, u32[]{:S(2)}, u32[]{:S(2)}) collective-permute-start(bf16[1024,512]{1,0:T(8,128)(2,1)S(1)} %chunk.8), channel_id=1, source_target_pairs={{0,2},{8,10},{16,18},{24,26}} | collective-permute-start | bytes 3145736 | tf_op jit(solution)/shard_map/ppermute | solution.py:444
  2.9 9.1 %collective-permute-start = (bf16[256,1536]{1,0:T(8,128)(2,1)}, bf16[256,1536]{1,0:T(8,128)(2,1)S(1)}, u32[]{:S(2)}, u32[]{:S(2)}) collective-permute-start(bf16[256,1536]{1,0:T(8,128)(2,1)} %chunk.6), channel_id=1, source_target_pairs={{0,4},{1,5},{2,6},{3,7}} | collective-permute-start | bytes 2359304 | tf_op jit(solution)/shard_map/ppermute | solution.py:523
  10.0 6.1 %collective-permute-start.5 = (bf16[256,1536]{1,0:T(8,128)(2,1)S(1)}, bf16[256,1536]{1,0:T(8,128)(2,1)S(1)}, u32[]{:S(2)}, u32[]{:S(2)}) collective-permute-start(bf16[256,1536]{1,0:T(8,128)(2,1)S(1)} %get-tuple-element.10), channel_id=1, source_target_pairs={{0,4},{4,0},{8,12},{12,8},{16,20},{20,16},{24,28},{28,24},{1,5},{5... | collective-permute-start | bytes 2359304 | tf_op jit(solution)/shard_map/ppermute | solution.py:527
  11.3 15.8 %collective-permute-start.7 = (bf16[1024,512]{1,0:T(8,128)(2,1)S(1)}, bf16[1024,512]{1,0:T(8,128)(2,1)S(1)}, u32[]{:S(2)}, u32[]{:S(2)}) collective-permute-start(bf16[1024,512]{1,0:T(8,128)(2,1)S(1)} %chunk.10), channel_id=1, source_target_pairs={{4,6},{12,14},{20,22},{28,30}} | collective-permute-start | bytes 3145736 | tf_op jit(solution)/shard_map/ppermute | solution.py:444
  12.6 13.0 %collective-permute-start.1 = (bf16[256,1536]{1,0:T(8,128)(2,1)S(1)}, bf16[256,1536]{1,0:T(8,128)(2,1)S(1)}, u32[]{:S(2)}, u32[]{:S(2)}) collective-permute-start(bf16[256,1536]{1,0:T(8,128)(2,1)S(1)} %chunk.7.refs_0_), channel_id=1, source_target_pairs={{0,8},{4,20},{1,9},{5,21},{2,10},{6,22},{3,11},{7,23}} | collective-permute-start | bytes 2359304 | tf_op jit(solution)/shard_map/ppermute | solution.py:532
  14.5 25.3 %collective-permute-start.9 = (bf16[1024,512]{1,0:T(8,128)(2,1)S(1)}, bf16[1024,512]{1,0:T(8,128)(2,1)S(1)}, u32[]{:S(2)}, u32[]{:S(2)}) collective-permute-start(bf16[1024,512]{1,0:T(8,128)(2,1)S(1)} %chunk.9.refs_2_.refs_4_), channel_id=1, source_target_pairs={{2,3},{10,11},{18,19},{26,27}} | collective-permute-start | bytes 3145736 | tf_op jit(solution)/shard_map/ppermute | solution.py:444
  15.3 24.6 %collective-permute-start.8 = (bf16[1024,512]{1,0:T(8,128)(2,1)S(1)}, bf16[1024,512]{1,0:T(8,128)(2,1)S(1)}, u32[]{:S(2)}, u32[]{:S(2)}) collective-permute-start(bf16[1024,512]{1,0:T(8,128)(2,1)S(1)} %chunk.9.refs_2_.refs_4_), channel_id=1, source_target_pairs={{0,2},{2,1},{8,10},{10,9},{16,18},{18,17},{24,26},{26,25}} | collective-permute-start | bytes 3145736 | tf_op jit(solution)/shard_map/ppermute | solution.py:444
  16.1 22.5 %collective-permute-start.6 = (bf16[256,1536]{1,0:T(8,128)(2,1)S(1)}, bf16[256,1536]{1,0:T(8,128)(2,1)S(1)}, u32[]{:S(2)}, u32[]{:S(2)}) collective-permute-start(bf16[256,1536]{1,0:T(8,128)(2,1)S(1)} %add.15.refs_0_), channel_id=1, source_target_pairs={{0,8},{4,20},{8,0},{12,28},{16,24},{20,4},{24,16},{28,12},{1,9},{5... | collective-permute-start | bytes 2359304 | tf_op jit(solution)/shard_map/ppermute | solution.py:533
  25.8 14.3 %collective-permute-start.3 = (bf16[256,1536]{1,0:T(8,128)(2,1)S(1)}, bf16[256,1536]{1,0:T(8,128)(2,1)S(1)}, u32[]{:S(2)}, u32[]{:S(2)}) collective-permute-start(bf16[256,1536]{1,0:T(8,128)(2,1)S(1)} %add.13.refs_0_), channel_id=1, source_target_pairs={{0,16},{8,24},{4,12},{20,28},{1,17},{9,25},{5,13},{21,29},{2,18},{... | collective-permute-start | bytes 2359304 | tf_op jit(solution)/shard_map/ppermute | solution.py:532
  27.7 17.3 %collective-permute-start.13 = (bf16[1024,512]{1,0:T(8,128)(2,1)S(1)}, bf16[1024,512]{1,0:T(8,128)(2,1)S(1)}, u32[]{:S(2)}, u32[]{:S(2)}) collective-permute-start(bf16[1024,512]{1,0:T(8,128)(2,1)S(1)} %chunk.11.refs_2_.refs_7_), channel_id=1, source_target_pairs={{6,7},{14,15},{22,23},{30,31}} | collective-permute-start | bytes 3145736 | tf_op jit(solution)/shard_map/ppermute | solution.py:444
  38.6 21.2 %collective-permute-start.12 = (bf16[1024,512]{1,0:T(8,128)(2,1)S(1)}, bf16[1024,512]{1,0:T(8,128)(2,1)S(1)}, u32[]{:S(2)}, u32[]{:S(2)}) collective-permute-start(bf16[1024,512]{1,0:T(8,128)(2,1)S(1)} %chunk.11.refs_2_.refs_7_), channel_id=1, source_target_pairs={{4,6},{6,5},{12,14},{14,13},{20,22},{22,21},{28,30},{30,29}} | collective-permute-start | bytes 3145736 | tf_op jit(solution)/shard_map/ppermute | solution.py:444
  40.0 20.5 %collective-permute-start.10 = (bf16[256,1536]{1,0:T(8,128)(2,1)S(1)}, bf16[256,1536]{1,0:T(8,128)(2,1)S(1)}, u32[]{:S(2)}, u32[]{:S(2)}) collective-permute-start(bf16[256,1536]{1,0:T(8,128)(2,1)S(1)} %add.16.refs_0_), channel_id=1, source_target_pairs={{0,16},{4,12},{8,24},{12,4},{16,0},{20,28},{24,8},{28,20},{1,17},{... | collective-permute-start | bytes 2359304 | tf_op jit(solution)/shard_map/ppermute | solution.py:533
  40.2 26.0 %copy-start = (bf16[512,512]{1,0:T(8,128)(2,1)S(1)}, bf16[512,512]{1,0:T(8,128)(2,1)}, u32[]{:S(2)}) copy-start(bf16[512,512]{1,0:T(8,128)(2,1)} %refs_0_.1) | copy-start | bytes 1572868
  40.2 21.7 %collective-permute-start.4 = (bf16[256,1536]{1,0:T(8,128)(2,1)S(1)}, bf16[256,1536]{1,0:T(8,128)(2,1)S(1)}, u32[]{:S(2)}, u32[]{:S(2)}) collective-permute-start(bf16[256,1536]{1,0:T(8,128)(2,1)S(1)} %add.14.down_ref), channel_id=1, source_target_pairs={{0,4},{4,0},{8,12},{12,8},{16,20},{20,16},{24,28},{28,24},{1,5},{5... | collective-permute-start | bytes 2359304 | tf_op jit(solution)/shard_map/ppermute | solution.py:535
  44.4 29.9 %collective-permute-start.15 = (bf16[1024,512]{1,0:T(8,128)(2,1)S(1)}, bf16[1024,512]{1,0:T(8,128)(2,1)S(1)}, u32[]{:S(2)}, u32[]{:S(2)}) collective-permute-start(bf16[1024,512]{1,0:T(8,128)(2,1)S(1)} %collective-permute-done.8.refs_3_.refs_5_.refs_0_), channel_id=1, source_target_pairs={{2,3},{10,11},{18,19},{26,27}} | collective-permute-start | bytes 3145736 | tf_op jit(solution)/shard_map/ppermute | solution.py:444
  45.1 29.2 %collective-permute-start.14 = (bf16[1024,512]{1,0:T(8,128)(2,1)S(1)}, bf16[1024,512]{1,0:T(8,128)(2,1)S(1)}, u32[]{:S(2)}, u32[]{:S(2)}) collective-permute-start(bf16[1024,512]{1,0:T(8,128)(2,1)S(1)} %collective-permute-done.8.refs_3_.refs_5_.refs_0_), channel_id=1, source_target_pairs={{2,1},{10,9},{18,17},{26,25}} | collective-permute-start | bytes 3145736 | tf_op jit(solution)/shard_map/ppermute | solution.py:444
  59.8 14.5 %collective-permute-start.17 = (bf16[1024,512]{1,0:T(8,128)(2,1)S(1)}, bf16[1024,512]{1,0:T(8,128)(2,1)S(1)}, u32[]{:S(2)}, u32[]{:S(2)}) collective-permute-start(bf16[1024,512]{1,0:T(8,128)(2,1)S(1)} %collective-permute-done.12.refs_8_.refs_3_), channel_id=1, source_target_pairs={{6,7},{14,15},{22,23},{30,31}} | collective-permute-start | bytes 3145736 | tf_op jit(solution)/shard_map/ppermute | solution.py:444
  60.5 17.6 %collective-permute-start.16 = (bf16[1024,512]{1,0:T(8,128)(2,1)S(1)}, bf16[1024,512]{1,0:T(8,128)(2,1)S(1)}, u32[]{:S(2)}, u32[]{:S(2)}) collective-permute-start(bf16[1024,512]{1,0:T(8,128)(2,1)S(1)} %collective-permute-done.12.refs_8_.refs_3_), channel_id=1, source_target_pairs={{6,5},{14,13},{22,21},{30,29}} | collective-permute-start | bytes 3145736 | tf_op jit(solution)/shard_map/ppermute | solution.py:444
  61.9 4.3 %collective-permute-start.11 = (bf16[256,1536]{1,0:T(8,128)(2,1)S(1)}, bf16[256,1536]{1,0:T(8,128)(2,1)S(1)}, u32[]{:S(2)}, u32[]{:S(2)}) collective-permute-start(bf16[256,1536]{1,0:T(8,128)(2,1)S(1)} %add.17.refs_1_), channel_id=1, source_target_pairs={{0,4},{4,0},{8,12},{12,8},{16,20},{20,16},{24,28},{28,24},{1,5},{5... | collective-permute-start | bytes 2359304 | tf_op jit(solution)/shard_map/ppermute | solution.py:537

commit v13 on v12

--- a/solution.py
+++ b/solution.py
@@ -466,7 +466,7 @@
         right = rights[number] if number < len(rights) else None
         if right is None:
             right = move(value, [(middle, middle + 1)], core, n_prow, size)
-        arrays = [value, left, right]
+        arrays = [value, right, left]
         both = jnp.where(place[1] < middle, left, right) if size > 4 else None
         distance = 1
         while middle - distance > 1 or middle + distance + 1 < size:
@@ -487,7 +487,7 @@
 
     def pick_source(place, core):
         away = jnp.abs(place - middle)
-        number = jnp.where(away == 0, 1, jnp.where(place < middle, 2, 3))
+        number = jnp.where(away == 0, 1, jnp.where(place < middle, 3, 2))
         number = jnp.where(away >= 2, away + 2, number)
         return jnp.where(place == 0, 0, number + core * per_core)
 

time: 82.4 us -> 80.9 us (0.982)
  the two profiles are of different devices: /device:TPU:13 before, /device:TPU:29 now
where the time goes in v13:
time: 80.9 us; the launch traced here: 80.5 us
  waiting for transfers between devices  33.7 us (42%)
  Pallas kernels  27.2 us (34%)
  starting transfers between devices  18.9 us (23%)
    ppermute x10, waiting for transfers between devices, move(): return lax.ppermute(value, ('prow', 'pcol'), pairs)  16.2 us
    ppermute x2, waiting for transfers between devices, per_device(): up_got = [lax.ppermute(up[0], 'prow', swap_pairs(n_prow, orders, step))]  10.1 us
    ppermute x10, starting transfers between devices, move(): return lax.ppermute(value, ('prow', 'pcol'), pairs)  8.37 us
    pallas_call x1, Pallas kernels, update(): pl.pallas_call(functools.partial(update_kernel, first_row, len(received),...  8.04 us
    ppermute x2, waiting for transfers between devices, per_device(): down_got = lax.ppermute(down, 'prow', grow_pairs(orders, step))  7.34 us
    pallas_call x1, Pallas kernels, pick(): pl.pallas_call(pick_kernel, in_specs=[SMEM, VMEM, ANY] + [ANY] * len(afte...  6.15 us
    pallas_call x6, Pallas kernels, chunk(): pl.pallas_call(functools.partial(chunk_kernel, first_row, axis, core), in...  4.41 us
    pallas_call x1, Pallas kernels, swap(): pl.pallas_call(functools.partial(swap_kernel, first_row), in_specs=[SMEM,...  4.19 us
  transfers between devices with their start and end apart: 18, of which 4 were waited for; matrix products, arithmetic and copies ran while one was open for 0% of the time, Pallas kernels for 28%

profile of v13, /device:TPU:29, one launch (start us, length us, event | category | flops | bytes accessed | tf_op | source)
XLA Modules:
  0.0 80.5 jit_solution(10133689115662638850)
XLA Ops:
  0.1 0.6 chunk.8
  0.7 0.7 collective-permute-start.2
  1.4 1.5 %chunk.6 = bf16[256,1536]{1,0:T(8,128)(2,1)} custom-call(s32[4]{0:T(128)S(1)} %pad_add_fusion.place_ref, bf16[2048,1536]{1,0:T(8,128)(2,1)} %matrix_ref.19), custom_call_target="tpu_custom_call" | custom-call | tf_op jit(solution)/shard_map/chunk/pallas_call | solution.py:62
  2.9 0.7 collective-permute-start
  3.6 0.1 copy.8.pivots_ref
  3.8 6.2 %pick_rows.1 = (bf16[256,1536]{1,0:T(8,128)(2,1)S(1)}, bf16[256,1536]{1,0:T(8,128)(2,1)S(1)}) custom-call(s32[4]{0:T(128)S(1)} %pad_add_fusion.place_ref, s32[512,1]{1,0:T(8,128)S(1)} %copy.8.pivots_ref, bf16[2048,1536]{1,0:T(8,128)(2,1)} %matrix_ref.19), custom_call_target="tpu_custom_call" | custom-call | tf_op jit(solution)/shard_map/pick_rows/pallas_call | solution.py:112
  10.0 0.7 collective-permute-start.5
  10.7 0.6 chunk.10
  11.3 0.7 collective-permute-start.7
  12.0 0.6 chunk.7.refs_0_
  12.6 1.3 %collective-permute-start.1 = (bf16[256,1536]{1,0:T(8,128)(2,1)S(1)}, bf16[256,1536]{1,0:T(8,128)(2,1)S(1)}, u32[]{:S(2)}, u32[]{:S(2)}) collective-permute-start(bf16[256,1536]{1,0:T(8,128)(2,1)S(1)} %chunk.7.refs_0_), channel_id=1, source_target_pairs={{0,8},{4,20},{1,9},{5,21},{2,10},{6,22},{3,11},{7,23}} | collective-permute-start | bytes 2359304 | tf_op jit(solution)/shard_map/ppermute | solution.py:532
  13.9 0.6 chunk.9.refs_2_.refs_4_
  14.5 0.7 collective-permute-start.9
  15.3 0.7 collective-permute-start.8
  16.1 2.2 %collective-permute-start.6 = (bf16[256,1536]{1,0:T(8,128)(2,1)S(1)}, bf16[256,1536]{1,0:T(8,128)(2,1)S(1)}, u32[]{:S(2)}, u32[]{:S(2)}) collective-permute-start(bf16[256,1536]{1,0:T(8,128)(2,1)S(1)} %add.15.refs_0_), channel_id=1, source_target_pairs={{0,8},{4,20},{8,0},{12,28},{16,24},{20,4},{24,16},{28,12},{1,9},{5... | collective-permute-start | bytes 2359304 | tf_op jit(solution)/shard_map/ppermute | solution.py:533
  18.3 7.3 %collective-permute-done.1.refs_1_ = bf16[256,1536]{1,0:T(8,128)(2,1)S(1)} collective-permute-done((bf16[256,1536]{1,0:T(8,128)(2,1)S(1)}, bf16[256,1536]{1,0:T(8,128)(2,1)S(1)}, u32[]{:S(2)}, u32[]{:S(2)}) %collective-permute-start.1) | collective-permute-done | bytes 786464 | tf_op jit(solution)/shard_map/ppermute | solution.py:532
  25.8 1.3 %collective-permute-start.3 = (bf16[256,1536]{1,0:T(8,128)(2,1)S(1)}, bf16[256,1536]{1,0:T(8,128)(2,1)S(1)}, u32[]{:S(2)}, u32[]{:S(2)}) collective-permute-start(bf16[256,1536]{1,0:T(8,128)(2,1)S(1)} %add.13.refs_0_), channel_id=1, source_target_pairs={{0,16},{8,24},{4,12},{20,28},{1,17},{9,25},{5,13},{21,29},{2,18},{... | collective-permute-start | bytes 2359304 | tf_op jit(solution)/shard_map/ppermute | solution.py:532
  27.1 0.6 chunk.11.refs_2_.refs_7_
  27.7 0.7 collective-permute-start.13
  28.5 10.1 %collective-permute-done.6.refs_1_ = bf16[256,1536]{1,0:T(8,128)(2,1)S(1)} collective-permute-done((bf16[256,1536]{1,0:T(8,128)(2,1)S(1)}, bf16[256,1536]{1,0:T(8,128)(2,1)S(1)}, u32[]{:S(2)}, u32[]{:S(2)}) %collective-permute-start.6) | collective-permute-done | bytes 786464 | tf_op jit(solution)/shard_map/ppermute | solution.py:533
  38.6 1.3 %collective-permute-start.12 = (bf16[1024,512]{1,0:T(8,128)(2,1)S(1)}, bf16[1024,512]{1,0:T(8,128)(2,1)S(1)}, u32[]{:S(2)}, u32[]{:S(2)}) collective-permute-start(bf16[1024,512]{1,0:T(8,128)(2,1)S(1)} %chunk.11.refs_2_.refs_7_), channel_id=1, source_target_pairs={{6,7},{14,15},{22,23},{30,31}} | collective-permute-start | bytes 3145736 | tf_op jit(solution)/shard_map/ppermute | solution.py:444
  40.2 4.2 %collective-permute-start.4 = (bf16[256,1536]{1,0:T(8,128)(2,1)S(1)}, bf16[256,1536]{1,0:T(8,128)(2,1)S(1)}, u32[]{:S(2)}, u32[]{:S(2)}) collective-permute-start(bf16[256,1536]{1,0:T(8,128)(2,1)S(1)} %add.14.down_ref), channel_id=1, source_target_pairs={{0,4},{4,0},{8,12},{12,8},{16,20},{20,16},{24,28},{28,24},{1,5},{5... | collective-permute-start | bytes 2359304 | tf_op jit(solution)/shard_map/ppermute | solution.py:535
  44.4 0.7 collective-permute-start.15
  45.1 0.7 collective-permute-start.14
  45.8 12.6 %collective-permute-done.12.refs_8_ = bf16[1024,512]{1,0:T(8,128)(2,1)S(1)} collective-permute-done((bf16[1024,512]{1,0:T(8,128)(2,1)S(1)}, bf16[1024,512]{1,0:T(8,128)(2,1)S(1)}, u32[]{:S(2)}, u32[]{:S(2)}) %collective-permute-start.12) | collective-permute-done | bytes 1048608 | tf_op jit(solution)/shard_map/ppermute | solution.py:444
  58.4 0.7 collective-permute-start.17
  59.2 1.3 %collective-permute-start.16 = (bf16[1024,512]{1,0:T(8,128)(2,1)S(1)}, bf16[1024,512]{1,0:T(8,128)(2,1)S(1)}, u32[]{:S(2)}, u32[]{:S(2)}) collective-permute-start(bf16[1024,512]{1,0:T(8,128)(2,1)S(1)} %collective-permute-done.13.refs_9_.refs_3_), channel_id=1, source_target_pairs={{6,7},{14,15},{22,23},{30,31}} | collective-permute-start | bytes 3145736 | tf_op jit(solution)/shard_map/ppermute | solution.py:444
  60.5 0.1 add.17.refs_1_
  60.7 4.2 %swap_rows.1.swapped_ref = bf16[1024,1536]{1,0:T(8,128)(2,1)S(1)} custom-call(s32[4]{0:T(128)S(1)} %pad_add_fusion.place_ref, s32[1,512]{1,0:T(1,128)S(1)} %bitcast.5, bf16[2048,1536]{1,0:T(8,128)(2,1)} %matrix_ref.19, bf16[256,1536]{1,0:T(8,128)(2,1)S(1)} %add.14.down_ref, bf16[256,1536]{1,0:T(8,128)(2,1)S(1)} %collective-permute-done.4.down_got_ref), custom_call_target="tpu_custom_call" | custom-call | tf_op jit(solution)/shard_map/swap_rows/pallas_call | solution.py:331
  64.9 8.0 %update_rows.1 = (bf16[2048,1536]{1,0:T(8,128)(2,1)}, bf16[512,1536]{1,0:T(8,128)(2,1)S(1)}) custom-call(s32[4]{0:T(128)S(1)} %pad_add_fusion.place_ref, s32[1,512]{1,0:T(1,128)S(1)} %bitcast.6, bf16[2048,1536]{1,0:T(8,128)(2,1)} %matrix_ref.19, bf16[256,1536]{1,0:T(8,128)(2,1)S(1)} %add.14.down_ref, ...), custom_call_target="tpu_custom_call" | custom-call | tf_op jit(solution)/shard_map/update_rows/pallas_call | solution.py:262
  73.0 3.6 %collective-permute-done.16.refs_4_ = bf16[1024,512]{1,0:T(8,128)(2,1)S(1)} collective-permute-done((bf16[1024,512]{1,0:T(8,128)(2,1)S(1)}, bf16[1024,512]{1,0:T(8,128)(2,1)S(1)}, u32[]{:S(2)}, u32[]{:S(2)}) %collective-permute-start.16) | collective-permute-done | bytes 1048608 | tf_op jit(solution)/shard_map/ppermute | solution.py:444
  76.6 3.9 %finish_rows.1 = bf16[2048,1536]{1,0:T(8,128)(2,1)} custom-call(s32[4]{0:T(128)S(1)} %pad_add_fusion.place_ref, bf16[2048,1536]{1,0:T(8,128)(2,1)} %matrix_ref.19, bf16[1024,1536]{1,0:T(8,128)(2,1)S(1)} %swap_rows.1.swapped_ref, bf16[512,1536]{1,0:T(8,128)(2,1)S(1)} %get-tuple-element.11.upper_ref, ...), custom_call_target="tpu_custom_call", output_to_operand_aliasing={{}: (10, {})} | custom-call | tf_op jit(solution)/shard_map/finish_rows/pallas_call | solution.py:410
  (27 shorter events, 0.7 us)
Async XLA Ops:
  0.1 3.5 %copy-start.1 = (s32[512]{0:T(512)S(1)}, s32[512]{0:T(512)}, u32[]{:S(2)}) copy-start(s32[512]{0:T(512)} %param.4) | copy-start | bytes 6148
  0.7 13.3 %collective-permute-start.2 = (bf16[1024,512]{1,0:T(8,128)(2,1)S(1)}, bf16[1024,512]{1,0:T(8,128)(2,1)S(1)}, u32[]{:S(2)}, u32[]{:S(2)}) collective-permute-start(bf16[1024,512]{1,0:T(8,128)(2,1)S(1)} %chunk.8), channel_id=1, source_target_pairs={{0,2},{8,10},{16,18},{24,26}} | collective-permute-start | bytes 3145736 | tf_op jit(solution)/shard_map/ppermute | solution.py:444
  2.9 9.1 %collective-permute-start = (bf16[256,1536]{1,0:T(8,128)(2,1)}, bf16[256,1536]{1,0:T(8,128)(2,1)S(1)}, u32[]{:S(2)}, u32[]{:S(2)}) collective-permute-start(bf16[256,1536]{1,0:T(8,128)(2,1)} %chunk.6), channel_id=1, source_target_pairs={{0,4},{1,5},{2,6},{3,7}} | collective-permute-start | bytes 2359304 | tf_op jit(solution)/shard_map/ppermute | solution.py:523
  10.0 6.1 %collective-permute-start.5 = (bf16[256,1536]{1,0:T(8,128)(2,1)S(1)}, bf16[256,1536]{1,0:T(8,128)(2,1)S(1)}, u32[]{:S(2)}, u32[]{:S(2)}) collective-permute-start(bf16[256,1536]{1,0:T(8,128)(2,1)S(1)} %get-tuple-element.10), channel_id=1, source_target_pairs={{0,4},{4,0},{8,12},{12,8},{16,20},{20,16},{24,28},{28,24},{1,5},{5... | collective-permute-start | bytes 2359304 | tf_op jit(solution)/shard_map/ppermute | solution.py:527
  11.3 15.8 %collective-permute-start.7 = (bf16[1024,512]{1,0:T(8,128)(2,1)S(1)}, bf16[1024,512]{1,0:T(8,128)(2,1)S(1)}, u32[]{:S(2)}, u32[]{:S(2)}) collective-permute-start(bf16[1024,512]{1,0:T(8,128)(2,1)S(1)} %chunk.10), channel_id=1, source_target_pairs={{4,6},{12,14},{20,22},{28,30}} | collective-permute-start | bytes 3145736 | tf_op jit(solution)/shard_map/ppermute | solution.py:444
  12.6 13.0 %collective-permute-start.1 = (bf16[256,1536]{1,0:T(8,128)(2,1)S(1)}, bf16[256,1536]{1,0:T(8,128)(2,1)S(1)}, u32[]{:S(2)}, u32[]{:S(2)}) collective-permute-start(bf16[256,1536]{1,0:T(8,128)(2,1)S(1)} %chunk.7.refs_0_), channel_id=1, source_target_pairs={{0,8},{4,20},{1,9},{5,21},{2,10},{6,22},{3,11},{7,23}} | collective-permute-start | bytes 2359304 | tf_op jit(solution)/shard_map/ppermute | solution.py:532
  14.5 25.3 %collective-permute-start.9 = (bf16[1024,512]{1,0:T(8,128)(2,1)S(1)}, bf16[1024,512]{1,0:T(8,128)(2,1)S(1)}, u32[]{:S(2)}, u32[]{:S(2)}) collective-permute-start(bf16[1024,512]{1,0:T(8,128)(2,1)S(1)} %chunk.9.refs_2_.refs_4_), channel_id=1, source_target_pairs={{2,3},{10,11},{18,19},{26,27}} | collective-permute-start | bytes 3145736 | tf_op jit(solution)/shard_map/ppermute | solution.py:444
  15.3 24.6 %collective-permute-start.8 = (bf16[1024,512]{1,0:T(8,128)(2,1)S(1)}, bf16[1024,512]{1,0:T(8,128)(2,1)S(1)}, u32[]{:S(2)}, u32[]{:S(2)}) collective-permute-start(bf16[1024,512]{1,0:T(8,128)(2,1)S(1)} %chunk.9.refs_2_.refs_4_), channel_id=1, source_target_pairs={{0,2},{2,1},{8,10},{10,9},{16,18},{18,17},{24,26},{26,25}} | collective-permute-start | bytes 3145736 | tf_op jit(solution)/shard_map/ppermute | solution.py:444
  16.1 22.5 %collective-permute-start.6 = (bf16[256,1536]{1,0:T(8,128)(2,1)S(1)}, bf16[256,1536]{1,0:T(8,128)(2,1)S(1)}, u32[]{:S(2)}, u32[]{:S(2)}) collective-permute-start(bf16[256,1536]{1,0:T(8,128)(2,1)S(1)} %add.15.refs_0_), channel_id=1, source_target_pairs={{0,8},{4,20},{8,0},{12,28},{16,24},{20,4},{24,16},{28,12},{1,9},{5... | collective-permute-start | bytes 2359304 | tf_op jit(solution)/shard_map/ppermute | solution.py:533
  25.8 14.3 %collective-permute-start.3 = (bf16[256,1536]{1,0:T(8,128)(2,1)S(1)}, bf16[256,1536]{1,0:T(8,128)(2,1)S(1)}, u32[]{:S(2)}, u32[]{:S(2)}) collective-permute-start(bf16[256,1536]{1,0:T(8,128)(2,1)S(1)} %add.13.refs_0_), channel_id=1, source_target_pairs={{0,16},{8,24},{4,12},{20,28},{1,17},{9,25},{5,13},{21,29},{2,18},{... | collective-permute-start | bytes 2359304 | tf_op jit(solution)/shard_map/ppermute | solution.py:532
  27.7 17.3 %collective-permute-start.13 = (bf16[1024,512]{1,0:T(8,128)(2,1)S(1)}, bf16[1024,512]{1,0:T(8,128)(2,1)S(1)}, u32[]{:S(2)}, u32[]{:S(2)}) collective-permute-start(bf16[1024,512]{1,0:T(8,128)(2,1)S(1)} %chunk.11.refs_2_.refs_7_), channel_id=1, source_target_pairs={{4,6},{6,5},{12,14},{14,13},{20,22},{22,21},{28,30},{30,29}} | collective-permute-start | bytes 3145736 | tf_op jit(solution)/shard_map/ppermute | solution.py:444
  38.6 19.9 %collective-permute-start.12 = (bf16[1024,512]{1,0:T(8,128)(2,1)S(1)}, bf16[1024,512]{1,0:T(8,128)(2,1)S(1)}, u32[]{:S(2)}, u32[]{:S(2)}) collective-permute-start(bf16[1024,512]{1,0:T(8,128)(2,1)S(1)} %chunk.11.refs_2_.refs_7_), channel_id=1, source_target_pairs={{6,7},{14,15},{22,23},{30,31}} | collective-permute-start | bytes 3145736 | tf_op jit(solution)/shard_map/ppermute | solution.py:444
  40.0 19.2 %collective-permute-start.10 = (bf16[256,1536]{1,0:T(8,128)(2,1)S(1)}, bf16[256,1536]{1,0:T(8,128)(2,1)S(1)}, u32[]{:S(2)}, u32[]{:S(2)}) collective-permute-start(bf16[256,1536]{1,0:T(8,128)(2,1)S(1)} %add.16.refs_0_), channel_id=1, source_target_pairs={{0,16},{4,12},{8,24},{12,4},{16,0},{20,28},{24,8},{28,20},{1,17},{... | collective-permute-start | bytes 2359304 | tf_op jit(solution)/shard_map/ppermute | solution.py:533
  40.2 24.7 %copy-start = (bf16[512,512]{1,0:T(8,128)(2,1)S(1)}, bf16[512,512]{1,0:T(8,128)(2,1)}, u32[]{:S(2)}) copy-start(bf16[512,512]{1,0:T(8,128)(2,1)} %refs_0_.1) | copy-start | bytes 1572868
  40.2 20.4 %collective-permute-start.4 = (bf16[256,1536]{1,0:T(8,128)(2,1)S(1)}, bf16[256,1536]{1,0:T(8,128)(2,1)S(1)}, u32[]{:S(2)}, u32[]{:S(2)}) collective-permute-start(bf16[256,1536]{1,0:T(8,128)(2,1)S(1)} %add.14.down_ref), channel_id=1, source_target_pairs={{0,4},{4,0},{8,12},{12,8},{16,20},{20,16},{24,28},{28,24},{1,5},{5... | collective-permute-start | bytes 2359304 | tf_op jit(solution)/shard_map/ppermute | solution.py:535
  44.4 28.6 %collective-permute-start.15 = (bf16[1024,512]{1,0:T(8,128)(2,1)S(1)}, bf16[1024,512]{1,0:T(8,128)(2,1)S(1)}, u32[]{:S(2)}, u32[]{:S(2)}) collective-permute-start(bf16[1024,512]{1,0:T(8,128)(2,1)S(1)} %collective-permute-done.8.refs_3_.refs_6_.refs_0_), channel_id=1, source_target_pairs={{2,1},{10,9},{18,17},{26,25}} | collective-permute-start | bytes 3145736 | tf_op jit(solution)/shard_map/ppermute | solution.py:444
  45.1 27.9 %collective-permute-start.14 = (bf16[1024,512]{1,0:T(8,128)(2,1)S(1)}, bf16[1024,512]{1,0:T(8,128)(2,1)S(1)}, u32[]{:S(2)}, u32[]{:S(2)}) collective-permute-start(bf16[1024,512]{1,0:T(8,128)(2,1)S(1)} %collective-permute-done.8.refs_3_.refs_6_.refs_0_), channel_id=1, source_target_pairs={{2,3},{10,11},{18,19},{26,27}} | collective-permute-start | bytes 3145736 | tf_op jit(solution)/shard_map/ppermute | solution.py:444
  58.4 14.5 %collective-permute-start.17 = (bf16[1024,512]{1,0:T(8,128)(2,1)S(1)}, bf16[1024,512]{1,0:T(8,128)(2,1)S(1)}, u32[]{:S(2)}, u32[]{:S(2)}) collective-permute-start(bf16[1024,512]{1,0:T(8,128)(2,1)S(1)} %collective-permute-done.13.refs_9_.refs_3_), channel_id=1, source_target_pairs={{6,5},{14,13},{22,21},{30,29}} | collective-permute-start | bytes 3145736 | tf_op jit(solution)/shard_map/ppermute | solution.py:444
  59.2 17.4 %collective-permute-start.16 = (bf16[1024,512]{1,0:T(8,128)(2,1)S(1)}, bf16[1024,512]{1,0:T(8,128)(2,1)S(1)}, u32[]{:S(2)}, u32[]{:S(2)}) collective-permute-start(bf16[1024,512]{1,0:T(8,128)(2,1)S(1)} %collective-permute-done.13.refs_9_.refs_3_), channel_id=1, source_target_pairs={{6,7},{14,15},{22,23},{30,31}} | collective-permute-start | bytes 3145736 | tf_op jit(solution)/shard_map/ppermute | solution.py:444
  60.6 4.3 %collective-permute-start.11 = (bf16[256,1536]{1,0:T(8,128)(2,1)S(1)}, bf16[256,1536]{1,0:T(8,128)(2,1)S(1)}, u32[]{:S(2)}, u32[]{:S(2)}) collective-permute-start(bf16[256,1536]{1,0:T(8,128)(2,1)S(1)} %add.17.refs_1_), channel_id=1, source_target_pairs={{0,4},{4,0},{8,12},{12,8},{16,20},{20,16},{24,28},{28,24},{1,5},{5... | collective-permute-start | bytes 2359304 | tf_op jit(solution)/shard_map/ppermute | solution.py:537

commit v14 on v13

--- a/solution.py
+++ b/solution.py
@@ -356,12 +356,12 @@
     piece = min(count, 512)
     here = pl.ds(first_row, count)
 
-    def fetch_panel(action):
+    def fetch_panel(action, first=0, last=COPIES):
         views = [sources[0].at[here, pl.ds(0, width)], *sources[1:]]
         for choice, view in enumerate(views):
             @pl.when(pick_source(col_place, core) == choice)
             def _():
-                for copy in row_copies(view, panel_ref, sem):
+                for copy in row_copies(view, panel_ref, sem)[first:last]:
                     action(copy)
 
     def store(number):
@@ -371,7 +371,6 @@
         )
 
     fetch_panel(lambda copy: copy.start())
-    fetch_panel(lambda copy: copy.wait())
 
     @pl.loop(0, cols // block)
     def _(number):
@@ -382,18 +381,24 @@
         def _():
             rows_ref[:, there] = swapped_ref[:, there]
 
-        @pl.when(updated)
-        def _():
-            upper = upper_ref[:, there]
-            for start in range(0, count, piece):
-                these = slice(start, start + piece)
-                product = jnp.dot(panel_ref[these], upper, preferred_element_type=F32)
+        for start in range(0, count, piece):
+            these = slice(start, start + piece)
+
+            @pl.when(number == 0)
+            def _():
+                parts = [COPIES * row // count for row in (start, start + piece)]
+                fetch_panel(lambda copy: copy.wait(), *parts)
+
+            @pl.when(updated)
+            def _():
+                product = jnp.dot(panel_ref[these], upper_ref[:, there], preferred_element_type=F32)
                 left = swapped_ref[these, there].astype(F32) - product
                 rows_ref[these, there] = left.astype(BF16)
-            if first_row < width:
-                @pl.when(row_place == 0)
-                def _():
-                    rows_ref[: width - first_row, there] = upper[first_row:]
+
+        if first_row < width:
+            @pl.when(updated & (row_place == 0))
+            def _():
+                rows_ref[: width - first_row, there] = upper_ref[first_row:, there]
 
         store(number).start()
 

time: 80.9 us -> 81.4 us (level)
  no operation moved by 1% of the time
where the time goes in v14:
time: 81.4 us; the launch traced here: 81 us
  waiting for transfers between devices  33.7 us (41%)
  Pallas kernels  27.7 us (34%)
  starting transfers between devices  18.9 us (23%)
    ppermute x10, waiting for transfers between devices, move(): return lax.ppermute(value, ('prow', 'pcol'), pairs)  16.2 us
    ppermute x2, waiting for transfers between devices, per_device(): up_got = [lax.ppermute(up[0], 'prow', swap_pairs(n_prow, orders, step))]  10.1 us
    ppermute x10, starting transfers between devices, move(): return lax.ppermute(value, ('prow', 'pcol'), pairs)  8.37 us
    pallas_call x1, Pallas kernels, update(): pl.pallas_call(functools.partial(update_kernel, first_row, len(received),...  8.04 us
    ppermute x2, waiting for transfers between devices, per_device(): down_got = lax.ppermute(down, 'prow', grow_pairs(orders, step))  7.34 us
    pallas_call x1, Pallas kernels, pick(): pl.pallas_call(pick_kernel, in_specs=[SMEM, VMEM, ANY] + [ANY] * len(afte...  6.15 us
    pallas_call x1, Pallas kernels, finish(): pl.pallas_call(functools.partial(finish_kernel, first_row, len(received),...  4.44 us
    pallas_call x6, Pallas kernels, chunk(): pl.pallas_call(functools.partial(chunk_kernel, first_row, axis, core), in...  4.41 us
  transfers between devices with their start and end apart: 18, of which 4 were waited for; matrix products, arithmetic and copies ran while one was open for 0% of the time, Pallas kernels for 28%

profile of v14, /device:TPU:29, one launch (start us, length us, event | category | flops | bytes accessed | tf_op | source)
XLA Modules:
  0.0 81.0 jit_solution(6500404769388601526)
XLA Ops:
  0.1 0.6 chunk.8
  0.7 0.7 collective-permute-start.2
  1.4 1.5 %chunk.6 = bf16[256,1536]{1,0:T(8,128)(2,1)} custom-call(s32[4]{0:T(128)S(1)} %pad_add_fusion.place_ref, bf16[2048,1536]{1,0:T(8,128)(2,1)} %matrix_ref.19), custom_call_target="tpu_custom_call" | custom-call | tf_op jit(solution)/shard_map/chunk/pallas_call | solution.py:62
  2.9 0.7 collective-permute-start
  3.6 0.1 copy.8.pivots_ref
  3.8 6.2 %pick_rows.1 = (bf16[256,1536]{1,0:T(8,128)(2,1)S(1)}, bf16[256,1536]{1,0:T(8,128)(2,1)S(1)}) custom-call(s32[4]{0:T(128)S(1)} %pad_add_fusion.place_ref, s32[512,1]{1,0:T(8,128)S(1)} %copy.8.pivots_ref, bf16[2048,1536]{1,0:T(8,128)(2,1)} %matrix_ref.19), custom_call_target="tpu_custom_call" | custom-call | tf_op jit(solution)/shard_map/pick_rows/pallas_call | solution.py:112
  10.0 0.7 collective-permute-start.5
  10.7 0.6 chunk.10
  11.3 0.7 collective-permute-start.7
  12.0 0.6 chunk.7.refs_0_
  12.6 1.3 %collective-permute-start.1 = (bf16[256,1536]{1,0:T(8,128)(2,1)S(1)}, bf16[256,1536]{1,0:T(8,128)(2,1)S(1)}, u32[]{:S(2)}, u32[]{:S(2)}) collective-permute-start(bf16[256,1536]{1,0:T(8,128)(2,1)S(1)} %chunk.7.refs_0_), channel_id=1, source_target_pairs={{0,8},{4,20},{1,9},{5,21},{2,10},{6,22},{3,11},{7,23}} | collective-permute-start | bytes 2359304 | tf_op jit(solution)/shard_map/ppermute | solution.py:537
  13.9 0.6 chunk.9.refs_2_.refs_4_
  14.5 0.7 collective-permute-start.9
  15.3 0.7 collective-permute-start.8
  16.1 2.2 %collective-permute-start.6 = (bf16[256,1536]{1,0:T(8,128)(2,1)S(1)}, bf16[256,1536]{1,0:T(8,128)(2,1)S(1)}, u32[]{:S(2)}, u32[]{:S(2)}) collective-permute-start(bf16[256,1536]{1,0:T(8,128)(2,1)S(1)} %add.15.refs_0_), channel_id=1, source_target_pairs={{0,8},{4,20},{8,0},{12,28},{16,24},{20,4},{24,16},{28,12},{1,9},{5... | collective-permute-start | bytes 2359304 | tf_op jit(solution)/shard_map/ppermute | solution.py:538
  18.3 7.3 %collective-permute-done.1.refs_1_ = bf16[256,1536]{1,0:T(8,128)(2,1)S(1)} collective-permute-done((bf16[256,1536]{1,0:T(8,128)(2,1)S(1)}, bf16[256,1536]{1,0:T(8,128)(2,1)S(1)}, u32[]{:S(2)}, u32[]{:S(2)}) %collective-permute-start.1) | collective-permute-done | bytes 786464 | tf_op jit(solution)/shard_map/ppermute | solution.py:537
  25.8 1.3 %collective-permute-start.3 = (bf16[256,1536]{1,0:T(8,128)(2,1)S(1)}, bf16[256,1536]{1,0:T(8,128)(2,1)S(1)}, u32[]{:S(2)}, u32[]{:S(2)}) collective-permute-start(bf16[256,1536]{1,0:T(8,128)(2,1)S(1)} %add.13.refs_0_), channel_id=1, source_target_pairs={{0,16},{8,24},{4,12},{20,28},{1,17},{9,25},{5,13},{21,29},{2,18},{... | collective-permute-start | bytes 2359304 | tf_op jit(solution)/shard_map/ppermute | solution.py:537
  27.1 0.6 chunk.11.refs_2_.refs_7_
  27.7 0.7 collective-permute-start.13
  28.5 10.1 %collective-permute-done.6.refs_1_ = bf16[256,1536]{1,0:T(8,128)(2,1)S(1)} collective-permute-done((bf16[256,1536]{1,0:T(8,128)(2,1)S(1)}, bf16[256,1536]{1,0:T(8,128)(2,1)S(1)}, u32[]{:S(2)}, u32[]{:S(2)}) %collective-permute-start.6) | collective-permute-done | bytes 786464 | tf_op jit(solution)/shard_map/ppermute | solution.py:538
  38.6 1.3 %collective-permute-start.12 = (bf16[1024,512]{1,0:T(8,128)(2,1)S(1)}, bf16[1024,512]{1,0:T(8,128)(2,1)S(1)}, u32[]{:S(2)}, u32[]{:S(2)}) collective-permute-start(bf16[1024,512]{1,0:T(8,128)(2,1)S(1)} %chunk.11.refs_2_.refs_7_), channel_id=1, source_target_pairs={{6,7},{14,15},{22,23},{30,31}} | collective-permute-start | bytes 3145736 | tf_op jit(solution)/shard_map/ppermute | solution.py:449
  40.2 4.2 %collective-permute-start.4 = (bf16[256,1536]{1,0:T(8,128)(2,1)S(1)}, bf16[256,1536]{1,0:T(8,128)(2,1)S(1)}, u32[]{:S(2)}, u32[]{:S(2)}) collective-permute-start(bf16[256,1536]{1,0:T(8,128)(2,1)S(1)} %add.14.down_ref), channel_id=1, source_target_pairs={{0,4},{4,0},{8,12},{12,8},{16,20},{20,16},{24,28},{28,24},{1,5},{5... | collective-permute-start | bytes 2359304 | tf_op jit(solution)/shard_map/ppermute | solution.py:540
  44.4 0.7 collective-permute-start.15
  45.1 0.7 collective-permute-start.14
  45.8 12.6 %collective-permute-done.12.refs_8_ = bf16[1024,512]{1,0:T(8,128)(2,1)S(1)} collective-permute-done((bf16[1024,512]{1,0:T(8,128)(2,1)S(1)}, bf16[1024,512]{1,0:T(8,128)(2,1)S(1)}, u32[]{:S(2)}, u32[]{:S(2)}) %collective-permute-start.12) | collective-permute-done | bytes 1048608 | tf_op jit(solution)/shard_map/ppermute | solution.py:449
  58.4 0.7 collective-permute-start.17
  59.2 1.3 %collective-permute-start.16 = (bf16[1024,512]{1,0:T(8,128)(2,1)S(1)}, bf16[1024,512]{1,0:T(8,128)(2,1)S(1)}, u32[]{:S(2)}, u32[]{:S(2)}) collective-permute-start(bf16[1024,512]{1,0:T(8,128)(2,1)S(1)} %collective-permute-done.13.refs_9_.refs_3_), channel_id=1, source_target_pairs={{6,7},{14,15},{22,23},{30,31}} | collective-permute-start | bytes 3145736 | tf_op jit(solution)/shard_map/ppermute | solution.py:449
  60.5 0.1 add.17.refs_1_
  60.7 4.2 %swap_rows.1.swapped_ref = bf16[1024,1536]{1,0:T(8,128)(2,1)S(1)} custom-call(s32[4]{0:T(128)S(1)} %pad_add_fusion.place_ref, s32[1,512]{1,0:T(1,128)S(1)} %bitcast.5, bf16[2048,1536]{1,0:T(8,128)(2,1)} %matrix_ref.19, bf16[256,1536]{1,0:T(8,128)(2,1)S(1)} %add.14.down_ref, bf16[256,1536]{1,0:T(8,128)(2,1)S(1)} %collective-permute-done.4.down_got_ref), custom_call_target="tpu_custom_call" | custom-call | tf_op jit(solution)/shard_map/swap_rows/pallas_call | solution.py:331
  64.9 8.0 %update_rows.1 = (bf16[2048,1536]{1,0:T(8,128)(2,1)}, bf16[512,1536]{1,0:T(8,128)(2,1)S(1)}) custom-call(s32[4]{0:T(128)S(1)} %pad_add_fusion.place_ref, s32[1,512]{1,0:T(1,128)S(1)} %bitcast.6, bf16[2048,1536]{1,0:T(8,128)(2,1)} %matrix_ref.19, bf16[256,1536]{1,0:T(8,128)(2,1)S(1)} %add.14.down_ref, ...), custom_call_target="tpu_custom_call" | custom-call | tf_op jit(solution)/shard_map/update_rows/pallas_call | solution.py:262
  73.0 3.6 %collective-permute-done.16.refs_4_ = bf16[1024,512]{1,0:T(8,128)(2,1)S(1)} collective-permute-done((bf16[1024,512]{1,0:T(8,128)(2,1)S(1)}, bf16[1024,512]{1,0:T(8,128)(2,1)S(1)}, u32[]{:S(2)}, u32[]{:S(2)}) %collective-permute-start.16) | collective-permute-done | bytes 1048608 | tf_op jit(solution)/shard_map/ppermute | solution.py:449
  76.6 4.4 %finish_rows.1 = bf16[2048,1536]{1,0:T(8,128)(2,1)} custom-call(s32[4]{0:T(128)S(1)} %pad_add_fusion.place_ref, bf16[2048,1536]{1,0:T(8,128)(2,1)} %matrix_ref.19, bf16[1024,1536]{1,0:T(8,128)(2,1)S(1)} %swap_rows.1.swapped_ref, bf16[512,1536]{1,0:T(8,128)(2,1)S(1)} %get-tuple-element.11.upper_ref, ...), custom_call_target="tpu_custom_call", output_to_operand_aliasing={{}: (10, {})} | custom-call | tf_op jit(solution)/shard_map/finish_rows/pallas_call | solution.py:415
  (27 shorter events, 0.7 us)
Async XLA Ops:
  0.1 3.5 %copy-start.1 = (s32[512]{0:T(512)S(1)}, s32[512]{0:T(512)}, u32[]{:S(2)}) copy-start(s32[512]{0:T(512)} %param.4) | copy-start | bytes 6148
  0.7 13.3 %collective-permute-start.2 = (bf16[1024,512]{1,0:T(8,128)(2,1)S(1)}, bf16[1024,512]{1,0:T(8,128)(2,1)S(1)}, u32[]{:S(2)}, u32[]{:S(2)}) collective-permute-start(bf16[1024,512]{1,0:T(8,128)(2,1)S(1)} %chunk.8), channel_id=1, source_target_pairs={{0,2},{8,10},{16,18},{24,26}} | collective-permute-start | bytes 3145736 | tf_op jit(solution)/shard_map/ppermute | solution.py:449
  2.9 9.1 %collective-permute-start = (bf16[256,1536]{1,0:T(8,128)(2,1)}, bf16[256,1536]{1,0:T(8,128)(2,1)S(1)}, u32[]{:S(2)}, u32[]{:S(2)}) collective-permute-start(bf16[256,1536]{1,0:T(8,128)(2,1)} %chunk.6), channel_id=1, source_target_pairs={{0,4},{1,5},{2,6},{3,7}} | collective-permute-start | bytes 2359304 | tf_op jit(solution)/shard_map/ppermute | solution.py:528
  10.0 6.1 %collective-permute-start.5 = (bf16[256,1536]{1,0:T(8,128)(2,1)S(1)}, bf16[256,1536]{1,0:T(8,128)(2,1)S(1)}, u32[]{:S(2)}, u32[]{:S(2)}) collective-permute-start(bf16[256,1536]{1,0:T(8,128)(2,1)S(1)} %get-tuple-element.10), channel_id=1, source_target_pairs={{0,4},{4,0},{8,12},{12,8},{16,20},{20,16},{24,28},{28,24},{1,5},{5... | collective-permute-start | bytes 2359304 | tf_op jit(solution)/shard_map/ppermute | solution.py:532
  11.3 15.8 %collective-permute-start.7 = (bf16[1024,512]{1,0:T(8,128)(2,1)S(1)}, bf16[1024,512]{1,0:T(8,128)(2,1)S(1)}, u32[]{:S(2)}, u32[]{:S(2)}) collective-permute-start(bf16[1024,512]{1,0:T(8,128)(2,1)S(1)} %chunk.10), channel_id=1, source_target_pairs={{4,6},{12,14},{20,22},{28,30}} | collective-permute-start | bytes 3145736 | tf_op jit(solution)/shard_map/ppermute | solution.py:449
  12.6 13.0 %collective-permute-start.1 = (bf16[256,1536]{1,0:T(8,128)(2,1)S(1)}, bf16[256,1536]{1,0:T(8,128)(2,1)S(1)}, u32[]{:S(2)}, u32[]{:S(2)}) collective-permute-start(bf16[256,1536]{1,0:T(8,128)(2,1)S(1)} %chunk.7.refs_0_), channel_id=1, source_target_pairs={{0,8},{4,20},{1,9},{5,21},{2,10},{6,22},{3,11},{7,23}} | collective-permute-start | bytes 2359304 | tf_op jit(solution)/shard_map/ppermute | solution.py:537
  14.5 25.3 %collective-permute-start.9 = (bf16[1024,512]{1,0:T(8,128)(2,1)S(1)}, bf16[1024,512]{1,0:T(8,128)(2,1)S(1)}, u32[]{:S(2)}, u32[]{:S(2)}) collective-permute-start(bf16[1024,512]{1,0:T(8,128)(2,1)S(1)} %chunk.9.refs_2_.refs_4_), channel_id=1, source_target_pairs={{2,3},{10,11},{18,19},{26,27}} | collective-permute-start | bytes 3145736 | tf_op jit(solution)/shard_map/ppermute | solution.py:449
  15.3 24.6 %collective-permute-start.8 = (bf16[1024,512]{1,0:T(8,128)(2,1)S(1)}, bf16[1024,512]{1,0:T(8,128)(2,1)S(1)}, u32[]{:S(2)}, u32[]{:S(2)}) collective-permute-start(bf16[1024,512]{1,0:T(8,128)(2,1)S(1)} %chunk.9.refs_2_.refs_4_), channel_id=1, source_target_pairs={{0,2},{2,1},{8,10},{10,9},{16,18},{18,17},{24,26},{26,25}} | collective-permute-start | bytes 3145736 | tf_op jit(solution)/shard_map/ppermute | solution.py:449
  16.1 22.5 %collective-permute-start.6 = (bf16[256,1536]{1,0:T(8,128)(2,1)S(1)}, bf16[256,1536]{1,0:T(8,128)(2,1)S(1)}, u32[]{:S(2)}, u32[]{:S(2)}) collective-permute-start(bf16[256,1536]{1,0:T(8,128)(2,1)S(1)} %add.15.refs_0_), channel_id=1, source_target_pairs={{0,8},{4,20},{8,0},{12,28},{16,24},{20,4},{24,16},{28,12},{1,9},{5... | collective-permute-start | bytes 2359304 | tf_op jit(solution)/shard_map/ppermute | solution.py:538
  25.8 14.3 %collective-permute-start.3 = (bf16[256,1536]{1,0:T(8,128)(2,1)S(1)}, bf16[256,1536]{1,0:T(8,128)(2,1)S(1)}, u32[]{:S(2)}, u32[]{:S(2)}) collective-permute-start(bf16[256,1536]{1,0:T(8,128)(2,1)S(1)} %add.13.refs_0_), channel_id=1, source_target_pairs={{0,16},{8,24},{4,12},{20,28},{1,17},{9,25},{5,13},{21,29},{2,18},{... | collective-permute-start | bytes 2359304 | tf_op jit(solution)/shard_map/ppermute | solution.py:537
  27.7 17.3 %collective-permute-start.13 = (bf16[1024,512]{1,0:T(8,128)(2,1)S(1)}, bf16[1024,512]{1,0:T(8,128)(2,1)S(1)}, u32[]{:S(2)}, u32[]{:S(2)}) collective-permute-start(bf16[1024,512]{1,0:T(8,128)(2,1)S(1)} %chunk.11.refs_2_.refs_7_), channel_id=1, source_target_pairs={{4,6},{6,5},{12,14},{14,13},{20,22},{22,21},{28,30},{30,29}} | collective-permute-start | bytes 3145736 | tf_op jit(solution)/shard_map/ppermute | solution.py:449
  38.6 19.9 %collective-permute-start.12 = (bf16[1024,512]{1,0:T(8,128)(2,1)S(1)}, bf16[1024,512]{1,0:T(8,128)(2,1)S(1)}, u32[]{:S(2)}, u32[]{:S(2)}) collective-permute-start(bf16[1024,512]{1,0:T(8,128)(2,1)S(1)} %chunk.11.refs_2_.refs_7_), channel_id=1, source_target_pairs={{6,7},{14,15},{22,23},{30,31}} | collective-permute-start | bytes 3145736 | tf_op jit(solution)/shard_map/ppermute | solution.py:449
  40.0 19.2 %collective-permute-start.10 = (bf16[256,1536]{1,0:T(8,128)(2,1)S(1)}, bf16[256,1536]{1,0:T(8,128)(2,1)S(1)}, u32[]{:S(2)}, u32[]{:S(2)}) collective-permute-start(bf16[256,1536]{1,0:T(8,128)(2,1)S(1)} %add.16.refs_0_), channel_id=1, source_target_pairs={{0,16},{4,12},{8,24},{12,4},{16,0},{20,28},{24,8},{28,20},{1,17},{... | collective-permute-start | bytes 2359304 | tf_op jit(solution)/shard_map/ppermute | solution.py:538
  40.2 24.7 %copy-start = (bf16[512,512]{1,0:T(8,128)(2,1)S(1)}, bf16[512,512]{1,0:T(8,128)(2,1)}, u32[]{:S(2)}) copy-start(bf16[512,512]{1,0:T(8,128)(2,1)} %refs_0_.1) | copy-start | bytes 1572868
  40.2 20.4 %collective-permute-start.4 = (bf16[256,1536]{1,0:T(8,128)(2,1)S(1)}, bf16[256,1536]{1,0:T(8,128)(2,1)S(1)}, u32[]{:S(2)}, u32[]{:S(2)}) collective-permute-start(bf16[256,1536]{1,0:T(8,128)(2,1)S(1)} %add.14.down_ref), channel_id=1, source_target_pairs={{0,4},{4,0},{8,12},{12,8},{16,20},{20,16},{24,28},{28,24},{1,5},{5... | collective-permute-start | bytes 2359304 | tf_op jit(solution)/shard_map/ppermute | solution.py:540
  44.4 28.6 %collective-permute-start.15 = (bf16[1024,512]{1,0:T(8,128)(2,1)S(1)}, bf16[1024,512]{1,0:T(8,128)(2,1)S(1)}, u32[]{:S(2)}, u32[]{:S(2)}) collective-permute-start(bf16[1024,512]{1,0:T(8,128)(2,1)S(1)} %collective-permute-done.8.refs_3_.refs_6_.refs_0_), channel_id=1, source_target_pairs={{2,1},{10,9},{18,17},{26,25}} | collective-permute-start | bytes 3145736 | tf_op jit(solution)/shard_map/ppermute | solution.py:449
  45.1 27.9 %collective-permute-start.14 = (bf16[1024,512]{1,0:T(8,128)(2,1)S(1)}, bf16[1024,512]{1,0:T(8,128)(2,1)S(1)}, u32[]{:S(2)}, u32[]{:S(2)}) collective-permute-start(bf16[1024,512]{1,0:T(8,128)(2,1)S(1)} %collective-permute-done.8.refs_3_.refs_6_.refs_0_), channel_id=1, source_target_pairs={{2,3},{10,11},{18,19},{26,27}} | collective-permute-start | bytes 3145736 | tf_op jit(solution)/shard_map/ppermute | solution.py:449
  58.4 14.5 %collective-permute-start.17 = (bf16[1024,512]{1,0:T(8,128)(2,1)S(1)}, bf16[1024,512]{1,0:T(8,128)(2,1)S(1)}, u32[]{:S(2)}, u32[]{:S(2)}) collective-permute-start(bf16[1024,512]{1,0:T(8,128)(2,1)S(1)} %collective-permute-done.13.refs_9_.refs_3_), channel_id=1, source_target_pairs={{6,5},{14,13},{22,21},{30,29}} | collective-permute-start | bytes 3145736 | tf_op jit(solution)/shard_map/ppermute | solution.py:449
  59.2 17.4 %collective-permute-start.16 = (bf16[1024,512]{1,0:T(8,128)(2,1)S(1)}, bf16[1024,512]{1,0:T(8,128)(2,1)S(1)}, u32[]{:S(2)}, u32[]{:S(2)}) collective-permute-start(bf16[1024,512]{1,0:T(8,128)(2,1)S(1)} %collective-permute-done.13.refs_9_.refs_3_), channel_id=1, source_target_pairs={{6,7},{14,15},{22,23},{30,31}} | collective-permute-start | bytes 3145736 | tf_op jit(solution)/shard_map/ppermute | solution.py:449
  60.6 4.3 %collective-permute-start.11 = (bf16[256,1536]{1,0:T(8,128)(2,1)S(1)}, bf16[256,1536]{1,0:T(8,128)(2,1)S(1)}, u32[]{:S(2)}, u32[]{:S(2)}) collective-permute-start(bf16[256,1536]{1,0:T(8,128)(2,1)S(1)} %add.17.refs_1_), channel_id=1, source_target_pairs={{0,4},{4,0},{8,12},{12,8},{16,20},{20,16},{24,28},{28,24},{1,5},{5... | collective-permute-start | bytes 2359304 | tf_op jit(solution)/shard_map/ppermute | solution.py:542

commit v15 on v13

--- a/solution.py
+++ b/solution.py
@@ -13,7 +13,7 @@
 DOWN_WEIGHTS, DOWN_AFTER = (0, 20), ((1, 0), (0, 0))
 PIECES = 2
 PICK_BLOCK, UPDATE_BLOCK = 256, 512
-COPIES = 4
+COPIES = 8
 F32, BF16 = jnp.float32, jnp.bfloat16
 VMEM = pl.BlockSpec(memory_space=pltpu.VMEM)
 ANY = pl.BlockSpec(memory_space=pl.ANY)

time: 80.9 us -> 82.5 us (1.020)
  Pallas kernels: 27.2 us -> 28.9 us
    pallas_call x1, Pallas kernels: 3.87 us -> 5.22 us  [finish(): pl.pallas_call(functools.partial(finish_kernel, first_row, len(received),...]
where the time goes in v15:
time: 82.5 us; the launch traced here: 82 us
  waiting for transfers between devices  33.7 us (41%)
  Pallas kernels  28.9 us (35%)
  starting transfers between devices  18.8 us (23%)
    ppermute x10, waiting for transfers between devices, move(): return lax.ppermute(value, ('prow', 'pcol'), pairs)  16.3 us
    ppermute x2, waiting for transfers between devices, per_device(): up_got = [lax.ppermute(up[0], 'prow', swap_pairs(n_prow, orders, step))]  10.1 us
    ppermute x10, starting transfers between devices, move(): return lax.ppermute(value, ('prow', 'pcol'), pairs)  8.37 us
    pallas_call x1, Pallas kernels, update(): pl.pallas_call(functools.partial(update_kernel, first_row, len(received),...  8.13 us
    ppermute x2, waiting for transfers between devices, per_device(): down_got = lax.ppermute(down, 'prow', grow_pairs(orders, step))  7.3 us
    pallas_call x1, Pallas kernels, pick(): pl.pallas_call(pick_kernel, in_specs=[SMEM, VMEM, ANY] + [ANY] * len(afte...  6.16 us
    pallas_call x1, Pallas kernels, finish(): pl.pallas_call(functools.partial(finish_kernel, first_row, len(received),...  5.22 us
    pallas_call x6, Pallas kernels, chunk(): pl.pallas_call(functools.partial(chunk_kernel, first_row, axis, core), in...  4.68 us
  transfers between devices with their start and end apart: 18, of which 4 were waited for; matrix products, arithmetic and copies ran while one was open for 0% of the time, Pallas kernels for 28%

profile of v15, /device:TPU:29, one launch (start us, length us, event | category | flops | bytes accessed | tf_op | source)
XLA Modules:
  0.0 82.0 jit_solution(17889857756662465084)
XLA Ops:
  0.1 0.6 chunk.8
  0.7 0.7 collective-permute-start.2
  1.5 1.5 %chunk.6 = bf16[256,1536]{1,0:T(8,128)(2,1)} custom-call(s32[4]{0:T(128)S(1)} %pad_add_fusion.place_ref, bf16[2048,1536]{1,0:T(8,128)(2,1)} %matrix_ref.19), custom_call_target="tpu_custom_call" | custom-call | tf_op jit(solution)/shard_map/chunk/pallas_call | solution.py:62
  3.0 0.7 collective-permute-start
  3.7 0.1 copy.8.pivots_ref
  3.9 6.2 %pick_rows.1 = (bf16[256,1536]{1,0:T(8,128)(2,1)S(1)}, bf16[256,1536]{1,0:T(8,128)(2,1)S(1)}) custom-call(s32[4]{0:T(128)S(1)} %pad_add_fusion.place_ref, s32[512,1]{1,0:T(8,128)S(1)} %copy.8.pivots_ref, bf16[2048,1536]{1,0:T(8,128)(2,1)} %matrix_ref.19), custom_call_target="tpu_custom_call" | custom-call | tf_op jit(solution)/shard_map/pick_rows/pallas_call | solution.py:112
  10.1 0.7 collective-permute-start.5
  10.8 0.6 chunk.10
  11.4 0.7 collective-permute-start.7
  12.2 0.6 chunk.7.refs_0_
  12.8 1.3 %collective-permute-start.1 = (bf16[256,1536]{1,0:T(8,128)(2,1)S(1)}, bf16[256,1536]{1,0:T(8,128)(2,1)S(1)}, u32[]{:S(2)}, u32[]{:S(2)}) collective-permute-start(bf16[256,1536]{1,0:T(8,128)(2,1)S(1)} %chunk.7.refs_0_), channel_id=1, source_target_pairs={{0,8},{4,20},{1,9},{5,21},{2,10},{6,22},{3,11},{7,23}} | collective-permute-start | bytes 2359304 | tf_op jit(solution)/shard_map/ppermute | solution.py:532
  14.1 0.6 chunk.9.refs_2_.refs_4_
  14.8 0.7 collective-permute-start.9
  15.5 0.7 collective-permute-start.8
  16.4 2.2 %collective-permute-start.6 = (bf16[256,1536]{1,0:T(8,128)(2,1)S(1)}, bf16[256,1536]{1,0:T(8,128)(2,1)S(1)}, u32[]{:S(2)}, u32[]{:S(2)}) collective-permute-start(bf16[256,1536]{1,0:T(8,128)(2,1)S(1)} %add.15.refs_0_), channel_id=1, source_target_pairs={{0,8},{4,20},{8,0},{12,28},{16,24},{20,4},{24,16},{28,12},{1,9},{5... | collective-permute-start | bytes 2359304 | tf_op jit(solution)/shard_map/ppermute | solution.py:533
  18.6 7.3 %collective-permute-done.1.refs_1_ = bf16[256,1536]{1,0:T(8,128)(2,1)S(1)} collective-permute-done((bf16[256,1536]{1,0:T(8,128)(2,1)S(1)}, bf16[256,1536]{1,0:T(8,128)(2,1)S(1)}, u32[]{:S(2)}, u32[]{:S(2)}) %collective-permute-start.1) | collective-permute-done | bytes 786464 | tf_op jit(solution)/shard_map/ppermute | solution.py:532
  26.0 1.3 %collective-permute-start.3 = (bf16[256,1536]{1,0:T(8,128)(2,1)S(1)}, bf16[256,1536]{1,0:T(8,128)(2,1)S(1)}, u32[]{:S(2)}, u32[]{:S(2)}) collective-permute-start(bf16[256,1536]{1,0:T(8,128)(2,1)S(1)} %add.13.refs_0_), channel_id=1, source_target_pairs={{0,16},{8,24},{4,12},{20,28},{1,17},{9,25},{5,13},{21,29},{2,18},{... | collective-permute-start | bytes 2359304 | tf_op jit(solution)/shard_map/ppermute | solution.py:532
  27.3 0.6 chunk.11.refs_2_.refs_7_
  28.0 0.7 collective-permute-start.13
  28.7 10.1 %collective-permute-done.6.refs_1_ = bf16[256,1536]{1,0:T(8,128)(2,1)S(1)} collective-permute-done((bf16[256,1536]{1,0:T(8,128)(2,1)S(1)}, bf16[256,1536]{1,0:T(8,128)(2,1)S(1)}, u32[]{:S(2)}, u32[]{:S(2)}) %collective-permute-start.6) | collective-permute-done | bytes 786464 | tf_op jit(solution)/shard_map/ppermute | solution.py:533
  38.8 1.3 %collective-permute-start.12 = (bf16[1024,512]{1,0:T(8,128)(2,1)S(1)}, bf16[1024,512]{1,0:T(8,128)(2,1)S(1)}, u32[]{:S(2)}, u32[]{:S(2)}) collective-permute-start(bf16[1024,512]{1,0:T(8,128)(2,1)S(1)} %chunk.11.refs_2_.refs_7_), channel_id=1, source_target_pairs={{6,7},{14,15},{22,23},{30,31}} | collective-permute-start | bytes 3145736 | tf_op jit(solution)/shard_map/ppermute | solution.py:444
  40.4 4.1 %collective-permute-start.4 = (bf16[256,1536]{1,0:T(8,128)(2,1)S(1)}, bf16[256,1536]{1,0:T(8,128)(2,1)S(1)}, u32[]{:S(2)}, u32[]{:S(2)}) collective-permute-start(bf16[256,1536]{1,0:T(8,128)(2,1)S(1)} %add.14.down_ref), channel_id=1, source_target_pairs={{0,4},{4,0},{8,12},{12,8},{16,20},{20,16},{24,28},{28,24},{1,5},{5... | collective-permute-start | bytes 2359304 | tf_op jit(solution)/shard_map/ppermute | solution.py:535
  44.5 0.7 collective-permute-start.15
  45.2 0.7 collective-permute-start.14
  45.9 12.8 %collective-permute-done.12.refs_8_ = bf16[1024,512]{1,0:T(8,128)(2,1)S(1)} collective-permute-done((bf16[1024,512]{1,0:T(8,128)(2,1)S(1)}, bf16[1024,512]{1,0:T(8,128)(2,1)S(1)}, u32[]{:S(2)}, u32[]{:S(2)}) %collective-permute-start.12) | collective-permute-done | bytes 1048608 | tf_op jit(solution)/shard_map/ppermute | solution.py:444
  58.8 0.7 collective-permute-start.17
  59.5 1.3 %collective-permute-start.16 = (bf16[1024,512]{1,0:T(8,128)(2,1)S(1)}, bf16[1024,512]{1,0:T(8,128)(2,1)S(1)}, u32[]{:S(2)}, u32[]{:S(2)}) collective-permute-start(bf16[1024,512]{1,0:T(8,128)(2,1)S(1)} %collective-permute-done.13.refs_9_.refs_3_), channel_id=1, source_target_pairs={{6,7},{14,15},{22,23},{30,31}} | collective-permute-start | bytes 3145736 | tf_op jit(solution)/shard_map/ppermute | solution.py:444
  60.8 0.1 add.17.refs_1_
  61.0 4.2 %swap_rows.1.swapped_ref = bf16[1024,1536]{1,0:T(8,128)(2,1)S(1)} custom-call(s32[4]{0:T(128)S(1)} %pad_add_fusion.place_ref, s32[1,512]{1,0:T(1,128)S(1)} %bitcast.5, bf16[2048,1536]{1,0:T(8,128)(2,1)} %matrix_ref.19, bf16[256,1536]{1,0:T(8,128)(2,1)S(1)} %add.14.down_ref, bf16[256,1536]{1,0:T(8,128)(2,1)S(1)} %collective-permute-done.4.down_got_ref), custom_call_target="tpu_custom_call" | custom-call | tf_op jit(solution)/shard_map/swap_rows/pallas_call | solution.py:331
  65.2 8.1 %update_rows.1 = (bf16[2048,1536]{1,0:T(8,128)(2,1)}, bf16[512,1536]{1,0:T(8,128)(2,1)S(1)}) custom-call(s32[4]{0:T(128)S(1)} %pad_add_fusion.place_ref, s32[1,512]{1,0:T(1,128)S(1)} %bitcast.6, bf16[2048,1536]{1,0:T(8,128)(2,1)} %matrix_ref.19, bf16[256,1536]{1,0:T(8,128)(2,1)S(1)} %add.14.down_ref, ...), custom_call_target="tpu_custom_call" | custom-call | tf_op jit(solution)/shard_map/update_rows/pallas_call | solution.py:262
  73.4 3.4 %collective-permute-done.16.refs_4_ = bf16[1024,512]{1,0:T(8,128)(2,1)S(1)} collective-permute-done((bf16[1024,512]{1,0:T(8,128)(2,1)S(1)}, bf16[1024,512]{1,0:T(8,128)(2,1)S(1)}, u32[]{:S(2)}, u32[]{:S(2)}) %collective-permute-start.16) | collective-permute-done | bytes 1048608 | tf_op jit(solution)/shard_map/ppermute | solution.py:444
  76.8 5.2 %finish_rows.1 = bf16[2048,1536]{1,0:T(8,128)(2,1)} custom-call(s32[4]{0:T(128)S(1)} %pad_add_fusion.place_ref, bf16[2048,1536]{1,0:T(8,128)(2,1)} %matrix_ref.19, bf16[1024,1536]{1,0:T(8,128)(2,1)S(1)} %swap_rows.1.swapped_ref, bf16[512,1536]{1,0:T(8,128)(2,1)S(1)} %get-tuple-element.11.upper_ref, ...), custom_call_target="tpu_custom_call", output_to_operand_aliasing={{}: (10, {})} | custom-call | tf_op jit(solution)/shard_map/finish_rows/pallas_call | solution.py:410
  (27 shorter events, 0.7 us)
Async XLA Ops:
  0.1 3.6 %copy-start.1 = (s32[512]{0:T(512)S(1)}, s32[512]{0:T(512)}, u32[]{:S(2)}) copy-start(s32[512]{0:T(512)} %param.4) | copy-start | bytes 6148
  0.7 13.4 %collective-permute-start.2 = (bf16[1024,512]{1,0:T(8,128)(2,1)S(1)}, bf16[1024,512]{1,0:T(8,128)(2,1)S(1)}, u32[]{:S(2)}, u32[]{:S(2)}) collective-permute-start(bf16[1024,512]{1,0:T(8,128)(2,1)S(1)} %chunk.8), channel_id=1, source_target_pairs={{0,2},{8,10},{16,18},{24,26}} | collective-permute-start | bytes 3145736 | tf_op jit(solution)/shard_map/ppermute | solution.py:444
  3.0 9.2 %collective-permute-start = (bf16[256,1536]{1,0:T(8,128)(2,1)}, bf16[256,1536]{1,0:T(8,128)(2,1)S(1)}, u32[]{:S(2)}, u32[]{:S(2)}) collective-permute-start(bf16[256,1536]{1,0:T(8,128)(2,1)} %chunk.6), channel_id=1, source_target_pairs={{0,4},{1,5},{2,6},{3,7}} | collective-permute-start | bytes 2359304 | tf_op jit(solution)/shard_map/ppermute | solution.py:523
  10.1 6.2 %collective-permute-start.5 = (bf16[256,1536]{1,0:T(8,128)(2,1)S(1)}, bf16[256,1536]{1,0:T(8,128)(2,1)S(1)}, u32[]{:S(2)}, u32[]{:S(2)}) collective-permute-start(bf16[256,1536]{1,0:T(8,128)(2,1)S(1)} %get-tuple-element.10), channel_id=1, source_target_pairs={{0,4},{4,0},{8,12},{12,8},{16,20},{20,16},{24,28},{28,24},{1,5},{5... | collective-permute-start | bytes 2359304 | tf_op jit(solution)/shard_map/ppermute | solution.py:527
  11.4 15.9 %collective-permute-start.7 = (bf16[1024,512]{1,0:T(8,128)(2,1)S(1)}, bf16[1024,512]{1,0:T(8,128)(2,1)S(1)}, u32[]{:S(2)}, u32[]{:S(2)}) collective-permute-start(bf16[1024,512]{1,0:T(8,128)(2,1)S(1)} %chunk.10), channel_id=1, source_target_pairs={{4,6},{12,14},{20,22},{28,30}} | collective-permute-start | bytes 3145736 | tf_op jit(solution)/shard_map/ppermute | solution.py:444
  12.8 13.0 %collective-permute-start.1 = (bf16[256,1536]{1,0:T(8,128)(2,1)S(1)}, bf16[256,1536]{1,0:T(8,128)(2,1)S(1)}, u32[]{:S(2)}, u32[]{:S(2)}) collective-permute-start(bf16[256,1536]{1,0:T(8,128)(2,1)S(1)} %chunk.7.refs_0_), channel_id=1, source_target_pairs={{0,8},{4,20},{1,9},{5,21},{2,10},{6,22},{3,11},{7,23}} | collective-permute-start | bytes 2359304 | tf_op jit(solution)/shard_map/ppermute | solution.py:532
  14.8 25.3 %collective-permute-start.9 = (bf16[1024,512]{1,0:T(8,128)(2,1)S(1)}, bf16[1024,512]{1,0:T(8,128)(2,1)S(1)}, u32[]{:S(2)}, u32[]{:S(2)}) collective-permute-start(bf16[1024,512]{1,0:T(8,128)(2,1)S(1)} %chunk.9.refs_2_.refs_4_), channel_id=1, source_target_pairs={{2,3},{10,11},{18,19},{26,27}} | collective-permute-start | bytes 3145736 | tf_op jit(solution)/shard_map/ppermute | solution.py:444
  15.5 24.6 %collective-permute-start.8 = (bf16[1024,512]{1,0:T(8,128)(2,1)S(1)}, bf16[1024,512]{1,0:T(8,128)(2,1)S(1)}, u32[]{:S(2)}, u32[]{:S(2)}) collective-permute-start(bf16[1024,512]{1,0:T(8,128)(2,1)S(1)} %chunk.9.refs_2_.refs_4_), channel_id=1, source_target_pairs={{0,2},{2,1},{8,10},{10,9},{16,18},{18,17},{24,26},{26,25}} | collective-permute-start | bytes 3145736 | tf_op jit(solution)/shard_map/ppermute | solution.py:444
  16.4 22.4 %collective-permute-start.6 = (bf16[256,1536]{1,0:T(8,128)(2,1)S(1)}, bf16[256,1536]{1,0:T(8,128)(2,1)S(1)}, u32[]{:S(2)}, u32[]{:S(2)}) collective-permute-start(bf16[256,1536]{1,0:T(8,128)(2,1)S(1)} %add.15.refs_0_), channel_id=1, source_target_pairs={{0,8},{4,20},{8,0},{12,28},{16,24},{20,4},{24,16},{28,12},{1,9},{5... | collective-permute-start | bytes 2359304 | tf_op jit(solution)/shard_map/ppermute | solution.py:533
  26.0 14.3 %collective-permute-start.3 = (bf16[256,1536]{1,0:T(8,128)(2,1)S(1)}, bf16[256,1536]{1,0:T(8,128)(2,1)S(1)}, u32[]{:S(2)}, u32[]{:S(2)}) collective-permute-start(bf16[256,1536]{1,0:T(8,128)(2,1)S(1)} %add.13.refs_0_), channel_id=1, source_target_pairs={{0,16},{8,24},{4,12},{20,28},{1,17},{9,25},{5,13},{21,29},{2,18},{... | collective-permute-start | bytes 2359304 | tf_op jit(solution)/shard_map/ppermute | solution.py:532
  28.0 17.2 %collective-permute-start.13 = (bf16[1024,512]{1,0:T(8,128)(2,1)S(1)}, bf16[1024,512]{1,0:T(8,128)(2,1)S(1)}, u32[]{:S(2)}, u32[]{:S(2)}) collective-permute-start(bf16[1024,512]{1,0:T(8,128)(2,1)S(1)} %chunk.11.refs_2_.refs_7_), channel_id=1, source_target_pairs={{4,6},{6,5},{12,14},{14,13},{20,22},{22,21},{28,30},{30,29}} | collective-permute-start | bytes 3145736 | tf_op jit(solution)/shard_map/ppermute | solution.py:444
  38.8 20.0 %collective-permute-start.12 = (bf16[1024,512]{1,0:T(8,128)(2,1)S(1)}, bf16[1024,512]{1,0:T(8,128)(2,1)S(1)}, u32[]{:S(2)}, u32[]{:S(2)}) collective-permute-start(bf16[1024,512]{1,0:T(8,128)(2,1)S(1)} %chunk.11.refs_2_.refs_7_), channel_id=1, source_target_pairs={{6,7},{14,15},{22,23},{30,31}} | collective-permute-start | bytes 3145736 | tf_op jit(solution)/shard_map/ppermute | solution.py:444
  40.2 19.3 %collective-permute-start.10 = (bf16[256,1536]{1,0:T(8,128)(2,1)S(1)}, bf16[256,1536]{1,0:T(8,128)(2,1)S(1)}, u32[]{:S(2)}, u32[]{:S(2)}) collective-permute-start(bf16[256,1536]{1,0:T(8,128)(2,1)S(1)} %add.16.refs_0_), channel_id=1, source_target_pairs={{0,16},{4,12},{8,24},{12,4},{16,0},{20,28},{24,8},{28,20},{1,17},{... | collective-permute-start | bytes 2359304 | tf_op jit(solution)/shard_map/ppermute | solution.py:533
  40.4 24.8 %copy-start = (bf16[512,512]{1,0:T(8,128)(2,1)S(1)}, bf16[512,512]{1,0:T(8,128)(2,1)}, u32[]{:S(2)}) copy-start(bf16[512,512]{1,0:T(8,128)(2,1)} %refs_0_.1) | copy-start | bytes 1572868
  40.4 20.5 %collective-permute-start.4 = (bf16[256,1536]{1,0:T(8,128)(2,1)S(1)}, bf16[256,1536]{1,0:T(8,128)(2,1)S(1)}, u32[]{:S(2)}, u32[]{:S(2)}) collective-permute-start(bf16[256,1536]{1,0:T(8,128)(2,1)S(1)} %add.14.down_ref), channel_id=1, source_target_pairs={{0,4},{4,0},{8,12},{12,8},{16,20},{20,16},{24,28},{28,24},{1,5},{5... | collective-permute-start | bytes 2359304 | tf_op jit(solution)/shard_map/ppermute | solution.py:535
  44.5 28.9 %collective-permute-start.15 = (bf16[1024,512]{1,0:T(8,128)(2,1)S(1)}, bf16[1024,512]{1,0:T(8,128)(2,1)S(1)}, u32[]{:S(2)}, u32[]{:S(2)}) collective-permute-start(bf16[1024,512]{1,0:T(8,128)(2,1)S(1)} %collective-permute-done.8.refs_3_.refs_6_.refs_0_), channel_id=1, source_target_pairs={{2,1},{10,9},{18,17},{26,25}} | collective-permute-start | bytes 3145736 | tf_op jit(solution)/shard_map/ppermute | solution.py:444
  45.2 28.2 %collective-permute-start.14 = (bf16[1024,512]{1,0:T(8,128)(2,1)S(1)}, bf16[1024,512]{1,0:T(8,128)(2,1)S(1)}, u32[]{:S(2)}, u32[]{:S(2)}) collective-permute-start(bf16[1024,512]{1,0:T(8,128)(2,1)S(1)} %collective-permute-done.8.refs_3_.refs_6_.refs_0_), channel_id=1, source_target_pairs={{2,3},{10,11},{18,19},{26,27}} | collective-permute-start | bytes 3145736 | tf_op jit(solution)/shard_map/ppermute | solution.py:444
  58.8 14.6 %collective-permute-start.17 = (bf16[1024,512]{1,0:T(8,128)(2,1)S(1)}, bf16[1024,512]{1,0:T(8,128)(2,1)S(1)}, u32[]{:S(2)}, u32[]{:S(2)}) collective-permute-start(bf16[1024,512]{1,0:T(8,128)(2,1)S(1)} %collective-permute-done.13.refs_9_.refs_3_), channel_id=1, source_target_pairs={{6,5},{14,13},{22,21},{30,29}} | collective-permute-start | bytes 3145736 | tf_op jit(solution)/shard_map/ppermute | solution.py:444
  59.5 17.3 %collective-permute-start.16 = (bf16[1024,512]{1,0:T(8,128)(2,1)S(1)}, bf16[1024,512]{1,0:T(8,128)(2,1)S(1)}, u32[]{:S(2)}, u32[]{:S(2)}) collective-permute-start(bf16[1024,512]{1,0:T(8,128)(2,1)S(1)} %collective-permute-done.13.refs_9_.refs_3_), channel_id=1, source_target_pairs={{6,7},{14,15},{22,23},{30,31}} | collective-permute-start | bytes 3145736 | tf_op jit(solution)/shard_map/ppermute | solution.py:444
  60.9 4.3 %collective-permute-start.11 = (bf16[256,1536]{1,0:T(8,128)(2,1)S(1)}, bf16[256,1536]{1,0:T(8,128)(2,1)S(1)}, u32[]{:S(2)}, u32[]{:S(2)}) collective-permute-start(bf16[256,1536]{1,0:T(8,128)(2,1)S(1)} %add.17.refs_1_), channel_id=1, source_target_pairs={{0,4},{4,0},{8,12},{12,8},{16,20},{20,16},{24,28},{28,24},{1,5},{5... | collective-permute-start | bytes 2359304 | tf_op jit(solution)/shard_map/ppermute | solution.py:537
